TPU v7x, 32 devices: a whole 2x2x4 slice. The times are simulated.
32 devices in a mesh: rep: 2 (over y), yz: 4 (over z), gx: 4 (over x, core).
Axes of the slice: x: 2, y: 2, z: 4, core: 2. Of those that a mesh axis runs over, the one named last changes fastest.
Arguments:
- saved_input: bfloat16 [8192, 9, 128], P(('rep', 'yz', 'gx')), parts along dimension 0, may hold values from -6 to 6
- cotangent: bfloat16 [4096, 9, 128], P(('rep', 'yz', 'gx')), parts along dimension 0, may hold values from -6 to 6
- neighbours: int32 [4096, 8], P(('rep', 'yz', 'gx')), parts along dimension 0, may hold values from 0 to 255
- rot_zero: float32 [32768], P(('rep', 'yz', 'gx')), parts along dimension 0, may hold values from -4 to 4
- rot_one: float32 [3, 3, 32768], P(None, None, ('rep', 'yz', 'gx')), parts along dimension 2, may hold values from -3 to 3
- rot_two: float32 [5, 5, 32768], P(None, None, ('rep', 'yz', 'gx')), parts along dimension 2, may hold values from -2.5 to 2.5
- send_index: int32 [128, 32], P(('rep', 'yz', 'gx')), parts along dimension 0, may hold values from 0 to 127
- atom_class: int32 [4096], P(('rep', 'yz', 'gx')), parts along dimension 0, may hold values from 0 to 1
- live_blocks: int32 [32], P(('rep', 'yz', 'gx')), parts along dimension 0, may hold values from 1 to 2, as said below
- merge_coef: float32 [2, 32], replicated, may hold values from 0.05 to 0.3
- experts: bfloat16 [32, 278528], P(None, 'yz'), may hold values from -0.375 to 0.375
Outputs:
- input_grad: bfloat16 [4096, 9, 128], P(('rep', 'yz', 'gx')), parts along dimension 0
- expert_grad: float32 [64, 278528], P(('rep', 'gx'), 'yz'), parts along dimension 0
There are 2 independent parts, one for each index of `rep`. A program takes and returns all parts, laid end to end along the dimension named above; an argument that names none is the same for every part. Nothing has to cross between parts.
Inputs may be any that keep to these rules, and one draw needn't show every extreme that they name: `neighbours`: rows of the tile's own block: below 128 its atoms, the rest its ghosts. `send_index`: own atom slots of the tile; repeats may occur. Tile t's live atoms are slots 0 to 64 * live_blocks[t] - 1; in every draw some tile has all 2 blocks live.
All inputs are finite; a program needn't handle non-finite values.
Results may differ from a plain program's by a relative error of at most 0.0065.
Values may be sent and summed in bfloat16 or wider, within the bound.
No kernel may reach another device: no remote copies, remote signals or barrier semaphores. Data moves between devices by JAX's collectives and lax.ppermute only.
A program may use at most 128 MiB of HBM per device.

v0:
```python
import math

import jax
import jax.numpy as jnp
from jax import lax
from jax.sharding import PartitionSpec as P

ATOM_BLOCK = 64


highest = lax.Precision.HIGHEST
zero_rows = (0, 2, 6)
pair_rows = (3, 7, 1, 5)


def extended(cells, sides, width):
    for axis, dim in sides:
        count = lax.axis_size(axis)
        head = lax.slice_in_dim(cells, 0, width, axis=dim)
        tail = lax.slice_in_dim(cells, cells.shape[dim] - width, cells.shape[dim], axis=dim)
        cells = jnp.concatenate(
            [
                lax.ppermute(tail, axis, [(i, (i + 1) % count) for i in range(count)]),
                cells,
                lax.ppermute(head, axis, [((i + 1) % count, i) for i in range(count)]),
            ],
            axis=dim,
        )
    return cells


def rotate(field, turn_zero, turn_one, turn_two):
    first_part = turn_zero[:, None, None] * field[:, 0:1]
    second_part = jnp.einsum("abe,ebc->eac", turn_one, field[:, 1:4], precision=highest)
    third_part = jnp.einsum("abe,ebc->eac", turn_two, field[:, 4:9], precision=highest)
    return jnp.concatenate([first_part, second_part, third_part], axis=1)


def rotate_back(field, turn_zero, turn_one, turn_two):
    first_part = turn_zero[:, None, None] * field[:, 0:1]
    second_part = jnp.einsum("bae,ebc->eac", turn_one, field[:, 1:4], precision=highest)
    third_part = jnp.einsum("bae,ebc->eac", turn_two, field[:, 4:9], precision=highest)
    return jnp.concatenate([first_part, second_part, third_part], axis=1)


def pick_rows(field, positions):
    return jnp.concatenate([field[:, position] for position in positions], axis=1)


def class_weights(merged, channels):
    zero_width = 3 * channels
    pair_width = 2 * channels
    zero_parts = []
    pair_parts = []
    for member in range(merged.shape[0]):
        vector = merged[member]
        zero_parts.append(vector[: zero_width * zero_width].reshape(zero_width, zero_width))
        coupled = vector[
            zero_width * zero_width : zero_width * zero_width + pair_width * pair_width
        ].reshape(pair_width, pair_width)
        crossed = vector[zero_width * zero_width + pair_width * pair_width :].reshape(
            pair_width, pair_width
        )
        top_rows = jnp.concatenate([coupled, crossed], axis=1)
        bottom_rows = jnp.concatenate([-crossed, coupled], axis=1)
        pair_parts.append(jnp.concatenate([top_rows, bottom_rows], axis=0))
    return (jnp.concatenate(zero_parts, axis=1), jnp.concatenate(pair_parts, axis=1))


def class_gradients(grad_zero, grad_pair, channels):
    zero_width = 3 * channels
    pair_width = 2 * channels
    members = grad_zero.shape[1] // zero_width
    vectors = []
    for member in range(members):
        zero_part = grad_zero[:, member * zero_width : (member + 1) * zero_width]
        pair_block = grad_pair[:, member * 2 * pair_width : (member + 1) * 2 * pair_width]
        coupled = pair_block[:pair_width, :pair_width] + pair_block[pair_width:, pair_width:]
        crossed = pair_block[:pair_width, pair_width:] - pair_block[pair_width:, :pair_width]
        vectors.append(
            jnp.concatenate([zero_part.reshape(-1), coupled.reshape(-1), crossed.reshape(-1)])
        )
    return jnp.stack(vectors)


def edge_terms(
    sources, targets, turn_zero, turn_one, turn_two, class_mask, zero_weight, pair_weight, fanout
):
    channels = sources.shape[2]
    rotated = rotate(sources.astype(jnp.float32), turn_zero, turn_one, turn_two).astype(
        jnp.bfloat16
    )
    pulled = (
        rotate(targets.astype(jnp.float32), turn_zero, turn_one, turn_two) / math.sqrt(fanout)
    ).astype(jnp.bfloat16)
    masks = class_mask.astype(jnp.bfloat16)
    members = class_mask.shape[1]
    zero_in = pick_rows(rotated, zero_rows)
    pair_in = pick_rows(rotated, pair_rows)
    zero_pulled = pick_rows(pulled, zero_rows)
    pair_pulled = pick_rows(pulled, pair_rows)
    zero_out = jnp.concatenate(
        [zero_pulled * masks[:, member : member + 1] for member in range(members)], axis=1
    )
    pair_out = jnp.concatenate(
        [pair_pulled * masks[:, member : member + 1] for member in range(members)], axis=1
    )
    over_edges = (((0,), (0,)), ((), ()))
    over_last = (((1,), (1,)), ((), ()))
    grad_zero = lax.dot_general(zero_in, zero_out, over_edges, preferred_element_type=jnp.float32)
    grad_pair = lax.dot_general(pair_in, pair_out, over_edges, preferred_element_type=jnp.float32)
    back_zero = lax.dot_general(
        zero_out, zero_weight, over_last, preferred_element_type=jnp.float32
    )
    back_pair = lax.dot_general(
        pair_out, pair_weight, over_last, preferred_element_type=jnp.float32
    )
    empty_part = jnp.zeros_like(back_zero[:, :channels])
    pieces = [empty_part] * 9
    for position, component in enumerate(zero_rows):
        pieces[component] = back_zero[:, position * channels : (position + 1) * channels]
    for position, component in enumerate(pair_rows):
        pieces[component] = back_pair[:, position * channels : (position + 1) * channels]
    turned = rotate_back(jnp.stack(pieces, axis=1), turn_zero, turn_one, turn_two)
    return (turned, grad_zero, grad_pair)


def local(
    saved_input,
    cotangent,
    neighbours,
    rot_zero,
    rot_one,
    rot_two,
    send_index,
    atom_class,
    live_blocks,
    merge_coef,
    experts,
):
    channels = cotangent.shape[2]
    fanout = neighbours.shape[1]
    atoms_here = cotangent.shape[0]
    members = merge_coef.shape[0]
    face_rows = send_index.shape[1]
    partial_merge = jnp.dot(merge_coef, experts.astype(jnp.float32), precision=highest).astype(
        jnp.bfloat16
    )
    merged = lax.all_gather(partial_merge, "yz", axis=1, tiled=True)
    zero_weight, pair_weight = class_weights(merged, channels)
    edge_count = ATOM_BLOCK * fanout
    member_ids = jnp.arange(members, dtype=jnp.int32)

    def block_step(block, state):
        grad_ext, grad_zero, grad_pair = state
        offset = block * ATOM_BLOCK
        source_rows = lax.dynamic_slice_in_dim(neighbours, offset, ATOM_BLOCK, 0).reshape(-1)
        targets = jnp.repeat(
            lax.dynamic_slice_in_dim(cotangent, offset, ATOM_BLOCK, 0), fanout, axis=0
        )
        classes_here = lax.dynamic_slice_in_dim(atom_class, offset, ATOM_BLOCK, 0)
        class_mask = jnp.repeat(
            (classes_here[:, None] == member_ids[None, :]).astype(jnp.float32), fanout, axis=0
        )
        edge_offset = offset * fanout
        turn_zero = lax.dynamic_slice_in_dim(rot_zero, edge_offset, edge_count, 0)
        turn_one = lax.dynamic_slice_in_dim(rot_one, edge_offset, edge_count, 2)
        turn_two = lax.dynamic_slice_in_dim(rot_two, edge_offset, edge_count, 2)
        turned, block_zero, block_pair = edge_terms(
            saved_input[source_rows],
            targets,
            turn_zero,
            turn_one,
            turn_two,
            class_mask,
            zero_weight,
            pair_weight,
            fanout,
        )
        return (
            grad_ext.at[source_rows].add(turned),
            grad_zero + block_zero,
            grad_pair + block_pair,
        )

    start_state = (
        jnp.zeros((saved_input.shape[0], 9, channels), jnp.float32),
        jnp.zeros((3 * channels, members * 3 * channels), jnp.float32),
        jnp.zeros((4 * channels, members * 4 * channels), jnp.float32),
    )
    grad_ext, grad_zero, grad_pair = lax.fori_loop(0, live_blocks[0], block_step, start_state)
    flattened = class_gradients(grad_zero, grad_pair, channels)
    summed_all = lax.psum(flattened, ("yz", "gx"))
    slice_width = flattened.shape[1] // lax.axis_size("yz")
    summed = lax.dynamic_slice_in_dim(
        summed_all, lax.axis_index("yz") * slice_width, slice_width, 1
    )
    ghosts = grad_ext[atoms_here:].reshape(4, face_rows, 9, channels)
    along_x = extended(ghosts[0:2].astype(jnp.bfloat16), (("gx", 0),), 1).astype(jnp.float32)
    along_yz = extended(ghosts[2:4].astype(jnp.bfloat16), (("yz", 0),), 1).astype(jnp.float32)
    returned = jnp.concatenate([along_x[0], along_x[3], along_yz[0], along_yz[3]], axis=0)
    input_grad = grad_ext[:atoms_here].at[send_index.reshape(-1)].add(returned).astype(jnp.bfloat16)
    per_owner = merge_coef.shape[1] // lax.axis_size("gx")
    owned_coef = lax.dynamic_slice_in_dim(
        merge_coef, lax.axis_index("gx") * per_owner, per_owner, 1
    )
    atoms_all = atoms_here * lax.axis_size("yz") * lax.axis_size("gx")
    grad_scale = math.sqrt(fanout / atoms_all)
    expert_grad = grad_scale * lax.dot_general(
        owned_coef, summed, (((0,), (0,)), ((), ())), precision=highest
    )
    return (input_grad, expert_grad)


def solution(mesh):
    in_specs = (
        P(("rep", "yz", "gx"), None, None),
        P(("rep", "yz", "gx"), None, None),
        P(("rep", "yz", "gx"), None),
        P(("rep", "yz", "gx")),
        P(None, None, ("rep", "yz", "gx")),
        P(None, None, ("rep", "yz", "gx")),
        P(("rep", "yz", "gx"), None),
        P(("rep", "yz", "gx")),
        P(("rep", "yz", "gx")),
        P(),
        P(None, "yz"),
    )
    out_specs = (P(("rep", "yz", "gx"), None, None), P(("rep", "gx"), "yz"))
    return jax.shard_map(local, mesh=mesh, in_specs=in_specs, out_specs=out_specs, check_vma=False)
```

profile of v0, /device:TPU:0, one launch (start us, length us, event | category | flops | bytes accessed | tf_op | source)
XLA Modules:
  0.0 396.5 jit_solution(12199581647016589615)
XLA Ops:
  7.8 4.8 %convolution_convert_fusion.2 = bf16[2,69632]{1,0:T(2,128)(2,1)} fusion(f32[2,32]{1,0:T(2,128)S(1)} %copy-done, bf16[32,69632]{1,0:T(8,128)(2,1)} %param.23), kind=kOutput, calls=%fused_computation.90 | convolution fusion | flops 53616640 | bytes 4735232 | tf_op jit(solution)/shard_map/dot_general | solution.py:146
  12.8 1.4 copy.107
  14.2 30.4 %all-gather.2.cloned.1.call-done = bf16[2,278528]{1,0:T(2,128)(2,1)} async-done(((bf16[2,69632]{1,0:T(2,128)(2,1)}), bf16[2,278528]{1,0:T(2,128)(2,1)}) %all-gather.2.cloned.1.call-update) | async-done | bytes 1114128 | tf_op jit(solution)/shard_map/all_gather | solution.py:149
  44.6 4.2 %slice_reduce_fusion.6 = (bf16[65536]{0:T(1024)(128)(2,1)S(1)}, bf16[65536]{0:T(1024)(128)(2,1)S(1)}, bf16[65536]{0:T(1024)(128)(2,1)S(1)}, bf16[65536]{0:T(1024)(128)(2,1)S(1)}) fusion(bf16[2,278528]{1,0:T(2,128)(2,1)} %all-gather.2.cloned.1.call-done), kind=kLoop, calls=%fused_computation.104 | loop fusion | bytes 1048576 | tf_op jit(solution)/shard_map/slice | solution.py:61
  49.0 6.2 %slice_reduce_fusion.3 = (bf16[147456]{0:T(1024)(128)(2,1)S(1)}, bf16[147456]{0:T(1024)(128)(2,1)S(1)}) fusion(bf16[2,278528]{1,0:T(2,128)(2,1)S(1)} %copy-done.15), kind=kLoop, calls=%fused_computation.97 | loop fusion | bytes 1179648 | tf_op jit(solution)/shard_map/slice | solution.py:57
  57.5 1.5 broadcast_in_dim.29
  59.0 1.6 broadcast_in_dim.31
  60.6 1.2 broadcast_in_dim.30
  61.7 118.2 %while.17 = (s32[]{:T(128)}, f32[256,9,128]{2,1,0:T(8,128)}, f32[384,768]{1,0:T(8,128)}, f32[512,1024]{1,0:T(8,128)}, s32[]{:T(128)}, /*index=5*/s32[128,8]{0,1:...) while((s32[]{:T(128)}, f32[256,9,128]{2,1,0:T(8,128)}, ...), condition=%wide.region_2.0_spmd.clone, body=%wide.region_0.0_spmd.clone.sunk | while | flops 1780386688 | bytes 120993768 | solution.py:191
  83.1 3.6 gather_fusion
  88.8 3.2 fusion.107
  93.7 4.9 %fusion.105 = f32[512,5,128]{2,1,0:T(8,128)} fusion(f32[5,5,512]{1,0,2:T(8,128)S(1)} %copy.176, bf16[512,9,128]{2,1,0:T(8,128)(2,1)} %bitcast.147), kind=kOutput, calls=%fused_computation.14.clone.1 | convolution fusion | flops 19660800 | bytes 2410496 | tf_op jit(solution)/shard_map/while/body/abe,ebc->eac/dot_general | solution.py:35
  99.8 3.3 fusion.106
  103.1 1.4 fusion.108
  104.5 2.1 fusion.109
  109.7 1.2 broadcast_multiply_fusion.6
  111.0 3.5 convolution_convert_fusion.5
  116.1 1.9 convolution_convert_fusion.6
  124.8 4.6 %fusion.116 = f32[512,3,128]{2,1,0:T(4,128)S(1)} fusion(f32[3,3,512]{1,0,2:T(4,128)S(1)} %copy.178, f32[512,3,128]{2,0,1:T(8,128)S(1)} %pad_maximum_fusion.29), kind=kOutput, calls=%fused_computation.17.clone.1 | convolution fusion | flops 7077888 | bytes 1591296 | tf_op jit(solution)/shard_map/while/body/bae,ebc->eac/dot_general | solution.py:41
  129.6 5.0 %fusion.115 = f32[512,5,128]{2,1,0:T(8,128)S(1)} fusion(f32[5,5,512]{1,0,2:T(8,128)S(1)} %copy.176, f32[512,5,128]{2,0,1:T(8,128)S(1)} %broadcast_dynamic-update-slice_fusion.5), kind=kOutput, calls=%fused_computation.7.clone.1 | convolution fusion | flops 19660800 | bytes 2672640 | tf_op jit(solution)/shard_map/while/body/bae,ebc->eac/dot_general | solution.py:42
  134.6 3.0 pad_maximum_fusion.30
  137.6 40.1 %scatter_fusion = f32[256,9,128]{2,1,0:T(8,128)S(1)} fusion(f32[256,9,128]{2,1,0:T(8,128)S(1)} %copy-done.1, s32[512]{0:T(512)S(1)} %bitcast.161, f32[512,9,128]{2,1,0:T(8,128)} %pad_maximum_fusion.30), kind=kCustom, calls=%fused_computation.1.clone.clone.1 | custom fusion | flops 589824 | bytes 7079936 | tf_op jit(solution)/shard_map/while/body/scatter-add | solution.py:181
  177.8 1.3 copy-done.2
  180.0 1.8 add_bitcast_fusion.1
  182.6 3.1 pad_maximum_fusion.10
  187.6 1.7 collective-permute-start.1
  189.5 1.4 collective-permute-start.2
  190.9 97.6 %collective-permute-start.3 = (bf16[1,32,9,128]{3,2,1,0:T(8,128)(2,1)S(1)}, bf16[1,32,9,128]{3,2,1,0:T(8,128)(2,1)S(1)}, u32[]{:S(2)}, u32[]{:S(2)}) collective-permute-start(bf16[1,32,9,128]{3,2,1,0:T(8,128)(2,1)S(1)} %get-tuple-element.414), channel_id=1, source_target_pairs={{4,0},{8,4},{12,8},{0,12},{5,1},{9,5},{13,9},{1,13},{6,2},{10,6},{... | collective-permute-start | bytes 221192 | tf_op jit(solution)/shard_map/ppermute | solution.py:25
  288.6 2.9 collective-permute-done.2
  291.8 5.2 %scatter_fusion.1 = f32[128,9,128]{2,1,0:T(8,128)S(1)} fusion(f32[128,9,128]{2,1,0:T(8,128)S(1)} %slice.314, s32[128]{0:T(128)S(1)} %fusion.40, f32[128,9,128]{2,1,0:T(8,128)S(1)} %pad_maximum_fusion.13), kind=kCustom, calls=%fused_computation.2 | custom fusion | flops 147456 | bytes 1769984 | tf_op jit(solution)/shard_map/scatter-add | solution.py:202
  297.8 86.6 %all-reduce.2.cloned.1.call-done = f32[2,278528]{1,0:T(2,128)} async-done(((f32[2,278528]{1,0:T(2,128)}), f32[2,278528]{1,0:T(2,128)}) %all-reduce.2.cloned.1.call-update) | async-done | bytes 2228240 | tf_op jit(solution)/shard_map/psum | solution.py:193
  384.4 4.8 %convolution_multiply_fusion = f32[8,69632]{1,0:T(8,128)} fusion(f32[2,278528]{1,0:T(2,128)} %all-reduce.2.cloned.1.call-done, s32[]{:T(128)S(6)} %select_n.48, f32[2,32]{1,0:T(2,128)S(1)} %copy-done, s32[]{:T(128)S(6)} %select_n.47), kind=kOutput, calls=%fused_computation.89 | convolution fusion | flops 13926400 | bytes 2785544 | tf_op jit(solution)/shard_map/dot_general | solution.py:209
  (122 shorter events, 24.6 us)
Async XLA Ops:
  7.2 0.7 copy-start
  7.2 5.6 %copy-start.17 = (bf16[256,9,128]{2,0,1:T(8,128)(2,1)S(1)}, bf16[256,9,128]{2,0,1:T(8,128)(2,1)}, u32[]{:S(2)}) copy-start(bf16[256,9,128]{2,0,1:T(8,128)(2,1)} %param.13) | copy-start | bytes 1769476
  7.2 37.4 %all-gather.2.cloned.1.call-start = ((), (), s32[]{:S(2)}) async-start(), calls=%async_computation | async-start | bytes 1392640 | tf_op jit(solution)/shard_map/all_gather | solution.py:149
  12.7 371.7 %all-reduce.2.cloned.1.call-start = ((), (), s32[]{:S(2)}) async-start(), calls=%async_computation.1 | async-start | bytes 4456448 | tf_op jit(solution)/shard_map/psum | solution.py:193
  44.6 4.5 %copy-start.15 = (bf16[2,278528]{1,0:T(2,128)(2,1)S(1)}, bf16[2,278528]{1,0:T(2,128)(2,1)}, u32[]{:S(2)}) copy-start(bf16[2,278528]{1,0:T(2,128)(2,1)} %all-gather.2.cloned.1.call-done) | copy-start | bytes 3342340
  59.0 2.7 copy-start.20
  88.0 4.0 %copy-start.4 = (bf16[64,8,9,128]{3,2,1,0:T(8,128)(2,1)}, bf16[64,8,9,128]{3,2,1,0:T(8,128)(2,1)S(1)}, u32[]{:S(2)}) copy-start(bf16[64,8,9,128]{3,2,1,0:T(8,128)(2,1)S(1)} %broadcast_in_dim.37) | copy-start | bytes 3538948 | tf_op jit(solution)/shard_map/while
  99.7 3.3 copy-start.6
  114.5 1.6 copy-start.5
  116.1 2.5 copy-start.7
  118.6 1.0 copy-start.12
  118.6 1.0 copy-start.13
  119.4 2.7 copy-start.8
  119.4 1.2 copy-start.14
  119.4 2.1 copy-start.9
  119.9 3.3 copy-start.18
  122.1 1.1 copy-start.10
  122.1 1.8 copy-start.16
  134.6 3.0 copy-start.1
  137.6 41.4 %copy-start.21 = (s32[128]{0:T(128)S(1)}, s32[128]{0:T(128)}, u32[]{:S(2)}) copy-start(s32[128]{0:T(128)} %get-tuple-element.679) | copy-start | bytes 1540 | tf_op jit(solution)/shard_map/while
  177.7 1.3 copy-start.2
  180.0 2.1 copy-start.11
  185.8 0.7 copy-start.19
  185.8 1.6 copy-start.3
  187.5 101.0 %collective-permute-start = (bf16[1,32,9,128]{3,2,1,0:T(8,128)(2,1)S(1)}, bf16[1,32,9,128]{3,2,1,0:T(8,128)(2,1)S(1)}, u32[]{:S(2)}, u32[]{:S(2)}) collective-permute-start(bf16[1,32,9,128]{3,2,1,0:T(8,128)(2,1)S(1)} %get-tuple-element.413), channel_id=1, source_target_pairs={{0,1},{1,2},{2,3},{3,0},{4,5},{5,6},{6,7},{7,4},{8,9},{9,10},{10,1... | collective-permute-start | bytes 221192 | tf_op jit(solution)/shard_map/ppermute | solution.py:23
  187.6 100.9 %collective-permute-start.1 = (bf16[1,32,9,128]{3,2,1,0:T(8,128)(2,1)S(1)}, bf16[1,32,9,128]{3,2,1,0:T(8,128)(2,1)S(1)}, u32[]{:S(2)}, u32[]{:S(2)}) collective-permute-start(bf16[1,32,9,128]{3,2,1,0:T(8,128)(2,1)S(1)} %get-tuple-element.416), channel_id=1, source_target_pairs={{1,0},{2,1},{3,2},{0,3},{5,4},{6,5},{7,6},{4,7},{9,8},{10,9},{11,1... | collective-permute-start | bytes 221192 | tf_op jit(solution)/shard_map/ppermute | solution.py:25
  189.5 102.0 %collective-permute-start.2 = (bf16[1,32,9,128]{3,2,1,0:T(8,128)(2,1)S(1)}, bf16[1,32,9,128]{3,2,1,0:T(8,128)(2,1)S(1)}, u32[]{:S(2)}, u32[]{:S(2)}) collective-permute-start(bf16[1,32,9,128]{3,2,1,0:T(8,128)(2,1)S(1)} %get-tuple-element.415), channel_id=1, source_target_pairs={{0,4},{4,8},{8,12},{12,0},{1,5},{5,9},{9,13},{13,1},{2,6},{6,10},{... | collective-permute-start | bytes 221192 | tf_op jit(solution)/shard_map/ppermute | solution.py:23
  190.9 100.7 %collective-permute-start.3 = (bf16[1,32,9,128]{3,2,1,0:T(8,128)(2,1)S(1)}, bf16[1,32,9,128]{3,2,1,0:T(8,128)(2,1)S(1)}, u32[]{:S(2)}, u32[]{:S(2)}) collective-permute-start(bf16[1,32,9,128]{3,2,1,0:T(8,128)(2,1)S(1)} %get-tuple-element.414), channel_id=1, source_target_pairs={{4,0},{8,4},{12,8},{0,12},{5,1},{9,5},{13,9},{1,13},{6,2},{10,6},{... | collective-permute-start | bytes 221192 | tf_op jit(solution)/shard_map/ppermute | solution.py:25
Sparse Core Ops, SparseCore 0:
  12.8 31.6 all-gather.1
  185.9 198.4 all-reduce.1
where the time goes:
time: 405 us; the launch traced here: 396 us
  waiting for transfers between devices  120 us (30%)
  starting transfers between devices  101 us (25%)
  other arithmetic  61.9 us (15%)
  local copies, waits for them, and re-layouts  41.8 us (10%)
  matrix products  35.5 us (9%)
  loops' own time  21.6 us (5%)
  between operations  14.7 us (4%)
    ppermute x2, starting transfers between devices, extended(): lax.ppermute(head, axis, [((i + 1) % count, i) for i in range(count)])  99.3 us
    psum x1, waiting for transfers between devices, local(): summed_all = lax.psum(flattened, ('yz', 'gx'))  86.6 us
    scatter-add x1, other arithmetic, block_step(): grad_ext.at[source_rows].add(turned)  40.1 us
    all_gather x1, waiting for transfers between devices, local(): merged = lax.all_gather(partial_merge, 'yz', axis=1, tiled=True)  30.4 us
    another operation x1, loops' own time, local(): lax.fori_loop(0, live_blocks[0], block_step, start_state)  21.6 us
    dot_general x2, matrix products, rotate(): jnp.einsum('abe,ebc->eac', turn_two, field[:, 4:9], precision=highest)  8.39 us
  transfers between devices with their start and end apart: 6, of which 4 were waited for; matrix products, arithmetic and copies ran while one was open for 2% of the time, Pallas kernels for 0%

commit v1 on v0

v1 whole, which is shorter than its diff:
```python
import functools
import math

import jax
import jax.numpy as jnp
from jax import lax
from jax.experimental import pallas as pl
from jax.experimental.pallas import tpu as pltpu
from jax.sharding import PartitionSpec as P

LIVE_BLOCK = 64
CHUNK = 256
SUB = 16
F32 = jnp.float32
BF16 = jnp.bfloat16

STACK = (0, 2, 6, 3, 7, 1, 5)
SLOT = {component: place for place, component in enumerate(STACK)}

VMEM = pl.BlockSpec(memory_space=pltpu.VMEM)
SMEM = pl.BlockSpec(memory_space=pltpu.SMEM)
PARAMS = pltpu.CompilerParams(vmem_limit_bytes=56 * 1024 * 1024)


def nn(left, right):
    return lax.dot_general(left, right, (((1,), (0,)), ((), ())), preferred_element_type=F32)


def nt(left, right):
    return lax.dot_general(left, right, (((1,), (1,)), ((), ())), preferred_element_type=F32)


def split3(value):
    high = value.astype(BF16)
    rest = value - high.astype(F32)
    middle = rest.astype(BF16)
    low = (rest - middle.astype(F32)).astype(BF16)
    return high, middle, low


def merge_kernel(coef_ref, experts_ref, out_ref):
    members, wide = coef_ref.shape
    experts = experts_ref.shape[0]
    rows = out_ref.shape[1]
    row = lax.broadcasted_iota(jnp.int32, (8, wide), 0)
    col = lax.broadcasted_iota(jnp.int32, (8, wide), 1)
    diagonal = row == col // experts
    pieces = []
    for member in range(members):
        pieces.append(jnp.where(diagonal, coef_ref[member : member + 1, :], 0.0))
    left = jnp.concatenate(pieces, axis=0)
    lefts = jnp.concatenate(split3(left), axis=0)
    height = 8 * members
    for block in range(rows // 16):
        right = jnp.concatenate(
            [
                jnp.concatenate(
                    [
                        experts_ref[:, (block * 16 + half * 8 + g) * 128 : (block * 16 + half * 8 + g + 1) * 128]
                        for g in range(8)
                    ],
                    axis=0,
                )
                for half in range(2)
            ],
            axis=1,
        )
        product = nn(lefts, right)
        total = product[:height] + product[height : 2 * height] + product[2 * height :]
        for member in range(members):
            part = total[member * 8 : member * 8 + 8]
            out_ref[member, block * 16 : block * 16 + 16, :] = jnp.concatenate(
                [part[:, :128], part[:, 128:]], axis=0
            ).astype(BF16)


def merge(coef, experts, core, parts):
    members, count = coef.shape
    columns = experts.shape[1] // parts
    rows = columns // 128
    return pl.pallas_call(
        lambda ids_ref, coef_ref, experts_ref, out_ref: merge_kernel(coef_ref, experts_ref, out_ref),
        grid_spec=pltpu.PrefetchScalarGridSpec(
            num_scalar_prefetch=1,
            grid=(1,),
            in_specs=[
                pl.BlockSpec((members, 8 * count), lambda i, ids: (0, 0)),
                pl.BlockSpec((count, columns), lambda i, ids: (0, ids[0])),
            ],
            out_specs=pl.BlockSpec((members, rows, 128), lambda i, ids: (0, 0, 0)),
        ),
        out_shape=jax.ShapeDtypeStruct((members, rows, 128), BF16),
        compiler_params=PARAMS,
        name="merge",
    )(core, jnp.tile(coef, (1, 8)), experts)


def features_kernel(
    ids_ref, live_ref, near_ref, class_ref, zero_ref, one_ref, two_ref, source_ref, target_ref,
    other_ref, own_ref, pulled_ref, edge_ref,
    source_t, target_t, moved, spread, rotated, grads,
    *, fanout,
):
    slots, channels = source_ref.shape[1:]
    atoms = target_ref.shape[1]
    edges = atoms * fanout
    for c in range(9):
        source_t[c * channels : (c + 1) * channels, :] = source_ref[c].T
        target_t[c * channels : (c + 1) * channels, :] = target_ref[c].T
    near = near_ref[...].astype(F32).astype(BF16)
    classes = class_ref[...].astype(F32).astype(BF16)
    live_edges = live_ref[0] * LIVE_BLOCK * fanout
    scale = 1.0 / math.sqrt(fanout)

    def chunk_step(chunk, carry):
        start = pl.multiple_of(chunk * CHUNK, CHUNK)
        here = pl.ds(start, CHUNK)
        edge = lax.broadcasted_iota(jnp.int32, (atoms, CHUNK), 1) + start
        atom = lax.broadcasted_iota(jnp.int32, (atoms, CHUNK), 0)
        repeat = (edge // fanout == atom).astype(F32).astype(BF16)
        edge8 = lax.broadcasted_iota(jnp.int32, (fanout, CHUNK), 1) + start
        lane8 = lax.broadcasted_iota(jnp.int32, (fanout, CHUNK), 0)
        picked = jnp.where(edge8 % fanout == lane8, nn(near, repeat), 0.0)
        near_row = jnp.sum(picked, axis=0, keepdims=True)
        class_row = nn(classes, repeat)
        edge_ref[0:1, here] = near_row
        edge_ref[1:2, here] = jnp.where(edge8[0:1] < live_edges, class_row, -1.0)
        slot = lax.broadcasted_iota(jnp.int32, (slots, CHUNK), 0).astype(F32)
        pick = (slot == near_row).astype(F32).astype(BF16)
        moved[...] = nn(source_t[...], pick)
        spread[...] = nn(target_t[...], repeat)

        def sub_step(sub, inner):
            at = pl.multiple_of(sub * SUB, SUB)

            def turn(field, write):
                def part(c):
                    return field[pl.ds(c * channels + at, SUB), :]

                write(0, zero_ref[0:1, here] * part(0))
                values = [part(c) for c in (1, 2, 3)]
                for a in range(3):
                    total = one_ref[a, 0:1, here] * values[0]
                    for b in range(1, 3):
                        total += one_ref[a, b : b + 1, here] * values[b]
                    write(1 + a, total)
                values = [part(c) for c in (4, 5, 6, 7, 8)]
                for a in range(1, 4):
                    total = two_ref[a, 0:1, here] * values[0]
                    for b in range(1, 5):
                        total += two_ref[a, b : b + 1, here] * values[b]
                    write(4 + a, total)

            def write_rotated(c, value):
                rotated[pl.ds(SLOT[c] * channels + at, SUB), here] = value.astype(BF16)

            def write_pulled(c, value):
                pulled_ref[pl.ds(SLOT[c] * channels + at, SUB), here] = (value * scale).astype(BF16)

            turn(moved, write_rotated)
            turn(spread, write_pulled)
            return inner

        lax.fori_loop(0, channels // SUB, sub_step, 0)
        return carry

    lax.fori_loop(0, edges // CHUNK, chunk_step, 0)
    zw, pw = 3 * channels, 2 * channels
    first = zw * zw // 128
    second = first + pw * pw // 128
    own = ids_ref[1].astype(F32)
    for out_ref, wanted in ((other_ref, 1.0 - own), (own_ref, own)):
        mask = (edge_ref[1:2, :] == wanted).astype(F32).astype(BF16)
        qz = pulled_ref[0:zw, :] * mask
        qp = pulled_ref[zw : zw + pw, :] * mask
        qn = pulled_ref[zw + pw : zw + 2 * pw, :] * mask
        z, p, n = rotated[0:zw, :], rotated[zw : zw + pw, :], rotated[zw + pw : zw + 2 * pw, :]
        whole = nt(z, qz)
        for j in range(zw // 128):
            grads[pl.ds(j, zw, stride=zw // 128), :] = whole[:, j * 128 : (j + 1) * 128]
        coupled = nt(p, qp) + nt(n, qn)
        crossed = nt(p, qn) - nt(n, qp)
        for j in range(pw // 128):
            grads[pl.ds(first + j, pw, stride=pw // 128), :] = coupled[:, j * 128 : (j + 1) * 128]
            grads[pl.ds(second + j, pw, stride=pw // 128), :] = crossed[:, j * 128 : (j + 1) * 128]
        out_ref[...] = grads[...].astype(BF16)


def features(ids, live, near, classes, zero, one, two, source, target, rows, fanout):
    slots, channels = source.shape[1:]
    atoms = target.shape[1]
    edges = atoms * fanout
    shape = jax.ShapeDtypeStruct
    return pl.pallas_call(
        functools.partial(features_kernel, fanout=fanout),
        in_specs=[SMEM, SMEM] + [VMEM] * 7,
        out_specs=[VMEM] * 4,
        out_shape=[
            shape((rows, 128), BF16),
            shape((rows, 128), BF16),
            shape((7 * channels, edges), BF16),
            shape((8, edges), F32),
        ],
        scratch_shapes=[
            pltpu.VMEM((9 * channels, slots), BF16),
            pltpu.VMEM((9 * channels, atoms), BF16),
            pltpu.VMEM((9 * channels, CHUNK), F32),
            pltpu.VMEM((9 * channels, CHUNK), F32),
            pltpu.VMEM((7 * channels, edges), BF16),
            pltpu.VMEM((rows, 128), F32),
        ],
        compiler_params=PARAMS,
        name="features",
    )(ids, live, near, classes, zero, one, two, source, target)


def back_kernel(
    places_ref, edge_ref, zero_ref, one_ref, two_ref, pulled_ref, *rest, pieces, members, atoms, face,
):
    piece_refs = rest[:pieces]
    own_ref, ghost_ref, flat, weight_zero, weight_pair, field, turned, pick_all = rest[pieces:]
    rows = flat.shape[1]
    channels = own_ref.shape[2]
    slots = pick_all.shape[0]
    edges = pulled_ref.shape[1]
    zw, pw = 3 * channels, 2 * channels
    first = zw * zw // 128
    second = first + pw * pw // 128
    for index, piece in enumerate(piece_refs):
        height = piece.shape[1]
        at = pl.ds(pl.multiple_of(places_ref[index], 16), height)
        for k in range(members):
            flat[k, at, :] = piece[k].astype(F32)
    for k in range(members):
        for j in range(zw // 128):
            weight_zero[:, k * zw + j * 128 : k * zw + (j + 1) * 128] = flat[
                k, pl.ds(j, zw, stride=zw // 128), :
            ].astype(BF16)
        for j in range(pw // 128):
            at = k * 2 * pw + j * 128
            weight_pair[:, at : at + 128] = flat[k, pl.ds(first + j, pw, stride=pw // 128), :].astype(BF16)
            weight_pair[:, at + pw : at + pw + 128] = flat[
                k, pl.ds(second + j, pw, stride=pw // 128), :
            ].astype(BF16)

    def chunk_step(chunk, carry):
        start = pl.multiple_of(chunk * CHUNK, CHUNK)
        here = pl.ds(start, CHUNK)
        slot = lax.broadcasted_iota(jnp.int32, (slots, CHUNK), 0).astype(F32)
        pick_all[:, here] = (slot == edge_ref[0:1, here]).astype(F32).astype(BF16)
        qz, qpn, qnp = [], [], []
        for k in range(members):
            mask = (edge_ref[1:2, here] == float(k)).astype(F32).astype(BF16)
            qz.append(pulled_ref[0:zw, here] * mask)
            qp = pulled_ref[zw : zw + pw, here] * mask
            qn = pulled_ref[zw + pw : zw + 2 * pw, here] * mask
            qpn += [qp, qn]
            qnp += [qn, -qp]
        field[0:zw, :] = nn(weight_zero[...], jnp.concatenate(qz, axis=0))
        field[zw : zw + pw, :] = nn(weight_pair[...], jnp.concatenate(qpn, axis=0))
        field[zw + pw : zw + 2 * pw, :] = nn(weight_pair[...], jnp.concatenate(qnp, axis=0))

        def sub_step(sub, inner):
            at = pl.multiple_of(sub * SUB, SUB)

            def part(c):
                return field[pl.ds(SLOT[c] * channels + at, SUB), :]

            def write(c, value):
                turned[pl.ds(c * channels + at, SUB), here] = value.astype(BF16)

            write(0, zero_ref[0:1, here] * part(0))
            values = [part(c) for c in (1, 2, 3)]
            for b in range(3):
                total = one_ref[0, b : b + 1, here] * values[0]
                for a in range(1, 3):
                    total += one_ref[a, b : b + 1, here] * values[a]
                write(1 + b, total)
            values = [part(c) for c in (5, 6, 7)]
            for b in range(5):
                total = two_ref[1, b : b + 1, here] * values[0]
                for a in range(2, 4):
                    total += two_ref[a, b : b + 1, here] * values[a - 1]
                write(4 + b, total)
            return inner

        lax.fori_loop(0, channels // SUB, sub_step, 0)
        return carry

    lax.fori_loop(0, edges // CHUNK, chunk_step, 0)
    for c in range(9):
        summed = nt(pick_all[...], turned[c * channels : (c + 1) * channels, :])
        own_ref[c] = summed[:atoms]
        for block in range(4):
            at = atoms + block * face
            ghost_ref[block, c] = summed[at : at + face].astype(BF16)


def back(places, edge, zero, one, two, pulled, pieces, rows, atoms, slots, face):
    members = pieces[0].shape[0]
    edges = pulled.shape[1]
    channels = pulled.shape[0] // 7
    shape = jax.ShapeDtypeStruct
    return pl.pallas_call(
        functools.partial(back_kernel, pieces=len(pieces), members=members, atoms=atoms, face=face),
        in_specs=[SMEM] + [VMEM] * (5 + len(pieces)),
        out_specs=[VMEM] * 2,
        out_shape=[shape((9, atoms, channels), F32), shape((4, 9, face, channels), BF16)],
        scratch_shapes=[
            pltpu.VMEM((members, rows, 128), F32),
            pltpu.VMEM((3 * channels, members * 3 * channels), BF16),
            pltpu.VMEM((2 * channels, members * 4 * channels), BF16),
            pltpu.VMEM((7 * channels, CHUNK), F32),
            pltpu.VMEM((9 * channels, edges), BF16),
            pltpu.VMEM((slots, edges), BF16),
        ],
        compiler_params=PARAMS,
        name="back",
    )(places, edge, zero, one, two, pulled, *pieces)


def pair_kernel(places_ref, own_ref, came_ref, *out_refs):
    height = out_refs[0].shape[0]
    for index, out_ref in enumerate(out_refs):
        at = pl.ds(pl.multiple_of(places_ref[index], 16), height)
        out_ref[...] = (own_ref[at, :].astype(F32) + came_ref[at, :].astype(F32)).astype(BF16)


def pair_sum(places, own, came, count):
    height = own.shape[0] // count
    return pl.pallas_call(
        pair_kernel,
        in_specs=[SMEM, VMEM, VMEM],
        out_specs=[VMEM] * count,
        out_shape=[jax.ShapeDtypeStruct((height, 128), BF16)] * count,
        compiler_params=PARAMS,
        name="pair_sum",
    )(places, own, came)


def total_kernel(*refs):
    total = refs[0][...].astype(F32)
    for ref in refs[1:-1]:
        total += ref[...].astype(F32)
    refs[-1][...] = total.astype(BF16)


def total_sum(parts):
    return pl.pallas_call(
        total_kernel,
        in_specs=[VMEM] * len(parts),
        out_specs=VMEM,
        out_shape=jax.ShapeDtypeStruct(parts[0].shape, BF16),
        compiler_params=PARAMS,
        name="total_sum",
    )(*parts)


def expert_kernel(coef_ref, *refs):
    sums, out_ref, summed = refs[:-2], refs[-2], refs[-1]
    half = len(sums) // 2
    for side in range(2):
        total = sums[side * half][...].astype(F32)
        for ref in sums[side * half + 1 : (side + 1) * half]:
            total += ref[...].astype(F32)
        summed[side] = total
    owned = coef_ref.shape[0]
    first = jnp.broadcast_to(coef_ref[:, 0:1], (owned, 128))
    second = jnp.broadcast_to(coef_ref[:, 1:2], (owned, 128))
    for row in range(summed.shape[1]):
        out_ref[:, row * 128 : (row + 1) * 128] = (
            first * summed[0, row : row + 1, :] + second * summed[1, row : row + 1, :]
        )


def expert_product(coef, sums):
    rows = sums[0].shape[0]
    owned = coef.shape[0]
    return pl.pallas_call(
        expert_kernel,
        in_specs=[VMEM] * (1 + len(sums)),
        out_specs=VMEM,
        out_shape=jax.ShapeDtypeStruct((owned, rows * 128), F32),
        scratch_shapes=[pltpu.VMEM((2, rows, 128), F32)],
        compiler_params=PARAMS,
        name="expert_product",
    )(coef, *sums)


def finish_kernel(send_ref, own_ref, a_ref, b_ref, c_ref, d_ref, out_ref):
    atoms = own_ref.shape[1]
    face = send_ref.shape[1]
    row = lax.broadcasted_iota(jnp.int32, (atoms, face), 0)
    picks = [(row == send_ref[b : b + 1, :]).astype(F32).astype(BF16) for b in range(4)]
    for c in range(9):
        total = own_ref[c]
        for pick, ref in zip(picks, (a_ref, b_ref, c_ref, d_ref)):
            total += nn(pick, ref[c])
        out_ref[c] = total.astype(BF16)


def finish(send, own, returned):
    return pl.pallas_call(
        finish_kernel,
        in_specs=[VMEM] * 6,
        out_specs=VMEM,
        out_shape=jax.ShapeDtypeStruct(own.shape, BF16),
        compiler_params=PARAMS,
        name="finish",
    )(send, own, *returned)


def swap(value, axis, bit):
    return lax.ppermute(value, axis, [(i, i ^ bit) for i in range(lax.axis_size(axis))])


def shift(value, axis, step):
    count = lax.axis_size(axis)
    return lax.ppermute(value, axis, [(i, (i + step) % count) for i in range(count)])


def local(
    saved_input, cotangent, neighbours, rot_zero, rot_one, rot_two, send_index, atom_class, live_blocks,
    merge_coef, experts,
):
    atoms, fanout = neighbours.shape
    slots = saved_input.shape[0]
    channels = cotangent.shape[2]
    face = send_index.shape[1]
    count_yz, count_gx = lax.axis_size("yz"), lax.axis_size("gx")
    row, column = lax.axis_index("yz"), lax.axis_index("gx")
    core = column % 2
    height = experts.shape[1] // 128
    rows = height * count_yz
    direct = height % 32 == 0 and count_yz & (count_yz - 1) == 0 and count_gx == 4

    zero = rot_zero.reshape(1, -1)
    source = jnp.transpose(saved_input, (1, 0, 2))
    target = jnp.transpose(cotangent, (1, 0, 2))
    ids = jnp.stack([core, core]).astype(jnp.int32)

    if direct:
        half = height // 2
        mine = merge(merge_coef, experts, core.reshape(1).astype(jnp.int32), 2)
        held = [mine] + [swap(mine, "yz", k) for k in range(1, count_yz)]
        facing = [swap(piece, "gx", 1) for piece in held]
        pieces = held + facing
        starts = jnp.stack([(row ^ k) * height for k in range(count_yz)])
        places = jnp.concatenate([starts + core * half, starts + (1 - core) * half]).astype(jnp.int32)
    else:
        part = jnp.dot(merge_coef, experts.astype(F32), precision=lax.Precision.HIGHEST).astype(BF16)
        merged = lax.all_gather(part, "yz", axis=1, tiled=True)
        pieces = [merged.reshape(merged.shape[0], rows, 128)]
        places = jnp.zeros((1,), jnp.int32)

    other, own, pulled, edge = features(
        ids, live_blocks, neighbours.T, atom_class.reshape(1, -1), zero, rot_one, rot_two, source, target,
        rows, fanout,
    )
    per_owner = merge_coef.shape[1] // count_gx
    owned = lax.dynamic_slice_in_dim(merge_coef, column * per_owner, per_owner, 1)
    grad_scale = math.sqrt(fanout / (atoms * count_yz * count_gx))
    owned = owned.T * grad_scale
    owned = jnp.where(core == 0, owned, owned[:, ::-1])
    if direct:
        came = swap(other, "gx", 1)
        parts = pair_sum(starts.astype(jnp.int32), own, came, count_yz)
        gathered = [parts[0]] + [swap(parts[k], "yz", k) for k in range(1, count_yz)]
    grad_own, ghosts = back(
        places, edge, zero, rot_one, rot_two, pulled, pieces, rows, atoms, slots, face
    )
    if direct:
        summed = total_sum(gathered)
        across = swap(summed, "gx", 2)
        sums = [summed, across, swap(summed, "gx", 1), swap(across, "gx", 1)]
    else:
        mixed = jnp.stack([own, other]).astype(F32)
        mixed = jnp.where(core == 0, mixed, mixed[::-1])
        whole = lax.psum(mixed, ("yz", "gx"))
        piece = lax.dynamic_slice_in_dim(whole, row * height, height, 1)
        piece = jnp.where(core == 0, piece, piece[::-1])
        sums = [piece[0], piece[1]]
    returned = [
        shift(ghosts[1], "gx", 1), shift(ghosts[0], "gx", -1), shift(ghosts[3], "yz", 1), shift(ghosts[2], "yz", -1),
    ]
    expert_grad = expert_product(owned, sums)
    input_grad = finish(send_index, grad_own, returned)
    return (jnp.transpose(input_grad, (1, 0, 2)), expert_grad)


def solution(mesh):
    tiles = ("rep", "yz", "gx")
    in_specs = (
        P(tiles, None, None),
        P(tiles, None, None),
        P(tiles, None),
        P(tiles),
        P(None, None, tiles),
        P(None, None, tiles),
        P(tiles, None),
        P(tiles),
        P(tiles),
        P(),
        P(None, "yz"),
    )
    out_specs = (P(tiles, None, None), P(("rep", "gx"), "yz"))
    return jax.shard_map(local, mesh=mesh, in_specs=in_specs, out_specs=out_specs, check_vma=False)
```

time: 405 us -> 73.5 us (0.18); the launches traced: 396 us -> 73.2 us
  waiting for transfers between devices: 120 us -> 13.4 us
  starting transfers between devices: 101 us -> 18.6 us
  other arithmetic: 61.9 us -> 3.09 us
  matrix products: 35.5 us -> 0 us
  local copies, waits for them, and re-layouts: 41.8 us -> 6.73 us
  Pallas kernels: 0 us -> 29.8 us
  loops' own time: 21.6 us -> 0 us
  between operations: 14.7 us -> 1.45 us
    psum x1 -> x0, waiting for transfers between devices: 86.6 us -> none  [local(): summed_all = lax.psum(flattened, ('yz', 'gx'))]
    ppermute x4 -> x18, starting transfers between devices: 101 us -> 18.6 us  [the longest x14 13 us: swap(): lax.ppermute(value, axis, [(i, i ^ bit) for i in range(lax.axis_size(axis...]
    scatter-add x2 -> x0, other arithmetic: 45.3 us -> none  [the longest x1 40.1 us: block_step(): grad_ext.at[source_rows].add(turned)]
    dot_general x12 -> x0, matrix products: 35.5 us -> none  [the longest x2 8.39 us: rotate(): jnp.einsum('abe,ebc->eac', turn_two, field[:, 4:9], precision=highest)]
    all_gather x1 -> x0, waiting for transfers between devices: 30.4 us -> none  [local(): merged = lax.all_gather(partial_merge, 'yz', axis=1, tiled=True)]
    pallas_call x0 -> x7, Pallas kernels: none -> 29.8 us  [the longest x1 9.79 us: features(): pl.pallas_call(functools.partial(features_kernel, fanout=fanout), in_spec...]
    another operation x1 -> x0, loops' own time: 21.6 us -> none  [local(): lax.fori_loop(0, live_blocks[0], block_step, start_state)]
    slice x10 -> x0, local copies, waits for them, and re-layouts: 14 us -> none  [the longest x1 6.22 us: class_weights(): vector[:zero_width * zero_width].reshape(zero_width, zero_width)]
  transfers between devices with their start and end apart: 6 -> 18, of which waited for: 4 -> 5; matrix products, arithmetic and copies ran while one was open for 2% -> 7% of each run, Pallas kernels for 0% -> 21%
where the time goes in v1:
time: 73.5 us; the launch traced here: 73.2 us
  Pallas kernels  29.8 us (41%)
  starting transfers between devices  18.6 us (25%)
  waiting for transfers between devices  13.4 us (18%)
  local copies, waits for them, and re-layouts  6.73 us (9%)
  other arithmetic  3.09 us (4%)
  between operations  1.45 us (2%)
    ppermute x14, starting transfers between devices, swap(): lax.ppermute(value, axis, [(i, i ^ bit) for i in range(lax.axis_size(axis...  13 us
    ppermute x14, waiting for transfers between devices, swap(): lax.ppermute(value, axis, [(i, i ^ bit) for i in range(lax.axis_size(axis...  11.3 us
    pallas_call x1, Pallas kernels, features(): pl.pallas_call(functools.partial(features_kernel, fanout=fanout), in_spec...  9.79 us
    pallas_call x1, Pallas kernels, back(): pl.pallas_call(functools.partial(back_kernel, pieces=len(pieces), members...  8.25 us
    ppermute x4, starting transfers between devices, shift(): lax.ppermute(value, axis, [(i, (i + step) % count) for i in range(count)])  5.6 us
    unnamed x39, local copies, waits for them, and re-layouts  4.23 us
    pallas_call x1, Pallas kernels, expert_product(): pl.pallas_call(expert_kernel, in_specs=[VMEM] * (1 + len(sums)), out_spec...  2.8 us
    pallas_call x1, Pallas kernels, merge(): pl.pallas_call(lambda ids_ref, coef_ref, experts_ref, out_ref: merge_kern...  2.77 us
  transfers between devices with their start and end apart: 18, of which 5 were waited for; matrix products, arithmetic and copies ran while one was open for 7% of the time, Pallas kernels for 21%

profile of v1, /device:TPU:0, one launch (start us, length us, event | category | flops | bytes accessed | tf_op | source)
XLA Modules:
  0.0 73.2 jit_solution(133279201108704165)
XLA Ops:
  1.9 9.8 %features.1 = (bf16[2176,128]{1,0:T(8,128)(2,1)}, bf16[2176,128]{1,0:T(8,128)(2,1)}, bf16[896,1024]{1,0:T(8,128)(2,1)}, f32[8,1024]{1,0:T(8,128)}) custom-call(s32[2]{0:T(128)} %pad_add_fusion.2.ids_ref, s32[1]{0:T(128)S(6)} %copy.15.live_ref, s32[8,128]{1,0:T(8,128)} %bitcast.27, s32[1,128]{1,0:T(1,128)} %bitcast.28, f32[1,1024]{1,0:T(1,128)} %bitcast.25, ...), custom_call_target="tpu_custom_call" | custom-call | tf_op jit(solution)/shard_map/features/pallas_call | solution.py:194
  12.1 0.7 tile.4
  12.8 0.7 tile.10.coef_ref
  13.5 2.8 %merge.1.rest_0_ = bf16[2,272,128]{2,1,0:T(8,128)(2,1)} custom-call(s32[1]{0:T(128)} %bitcast.4.ids_ref, f32[2,256]{1,0:T(2,128)} %tile.10.coef_ref, bf16[32,69632]{1,0:T(8,128)(2,1)} %experts_ref.1), custom_call_target="tpu_custom_call" | custom-call | tf_op jit(solution)/shard_map/merge/pallas_call | solution.py:81
  16.2 2.6 %collective-permute-start = (bf16[2,272,128]{2,1,0:T(8,128)(2,1)}, bf16[2,272,128]{2,1,0:T(8,128)(2,1)S(1)}, u32[]{:S(2)}, u32[]{:S(2)}) collective-permute-start(bf16[2,272,128]{2,1,0:T(8,128)(2,1)} %merge.1.rest_0_), channel_id=1, source_target_pairs={{0,4},{4,0},{8,12},{12,8},{1,5},{5,1},{9,13},{13,9},{2,6},{6,2},{1... | collective-permute-start | bytes 417800 | tf_op jit(solution)/shard_map/ppermute | solution.py:414
  18.8 2.6 %collective-permute-start.1 = (bf16[2,272,128]{2,1,0:T(8,128)(2,1)}, bf16[2,272,128]{2,1,0:T(8,128)(2,1)S(1)}, u32[]{:S(2)}, u32[]{:S(2)}) collective-permute-start(bf16[2,272,128]{2,1,0:T(8,128)(2,1)} %merge.1.rest_0_), channel_id=1, source_target_pairs={{0,8},{4,12},{8,0},{12,4},{1,9},{5,13},{9,1},{13,5},{2,10},{6,14},... | collective-permute-start | bytes 417800 | tf_op jit(solution)/shard_map/ppermute | solution.py:414
  21.4 4.5 %collective-permute-done.rest_1_ = bf16[2,272,128]{2,1,0:T(8,128)(2,1)S(1)} collective-permute-done((bf16[2,272,128]{2,1,0:T(8,128)(2,1)}, bf16[2,272,128]{2,1,0:T(8,128)(2,1)S(1)}, u32[]{:S(2)}, u32[]{:S(2)}) %collective-permute-start) | collective-permute-done | bytes 139296 | tf_op jit(solution)/shard_map/ppermute | solution.py:414
  25.9 0.7 broadcast_add_fusion.1
  26.5 5.9 %collective-permute-done.1.rest_2_ = bf16[2,272,128]{2,1,0:T(8,128)(2,1)S(1)} collective-permute-done((bf16[2,272,128]{2,1,0:T(8,128)(2,1)}, bf16[2,272,128]{2,1,0:T(8,128)(2,1)S(1)}, u32[]{:S(2)}, u32[]{:S(2)}) %collective-permute-start.1) | collective-permute-done | bytes 139296 | tf_op jit(solution)/shard_map/ppermute | solution.py:414
  33.0 0.8 %copy-done = bf16[2176,128]{1,0:T(8,128)(2,1)} copy-done((bf16[2176,128]{1,0:T(8,128)(2,1)}, bf16[2176,128]{1,0:T(8,128)(2,1)S(1)}, u32[]{:S(2)}) %copy-start) | copy-done | bytes 557080
  33.8 2.1 %pair_sum.1 = (bf16[544,128]{1,0:T(8,128)(2,1)}, bf16[544,128]{1,0:T(8,128)(2,1)}, bf16[544,128]{1,0:T(8,128)(2,1)}, bf16[544,128]{1,0:T(8,128)(2,1)}) custom-call(s32[4]{0:T(128)} %get-tuple-element.23.places_ref, bf16[2176,128]{1,0:T(8,128)(2,1)} %get-tuple-element.16.own_ref, bf16[2176,128]{1,0:T(8,128)(2,1)} %copy-done), custom_call_target="tpu_custom_call" | custom-call | tf_op jit(solution)/shard_map/pair_sum/pallas_call | solution.py:331
  35.9 2.4 %collective-permute-start.12 = (bf16[544,128]{1,0:T(8,128)(2,1)}, bf16[544,128]{1,0:T(8,128)(2,1)S(1)}, u32[]{:S(2)}, u32[]{:S(2)}) collective-permute-start(bf16[544,128]{1,0:T(8,128)(2,1)} %get-tuple-element.19), channel_id=1, source_target_pairs={{0,4},{4,0},{8,12},{12,8},{1,5},{5,1},{9,13},{13,9},{2,6},{6,2},{1... | collective-permute-start | bytes 417800 | tf_op jit(solution)/shard_map/ppermute | solution.py:414
  38.3 1.1 %collective-permute-start.13 = (bf16[544,128]{1,0:T(8,128)(2,1)}, bf16[544,128]{1,0:T(8,128)(2,1)S(1)}, u32[]{:S(2)}, u32[]{:S(2)}) collective-permute-start(bf16[544,128]{1,0:T(8,128)(2,1)} %get-tuple-element.20), channel_id=1, source_target_pairs={{0,8},{4,12},{8,0},{12,4},{1,9},{5,13},{9,1},{13,5},{2,10},{6,14},... | collective-permute-start | bytes 417800 | tf_op jit(solution)/shard_map/ppermute | solution.py:414
  39.3 1.5 %collective-permute-start.14 = (bf16[544,128]{1,0:T(8,128)(2,1)}, bf16[544,128]{1,0:T(8,128)(2,1)S(1)}, u32[]{:S(2)}, u32[]{:S(2)}) collective-permute-start(bf16[544,128]{1,0:T(8,128)(2,1)} %get-tuple-element.21), channel_id=1, source_target_pairs={{0,12},{4,8},{8,4},{12,0},{1,13},{5,9},{9,5},{13,1},{2,14},{6,10},... | collective-permute-start | bytes 417800 | tf_op jit(solution)/shard_map/ppermute | solution.py:414
  40.8 0.7 broadcast_add_fusion
  42.8 8.2 %back.1 = (f32[9,128,128]{2,1,0:T(8,128)}, bf16[4,9,32,128]{3,2,1,0:T(8,128)(2,1)}) custom-call(s32[8]{0:T(128)} %pad_add_fusion.1.places_ref, f32[8,1024]{1,0:T(8,128)} %get-tuple-element.12.edge_ref, f32[1,1024]{1,0:T(1,128)} %bitcast.26, f32[3,3,1024]{2,1,0:T(4,128)} %one_ref.3, f32[5,5,1024]{2,1,0:T(8,128)} %two_ref.3, ...), custom_call_target="tpu_custom_call" | custom-call | tf_op jit(solution)/shard_map/back/pallas_call | solution.py:304
  51.0 0.8 %collective-permute-done.13.refs_2_ = bf16[544,128]{1,0:T(8,128)(2,1)S(1)} collective-permute-done((bf16[544,128]{1,0:T(8,128)(2,1)}, bf16[544,128]{1,0:T(8,128)(2,1)S(1)}, u32[]{:S(2)}, u32[]{:S(2)}) %collective-permute-start.13) | collective-permute-done | bytes 139296 | tf_op jit(solution)/shard_map/ppermute | solution.py:414
  51.9 0.7 copy-done.5
  52.6 1.8 %total_sum.1.refs_0_ = bf16[544,128]{1,0:T(8,128)(2,1)} custom-call(bf16[544,128]{1,0:T(8,128)(2,1)} %get-tuple-element.18.refs_0_, bf16[544,128]{1,0:T(8,128)(2,1)} %copy-done.4, bf16[544,128]{1,0:T(8,128)(2,1)} %copy-done.5, bf16[544,128]{1,0:T(8,128)(2,1)} %copy-done.6), custom_call_target="tpu_custom_call" | custom-call | tf_op jit(solution)/shard_map/total_sum/pallas_call | solution.py:349
  54.5 1.5 %collective-permute-start.15 = (bf16[544,128]{1,0:T(8,128)(2,1)}, bf16[544,128]{1,0:T(8,128)(2,1)S(1)}, u32[]{:S(2)}, u32[]{:S(2)}) collective-permute-start(bf16[544,128]{1,0:T(8,128)(2,1)} %total_sum.1.refs_0_), channel_id=1, source_target_pairs={{0,2},{1,3},{2,0},{3,1},{4,6},{5,7},{6,4},{7,5},{8,10},{9,11},{10,... | collective-permute-start | bytes 417800 | tf_op jit(solution)/shard_map/ppermute | solution.py:414
  55.9 1.0 %slice_bitcast_fusion = (bf16[9,32,128]{2,1,0:T(8,128)(2,1)S(1)}, bf16[9,32,128]{2,1,0:T(8,128)(2,1)S(1)}, bf16[9,32,128]{2,1,0:T(8,128)(2,1)S(1)}, bf16[9,32,128]{2,1,0:T(8,128)(2,1)S(1)}) fusion(bf16[4,9,32,128]{3,2,1,0:T(8,128)(2,1)} %get-tuple-element.15), kind=kLoop, calls=%fused_computation | loop fusion | bytes 589824 | tf_op jit(solution)/shard_map/squeeze | solution.py:484
  57.3 1.7 %collective-permute-start.8 = (bf16[9,32,128]{2,1,0:T(8,128)(2,1)S(1)}, bf16[9,32,128]{2,1,0:T(8,128)(2,1)S(1)}, u32[]{:S(2)}, u32[]{:S(2)}) collective-permute-start(bf16[9,32,128]{2,1,0:T(8,128)(2,1)S(1)} %get-tuple-element.26), channel_id=1, source_target_pairs={{0,3},{1,0},{2,1},{3,2},{4,7},{5,4},{6,5},{7,6},{8,11},{9,8},{10,9... | collective-permute-start | bytes 221192 | tf_op jit(solution)/shard_map/ppermute | solution.py:419
  59.0 2.7 %collective-permute-start.9 = (bf16[9,32,128]{2,1,0:T(8,128)(2,1)S(1)}, bf16[9,32,128]{2,1,0:T(8,128)(2,1)S(1)}, u32[]{:S(2)}, u32[]{:S(2)}) collective-permute-start(bf16[9,32,128]{2,1,0:T(8,128)(2,1)S(1)} %get-tuple-element.25), channel_id=1, source_target_pairs={{0,4},{4,8},{8,12},{12,0},{1,5},{5,9},{9,13},{13,1},{2,6},{6,10},{... | collective-permute-start | bytes 221192 | tf_op jit(solution)/shard_map/ppermute | solution.py:419
  61.7 1.1 %collective-permute-start.10 = (bf16[9,32,128]{2,1,0:T(8,128)(2,1)S(1)}, bf16[9,32,128]{2,1,0:T(8,128)(2,1)S(1)}, u32[]{:S(2)}, u32[]{:S(2)}) collective-permute-start(bf16[9,32,128]{2,1,0:T(8,128)(2,1)S(1)} %get-tuple-element.24), channel_id=1, source_target_pairs={{0,12},{4,0},{8,4},{12,8},{1,13},{5,1},{9,5},{13,9},{2,14},{6,2},{... | collective-permute-start | bytes 221192 | tf_op jit(solution)/shard_map/ppermute | solution.py:419
  63.3 0.6 multiply_select_fusion.coef_ref
  63.9 1.4 %collective-permute-done.9.c_ref = bf16[9,32,128]{2,1,0:T(8,128)(2,1)S(1)} collective-permute-done((bf16[9,32,128]{2,1,0:T(8,128)(2,1)S(1)}, bf16[9,32,128]{2,1,0:T(8,128)(2,1)S(1)}, u32[]{:S(2)}, u32[]{:S(2)}) %collective-permute-start.9) | collective-permute-done | bytes 73760 | tf_op jit(solution)/shard_map/ppermute | solution.py:419
  65.3 0.8 %collective-permute-done.10.d_ref = bf16[9,32,128]{2,1,0:T(8,128)(2,1)S(1)} collective-permute-done((bf16[9,32,128]{2,1,0:T(8,128)(2,1)S(1)}, bf16[9,32,128]{2,1,0:T(8,128)(2,1)S(1)}, u32[]{:S(2)}, u32[]{:S(2)}) %collective-permute-start.10) | collective-permute-done | bytes 73760 | tf_op jit(solution)/shard_map/ppermute | solution.py:419
  66.1 0.6 copy-done.17
  66.7 2.3 %finish.1 = bf16[9,128,128]{2,1,0:T(8,128)(2,1)} custom-call(s32[4,32]{1,0:T(4,128)} %send_ref.1, f32[9,128,128]{2,1,0:T(8,128)} %get-tuple-element.14.own_ref, bf16[9,32,128]{2,1,0:T(8,128)(2,1)} %copy-done.14, bf16[9,32,128]{2,1,0:T(8,128)(2,1)} %copy-done.15, bf16[9,32,128]{2,1,0:T(8,128)(2,1)} %copy-done.16, bf16[9,32,128]{2,1,0:T(8,128)(2,1)} %copy-done.17), custom_call_target="tpu_custom_call" | custom-call | tf_op jit(solution)/shard_map/finish/pallas_call | solution.py:403
  69.1 0.6 copy-done.2
  69.7 0.7 copy-done.3
  70.4 2.8 %expert_product.1 = f32[8,69632]{1,0:T(8,128)} custom-call(f32[8,2]{1,0:T(8,128)} %multiply_select_fusion.coef_ref, bf16[544,128]{1,0:T(8,128)(2,1)} %total_sum.1.refs_0_, bf16[544,128]{1,0:T(8,128)(2,1)} %copy-done.1, bf16[544,128]{1,0:T(8,128)(2,1)} %copy-done.2, bf16[544,128]{1,0:T(8,128)(2,1)} %copy-done.3), custom_call_target="tpu_custom_call" | custom-call | tf_op jit(solution)/shard_map/expert_product/pallas_call | solution.py:379
  (60 shorter events, 3.7 us)
Async XLA Ops:
  11.7 21.3 %collective-permute-start.11 = (bf16[2176,128]{1,0:T(8,128)(2,1)}, bf16[2176,128]{1,0:T(8,128)(2,1)S(1)}, u32[]{:S(2)}, u32[]{:S(2)}) collective-permute-start(bf16[2176,128]{1,0:T(8,128)(2,1)} %get-tuple-element.17), channel_id=1, source_target_pairs={{0,1},{1,0},{2,3},{3,2},{4,5},{5,4},{6,7},{7,6},{8,9},{9,8},{10,11... | collective-permute-start | bytes 1671176 | tf_op jit(solution)/shard_map/ppermute | solution.py:414
  16.2 9.6 %collective-permute-start = (bf16[2,272,128]{2,1,0:T(8,128)(2,1)}, bf16[2,272,128]{2,1,0:T(8,128)(2,1)S(1)}, u32[]{:S(2)}, u32[]{:S(2)}) collective-permute-start(bf16[2,272,128]{2,1,0:T(8,128)(2,1)} %merge.1.rest_0_), channel_id=1, source_target_pairs={{0,4},{4,0},{8,12},{12,8},{1,5},{5,1},{9,13},{13,9},{2,6},{6,2},{1... | collective-permute-start | bytes 417800 | tf_op jit(solution)/shard_map/ppermute | solution.py:414
  18.8 13.6 %collective-permute-start.1 = (bf16[2,272,128]{2,1,0:T(8,128)(2,1)}, bf16[2,272,128]{2,1,0:T(8,128)(2,1)S(1)}, u32[]{:S(2)}, u32[]{:S(2)}) collective-permute-start(bf16[2,272,128]{2,1,0:T(8,128)(2,1)} %merge.1.rest_0_), channel_id=1, source_target_pairs={{0,8},{4,12},{8,0},{12,4},{1,9},{5,13},{9,1},{13,5},{2,10},{6,14},... | collective-permute-start | bytes 417800 | tf_op jit(solution)/shard_map/ppermute | solution.py:414
  21.4 11.1 %collective-permute-start.2 = (bf16[2,272,128]{2,1,0:T(8,128)(2,1)}, bf16[2,272,128]{2,1,0:T(8,128)(2,1)S(1)}, u32[]{:S(2)}, u32[]{:S(2)}) collective-permute-start(bf16[2,272,128]{2,1,0:T(8,128)(2,1)} %merge.1.rest_0_), channel_id=1, source_target_pairs={{0,12},{4,8},{8,4},{12,0},{1,13},{5,9},{9,5},{13,1},{2,14},{6,10},... | collective-permute-start | bytes 417800 | tf_op jit(solution)/shard_map/ppermute | solution.py:414
  21.4 16.9 %collective-permute-start.3 = (bf16[2,272,128]{2,1,0:T(8,128)(2,1)}, bf16[2,272,128]{2,1,0:T(8,128)(2,1)S(1)}, u32[]{:S(2)}, u32[]{:S(2)}) collective-permute-start(bf16[2,272,128]{2,1,0:T(8,128)(2,1)} %merge.1.rest_0_), channel_id=1, source_target_pairs={{0,1},{1,0},{2,3},{3,2},{4,5},{5,4},{6,7},{7,6},{8,9},{9,8},{10,11... | collective-permute-start | bytes 417800 | tf_op jit(solution)/shard_map/ppermute | solution.py:414
  25.9 16.2 %copy-start.7 = (bf16[2,272,128]{2,1,0:T(8,128)(2,1)}, bf16[2,272,128]{2,1,0:T(8,128)(2,1)S(1)}, u32[]{:S(2)}) copy-start(bf16[2,272,128]{2,1,0:T(8,128)(2,1)S(1)} %collective-permute-done.rest_1_) | copy-start | bytes 417796
  25.9 13.5 %collective-permute-start.4 = (bf16[2,272,128]{2,1,0:T(8,128)(2,1)S(1)}, bf16[2,272,128]{2,1,0:T(8,128)(2,1)S(1)}, u32[]{:S(2)}, u32[]{:S(2)}) collective-permute-start(bf16[2,272,128]{2,1,0:T(8,128)(2,1)S(1)} %collective-permute-done.rest_1_), channel_id=1, source_target_pairs={{0,1},{1,0},{2,3},{3,2},{4,5},{5,4},{6,7},{7,6},{8,9},{9,8},{10,11... | collective-permute-start | bytes 417800 | tf_op jit(solution)/shard_map/ppermute | solution.py:414
  32.5 9.6 %copy-start.8 = (bf16[2,272,128]{2,1,0:T(8,128)(2,1)}, bf16[2,272,128]{2,1,0:T(8,128)(2,1)S(1)}, u32[]{:S(2)}) copy-start(bf16[2,272,128]{2,1,0:T(8,128)(2,1)S(1)} %collective-permute-done.1.rest_2_) | copy-start | bytes 417796
  32.5 9.6 %collective-permute-start.5 = (bf16[2,272,128]{2,1,0:T(8,128)(2,1)S(1)}, bf16[2,272,128]{2,1,0:T(8,128)(2,1)S(1)}, u32[]{:S(2)}, u32[]{:S(2)}) collective-permute-start(bf16[2,272,128]{2,1,0:T(8,128)(2,1)S(1)} %collective-permute-done.1.rest_2_), channel_id=1, source_target_pairs={{0,1},{1,0},{2,3},{3,2},{4,5},{5,4},{6,7},{7,6},{8,9},{9,8},{10,11... | collective-permute-start | bytes 417800 | tf_op jit(solution)/shard_map/ppermute | solution.py:414
  32.5 9.6 %copy-start.9 = (bf16[2,272,128]{2,1,0:T(8,128)(2,1)}, bf16[2,272,128]{2,1,0:T(8,128)(2,1)S(1)}, u32[]{:S(2)}) copy-start(bf16[2,272,128]{2,1,0:T(8,128)(2,1)S(1)} %collective-permute-done.2.rest_3_) | copy-start | bytes 417796
  32.5 9.6 %collective-permute-start.6 = (bf16[2,272,128]{2,1,0:T(8,128)(2,1)S(1)}, bf16[2,272,128]{2,1,0:T(8,128)(2,1)S(1)}, u32[]{:S(2)}, u32[]{:S(2)}) collective-permute-start(bf16[2,272,128]{2,1,0:T(8,128)(2,1)S(1)} %collective-permute-done.2.rest_3_), channel_id=1, source_target_pairs={{0,1},{1,0},{2,3},{3,2},{4,5},{5,4},{6,7},{7,6},{8,9},{9,8},{10,11... | collective-permute-start | bytes 417800 | tf_op jit(solution)/shard_map/ppermute | solution.py:414
  33.0 0.8 %copy-start = (bf16[2176,128]{1,0:T(8,128)(2,1)}, bf16[2176,128]{1,0:T(8,128)(2,1)S(1)}, u32[]{:S(2)}) copy-start(bf16[2176,128]{1,0:T(8,128)(2,1)S(1)} %collective-permute-done.11.came_ref) | copy-start | bytes 1671172
  35.9 15.2 %collective-permute-start.12 = (bf16[544,128]{1,0:T(8,128)(2,1)}, bf16[544,128]{1,0:T(8,128)(2,1)S(1)}, u32[]{:S(2)}, u32[]{:S(2)}) collective-permute-start(bf16[544,128]{1,0:T(8,128)(2,1)} %get-tuple-element.19), channel_id=1, source_target_pairs={{0,4},{4,0},{8,12},{12,8},{1,5},{5,1},{9,13},{13,9},{2,6},{6,2},{1... | collective-permute-start | bytes 417800 | tf_op jit(solution)/shard_map/ppermute | solution.py:414
  38.3 3.9 %copy-start.10 = (bf16[2,272,128]{2,1,0:T(8,128)(2,1)}, bf16[2,272,128]{2,1,0:T(8,128)(2,1)S(1)}, u32[]{:S(2)}) copy-start(bf16[2,272,128]{2,1,0:T(8,128)(2,1)S(1)} %collective-permute-done.3.rest_4_) | copy-start | bytes 417796
  38.3 13.6 %collective-permute-start.13 = (bf16[544,128]{1,0:T(8,128)(2,1)}, bf16[544,128]{1,0:T(8,128)(2,1)S(1)}, u32[]{:S(2)}, u32[]{:S(2)}) collective-permute-start(bf16[544,128]{1,0:T(8,128)(2,1)} %get-tuple-element.20), channel_id=1, source_target_pairs={{0,8},{4,12},{8,0},{12,4},{1,9},{5,13},{9,1},{13,5},{2,10},{6,14},... | collective-permute-start | bytes 417800 | tf_op jit(solution)/shard_map/ppermute | solution.py:414
  39.3 2.8 %copy-start.11 = (bf16[2,272,128]{2,1,0:T(8,128)(2,1)}, bf16[2,272,128]{2,1,0:T(8,128)(2,1)S(1)}, u32[]{:S(2)}) copy-start(bf16[2,272,128]{2,1,0:T(8,128)(2,1)S(1)} %collective-permute-done.4.rest_5_) | copy-start | bytes 417796
  39.3 12.6 %collective-permute-start.14 = (bf16[544,128]{1,0:T(8,128)(2,1)}, bf16[544,128]{1,0:T(8,128)(2,1)S(1)}, u32[]{:S(2)}, u32[]{:S(2)}) collective-permute-start(bf16[544,128]{1,0:T(8,128)(2,1)} %get-tuple-element.21), channel_id=1, source_target_pairs={{0,12},{4,8},{8,4},{12,0},{1,13},{5,9},{9,5},{13,1},{2,14},{6,10},... | collective-permute-start | bytes 417800 | tf_op jit(solution)/shard_map/ppermute | solution.py:414
  42.1 0.7 copy-start.13
  42.8 14.2 %copy-start.18 = (f32[2,32]{1,0:T(2,128)S(1)}, f32[2,32]{1,0:T(2,128)}, u32[]{:S(2)}) copy-start(f32[2,32]{1,0:T(2,128)} %param.20) | copy-start | bytes 772
  51.0 0.9 %copy-start.4 = (bf16[544,128]{1,0:T(8,128)(2,1)}, bf16[544,128]{1,0:T(8,128)(2,1)S(1)}, u32[]{:S(2)}) copy-start(bf16[544,128]{1,0:T(8,128)(2,1)S(1)} %collective-permute-done.12.refs_1_) | copy-start | bytes 417796
  51.9 0.7 copy-start.6
  54.5 8.4 %collective-permute-start.15 = (bf16[544,128]{1,0:T(8,128)(2,1)}, bf16[544,128]{1,0:T(8,128)(2,1)S(1)}, u32[]{:S(2)}, u32[]{:S(2)}) collective-permute-start(bf16[544,128]{1,0:T(8,128)(2,1)} %total_sum.1.refs_0_), channel_id=1, source_target_pairs={{0,2},{1,3},{2,0},{3,1},{4,6},{5,7},{6,4},{7,5},{8,10},{9,11},{10,... | collective-permute-start | bytes 417800 | tf_op jit(solution)/shard_map/ppermute | solution.py:414
  57.0 5.9 %collective-permute-start.7 = (bf16[9,32,128]{2,1,0:T(8,128)(2,1)S(1)}, bf16[9,32,128]{2,1,0:T(8,128)(2,1)S(1)}, u32[]{:S(2)}, u32[]{:S(2)}) collective-permute-start(bf16[9,32,128]{2,1,0:T(8,128)(2,1)S(1)} %get-tuple-element.27), channel_id=1, source_target_pairs={{0,1},{1,2},{2,3},{3,0},{4,5},{5,6},{6,7},{7,4},{8,9},{9,10},{10,1... | collective-permute-start | bytes 221192 | tf_op jit(solution)/shard_map/ppermute | solution.py:419
  57.3 6.7 %collective-permute-start.8 = (bf16[9,32,128]{2,1,0:T(8,128)(2,1)S(1)}, bf16[9,32,128]{2,1,0:T(8,128)(2,1)S(1)}, u32[]{:S(2)}, u32[]{:S(2)}) collective-permute-start(bf16[9,32,128]{2,1,0:T(8,128)(2,1)S(1)} %get-tuple-element.26), channel_id=1, source_target_pairs={{0,3},{1,0},{2,1},{3,2},{4,7},{5,4},{6,5},{7,6},{8,11},{9,8},{10,9... | collective-permute-start | bytes 221192 | tf_op jit(solution)/shard_map/ppermute | solution.py:419
  59.0 6.3 %collective-permute-start.9 = (bf16[9,32,128]{2,1,0:T(8,128)(2,1)S(1)}, bf16[9,32,128]{2,1,0:T(8,128)(2,1)S(1)}, u32[]{:S(2)}, u32[]{:S(2)}) collective-permute-start(bf16[9,32,128]{2,1,0:T(8,128)(2,1)S(1)} %get-tuple-element.25), channel_id=1, source_target_pairs={{0,4},{4,8},{8,12},{12,0},{1,5},{5,9},{9,13},{13,1},{2,6},{6,10},{... | collective-permute-start | bytes 221192 | tf_op jit(solution)/shard_map/ppermute | solution.py:419
  61.7 4.4 %collective-permute-start.10 = (bf16[9,32,128]{2,1,0:T(8,128)(2,1)S(1)}, bf16[9,32,128]{2,1,0:T(8,128)(2,1)S(1)}, u32[]{:S(2)}, u32[]{:S(2)}) collective-permute-start(bf16[9,32,128]{2,1,0:T(8,128)(2,1)S(1)} %get-tuple-element.24), channel_id=1, source_target_pairs={{0,12},{4,0},{8,4},{12,8},{1,13},{5,1},{9,5},{13,9},{2,14},{6,2},{... | collective-permute-start | bytes 221192 | tf_op jit(solution)/shard_map/ppermute | solution.py:419
  62.8 3.3 %copy-start.14 = (bf16[9,32,128]{2,1,0:T(8,128)(2,1)}, bf16[9,32,128]{2,1,0:T(8,128)(2,1)S(1)}, u32[]{:S(2)}) copy-start(bf16[9,32,128]{2,1,0:T(8,128)(2,1)S(1)} %collective-permute-done.7.a_ref) | copy-start | bytes 221188
  62.8 6.2 %collective-permute-start.16 = (bf16[544,128]{1,0:T(8,128)(2,1)}, bf16[544,128]{1,0:T(8,128)(2,1)S(1)}, u32[]{:S(2)}, u32[]{:S(2)}) collective-permute-start(bf16[544,128]{1,0:T(8,128)(2,1)} %total_sum.1.refs_0_), channel_id=1, source_target_pairs={{0,1},{1,0},{2,3},{3,2},{4,5},{5,4},{6,7},{7,6},{8,9},{9,8},{10,11... | collective-permute-start | bytes 417800 | tf_op jit(solution)/shard_map/ppermute | solution.py:414
  62.8 6.2 %copy-start.1 = (bf16[544,128]{1,0:T(8,128)(2,1)}, bf16[544,128]{1,0:T(8,128)(2,1)S(1)}, u32[]{:S(2)}) copy-start(bf16[544,128]{1,0:T(8,128)(2,1)S(1)} %collective-permute-done.15.refs_1_) | copy-start | bytes 417796
  62.8 6.2 %collective-permute-start.17 = (bf16[544,128]{1,0:T(8,128)(2,1)S(1)}, bf16[544,128]{1,0:T(8,128)(2,1)S(1)}, u32[]{:S(2)}, u32[]{:S(2)}) collective-permute-start(bf16[544,128]{1,0:T(8,128)(2,1)S(1)} %collective-permute-done.15.refs_1_), channel_id=1, source_target_pairs={{0,1},{1,0},{2,3},{3,2},{4,5},{5,4},{6,7},{7,6},{8,9},{9,8},{10,11... | collective-permute-start | bytes 417800 | tf_op jit(solution)/shard_map/ppermute | solution.py:414
  63.9 2.2 %copy-start.15 = (bf16[9,32,128]{2,1,0:T(8,128)(2,1)}, bf16[9,32,128]{2,1,0:T(8,128)(2,1)S(1)}, u32[]{:S(2)}) copy-start(bf16[9,32,128]{2,1,0:T(8,128)(2,1)S(1)} %collective-permute-done.8.b_ref) | copy-start | bytes 221188
  65.3 0.8 %copy-start.16 = (bf16[9,32,128]{2,1,0:T(8,128)(2,1)}, bf16[9,32,128]{2,1,0:T(8,128)(2,1)S(1)}, u32[]{:S(2)}) copy-start(bf16[9,32,128]{2,1,0:T(8,128)(2,1)S(1)} %collective-permute-done.9.c_ref) | copy-start | bytes 221188
  (5 other events, 3.3 us)

commit v2 on v1

--- a/solution.py
+++ b/solution.py
@@ -19,7 +19,15 @@
 
 VMEM = pl.BlockSpec(memory_space=pltpu.VMEM)
 SMEM = pl.BlockSpec(memory_space=pltpu.SMEM)
-PARAMS = pltpu.CompilerParams(vmem_limit_bytes=56 * 1024 * 1024)
+HBM = pl.BlockSpec(memory_space=pltpu.HBM)
+
+
+def limits(mebibytes):
+    return pltpu.CompilerParams(vmem_limit_bytes=mebibytes * 1024 * 1024)
+
+
+def cost(flops, moved):
+    return pl.CostEstimate(flops=flops, bytes_accessed=moved, transcendentals=0)
 
 
 def nn(left, right):
@@ -38,34 +46,45 @@
     return high, middle, low
 
 
-def merge_kernel(coef_ref, experts_ref, out_ref):
-    members, wide = coef_ref.shape
-    experts = experts_ref.shape[0]
+def merge_kernel(coef_ref, experts_ref, out_ref, held, arrived):
+    members, experts = coef_ref.shape
     rows = out_ref.shape[1]
+    start = pl.multiple_of(lax.rem(lax.axis_index("gx"), 2) * rows * 128, 128)
+    stripes = arrived.shape[0]
+    blocks = rows // 16
+    edges = [blocks * stripe // stripes for stripe in range(stripes + 1)]
+    copies = []
+    for stripe in range(stripes):
+        at, wide = edges[stripe] * 2048, (edges[stripe + 1] - edges[stripe]) * 2048
+        copies.append(
+            pltpu.make_async_copy(
+                experts_ref.at[:, pl.ds(start + at, wide)], held.at[:, pl.ds(at, wide)], arrived.at[stripe]
+            )
+        )
+        copies[-1].start()
+    wide = 8 * experts
     row = lax.broadcasted_iota(jnp.int32, (8, wide), 0)
     col = lax.broadcasted_iota(jnp.int32, (8, wide), 1)
     diagonal = row == col // experts
-    pieces = []
-    for member in range(members):
-        pieces.append(jnp.where(diagonal, coef_ref[member : member + 1, :], 0.0))
-    left = jnp.concatenate(pieces, axis=0)
-    lefts = jnp.concatenate(split3(left), axis=0)
+    source = lax.broadcasted_iota(jnp.int32, (experts, wide), 0)
+    target = lax.broadcasted_iota(jnp.int32, (experts, wide), 1)
+    tile = (source == target % experts).astype(F32).astype(BF16)
+    lefts = []
+    for term in split3(coef_ref[...]):
+        tiled = nn(term, tile)
+        for member in range(members):
+            lefts.append(jnp.where(diagonal, tiled[member : member + 1, :], 0.0).astype(BF16))
+    lefts = jnp.concatenate(lefts, axis=0)
     height = 8 * members
-    for block in range(rows // 16):
-        right = jnp.concatenate(
-            [
-                jnp.concatenate(
-                    [
-                        experts_ref[:, (block * 16 + half * 8 + g) * 128 : (block * 16 + half * 8 + g + 1) * 128]
-                        for g in range(8)
-                    ],
-                    axis=0,
-                )
-                for half in range(2)
-            ],
-            axis=1,
-        )
-        product = nn(lefts, right)
+    for block in range(blocks):
+        if block in edges:
+            copies[edges.index(block)].wait()
+        halves = []
+        for half in range(2):
+            first = block * 16 + half * 8
+            groups = [held[:, (first + g) * 128 : (first + g + 1) * 128] for g in range(8)]
+            halves.append(jnp.concatenate(groups, axis=0))
+        product = nn(lefts, jnp.concatenate(halves, axis=1))
         total = product[:height] + product[height : 2 * height] + product[2 * height :]
         for member in range(members):
             part = total[member * 8 : member * 8 + 8]
@@ -74,29 +93,24 @@
             ).astype(BF16)
 
 
-def merge(coef, experts, core, parts):
+def merge(coef, experts, parts):
     members, count = coef.shape
     columns = experts.shape[1] // parts
     rows = columns // 128
     return pl.pallas_call(
-        lambda ids_ref, coef_ref, experts_ref, out_ref: merge_kernel(coef_ref, experts_ref, out_ref),
-        grid_spec=pltpu.PrefetchScalarGridSpec(
-            num_scalar_prefetch=1,
-            grid=(1,),
-            in_specs=[
-                pl.BlockSpec((members, 8 * count), lambda i, ids: (0, 0)),
-                pl.BlockSpec((count, columns), lambda i, ids: (0, ids[0])),
-            ],
-            out_specs=pl.BlockSpec((members, rows, 128), lambda i, ids: (0, 0, 0)),
-        ),
+        merge_kernel,
+        in_specs=[VMEM, HBM],
+        out_specs=VMEM,
         out_shape=jax.ShapeDtypeStruct((members, rows, 128), BF16),
-        compiler_params=PARAMS,
+        scratch_shapes=[pltpu.VMEM((count, columns), BF16), pltpu.SemaphoreType.DMA((4,))],
+        compiler_params=limits(60),
+        cost_estimate=cost(96 * 16 * columns, 2 * count * columns),
         name="merge",
-    )(core, jnp.tile(coef, (1, 8)), experts)
+    )(coef, experts)
 
 
 def features_kernel(
-    ids_ref, live_ref, near_ref, class_ref, zero_ref, one_ref, two_ref, source_ref, target_ref,
+    live_ref, near_ref, class_ref, zero_ref, one_ref, two_ref, source_ref, target_ref,
     other_ref, own_ref, pulled_ref, edge_ref,
     source_t, target_t, moved, spread, rotated, grads,
     *, fanout,
@@ -168,7 +182,7 @@
     zw, pw = 3 * channels, 2 * channels
     first = zw * zw // 128
     second = first + pw * pw // 128
-    own = ids_ref[1].astype(F32)
+    own = lax.rem(lax.axis_index("gx"), 2).astype(F32)
     for out_ref, wanted in ((other_ref, 1.0 - own), (own_ref, own)):
         mask = (edge_ref[1:2, :] == wanted).astype(F32).astype(BF16)
         qz = pulled_ref[0:zw, :] * mask
@@ -186,14 +200,14 @@
         out_ref[...] = grads[...].astype(BF16)
 
 
-def features(ids, live, near, classes, zero, one, two, source, target, rows, fanout):
+def features(live, near, classes, zero, one, two, source, target, rows, fanout):
     slots, channels = source.shape[1:]
     atoms = target.shape[1]
     edges = atoms * fanout
     shape = jax.ShapeDtypeStruct
     return pl.pallas_call(
         functools.partial(features_kernel, fanout=fanout),
-        in_specs=[SMEM, SMEM] + [VMEM] * 7,
+        in_specs=[SMEM] + [VMEM] * 7,
         out_specs=[VMEM] * 4,
         out_shape=[
             shape((rows, 128), BF16),
@@ -209,16 +223,18 @@
             pltpu.VMEM((7 * channels, edges), BF16),
             pltpu.VMEM((rows, 128), F32),
         ],
-        compiler_params=PARAMS,
+        compiler_params=limits(24),
+        cost_estimate=cost(9 * 10**9, 7 * 10**6),
         name="features",
-    )(ids, live, near, classes, zero, one, two, source, target)
+    )(live, near, classes, zero, one, two, source, target)
 
 
 def back_kernel(
-    places_ref, edge_ref, zero_ref, one_ref, two_ref, pulled_ref, *rest, pieces, members, atoms, face,
+    edge_ref, zero_ref, one_ref, two_ref, pulled_ref, *rest, pieces, members, atoms, face, places,
 ):
     piece_refs = rest[:pieces]
-    own_ref, ghost_ref, flat, weight_zero, weight_pair, field, turned, pick_all = rest[pieces:]
+    own_ref, *ghost_refs = rest[pieces : pieces + 5]
+    flat, weight_zero, weight_pair, field, turned, pick_all = rest[pieces + 5 :]
     rows = flat.shape[1]
     channels = own_ref.shape[2]
     slots = pick_all.shape[0]
@@ -226,9 +242,9 @@
     zw, pw = 3 * channels, 2 * channels
     first = zw * zw // 128
     second = first + pw * pw // 128
-    for index, piece in enumerate(piece_refs):
+    for piece, place in zip(piece_refs, places()):
         height = piece.shape[1]
-        at = pl.ds(pl.multiple_of(places_ref[index], 16), height)
+        at = pl.ds(pl.multiple_of(place, 16), height)
         for k in range(members):
             flat[k, at, :] = piece[k].astype(F32)
     for k in range(members):
@@ -293,19 +309,21 @@
         own_ref[c] = summed[:atoms]
         for block in range(4):
             at = atoms + block * face
-            ghost_ref[block, c] = summed[at : at + face].astype(BF16)
-
-
-def back(places, edge, zero, one, two, pulled, pieces, rows, atoms, slots, face):
+            ghost_refs[block][c] = summed[at : at + face].astype(BF16)
+
+
+def back(edge, zero, one, two, pulled, pieces, places, rows, atoms, slots, face):
     members = pieces[0].shape[0]
     edges = pulled.shape[1]
     channels = pulled.shape[0] // 7
     shape = jax.ShapeDtypeStruct
     return pl.pallas_call(
-        functools.partial(back_kernel, pieces=len(pieces), members=members, atoms=atoms, face=face),
-        in_specs=[SMEM] + [VMEM] * (5 + len(pieces)),
-        out_specs=[VMEM] * 2,
-        out_shape=[shape((9, atoms, channels), F32), shape((4, 9, face, channels), BF16)],
+        functools.partial(
+            back_kernel, pieces=len(pieces), members=members, atoms=atoms, face=face, places=places
+        ),
+        in_specs=[VMEM] * (5 + len(pieces)),
+        out_specs=[VMEM] * 5,
+        out_shape=[shape((9, atoms, channels), F32), *[shape((9, face, channels), BF16)] * 4],
         scratch_shapes=[
             pltpu.VMEM((members, rows, 128), F32),
             pltpu.VMEM((3 * channels, members * 3 * channels), BF16),
@@ -314,28 +332,31 @@
             pltpu.VMEM((9 * channels, edges), BF16),
             pltpu.VMEM((slots, edges), BF16),
         ],
-        compiler_params=PARAMS,
+        compiler_params=limits(24),
+        cost_estimate=cost(9 * 10**9, 7 * 10**6),
         name="back",
-    )(places, edge, zero, one, two, pulled, *pieces)
-
-
-def pair_kernel(places_ref, own_ref, came_ref, *out_refs):
+    )(edge, zero, one, two, pulled, *pieces)
+
+
+def pair_kernel(own_ref, came_ref, *out_refs):
     height = out_refs[0].shape[0]
+    row = lax.axis_index("yz")
     for index, out_ref in enumerate(out_refs):
-        at = pl.ds(pl.multiple_of(places_ref[index], 16), height)
+        at = pl.ds(pl.multiple_of((row ^ index) * height, 16), height)
         out_ref[...] = (own_ref[at, :].astype(F32) + came_ref[at, :].astype(F32)).astype(BF16)
 
 
-def pair_sum(places, own, came, count):
+def pair_sum(own, came, count):
     height = own.shape[0] // count
     return pl.pallas_call(
         pair_kernel,
-        in_specs=[SMEM, VMEM, VMEM],
+        in_specs=[VMEM, VMEM],
         out_specs=[VMEM] * count,
         out_shape=[jax.ShapeDtypeStruct((height, 128), BF16)] * count,
-        compiler_params=PARAMS,
+        compiler_params=limits(6),
+        cost_estimate=cost(10**6, 2 * 10**6),
         name="pair_sum",
-    )(places, own, came)
+    )(own, came)
 
 
 def total_kernel(*refs):
@@ -351,38 +372,47 @@
         in_specs=[VMEM] * len(parts),
         out_specs=VMEM,
         out_shape=jax.ShapeDtypeStruct(parts[0].shape, BF16),
-        compiler_params=PARAMS,
+        compiler_params=limits(6),
+        cost_estimate=cost(10**6, 10**6),
         name="total_sum",
     )(*parts)
 
 
-def expert_kernel(coef_ref, *refs):
+def expert_kernel(coef_ref, *refs, scale):
     sums, out_ref, summed = refs[:-2], refs[-2], refs[-1]
+    owned = out_ref.shape[0]
+    place = lax.axis_index("gx")
+    row = lax.broadcasted_iota(jnp.int32, (owned, coef_ref.shape[1]), 0)
+    col = lax.broadcasted_iota(jnp.int32, (owned, coef_ref.shape[1]), 1)
+    chosen = col == row + place * owned
+    picked = [
+        jnp.sum(jnp.where(chosen, coef_ref[k : k + 1, :], 0.0), axis=1, keepdims=True) * scale for k in range(2)
+    ]
+    even = lax.rem(place, 2) == 0
+    first = jnp.broadcast_to(jnp.where(even, picked[0], picked[1]), (owned, 128))
+    second = jnp.broadcast_to(jnp.where(even, picked[1], picked[0]), (owned, 128))
     half = len(sums) // 2
     for side in range(2):
         total = sums[side * half][...].astype(F32)
         for ref in sums[side * half + 1 : (side + 1) * half]:
             total += ref[...].astype(F32)
         summed[side] = total
-    owned = coef_ref.shape[0]
-    first = jnp.broadcast_to(coef_ref[:, 0:1], (owned, 128))
-    second = jnp.broadcast_to(coef_ref[:, 1:2], (owned, 128))
     for row in range(summed.shape[1]):
         out_ref[:, row * 128 : (row + 1) * 128] = (
             first * summed[0, row : row + 1, :] + second * summed[1, row : row + 1, :]
         )
 
 
-def expert_product(coef, sums):
+def expert_product(coef, sums, owned, scale):
     rows = sums[0].shape[0]
-    owned = coef.shape[0]
-    return pl.pallas_call(
-        expert_kernel,
+    return pl.pallas_call(
+        functools.partial(expert_kernel, scale=scale),
         in_specs=[VMEM] * (1 + len(sums)),
         out_specs=VMEM,
         out_shape=jax.ShapeDtypeStruct((owned, rows * 128), F32),
         scratch_shapes=[pltpu.VMEM((2, rows, 128), F32)],
-        compiler_params=PARAMS,
+        compiler_params=limits(8),
+        cost_estimate=cost(10**6, 4 * 10**6),
         name="expert_product",
     )(coef, *sums)
 
@@ -405,7 +435,8 @@
         in_specs=[VMEM] * 6,
         out_specs=VMEM,
         out_shape=jax.ShapeDtypeStruct(own.shape, BF16),
-        compiler_params=PARAMS,
+        compiler_params=limits(6),
+        cost_estimate=cost(10**8, 2 * 10**6),
         name="finish",
     )(send, own, *returned)
 
@@ -437,39 +468,37 @@
     zero = rot_zero.reshape(1, -1)
     source = jnp.transpose(saved_input, (1, 0, 2))
     target = jnp.transpose(cotangent, (1, 0, 2))
-    ids = jnp.stack([core, core]).astype(jnp.int32)
 
     if direct:
         half = height // 2
-        mine = merge(merge_coef, experts, core.reshape(1).astype(jnp.int32), 2)
+        mine = merge(merge_coef, experts, 2)
         held = [mine] + [swap(mine, "yz", k) for k in range(1, count_yz)]
-        facing = [swap(piece, "gx", 1) for piece in held]
-        pieces = held + facing
-        starts = jnp.stack([(row ^ k) * height for k in range(count_yz)])
-        places = jnp.concatenate([starts + core * half, starts + (1 - core) * half]).astype(jnp.int32)
+        source, target, mine = lax.optimization_barrier((source, target, mine))
+
+        def places():
+            here, side = lax.axis_index("yz"), lax.rem(lax.axis_index("gx"), 2)
+            starts = [(here ^ k) * height for k in range(count_yz)]
+            return [at + side * half for at in starts] + [at + (1 - side) * half for at in starts]
     else:
         part = jnp.dot(merge_coef, experts.astype(F32), precision=lax.Precision.HIGHEST).astype(BF16)
         merged = lax.all_gather(part, "yz", axis=1, tiled=True)
         pieces = [merged.reshape(merged.shape[0], rows, 128)]
-        places = jnp.zeros((1,), jnp.int32)
+
+        def places():
+            return [0]
 
     other, own, pulled, edge = features(
-        ids, live_blocks, neighbours.T, atom_class.reshape(1, -1), zero, rot_one, rot_two, source, target,
-        rows, fanout,
-    )
-    per_owner = merge_coef.shape[1] // count_gx
-    owned = lax.dynamic_slice_in_dim(merge_coef, column * per_owner, per_owner, 1)
-    grad_scale = math.sqrt(fanout / (atoms * count_yz * count_gx))
-    owned = owned.T * grad_scale
-    owned = jnp.where(core == 0, owned, owned[:, ::-1])
-    if direct:
-        came = swap(other, "gx", 1)
-        parts = pair_sum(starts.astype(jnp.int32), own, came, count_yz)
-        gathered = [parts[0]] + [swap(parts[k], "yz", k) for k in range(1, count_yz)]
-    grad_own, ghosts = back(
-        places, edge, zero, rot_one, rot_two, pulled, pieces, rows, atoms, slots, face
+        live_blocks, neighbours.T, atom_class.reshape(1, -1), zero, rot_one, rot_two, source, target, rows, fanout
     )
     if direct:
+        other, *held = lax.optimization_barrier((other, *held))
+        came = swap(other, "gx", 1)
+        parts = pair_sum(own, came, count_yz)
+        gathered = [parts[0]] + [swap(parts[k], "yz", k) for k in range(1, count_yz)]
+        pieces = held + [swap(piece, "gx", 1) for piece in held]
+    grad_own, *ghosts = back(edge, zero, rot_one, rot_two, pulled, pieces, places, rows, atoms, slots, face)
+    if direct:
+        grad_own, *gathered = lax.optimization_barrier((grad_own, *gathered))
         summed = total_sum(gathered)
         across = swap(summed, "gx", 2)
         sums = [summed, across, swap(summed, "gx", 1), swap(across, "gx", 1)]
@@ -483,7 +512,8 @@
     returned = [
         shift(ghosts[1], "gx", 1), shift(ghosts[0], "gx", -1), shift(ghosts[3], "yz", 1), shift(ghosts[2], "yz", -1),
     ]
-    expert_grad = expert_product(owned, sums)
+    grad_scale = math.sqrt(fanout / (atoms * count_yz * count_gx))
+    expert_grad = expert_product(merge_coef, sums, merge_coef.shape[1] // count_gx, grad_scale)
     input_grad = finish(send_index, grad_own, returned)
     return (jnp.transpose(input_grad, (1, 0, 2)), expert_grad)
 

time: 73.5 us -> 54.7 us (0.74)
  Pallas kernels: 29.8 us -> 19.3 us
  local copies, waits for them, and re-layouts: 6.73 us -> 0.04 us
  other arithmetic: 3.09 us -> 0 us
  waiting for transfers between devices: 13.4 us -> 14.6 us
    unnamed x39 -> x20, local copies, waits for them, and re-layouts: 4.23 us -> 0.04 us
    pallas_call x1, Pallas kernels: 8.25 us -> 5.47 us  [back(): pl.pallas_call(functools.partial(back_kernel, pieces=len(pieces), members...]
    pallas_call x1, Pallas kernels: 9.79 us -> 7.32 us  [features(): pl.pallas_call(functools.partial(features_kernel, fanout=fanout), in_spec...]
    pallas_call x3, Pallas kernels: 7.68 us -> 5.24 us  [the longest x1 3.39 us: merge(): pl.pallas_call(merge_kernel, in_specs=[VMEM, HBM], out_specs=VMEM, out_sh...]
    pallas_call x1, Pallas kernels: 1.82 us -> 0.07 us  [total_sum(): pl.pallas_call(total_kernel, in_specs=[VMEM] * len(parts), out_specs=VMEM...]
    another operation x3 -> x0, local copies, waits for them, and re-layouts: 1.41 us -> none  [the longest x2 1.34 us: merge(): jnp.tile(coef, (1, 8))]
    add x2 -> x0, other arithmetic: 1.32 us -> none  [the longest x1 0.67 us: local(): starts + (1 - core) * half]
    pallas_call x1, Pallas kernels: 2.3 us -> 1.17 us  [finish(): pl.pallas_call(finish_kernel, in_specs=[VMEM] * 6, out_specs=VMEM, out_sh...]
  transfers between devices with their start and end apart: 18 -> 18, of which waited for: 5 -> 6; matrix products, arithmetic and copies ran while one was open for 7% -> 0% of each run, Pallas kernels for 21% -> 26%
where the time goes in v2:
time: 54.7 us; the launch traced here: 54.5 us
  Pallas kernels  19.3 us (35%)
  starting transfers between devices  19.1 us (35%)
  waiting for transfers between devices  14.6 us (27%)
  between operations  1.5 us (3%)
    ppermute x14, starting transfers between devices, swap(): lax.ppermute(value, axis, [(i, i ^ bit) for i in range(lax.axis_size(axis...  13.5 us
    ppermute x14, waiting for transfers between devices, swap(): lax.ppermute(value, axis, [(i, i ^ bit) for i in range(lax.axis_size(axis...  11.3 us
    pallas_call x1, Pallas kernels, features(): pl.pallas_call(functools.partial(features_kernel, fanout=fanout), in_spec...  7.32 us
    ppermute x4, starting transfers between devices, shift(): lax.ppermute(value, axis, [(i, (i + step) % count) for i in range(count)])  5.59 us
    pallas_call x1, Pallas kernels, back(): pl.pallas_call(functools.partial(back_kernel, pieces=len(pieces), members...  5.47 us
    pallas_call x1, Pallas kernels, merge(): pl.pallas_call(merge_kernel, in_specs=[VMEM, HBM], out_specs=VMEM, out_sh...  3.39 us
    ppermute x4, waiting for transfers between devices, shift(): lax.ppermute(value, axis, [(i, (i + step) % count) for i in range(count)])  3.27 us
    pallas_call x1, Pallas kernels, expert_product(): pl.pallas_call(functools.partial(expert_kernel, scale=scale), in_specs=[V...  1.73 us
  transfers between devices with their start and end apart: 18, of which 6 were waited for; matrix products, arithmetic and copies ran while one was open for 0% of the time, Pallas kernels for 26%

profile of v2, /device:TPU:0, one launch (start us, length us, event | category | flops | bytes accessed | tf_op | source)
XLA Modules:
  0.0 54.5 jit_solution(2525738988992490133)
XLA Ops:
  0.7 3.4 %merge.1.rest_0_ = bf16[2,272,128]{2,1,0:T(8,128)(2,1)} custom-call(f32[2,32]{1,0:T(2,128)} %coef_ref.3, bf16[32,69632]{1,0:T(8,128)(2,1)} %experts_ref.1), custom_call_target="tpu_custom_call" | custom-call | flops 53477376 | bytes 2228224 | tf_op jit(solution)/shard_map/merge/pallas_call | solution.py:100
  4.1 5.1 %collective-permute-start.2 = (bf16[2,272,128]{2,1,0:T(8,128)(2,1)}, bf16[2,272,128]{2,1,0:T(8,128)(2,1)S(1)}, u32[]{:S(2)}, u32[]{:S(2)}) collective-permute-start(bf16[2,272,128]{2,1,0:T(8,128)(2,1)} %merge.1.rest_0_), channel_id=1, source_target_pairs={{0,12},{4,8},{8,4},{12,0},{1,13},{5,9},{9,5},{13,1},{2,14},{6,10},... | collective-permute-start | bytes 417800 | tf_op jit(solution)/shard_map/ppermute | solution.py:445
  9.2 0.0 collective-permute-start.1
  9.2 0.6 %collective-permute-start = (bf16[2,272,128]{2,1,0:T(8,128)(2,1)}, bf16[2,272,128]{2,1,0:T(8,128)(2,1)S(1)}, u32[]{:S(2)}, u32[]{:S(2)}) collective-permute-start(bf16[2,272,128]{2,1,0:T(8,128)(2,1)} %merge.1.rest_0_), channel_id=1, source_target_pairs={{0,4},{4,0},{8,12},{12,8},{1,5},{5,1},{9,13},{13,9},{2,6},{6,2},{1... | collective-permute-start | bytes 417800 | tf_op jit(solution)/shard_map/ppermute | solution.py:445
  10.6 7.3 %features.1 = (bf16[2176,128]{1,0:T(8,128)(2,1)S(1)}, bf16[2176,128]{1,0:T(8,128)(2,1)S(1)}, bf16[896,1024]{1,0:T(8,128)(2,1)S(1)}, f32[8,1024]{1,0:T(8,128)S(1)}) custom-call(s32[1]{0:T(128)S(6)} %copy.13.live_ref, s32[8,128]{1,0:T(8,128)S(1)} %bitcast.8, s32[1,128]{1,0:T(1,128)S(1)} %bitcast.11, f32[1,1024]{1,0:T(1,128)S(1)} %bitcast.9, ...), custom_call_target="tpu_custom_call" | custom-call | flops 8999999488 | bytes 7000000 | tf_op jit(solution)/shard_map/features/pallas_call | solution.py:208
  17.9 0.0 collective-permute-done.2.rest_3_
  17.9 3.3 %collective-permute-done.1.rest_2_ = bf16[2,272,128]{2,1,0:T(8,128)(2,1)S(1)} collective-permute-done((bf16[2,272,128]{2,1,0:T(8,128)(2,1)}, bf16[2,272,128]{2,1,0:T(8,128)(2,1)S(1)}, u32[]{:S(2)}, u32[]{:S(2)}) %collective-permute-start.1) | collective-permute-done | bytes 139296 | tf_op jit(solution)/shard_map/ppermute | solution.py:445
  21.2 0.0 collective-permute-start.7
  21.2 0.5 collective-permute-start.3
  21.7 0.1 collective-permute-start.4
  21.8 0.4 collective-permute-start.5
  22.2 0.1 collective-permute-start.6
  22.3 0.9 %collective-permute-done.7.came_ref = bf16[2176,128]{1,0:T(8,128)(2,1)S(1)} collective-permute-done((bf16[2176,128]{1,0:T(8,128)(2,1)S(1)}, bf16[2176,128]{1,0:T(8,128)(2,1)S(1)}, u32[]{:S(2)}, u32[]{:S(2)}) %collective-permute-start.7) | collective-permute-done | bytes 557088 | tf_op jit(solution)/shard_map/ppermute | solution.py:445
  23.2 0.1 pair_sum.1
  23.3 0.1 collective-permute-start.8
  23.4 0.0 collective-permute-done.3.rest_4_
  23.4 3.0 %collective-permute-start.9 = (bf16[544,128]{1,0:T(8,128)(2,1)S(1)}, bf16[544,128]{1,0:T(8,128)(2,1)S(1)}, u32[]{:S(2)}, u32[]{:S(2)}) collective-permute-start(bf16[544,128]{1,0:T(8,128)(2,1)S(1)} %get-tuple-element.41), channel_id=1, source_target_pairs={{0,8},{4,12},{8,0},{12,4},{1,9},{5,13},{9,1},{13,5},{2,10},{6,14},... | collective-permute-start | bytes 417800 | tf_op jit(solution)/shard_map/ppermute | solution.py:445
  26.4 1.3 %collective-permute-start.10 = (bf16[544,128]{1,0:T(8,128)(2,1)S(1)}, bf16[544,128]{1,0:T(8,128)(2,1)S(1)}, u32[]{:S(2)}, u32[]{:S(2)}) collective-permute-start(bf16[544,128]{1,0:T(8,128)(2,1)S(1)} %get-tuple-element.42), channel_id=1, source_target_pairs={{0,12},{4,8},{8,4},{12,0},{1,13},{5,9},{9,5},{13,1},{2,14},{6,10},... | collective-permute-start | bytes 417800 | tf_op jit(solution)/shard_map/ppermute | solution.py:445
  27.8 0.0 copy-start.1
  27.8 5.5 %back.1 = (f32[9,128,128]{2,1,0:T(8,128)S(1)}, bf16[9,32,128]{2,1,0:T(8,128)(2,1)S(1)}, bf16[9,32,128]{2,1,0:T(8,128)(2,1)S(1)}, bf16[9,32,128]{2,1,0:T(8,128)(2,1)S(1)}, bf16[9,32,128]{2,1,0:T(8,128)(2,1)S(1)}) custom-call(f32[8,1024]{1,0:T(8,128)S(1)} %get-tuple-element.29.edge_ref, f32[1,1024]{1,0:T(1,128)S(1)} %bitcast.10, f32[3,3,1024]{2,1,0:T(4,128)S(1)} %copy-done.6, ...), custom_call_target="tpu_custom_call" | custom-call | flops 8999999488 | bytes 7000000 | tf_op jit(solution)/shard_map/back/pallas_call | solution.py:320
  33.3 3.7 %collective-permute-done.9.refs_2_ = bf16[544,128]{1,0:T(8,128)(2,1)S(1)} collective-permute-done((bf16[544,128]{1,0:T(8,128)(2,1)S(1)}, bf16[544,128]{1,0:T(8,128)(2,1)S(1)}, u32[]{:S(2)}, u32[]{:S(2)}) %collective-permute-start.9) | collective-permute-done | bytes 139296 | tf_op jit(solution)/shard_map/ppermute | solution.py:445
  36.9 0.1 total_sum.1.refs_0_
  37.0 1.6 %collective-permute-start.15 = (bf16[544,128]{1,0:T(8,128)(2,1)S(1)}, bf16[544,128]{1,0:T(8,128)(2,1)S(1)}, u32[]{:S(2)}, u32[]{:S(2)}) collective-permute-start(bf16[544,128]{1,0:T(8,128)(2,1)S(1)} %total_sum.1.refs_0_), channel_id=1, source_target_pairs={{0,2},{1,3},{2,0},{3,1},{4,6},{5,7},{6,4},{7,5},{8,10},{9,11},{10,... | collective-permute-start | bytes 417800 | tf_op jit(solution)/shard_map/ppermute | solution.py:445
  38.6 0.6 %collective-permute-start.16 = (bf16[544,128]{1,0:T(8,128)(2,1)S(1)}, bf16[544,128]{1,0:T(8,128)(2,1)S(1)}, u32[]{:S(2)}, u32[]{:S(2)}) collective-permute-start(bf16[544,128]{1,0:T(8,128)(2,1)S(1)} %total_sum.1.refs_0_), channel_id=1, source_target_pairs={{0,1},{1,0},{2,3},{3,2},{4,5},{5,4},{6,7},{7,6},{8,9},{9,8},{10,11... | collective-permute-start | bytes 417800 | tf_op jit(solution)/shard_map/ppermute | solution.py:445
  39.2 3.5 %collective-permute-done.15.refs_1_ = bf16[544,128]{1,0:T(8,128)(2,1)S(1)} collective-permute-done((bf16[544,128]{1,0:T(8,128)(2,1)S(1)}, bf16[544,128]{1,0:T(8,128)(2,1)S(1)}, u32[]{:S(2)}, u32[]{:S(2)}) %collective-permute-start.15) | collective-permute-done | bytes 139296 | tf_op jit(solution)/shard_map/ppermute | solution.py:445
  42.7 1.8 %collective-permute-start.12 = (bf16[9,32,128]{2,1,0:T(8,128)(2,1)S(1)}, bf16[9,32,128]{2,1,0:T(8,128)(2,1)S(1)}, u32[]{:S(2)}, u32[]{:S(2)}) collective-permute-start(bf16[9,32,128]{2,1,0:T(8,128)(2,1)S(1)} %get-tuple-element.45), channel_id=1, source_target_pairs={{0,3},{1,0},{2,1},{3,2},{4,7},{5,4},{6,5},{7,6},{8,11},{9,8},{10,9... | collective-permute-start | bytes 221192 | tf_op jit(solution)/shard_map/ppermute | solution.py:450
  44.5 2.7 %collective-permute-start.13 = (bf16[9,32,128]{2,1,0:T(8,128)(2,1)S(1)}, bf16[9,32,128]{2,1,0:T(8,128)(2,1)S(1)}, u32[]{:S(2)}, u32[]{:S(2)}) collective-permute-start(bf16[9,32,128]{2,1,0:T(8,128)(2,1)S(1)} %get-tuple-element.46), channel_id=1, source_target_pairs={{0,4},{4,8},{8,12},{12,0},{1,5},{5,9},{9,13},{13,1},{2,6},{6,10},{... | collective-permute-start | bytes 221192 | tf_op jit(solution)/shard_map/ppermute | solution.py:450
  47.2 1.1 %collective-permute-start.14 = (bf16[9,32,128]{2,1,0:T(8,128)(2,1)S(1)}, bf16[9,32,128]{2,1,0:T(8,128)(2,1)S(1)}, u32[]{:S(2)}, u32[]{:S(2)}) collective-permute-start(bf16[9,32,128]{2,1,0:T(8,128)(2,1)S(1)} %get-tuple-element.47), channel_id=1, source_target_pairs={{0,12},{4,0},{8,4},{12,8},{1,13},{5,1},{9,5},{13,9},{2,14},{6,2},{... | collective-permute-start | bytes 221192 | tf_op jit(solution)/shard_map/ppermute | solution.py:450
  48.3 2.4 %collective-permute-done.13.c_ref = bf16[9,32,128]{2,1,0:T(8,128)(2,1)S(1)} collective-permute-done((bf16[9,32,128]{2,1,0:T(8,128)(2,1)S(1)}, bf16[9,32,128]{2,1,0:T(8,128)(2,1)S(1)}, u32[]{:S(2)}, u32[]{:S(2)}) %collective-permute-start.13) | collective-permute-done | bytes 73760 | tf_op jit(solution)/shard_map/ppermute | solution.py:450
  50.7 0.8 %collective-permute-done.14.d_ref = bf16[9,32,128]{2,1,0:T(8,128)(2,1)S(1)} collective-permute-done((bf16[9,32,128]{2,1,0:T(8,128)(2,1)S(1)}, bf16[9,32,128]{2,1,0:T(8,128)(2,1)S(1)}, u32[]{:S(2)}, u32[]{:S(2)}) %collective-permute-start.14) | collective-permute-done | bytes 73760 | tf_op jit(solution)/shard_map/ppermute | solution.py:450
  51.6 1.2 %finish.1 = bf16[9,128,128]{2,1,0:T(8,128)(2,1)} custom-call(s32[4,32]{1,0:T(4,128)S(1)} %copy-done.2, f32[9,128,128]{2,1,0:T(8,128)S(1)} %get-tuple-element.43.own_ref, bf16[9,32,128]{2,1,0:T(8,128)(2,1)S(1)} %collective-permute-done.11.a_ref, bf16[9,32,128]{2,1,0:T(8,128)(2,1)S(1)} %collective-permute-done.12.b_ref, ...), custom_call_target="tpu_custom_call" | custom-call | flops 100000000 | bytes 2000000 | tf_op jit(solution)/shard_map/finish/pallas_call | solution.py:433
  52.8 1.7 %expert_product.1 = f32[8,69632]{1,0:T(8,128)} custom-call(f32[2,32]{1,0:T(2,128)S(1)} %copy-done.1, bf16[544,128]{1,0:T(8,128)(2,1)S(1)} %total_sum.1.refs_0_, bf16[544,128]{1,0:T(8,128)(2,1)S(1)} %collective-permute-done.15.refs_1_, bf16[544,128]{1,0:T(8,128)(2,1)S(1)} %collective-permute-done.16.refs_2_, bf16[544,128]{1,0:T(8,128)(2,1)S(1)} %collective-permute-done.17.refs_3_), custom_call_target="tpu_custom_call" | custom-call | flops 1000000 | bytes 4000000 | tf_op jit(solution)/shard_map/expert_product/pallas_call | solution.py:408
  (31 shorter events, 0.1 us)
Async XLA Ops:
  0.6 9.9 %copy-start.4 = (bf16[128,9,128]{2,0,1:T(8,128)(2,1)S(1)}, bf16[128,9,128]{2,0,1:T(8,128)(2,1)}, u32[]{:S(2)}) copy-start(bf16[128,9,128]{2,0,1:T(8,128)(2,1)} %param.12) | copy-start | bytes 884740
  0.6 9.9 %copy-start.3 = (bf16[256,9,128]{2,0,1:T(8,128)(2,1)S(1)}, bf16[256,9,128]{2,0,1:T(8,128)(2,1)}, u32[]{:S(2)}) copy-start(bf16[256,9,128]{2,0,1:T(8,128)(2,1)} %param.11) | copy-start | bytes 1769476
  0.7 9.9 %copy-start.5 = (f32[5,5,1024]{2,1,0:T(8,128)S(1)}, f32[5,5,1024]{2,1,0:T(8,128)}, u32[]{:S(2)}) copy-start(f32[5,5,1024]{2,1,0:T(8,128)} %two_ref.3) | copy-start | bytes 307204
  0.7 9.9 %copy-start.6 = (f32[3,3,1024]{2,1,0:T(4,128)S(1)}, f32[3,3,1024]{2,1,0:T(4,128)}, u32[]{:S(2)}) copy-start(f32[3,3,1024]{2,1,0:T(4,128)} %one_ref.3) | copy-start | bytes 110596
  0.7 9.9 %copy-start.9 = (s32[128]{0:T(128)S(1)}, s32[128]{0:T(128)}, u32[]{:S(2)}) copy-start(s32[128]{0:T(128)} %param.18) | copy-start | bytes 1540
  0.7 9.9 %copy-start.8 = (f32[1024]{0:T(1024)S(1)}, f32[1024]{0:T(1024)}, u32[]{:S(2)}) copy-start(f32[1024]{0:T(1024)} %param.14) | copy-start | bytes 12292
  0.7 9.9 %copy-start.7 = (s32[128,8]{0,1:T(8,128)S(1)}, s32[128,8]{0,1:T(8,128)}, u32[]{:S(2)}) copy-start(s32[128,8]{0,1:T(8,128)} %param.13) | copy-start | bytes 12292
  4.1 13.8 %collective-permute-start.2 = (bf16[2,272,128]{2,1,0:T(8,128)(2,1)}, bf16[2,272,128]{2,1,0:T(8,128)(2,1)S(1)}, u32[]{:S(2)}, u32[]{:S(2)}) collective-permute-start(bf16[2,272,128]{2,1,0:T(8,128)(2,1)} %merge.1.rest_0_), channel_id=1, source_target_pairs={{0,12},{4,8},{8,4},{12,0},{1,13},{5,9},{9,5},{13,1},{2,14},{6,10},... | collective-permute-start | bytes 417800 | tf_op jit(solution)/shard_map/ppermute | solution.py:445
  9.2 12.0 %collective-permute-start.1 = (bf16[2,272,128]{2,1,0:T(8,128)(2,1)}, bf16[2,272,128]{2,1,0:T(8,128)(2,1)S(1)}, u32[]{:S(2)}, u32[]{:S(2)}) collective-permute-start(bf16[2,272,128]{2,1,0:T(8,128)(2,1)} %merge.1.rest_0_), channel_id=1, source_target_pairs={{0,8},{4,12},{8,0},{12,4},{1,9},{5,13},{9,1},{13,5},{2,10},{6,14},... | collective-permute-start | bytes 417800 | tf_op jit(solution)/shard_map/ppermute | solution.py:445
  9.2 12.0 %collective-permute-start = (bf16[2,272,128]{2,1,0:T(8,128)(2,1)}, bf16[2,272,128]{2,1,0:T(8,128)(2,1)S(1)}, u32[]{:S(2)}, u32[]{:S(2)}) collective-permute-start(bf16[2,272,128]{2,1,0:T(8,128)(2,1)} %merge.1.rest_0_), channel_id=1, source_target_pairs={{0,4},{4,0},{8,12},{12,8},{1,5},{5,1},{9,13},{13,9},{2,6},{6,2},{1... | collective-permute-start | bytes 417800 | tf_op jit(solution)/shard_map/ppermute | solution.py:445
  10.6 10.6 %copy-start = (bf16[2,272,128]{2,1,0:T(8,128)(2,1)S(1)}, bf16[2,272,128]{2,1,0:T(8,128)(2,1)}, u32[]{:S(2)}) copy-start(bf16[2,272,128]{2,1,0:T(8,128)(2,1)} %merge.1.rest_0_) | copy-start | bytes 417796
  21.2 2.0 %collective-permute-start.7 = (bf16[2176,128]{1,0:T(8,128)(2,1)S(1)}, bf16[2176,128]{1,0:T(8,128)(2,1)S(1)}, u32[]{:S(2)}, u32[]{:S(2)}) collective-permute-start(bf16[2176,128]{1,0:T(8,128)(2,1)S(1)} %get-tuple-element.38), channel_id=1, source_target_pairs={{0,1},{1,0},{2,3},{3,2},{4,5},{5,4},{6,7},{7,6},{8,9},{9,8},{10,11... | collective-permute-start | bytes 1671176 | tf_op jit(solution)/shard_map/ppermute | solution.py:445
  21.2 2.2 %collective-permute-start.3 = (bf16[2,272,128]{2,1,0:T(8,128)(2,1)S(1)}, bf16[2,272,128]{2,1,0:T(8,128)(2,1)S(1)}, u32[]{:S(2)}, u32[]{:S(2)}) collective-permute-start(bf16[2,272,128]{2,1,0:T(8,128)(2,1)S(1)} %copy-done), channel_id=1, source_target_pairs={{0,1},{1,0},{2,3},{3,2},{4,5},{5,4},{6,7},{7,6},{8,9},{9,8},{10,11... | collective-permute-start | bytes 417800 | tf_op jit(solution)/shard_map/ppermute | solution.py:445
  21.7 4.7 %collective-permute-start.4 = (bf16[2,272,128]{2,1,0:T(8,128)(2,1)S(1)}, bf16[2,272,128]{2,1,0:T(8,128)(2,1)S(1)}, u32[]{:S(2)}, u32[]{:S(2)}) collective-permute-start(bf16[2,272,128]{2,1,0:T(8,128)(2,1)S(1)} %collective-permute-done.rest_1_), channel_id=1, source_target_pairs={{0,1},{1,0},{2,3},{3,2},{4,5},{5,4},{6,7},{7,6},{8,9},{9,8},{10,11... | collective-permute-start | bytes 417800 | tf_op jit(solution)/shard_map/ppermute | solution.py:445
  21.8 6.0 %collective-permute-start.5 = (bf16[2,272,128]{2,1,0:T(8,128)(2,1)S(1)}, bf16[2,272,128]{2,1,0:T(8,128)(2,1)S(1)}, u32[]{:S(2)}, u32[]{:S(2)}) collective-permute-start(bf16[2,272,128]{2,1,0:T(8,128)(2,1)S(1)} %collective-permute-done.1.rest_2_), channel_id=1, source_target_pairs={{0,1},{1,0},{2,3},{3,2},{4,5},{5,4},{6,7},{7,6},{8,9},{9,8},{10,11... | collective-permute-start | bytes 417800 | tf_op jit(solution)/shard_map/ppermute | solution.py:445
  22.2 5.5 %collective-permute-start.6 = (bf16[2,272,128]{2,1,0:T(8,128)(2,1)S(1)}, bf16[2,272,128]{2,1,0:T(8,128)(2,1)S(1)}, u32[]{:S(2)}, u32[]{:S(2)}) collective-permute-start(bf16[2,272,128]{2,1,0:T(8,128)(2,1)S(1)} %collective-permute-done.2.rest_3_), channel_id=1, source_target_pairs={{0,1},{1,0},{2,3},{3,2},{4,5},{5,4},{6,7},{7,6},{8,9},{9,8},{10,11... | collective-permute-start | bytes 417800 | tf_op jit(solution)/shard_map/ppermute | solution.py:445
  23.3 10.0 %collective-permute-start.8 = (bf16[544,128]{1,0:T(8,128)(2,1)S(1)}, bf16[544,128]{1,0:T(8,128)(2,1)S(1)}, u32[]{:S(2)}, u32[]{:S(2)}) collective-permute-start(bf16[544,128]{1,0:T(8,128)(2,1)S(1)} %get-tuple-element.40), channel_id=1, source_target_pairs={{0,4},{4,0},{8,12},{12,8},{1,5},{5,1},{9,13},{13,9},{2,6},{6,2},{1... | collective-permute-start | bytes 417800 | tf_op jit(solution)/shard_map/ppermute | solution.py:445
  23.4 13.5 %collective-permute-start.9 = (bf16[544,128]{1,0:T(8,128)(2,1)S(1)}, bf16[544,128]{1,0:T(8,128)(2,1)S(1)}, u32[]{:S(2)}, u32[]{:S(2)}) collective-permute-start(bf16[544,128]{1,0:T(8,128)(2,1)S(1)} %get-tuple-element.41), channel_id=1, source_target_pairs={{0,8},{4,12},{8,0},{12,4},{1,9},{5,13},{9,1},{13,5},{2,10},{6,14},... | collective-permute-start | bytes 417800 | tf_op jit(solution)/shard_map/ppermute | solution.py:445
  26.4 10.5 %collective-permute-start.10 = (bf16[544,128]{1,0:T(8,128)(2,1)S(1)}, bf16[544,128]{1,0:T(8,128)(2,1)S(1)}, u32[]{:S(2)}, u32[]{:S(2)}) collective-permute-start(bf16[544,128]{1,0:T(8,128)(2,1)S(1)} %get-tuple-element.42), channel_id=1, source_target_pairs={{0,12},{4,8},{8,4},{12,0},{1,13},{5,9},{9,5},{13,1},{2,14},{6,10},... | collective-permute-start | bytes 417800 | tf_op jit(solution)/shard_map/ppermute | solution.py:445
  27.8 23.8 %copy-start.2 = (s32[4,32]{1,0:T(4,128)S(1)}, s32[4,32]{1,0:T(4,128)}, u32[]{:S(2)}) copy-start(s32[4,32]{1,0:T(4,128)} %send_ref.1) | copy-start | bytes 1540
  27.8 25.0 %copy-start.1 = (f32[2,32]{1,0:T(2,128)S(1)}, f32[2,32]{1,0:T(2,128)}, u32[]{:S(2)}) copy-start(f32[2,32]{1,0:T(2,128)} %coef_ref.3) | copy-start | bytes 772
  37.0 5.7 %collective-permute-start.15 = (bf16[544,128]{1,0:T(8,128)(2,1)S(1)}, bf16[544,128]{1,0:T(8,128)(2,1)S(1)}, u32[]{:S(2)}, u32[]{:S(2)}) collective-permute-start(bf16[544,128]{1,0:T(8,128)(2,1)S(1)} %total_sum.1.refs_0_), channel_id=1, source_target_pairs={{0,2},{1,3},{2,0},{3,1},{4,6},{5,7},{6,4},{7,5},{8,10},{9,11},{10,... | collective-permute-start | bytes 417800 | tf_op jit(solution)/shard_map/ppermute | solution.py:445
  38.6 8.7 %collective-permute-start.11 = (bf16[9,32,128]{2,1,0:T(8,128)(2,1)S(1)}, bf16[9,32,128]{2,1,0:T(8,128)(2,1)S(1)}, u32[]{:S(2)}, u32[]{:S(2)}) collective-permute-start(bf16[9,32,128]{2,1,0:T(8,128)(2,1)S(1)} %get-tuple-element.44), channel_id=1, source_target_pairs={{0,1},{1,2},{2,3},{3,0},{4,5},{5,6},{6,7},{7,4},{8,9},{9,10},{10,1... | collective-permute-start | bytes 221192 | tf_op jit(solution)/shard_map/ppermute | solution.py:450
  38.6 14.2 %collective-permute-start.16 = (bf16[544,128]{1,0:T(8,128)(2,1)S(1)}, bf16[544,128]{1,0:T(8,128)(2,1)S(1)}, u32[]{:S(2)}, u32[]{:S(2)}) collective-permute-start(bf16[544,128]{1,0:T(8,128)(2,1)S(1)} %total_sum.1.refs_0_), channel_id=1, source_target_pairs={{0,1},{1,0},{2,3},{3,2},{4,5},{5,4},{6,7},{7,6},{8,9},{9,8},{10,11... | collective-permute-start | bytes 417800 | tf_op jit(solution)/shard_map/ppermute | solution.py:445
  42.7 10.0 %collective-permute-start.17 = (bf16[544,128]{1,0:T(8,128)(2,1)S(1)}, bf16[544,128]{1,0:T(8,128)(2,1)S(1)}, u32[]{:S(2)}, u32[]{:S(2)}) collective-permute-start(bf16[544,128]{1,0:T(8,128)(2,1)S(1)} %collective-permute-done.15.refs_1_), channel_id=1, source_target_pairs={{0,1},{1,0},{2,3},{3,2},{4,5},{5,4},{6,7},{7,6},{8,9},{9,8},{10,11... | collective-permute-start | bytes 417800 | tf_op jit(solution)/shard_map/ppermute | solution.py:445
  42.7 5.6 %collective-permute-start.12 = (bf16[9,32,128]{2,1,0:T(8,128)(2,1)S(1)}, bf16[9,32,128]{2,1,0:T(8,128)(2,1)S(1)}, u32[]{:S(2)}, u32[]{:S(2)}) collective-permute-start(bf16[9,32,128]{2,1,0:T(8,128)(2,1)S(1)} %get-tuple-element.45), channel_id=1, source_target_pairs={{0,3},{1,0},{2,1},{3,2},{4,7},{5,4},{6,5},{7,6},{8,11},{9,8},{10,9... | collective-permute-start | bytes 221192 | tf_op jit(solution)/shard_map/ppermute | solution.py:450
  44.5 6.3 %collective-permute-start.13 = (bf16[9,32,128]{2,1,0:T(8,128)(2,1)S(1)}, bf16[9,32,128]{2,1,0:T(8,128)(2,1)S(1)}, u32[]{:S(2)}, u32[]{:S(2)}) collective-permute-start(bf16[9,32,128]{2,1,0:T(8,128)(2,1)S(1)} %get-tuple-element.46), channel_id=1, source_target_pairs={{0,4},{4,8},{8,12},{12,0},{1,5},{5,9},{9,13},{13,1},{2,6},{6,10},{... | collective-permute-start | bytes 221192 | tf_op jit(solution)/shard_map/ppermute | solution.py:450
  47.2 4.4 %collective-permute-start.14 = (bf16[9,32,128]{2,1,0:T(8,128)(2,1)S(1)}, bf16[9,32,128]{2,1,0:T(8,128)(2,1)S(1)}, u32[]{:S(2)}, u32[]{:S(2)}) collective-permute-start(bf16[9,32,128]{2,1,0:T(8,128)(2,1)S(1)} %get-tuple-element.47), channel_id=1, source_target_pairs={{0,12},{4,0},{8,4},{12,8},{1,13},{5,1},{9,5},{13,9},{2,14},{6,2},{... | collective-permute-start | bytes 221192 | tf_op jit(solution)/shard_map/ppermute | solution.py:450

commit v3 on v2

--- a/solution.py
+++ b/solution.py
@@ -307,9 +307,12 @@
     for c in range(9):
         summed = nt(pick_all[...], turned[c * channels : (c + 1) * channels, :])
         own_ref[c] = summed[:atoms]
-        for block in range(4):
-            at = atoms + block * face
-            ghost_refs[block][c] = summed[at : at + face].astype(BF16)
+        blocks = [summed[atoms + block * face : atoms + (block + 1) * face] for block in range(4)]
+        for side in range(2):
+            even = lax.rem(lax.axis_index(("gx", "yz")[side]), 2) == 0
+            low, high = blocks[2 * side], blocks[2 * side + 1]
+            ghost_refs[2 * side][c] = jnp.where(even, high, low).astype(BF16)
+            ghost_refs[2 * side + 1][c] = jnp.where(even, low, high).astype(BF16)
 
 
 def back(edge, zero, one, two, pulled, pieces, places, rows, atoms, slots, face):
@@ -421,7 +424,12 @@
     atoms = own_ref.shape[1]
     face = send_ref.shape[1]
     row = lax.broadcasted_iota(jnp.int32, (atoms, face), 0)
-    picks = [(row == send_ref[b : b + 1, :]).astype(F32).astype(BF16) for b in range(4)]
+    picks = []
+    for side in range(2):
+        even = lax.rem(lax.axis_index(("gx", "yz")[side]), 2) == 0
+        below, above = send_ref[2 * side : 2 * side + 1, :], send_ref[2 * side + 1 : 2 * side + 2, :]
+        for faces in (jnp.where(even, above, below), jnp.where(even, below, above)):
+            picks.append((row == faces).astype(F32).astype(BF16))
     for c in range(9):
         total = own_ref[c]
         for pick, ref in zip(picks, (a_ref, b_ref, c_ref, d_ref)):
@@ -445,9 +453,13 @@
     return lax.ppermute(value, axis, [(i, i ^ bit) for i in range(lax.axis_size(axis))])
 
 
-def shift(value, axis, step):
+def neighbour_pairs(value, axis, first):
     count = lax.axis_size(axis)
-    return lax.ppermute(value, axis, [(i, (i + step) % count) for i in range(count)])
+    moves = []
+    for low in range(first, count, 2):
+        high = (low + 1) % count
+        moves += [(low, high), (high, low)]
+    return lax.ppermute(value, axis, moves)
 
 
 def local(
@@ -497,10 +509,16 @@
         gathered = [parts[0]] + [swap(parts[k], "yz", k) for k in range(1, count_yz)]
         pieces = held + [swap(piece, "gx", 1) for piece in held]
     grad_own, *ghosts = back(edge, zero, rot_one, rot_two, pulled, pieces, places, rows, atoms, slots, face)
+    returned = [
+        neighbour_pairs(ghost, axis, first)
+        for ghost, axis, first in zip(ghosts, ("gx", "gx", "yz", "yz"), (0, 1, 0, 1))
+    ]
     if direct:
         grad_own, *gathered = lax.optimization_barrier((grad_own, *gathered))
-        summed = total_sum(gathered)
+        summed, *returned = lax.optimization_barrier((total_sum(gathered), *returned))
         across = swap(summed, "gx", 2)
+        input_grad = finish(send_index, grad_own, returned)
+        across, input_grad = lax.optimization_barrier((across, input_grad))
         sums = [summed, across, swap(summed, "gx", 1), swap(across, "gx", 1)]
     else:
         mixed = jnp.stack([own, other]).astype(F32)
@@ -509,12 +527,9 @@
         piece = lax.dynamic_slice_in_dim(whole, row * height, height, 1)
         piece = jnp.where(core == 0, piece, piece[::-1])
         sums = [piece[0], piece[1]]
-    returned = [
-        shift(ghosts[1], "gx", 1), shift(ghosts[0], "gx", -1), shift(ghosts[3], "yz", 1), shift(ghosts[2], "yz", -1),
-    ]
+        input_grad = finish(send_index, grad_own, returned)
     grad_scale = math.sqrt(fanout / (atoms * count_yz * count_gx))
     expert_grad = expert_product(merge_coef, sums, merge_coef.shape[1] // count_gx, grad_scale)
-    input_grad = finish(send_index, grad_own, returned)
     return (jnp.transpose(input_grad, (1, 0, 2)), expert_grad)
 
 

time: 54.7 us -> 51.4 us (0.940)
  starting transfers between devices: 19.1 us -> 16.9 us
  waiting for transfers between devices: 14.6 us -> 13.6 us
    ppermute x4, starting transfers between devices: 5.59 us -> 4.12 us  [neighbour_pairs(): return lax.ppermute(value, axis, moves)]
    ppermute x14, waiting for transfers between devices: 11.3 us -> 9.96 us  [swap(): lax.ppermute(value, axis, [(i, i ^ bit) for i in range(lax.axis_size(axis...]
    ppermute x14, starting transfers between devices: 13.5 us -> 12.8 us  [swap(): lax.ppermute(value, axis, [(i, i ^ bit) for i in range(lax.axis_size(axis...]
  transfers between devices with their start and end apart: 18 -> 18, of which waited for: 6 -> 6; matrix products, arithmetic and copies ran while one was open for 0% -> 0% of each run, Pallas kernels for 26% -> 28%
where the time goes in v3:
time: 51.4 us; the launch traced here: 51.2 us
  Pallas kernels  19.2 us (37%)
  starting transfers between devices  16.9 us (33%)
  waiting for transfers between devices  13.6 us (26%)
  between operations  1.52 us (3%)
    ppermute x14, starting transfers between devices, swap(): lax.ppermute(value, axis, [(i, i ^ bit) for i in range(lax.axis_size(axis...  12.8 us
    ppermute x14, waiting for transfers between devices, swap(): lax.ppermute(value, axis, [(i, i ^ bit) for i in range(lax.axis_size(axis...  9.96 us
    pallas_call x1, Pallas kernels, features(): pl.pallas_call(functools.partial(features_kernel, fanout=fanout), in_spec...  7.23 us
    pallas_call x1, Pallas kernels, back(): pl.pallas_call(functools.partial(back_kernel, pieces=len(pieces), members...  5.49 us
    ppermute x4, starting transfers between devices, neighbour_pairs(): return lax.ppermute(value, axis, moves)  4.12 us
    ppermute x4, waiting for transfers between devices, neighbour_pairs(): return lax.ppermute(value, axis, moves)  3.6 us
    pallas_call x1, Pallas kernels, merge(): pl.pallas_call(merge_kernel, in_specs=[VMEM, HBM], out_specs=VMEM, out_sh...  3.39 us
    pallas_call x1, Pallas kernels, expert_product(): pl.pallas_call(functools.partial(expert_kernel, scale=scale), in_specs=[V...  1.73 us
  transfers between devices with their start and end apart: 18, of which 6 were waited for; matrix products, arithmetic and copies ran while one was open for 0% of the time, Pallas kernels for 28%

profile of v3, /device:TPU:0, one launch (start us, length us, event | category | flops | bytes accessed | tf_op | source)
XLA Modules:
  0.0 51.2 jit_solution(9433479971240251311)
XLA Ops:
  0.7 3.4 %merge.1.rest_0_ = bf16[2,272,128]{2,1,0:T(8,128)(2,1)} custom-call(f32[2,32]{1,0:T(2,128)} %coef_ref.3, bf16[32,69632]{1,0:T(8,128)(2,1)} %experts_ref.1), custom_call_target="tpu_custom_call" | custom-call | flops 53477376 | bytes 2228224 | tf_op jit(solution)/shard_map/merge/pallas_call | solution.py:100
  4.1 5.1 %collective-permute-start.2 = (bf16[2,272,128]{2,1,0:T(8,128)(2,1)}, bf16[2,272,128]{2,1,0:T(8,128)(2,1)S(1)}, u32[]{:S(2)}, u32[]{:S(2)}) collective-permute-start(bf16[2,272,128]{2,1,0:T(8,128)(2,1)} %merge.1.rest_0_), channel_id=1, source_target_pairs={{0,12},{4,8},{8,4},{12,0},{1,13},{5,9},{9,5},{13,1},{2,14},{6,10},... | collective-permute-start | bytes 417800 | tf_op jit(solution)/shard_map/ppermute | solution.py:453
  9.2 0.6 %collective-permute-start = (bf16[2,272,128]{2,1,0:T(8,128)(2,1)}, bf16[2,272,128]{2,1,0:T(8,128)(2,1)S(1)}, u32[]{:S(2)}, u32[]{:S(2)}) collective-permute-start(bf16[2,272,128]{2,1,0:T(8,128)(2,1)} %merge.1.rest_0_), channel_id=1, source_target_pairs={{0,4},{4,0},{8,12},{12,8},{1,5},{5,1},{9,13},{13,9},{2,6},{6,2},{1... | collective-permute-start | bytes 417800 | tf_op jit(solution)/shard_map/ppermute | solution.py:453
  10.6 0.0 copy-start
  10.6 7.2 %features.1 = (bf16[2176,128]{1,0:T(8,128)(2,1)S(1)}, bf16[2176,128]{1,0:T(8,128)(2,1)S(1)}, bf16[896,1024]{1,0:T(8,128)(2,1)S(1)}, f32[8,1024]{1,0:T(8,128)S(1)}) custom-call(s32[1]{0:T(128)S(6)} %copy.13.live_ref, s32[8,128]{1,0:T(8,128)S(1)} %bitcast.8, s32[1,128]{1,0:T(1,128)S(1)} %bitcast.11, f32[1,1024]{1,0:T(1,128)S(1)} %bitcast.9, ...), custom_call_target="tpu_custom_call" | custom-call | flops 8999999488 | bytes 7000000 | tf_op jit(solution)/shard_map/features/pallas_call | solution.py:208
  17.8 0.0 collective-permute-done.2.rest_3_
  17.8 3.4 %collective-permute-done.1.rest_2_ = bf16[2,272,128]{2,1,0:T(8,128)(2,1)S(1)} collective-permute-done((bf16[2,272,128]{2,1,0:T(8,128)(2,1)}, bf16[2,272,128]{2,1,0:T(8,128)(2,1)S(1)}, u32[]{:S(2)}, u32[]{:S(2)}) %collective-permute-start.1) | collective-permute-done | bytes 139296 | tf_op jit(solution)/shard_map/ppermute | solution.py:453
  21.2 0.5 collective-permute-start.3
  21.7 0.1 collective-permute-start.4
  21.8 0.4 collective-permute-start.5
  22.2 0.1 collective-permute-start.6
  22.3 0.9 %collective-permute-done.7.came_ref = bf16[2176,128]{1,0:T(8,128)(2,1)S(1)} collective-permute-done((bf16[2176,128]{1,0:T(8,128)(2,1)S(1)}, bf16[2176,128]{1,0:T(8,128)(2,1)S(1)}, u32[]{:S(2)}, u32[]{:S(2)}) %collective-permute-start.7) | collective-permute-done | bytes 557088 | tf_op jit(solution)/shard_map/ppermute | solution.py:453
  23.2 0.1 pair_sum.1
  23.3 0.1 collective-permute-start.8
  23.4 0.0 collective-permute-done.3.rest_4_
  23.4 3.0 %collective-permute-start.9 = (bf16[544,128]{1,0:T(8,128)(2,1)S(1)}, bf16[544,128]{1,0:T(8,128)(2,1)S(1)}, u32[]{:S(2)}, u32[]{:S(2)}) collective-permute-start(bf16[544,128]{1,0:T(8,128)(2,1)S(1)} %get-tuple-element.48), channel_id=1, source_target_pairs={{0,8},{4,12},{8,0},{12,4},{1,9},{5,13},{9,1},{13,5},{2,10},{6,14},... | collective-permute-start | bytes 417800 | tf_op jit(solution)/shard_map/ppermute | solution.py:453
  26.4 1.3 %collective-permute-start.10 = (bf16[544,128]{1,0:T(8,128)(2,1)S(1)}, bf16[544,128]{1,0:T(8,128)(2,1)S(1)}, u32[]{:S(2)}, u32[]{:S(2)}) collective-permute-start(bf16[544,128]{1,0:T(8,128)(2,1)S(1)} %get-tuple-element.49), channel_id=1, source_target_pairs={{0,12},{4,8},{8,4},{12,0},{1,13},{5,9},{9,5},{13,1},{2,14},{6,10},... | collective-permute-start | bytes 417800 | tf_op jit(solution)/shard_map/ppermute | solution.py:453
  27.8 0.0 copy-start.1
  27.8 5.5 %back.1 = (f32[9,128,128]{2,1,0:T(8,128)S(1)}, bf16[9,32,128]{2,1,0:T(8,128)(2,1)S(1)}, bf16[9,32,128]{2,1,0:T(8,128)(2,1)S(1)}, bf16[9,32,128]{2,1,0:T(8,128)(2,1)S(1)}, bf16[9,32,128]{2,1,0:T(8,128)(2,1)S(1)}) custom-call(f32[8,1024]{1,0:T(8,128)S(1)} %get-tuple-element.36.edge_ref, f32[1,1024]{1,0:T(1,128)S(1)} %bitcast.10, f32[3,3,1024]{2,1,0:T(4,128)S(1)} %copy-done.6, ...), custom_call_target="tpu_custom_call" | custom-call | flops 8999999488 | bytes 7000000 | tf_op jit(solution)/shard_map/back/pallas_call | solution.py:323
  33.3 0.1 collective-permute-start.11
  33.4 1.6 %collective-permute-start.12 = (bf16[9,32,128]{2,1,0:T(8,128)(2,1)S(1)}, bf16[9,32,128]{2,1,0:T(8,128)(2,1)S(1)}, u32[]{:S(2)}, u32[]{:S(2)}) collective-permute-start(bf16[9,32,128]{2,1,0:T(8,128)(2,1)S(1)} %get-tuple-element.55), channel_id=1, source_target_pairs={{1,2},{2,1},{3,0},{0,3},{5,6},{6,5},{7,4},{4,7},{9,10},{10,9},{11,... | collective-permute-start | bytes 221192 | tf_op jit(solution)/shard_map/ppermute | solution.py:462
  35.0 2.0 %collective-permute-done.9.refs_2_ = bf16[544,128]{1,0:T(8,128)(2,1)S(1)} collective-permute-done((bf16[544,128]{1,0:T(8,128)(2,1)S(1)}, bf16[544,128]{1,0:T(8,128)(2,1)S(1)}, u32[]{:S(2)}, u32[]{:S(2)}) %collective-permute-start.9) | collective-permute-done | bytes 139296 | tf_op jit(solution)/shard_map/ppermute | solution.py:453
  36.9 2.4 %collective-permute-start.14 = (bf16[9,32,128]{2,1,0:T(8,128)(2,1)S(1)}, bf16[9,32,128]{2,1,0:T(8,128)(2,1)S(1)}, u32[]{:S(2)}, u32[]{:S(2)}) collective-permute-start(bf16[9,32,128]{2,1,0:T(8,128)(2,1)S(1)} %get-tuple-element.57), channel_id=1, source_target_pairs={{4,8},{8,4},{12,0},{0,12},{5,9},{9,5},{13,1},{1,13},{6,10},{10,6},... | collective-permute-start | bytes 221192 | tf_op jit(solution)/shard_map/ppermute | solution.py:462
  39.4 0.0 collective-permute-done.10.refs_3_
  39.4 0.1 total_sum.1.refs_0_
  39.5 0.0 collective-permute-done.11.a_ref
  39.5 3.6 %collective-permute-done.14.d_ref = bf16[9,32,128]{2,1,0:T(8,128)(2,1)S(1)} collective-permute-done((bf16[9,32,128]{2,1,0:T(8,128)(2,1)S(1)}, bf16[9,32,128]{2,1,0:T(8,128)(2,1)S(1)}, u32[]{:S(2)}, u32[]{:S(2)}) %collective-permute-start.14) | collective-permute-done | bytes 73760 | tf_op jit(solution)/shard_map/ppermute | solution.py:462
  43.1 1.5 %collective-permute-start.15 = (bf16[544,128]{1,0:T(8,128)(2,1)S(1)}, bf16[544,128]{1,0:T(8,128)(2,1)S(1)}, u32[]{:S(2)}, u32[]{:S(2)}) collective-permute-start(bf16[544,128]{1,0:T(8,128)(2,1)S(1)} %total_sum.1.refs_0_), channel_id=1, source_target_pairs={{0,2},{1,3},{2,0},{3,1},{4,6},{5,7},{6,4},{7,5},{8,10},{9,11},{10,... | collective-permute-start | bytes 417800 | tf_op jit(solution)/shard_map/ppermute | solution.py:453
  44.6 1.2 %finish.1 = bf16[9,128,128]{2,1,0:T(8,128)(2,1)} custom-call(s32[4,32]{1,0:T(4,128)S(1)} %copy-done.2, f32[9,128,128]{2,1,0:T(8,128)S(1)} %get-tuple-element.59.own_ref, bf16[9,32,128]{2,1,0:T(8,128)(2,1)S(1)} %collective-permute-done.11.a_ref, bf16[9,32,128]{2,1,0:T(8,128)(2,1)S(1)} %collective-permute-done.12.b_ref, ...), custom_call_target="tpu_custom_call" | custom-call | flops 100000000 | bytes 2000000 | tf_op jit(solution)/shard_map/finish/pallas_call | solution.py:441
  45.7 2.4 %collective-permute-done.15.refs_1_ = bf16[544,128]{1,0:T(8,128)(2,1)S(1)} collective-permute-done((bf16[544,128]{1,0:T(8,128)(2,1)S(1)}, bf16[544,128]{1,0:T(8,128)(2,1)S(1)}, u32[]{:S(2)}, u32[]{:S(2)}) %collective-permute-start.15) | collective-permute-done | bytes 139296 | tf_op jit(solution)/shard_map/ppermute | solution.py:453
  48.1 1.4 %collective-permute-done.17.refs_3_ = bf16[544,128]{1,0:T(8,128)(2,1)S(1)} collective-permute-done((bf16[544,128]{1,0:T(8,128)(2,1)S(1)}, bf16[544,128]{1,0:T(8,128)(2,1)S(1)}, u32[]{:S(2)}, u32[]{:S(2)}) %collective-permute-start.17) | collective-permute-done | bytes 139296 | tf_op jit(solution)/shard_map/ppermute | solution.py:453
  49.5 1.7 %expert_product.1 = f32[8,69632]{1,0:T(8,128)} custom-call(f32[2,32]{1,0:T(2,128)S(1)} %copy-done.1, bf16[544,128]{1,0:T(8,128)(2,1)S(1)} %total_sum.1.refs_0_, bf16[544,128]{1,0:T(8,128)(2,1)S(1)} %collective-permute-done.15.refs_1_, bf16[544,128]{1,0:T(8,128)(2,1)S(1)} %collective-permute-done.16.refs_2_, bf16[544,128]{1,0:T(8,128)(2,1)S(1)} %collective-permute-done.17.refs_3_), custom_call_target="tpu_custom_call" | custom-call | flops 1000000 | bytes 4000000 | tf_op jit(solution)/shard_map/expert_product/pallas_call | solution.py:411
  (31 shorter events, 0.1 us)
Async XLA Ops:
  0.6 9.9 %copy-start.4 = (bf16[128,9,128]{2,0,1:T(8,128)(2,1)S(1)}, bf16[128,9,128]{2,0,1:T(8,128)(2,1)}, u32[]{:S(2)}) copy-start(bf16[128,9,128]{2,0,1:T(8,128)(2,1)} %param.12) | copy-start | bytes 884740
  0.6 9.9 %copy-start.3 = (bf16[256,9,128]{2,0,1:T(8,128)(2,1)S(1)}, bf16[256,9,128]{2,0,1:T(8,128)(2,1)}, u32[]{:S(2)}) copy-start(bf16[256,9,128]{2,0,1:T(8,128)(2,1)} %param.11) | copy-start | bytes 1769476
  0.7 9.9 %copy-start.5 = (f32[5,5,1024]{2,1,0:T(8,128)S(1)}, f32[5,5,1024]{2,1,0:T(8,128)}, u32[]{:S(2)}) copy-start(f32[5,5,1024]{2,1,0:T(8,128)} %two_ref.3) | copy-start | bytes 307204
  0.7 9.9 %copy-start.6 = (f32[3,3,1024]{2,1,0:T(4,128)S(1)}, f32[3,3,1024]{2,1,0:T(4,128)}, u32[]{:S(2)}) copy-start(f32[3,3,1024]{2,1,0:T(4,128)} %one_ref.3) | copy-start | bytes 110596
  0.7 9.9 %copy-start.9 = (s32[128]{0:T(128)S(1)}, s32[128]{0:T(128)}, u32[]{:S(2)}) copy-start(s32[128]{0:T(128)} %param.18) | copy-start | bytes 1540
  0.7 9.9 %copy-start.8 = (f32[1024]{0:T(1024)S(1)}, f32[1024]{0:T(1024)}, u32[]{:S(2)}) copy-start(f32[1024]{0:T(1024)} %param.14) | copy-start | bytes 12292
  0.7 9.9 %copy-start.7 = (s32[128,8]{0,1:T(8,128)S(1)}, s32[128,8]{0,1:T(8,128)}, u32[]{:S(2)}) copy-start(s32[128,8]{0,1:T(8,128)} %param.13) | copy-start | bytes 12292
  4.1 13.7 %collective-permute-start.2 = (bf16[2,272,128]{2,1,0:T(8,128)(2,1)}, bf16[2,272,128]{2,1,0:T(8,128)(2,1)S(1)}, u32[]{:S(2)}, u32[]{:S(2)}) collective-permute-start(bf16[2,272,128]{2,1,0:T(8,128)(2,1)} %merge.1.rest_0_), channel_id=1, source_target_pairs={{0,12},{4,8},{8,4},{12,0},{1,13},{5,9},{9,5},{13,1},{2,14},{6,10},... | collective-permute-start | bytes 417800 | tf_op jit(solution)/shard_map/ppermute | solution.py:453
  9.2 12.0 %collective-permute-start.1 = (bf16[2,272,128]{2,1,0:T(8,128)(2,1)}, bf16[2,272,128]{2,1,0:T(8,128)(2,1)S(1)}, u32[]{:S(2)}, u32[]{:S(2)}) collective-permute-start(bf16[2,272,128]{2,1,0:T(8,128)(2,1)} %merge.1.rest_0_), channel_id=1, source_target_pairs={{0,8},{4,12},{8,0},{12,4},{1,9},{5,13},{9,1},{13,5},{2,10},{6,14},... | collective-permute-start | bytes 417800 | tf_op jit(solution)/shard_map/ppermute | solution.py:453
  9.2 12.0 %collective-permute-start = (bf16[2,272,128]{2,1,0:T(8,128)(2,1)}, bf16[2,272,128]{2,1,0:T(8,128)(2,1)S(1)}, u32[]{:S(2)}, u32[]{:S(2)}) collective-permute-start(bf16[2,272,128]{2,1,0:T(8,128)(2,1)} %merge.1.rest_0_), channel_id=1, source_target_pairs={{0,4},{4,0},{8,12},{12,8},{1,5},{5,1},{9,13},{13,9},{2,6},{6,2},{1... | collective-permute-start | bytes 417800 | tf_op jit(solution)/shard_map/ppermute | solution.py:453
  10.6 10.6 %copy-start = (bf16[2,272,128]{2,1,0:T(8,128)(2,1)S(1)}, bf16[2,272,128]{2,1,0:T(8,128)(2,1)}, u32[]{:S(2)}) copy-start(bf16[2,272,128]{2,1,0:T(8,128)(2,1)} %merge.1.rest_0_) | copy-start | bytes 417796
  21.2 2.0 %collective-permute-start.7 = (bf16[2176,128]{1,0:T(8,128)(2,1)S(1)}, bf16[2176,128]{1,0:T(8,128)(2,1)S(1)}, u32[]{:S(2)}, u32[]{:S(2)}) collective-permute-start(bf16[2176,128]{1,0:T(8,128)(2,1)S(1)} %get-tuple-element.45), channel_id=1, source_target_pairs={{0,1},{1,0},{2,3},{3,2},{4,5},{5,4},{6,7},{7,6},{8,9},{9,8},{10,11... | collective-permute-start | bytes 1671176 | tf_op jit(solution)/shard_map/ppermute | solution.py:453
  21.2 2.2 %collective-permute-start.3 = (bf16[2,272,128]{2,1,0:T(8,128)(2,1)S(1)}, bf16[2,272,128]{2,1,0:T(8,128)(2,1)S(1)}, u32[]{:S(2)}, u32[]{:S(2)}) collective-permute-start(bf16[2,272,128]{2,1,0:T(8,128)(2,1)S(1)} %copy-done), channel_id=1, source_target_pairs={{0,1},{1,0},{2,3},{3,2},{4,5},{5,4},{6,7},{7,6},{8,9},{9,8},{10,11... | collective-permute-start | bytes 417800 | tf_op jit(solution)/shard_map/ppermute | solution.py:453
  21.7 4.7 %collective-permute-start.4 = (bf16[2,272,128]{2,1,0:T(8,128)(2,1)S(1)}, bf16[2,272,128]{2,1,0:T(8,128)(2,1)S(1)}, u32[]{:S(2)}, u32[]{:S(2)}) collective-permute-start(bf16[2,272,128]{2,1,0:T(8,128)(2,1)S(1)} %collective-permute-done.rest_1_), channel_id=1, source_target_pairs={{0,1},{1,0},{2,3},{3,2},{4,5},{5,4},{6,7},{7,6},{8,9},{9,8},{10,11... | collective-permute-start | bytes 417800 | tf_op jit(solution)/shard_map/ppermute | solution.py:453
  21.8 6.0 %collective-permute-start.5 = (bf16[2,272,128]{2,1,0:T(8,128)(2,1)S(1)}, bf16[2,272,128]{2,1,0:T(8,128)(2,1)S(1)}, u32[]{:S(2)}, u32[]{:S(2)}) collective-permute-start(bf16[2,272,128]{2,1,0:T(8,128)(2,1)S(1)} %collective-permute-done.1.rest_2_), channel_id=1, source_target_pairs={{0,1},{1,0},{2,3},{3,2},{4,5},{5,4},{6,7},{7,6},{8,9},{9,8},{10,11... | collective-permute-start | bytes 417800 | tf_op jit(solution)/shard_map/ppermute | solution.py:453
  22.2 5.5 %collective-permute-start.6 = (bf16[2,272,128]{2,1,0:T(8,128)(2,1)S(1)}, bf16[2,272,128]{2,1,0:T(8,128)(2,1)S(1)}, u32[]{:S(2)}, u32[]{:S(2)}) collective-permute-start(bf16[2,272,128]{2,1,0:T(8,128)(2,1)S(1)} %collective-permute-done.2.rest_3_), channel_id=1, source_target_pairs={{0,1},{1,0},{2,3},{3,2},{4,5},{5,4},{6,7},{7,6},{8,9},{9,8},{10,11... | collective-permute-start | bytes 417800 | tf_op jit(solution)/shard_map/ppermute | solution.py:453
  23.3 11.7 %collective-permute-start.8 = (bf16[544,128]{1,0:T(8,128)(2,1)S(1)}, bf16[544,128]{1,0:T(8,128)(2,1)S(1)}, u32[]{:S(2)}, u32[]{:S(2)}) collective-permute-start(bf16[544,128]{1,0:T(8,128)(2,1)S(1)} %get-tuple-element.47), channel_id=1, source_target_pairs={{0,4},{4,0},{8,12},{12,8},{1,5},{5,1},{9,13},{13,9},{2,6},{6,2},{1... | collective-permute-start | bytes 417800 | tf_op jit(solution)/shard_map/ppermute | solution.py:453
  23.4 13.5 %collective-permute-start.9 = (bf16[544,128]{1,0:T(8,128)(2,1)S(1)}, bf16[544,128]{1,0:T(8,128)(2,1)S(1)}, u32[]{:S(2)}, u32[]{:S(2)}) collective-permute-start(bf16[544,128]{1,0:T(8,128)(2,1)S(1)} %get-tuple-element.48), channel_id=1, source_target_pairs={{0,8},{4,12},{8,0},{12,4},{1,9},{5,13},{9,1},{13,5},{2,10},{6,14},... | collective-permute-start | bytes 417800 | tf_op jit(solution)/shard_map/ppermute | solution.py:453
  26.4 13.0 %collective-permute-start.10 = (bf16[544,128]{1,0:T(8,128)(2,1)S(1)}, bf16[544,128]{1,0:T(8,128)(2,1)S(1)}, u32[]{:S(2)}, u32[]{:S(2)}) collective-permute-start(bf16[544,128]{1,0:T(8,128)(2,1)S(1)} %get-tuple-element.49), channel_id=1, source_target_pairs={{0,12},{4,8},{8,4},{12,0},{1,13},{5,9},{9,5},{13,1},{2,14},{6,10},... | collective-permute-start | bytes 417800 | tf_op jit(solution)/shard_map/ppermute | solution.py:453
  27.8 16.8 %copy-start.2 = (s32[4,32]{1,0:T(4,128)S(1)}, s32[4,32]{1,0:T(4,128)}, u32[]{:S(2)}) copy-start(s32[4,32]{1,0:T(4,128)} %send_ref.1) | copy-start | bytes 1540
  27.8 21.7 %copy-start.1 = (f32[2,32]{1,0:T(2,128)S(1)}, f32[2,32]{1,0:T(2,128)}, u32[]{:S(2)}) copy-start(f32[2,32]{1,0:T(2,128)} %coef_ref.3) | copy-start | bytes 772
  33.3 6.2 %collective-permute-start.11 = (bf16[9,32,128]{2,1,0:T(8,128)(2,1)S(1)}, bf16[9,32,128]{2,1,0:T(8,128)(2,1)S(1)}, u32[]{:S(2)}, u32[]{:S(2)}) collective-permute-start(bf16[9,32,128]{2,1,0:T(8,128)(2,1)S(1)} %get-tuple-element.54), channel_id=1, source_target_pairs={{0,1},{1,0},{2,3},{3,2},{4,5},{5,4},{6,7},{7,6},{8,9},{9,8},{10,11... | collective-permute-start | bytes 221192 | tf_op jit(solution)/shard_map/ppermute | solution.py:462
  33.4 6.1 %collective-permute-start.12 = (bf16[9,32,128]{2,1,0:T(8,128)(2,1)S(1)}, bf16[9,32,128]{2,1,0:T(8,128)(2,1)S(1)}, u32[]{:S(2)}, u32[]{:S(2)}) collective-permute-start(bf16[9,32,128]{2,1,0:T(8,128)(2,1)S(1)} %get-tuple-element.55), channel_id=1, source_target_pairs={{1,2},{2,1},{3,0},{0,3},{5,6},{6,5},{7,4},{4,7},{9,10},{10,9},{11,... | collective-permute-start | bytes 221192 | tf_op jit(solution)/shard_map/ppermute | solution.py:462
  35.0 4.5 %collective-permute-start.13 = (bf16[9,32,128]{2,1,0:T(8,128)(2,1)S(1)}, bf16[9,32,128]{2,1,0:T(8,128)(2,1)S(1)}, u32[]{:S(2)}, u32[]{:S(2)}) collective-permute-start(bf16[9,32,128]{2,1,0:T(8,128)(2,1)S(1)} %get-tuple-element.56), channel_id=1, source_target_pairs={{0,4},{4,0},{8,12},{12,8},{1,5},{5,1},{9,13},{13,9},{2,6},{6,2},{1... | collective-permute-start | bytes 221192 | tf_op jit(solution)/shard_map/ppermute | solution.py:462
  36.9 6.2 %collective-permute-start.14 = (bf16[9,32,128]{2,1,0:T(8,128)(2,1)S(1)}, bf16[9,32,128]{2,1,0:T(8,128)(2,1)S(1)}, u32[]{:S(2)}, u32[]{:S(2)}) collective-permute-start(bf16[9,32,128]{2,1,0:T(8,128)(2,1)S(1)} %get-tuple-element.57), channel_id=1, source_target_pairs={{4,8},{8,4},{12,0},{0,12},{5,9},{9,5},{13,1},{1,13},{6,10},{10,6},... | collective-permute-start | bytes 221192 | tf_op jit(solution)/shard_map/ppermute | solution.py:462
  43.1 5.1 %collective-permute-start.15 = (bf16[544,128]{1,0:T(8,128)(2,1)S(1)}, bf16[544,128]{1,0:T(8,128)(2,1)S(1)}, u32[]{:S(2)}, u32[]{:S(2)}) collective-permute-start(bf16[544,128]{1,0:T(8,128)(2,1)S(1)} %total_sum.1.refs_0_), channel_id=1, source_target_pairs={{0,2},{1,3},{2,0},{3,1},{4,6},{5,7},{6,4},{7,5},{8,10},{9,11},{10,... | collective-permute-start | bytes 417800 | tf_op jit(solution)/shard_map/ppermute | solution.py:453
  44.6 3.6 %collective-permute-start.16 = (bf16[544,128]{1,0:T(8,128)(2,1)S(1)}, bf16[544,128]{1,0:T(8,128)(2,1)S(1)}, u32[]{:S(2)}, u32[]{:S(2)}) collective-permute-start(bf16[544,128]{1,0:T(8,128)(2,1)S(1)} %total_sum.1.refs_0_), channel_id=1, source_target_pairs={{0,1},{1,0},{2,3},{3,2},{4,5},{5,4},{6,7},{7,6},{8,9},{9,8},{10,11... | collective-permute-start | bytes 417800 | tf_op jit(solution)/shard_map/ppermute | solution.py:453
  48.1 1.4 %collective-permute-start.17 = (bf16[544,128]{1,0:T(8,128)(2,1)S(1)}, bf16[544,128]{1,0:T(8,128)(2,1)S(1)}, u32[]{:S(2)}, u32[]{:S(2)}) collective-permute-start(bf16[544,128]{1,0:T(8,128)(2,1)S(1)} %collective-permute-done.15.refs_1_), channel_id=1, source_target_pairs={{0,1},{1,0},{2,3},{3,2},{4,5},{5,4},{6,7},{7,6},{8,9},{9,8},{10,11... | collective-permute-start | bytes 417800 | tf_op jit(solution)/shard_map/ppermute | solution.py:453

commit v4 on v3

--- a/solution.py
+++ b/solution.py
@@ -242,11 +242,12 @@
     zw, pw = 3 * channels, 2 * channels
     first = zw * zw // 128
     second = first + pw * pw // 128
-    for piece, place in zip(piece_refs, places()):
-        height = piece.shape[1]
+    placed = [(piece, index) for piece in piece_refs for index in range(piece.shape[0])]
+    for (piece, index), place in zip(placed, places()):
+        height = piece.shape[2]
         at = pl.ds(pl.multiple_of(place, 16), height)
         for k in range(members):
-            flat[k, at, :] = piece[k].astype(F32)
+            flat[k, at, :] = piece[index, k].astype(F32)
     for k in range(members):
         for j in range(zw // 128):
             weight_zero[:, k * zw + j * 128 : k * zw + (j + 1) * 128] = flat[
@@ -311,12 +312,13 @@
         for side in range(2):
             even = lax.rem(lax.axis_index(("gx", "yz")[side]), 2) == 0
             low, high = blocks[2 * side], blocks[2 * side + 1]
-            ghost_refs[2 * side][c] = jnp.where(even, high, low).astype(BF16)
-            ghost_refs[2 * side + 1][c] = jnp.where(even, low, high).astype(BF16)
+            at = pl.ds(c * face, face)
+            ghost_refs[2 * side][at, :] = jnp.where(even, high, low).astype(BF16)
+            ghost_refs[2 * side + 1][at, :] = jnp.where(even, low, high).astype(BF16)
 
 
 def back(edge, zero, one, two, pulled, pieces, places, rows, atoms, slots, face):
-    members = pieces[0].shape[0]
+    members = pieces[0].shape[1]
     edges = pulled.shape[1]
     channels = pulled.shape[0] // 7
     shape = jax.ShapeDtypeStruct
@@ -326,7 +328,7 @@
         ),
         in_specs=[VMEM] * (5 + len(pieces)),
         out_specs=[VMEM] * 5,
-        out_shape=[shape((9, atoms, channels), F32), *[shape((9, face, channels), BF16)] * 4],
+        out_shape=[shape((9, atoms, channels), F32), *[shape((9 * face, channels), BF16)] * 4],
         scratch_shapes=[
             pltpu.VMEM((members, rows, 128), F32),
             pltpu.VMEM((3 * channels, members * 3 * channels), BF16),
@@ -341,31 +343,63 @@
     )(edge, zero, one, two, pulled, *pieces)
 
 
-def pair_kernel(own_ref, came_ref, *out_refs):
-    height = out_refs[0].shape[0]
-    row = lax.axis_index("yz")
-    for index, out_ref in enumerate(out_refs):
-        at = pl.ds(pl.multiple_of((row ^ index) * height, 16), height)
-        out_ref[...] = (own_ref[at, :].astype(F32) + came_ref[at, :].astype(F32)).astype(BF16)
-
-
-def pair_sum(own, came, count):
-    height = own.shape[0] // count
-    return pl.pallas_call(
-        pair_kernel,
-        in_specs=[VMEM, VMEM],
-        out_specs=[VMEM] * count,
-        out_shape=[jax.ShapeDtypeStruct((height, 128), BF16)] * count,
+def core_kernel(own_ref, came_ref, away_ref, keep_ref):
+    count = lax.axis_size("yz")
+    half = keep_ref.shape[0] // count
+    row, side = lax.axis_index("yz"), lax.axis_index("gx") // 2
+    for k in range(count):
+        start = (row ^ k) * 2 * half
+        here = pl.ds(k * half, half)
+        near = pl.ds(pl.multiple_of(start + side * half, 16), half)
+        far = pl.ds(pl.multiple_of(start + (1 - side) * half, 16), half)
+        keep_ref[here, :] = own_ref[near, :].astype(F32) + came_ref[near, :].astype(F32)
+        away_ref[here, :] = (own_ref[far, :].astype(F32) + came_ref[far, :].astype(F32)).astype(BF16)
+
+
+def core_sum(own, came):
+    shape = (own.shape[0] // 2, 128)
+    return pl.pallas_call(
+        core_kernel,
+        in_specs=[VMEM] * 2,
+        out_specs=[VMEM] * 2,
+        out_shape=[jax.ShapeDtypeStruct(shape, BF16), jax.ShapeDtypeStruct(shape, F32)],
         compiler_params=limits(6),
         cost_estimate=cost(10**6, 2 * 10**6),
-        name="pair_sum",
+        name="core_sum",
     )(own, came)
 
 
+def side_kernel(keep_ref, came_ref, low_ref, high_ref, own_ref, *out_refs):
+    half = own_ref.shape[0]
+    own_ref[...] = keep_ref[:half] + came_ref[:half].astype(F32)
+    for k, out_ref in enumerate(out_refs, 1):
+        at = pl.ds(k * half, half)
+        out_ref[:half] = (keep_ref[at, :] + came_ref[at, :].astype(F32)).astype(BF16)
+    out_refs[0][half:] = low_ref[...]
+    out_refs[-1][half:] = high_ref[...]
+
+
+def side_sum(keep, came, low, high, count):
+    half = keep.shape[0] // count
+    faces = low.shape[0]
+    shape = jax.ShapeDtypeStruct
+    sent = [shape((half + (faces if k in (1, count - 1) else 0), 128), BF16) for k in range(1, count)]
+    return pl.pallas_call(
+        side_kernel,
+        in_specs=[VMEM] * 4,
+        out_specs=[VMEM] * count,
+        out_shape=[shape((half, 128), F32), *sent],
+        compiler_params=limits(6),
+        cost_estimate=cost(10**6, 2 * 10**6),
+        name="side_sum",
+    )(keep, came, low, high)
+
+
 def total_kernel(*refs):
-    total = refs[0][...].astype(F32)
+    half = refs[-1].shape[0]
+    total = refs[0][...]
     for ref in refs[1:-1]:
-        total += ref[...].astype(F32)
+        total += ref[:half].astype(F32)
     refs[-1][...] = total.astype(BF16)
 
 
@@ -379,6 +413,23 @@
         cost_estimate=cost(10**6, 10**6),
         name="total_sum",
     )(*parts)
+
+
+def pack_kernel(*refs):
+    for index, ref in enumerate(refs[:-1]):
+        refs[-1][index] = ref[...]
+
+
+def pack(pieces):
+    return pl.pallas_call(
+        pack_kernel,
+        in_specs=[VMEM] * len(pieces),
+        out_specs=VMEM,
+        out_shape=jax.ShapeDtypeStruct((len(pieces), *pieces[0].shape), pieces[0].dtype),
+        compiler_params=limits(6),
+        cost_estimate=cost(10**5, 10**6),
+        name="pack",
+    )(*pieces)
 
 
 def expert_kernel(coef_ref, *refs, scale):
@@ -394,12 +445,15 @@
     even = lax.rem(place, 2) == 0
     first = jnp.broadcast_to(jnp.where(even, picked[0], picked[1]), (owned, 128))
     second = jnp.broadcast_to(jnp.where(even, picked[1], picked[0]), (owned, 128))
-    half = len(sums) // 2
-    for side in range(2):
-        total = sums[side * half][...].astype(F32)
-        for ref in sums[side * half + 1 : (side + 1) * half]:
-            total += ref[...].astype(F32)
-        summed[side] = total
+    if len(sums) == 4:
+        half = sums[0].shape[0]
+        side = place // 2
+        for index, ref in enumerate(sums):
+            at = (side if index % 2 == 0 else 1 - side) * half
+            summed[index // 2, pl.ds(pl.multiple_of(at, 16), half), :] = ref[...].astype(F32)
+    else:
+        for index, ref in enumerate(sums):
+            summed[index] = ref[...].astype(F32)
     for row in range(summed.shape[1]):
         out_ref[:, row * 128 : (row + 1) * 128] = (
             first * summed[0, row : row + 1, :] + second * summed[1, row : row + 1, :]
@@ -407,7 +461,7 @@
 
 
 def expert_product(coef, sums, owned, scale):
-    rows = sums[0].shape[0]
+    rows = sums[0].shape[0] * len(sums) // 2
     return pl.pallas_call(
         functools.partial(expert_kernel, scale=scale),
         in_specs=[VMEM] * (1 + len(sums)),
@@ -433,7 +487,8 @@
     for c in range(9):
         total = own_ref[c]
         for pick, ref in zip(picks, (a_ref, b_ref, c_ref, d_ref)):
-            total += nn(pick, ref[c])
+            at = ref.shape[0] - 9 * face + c * face
+            total += nn(pick, ref[at : at + face])
         out_ref[c] = total.astype(BF16)
 
 
@@ -475,7 +530,7 @@
     core = column % 2
     height = experts.shape[1] // 128
     rows = height * count_yz
-    direct = height % 32 == 0 and count_yz & (count_yz - 1) == 0 and count_gx == 4
+    direct = height % 32 == 0 and count_yz == 4 and count_gx == 4
 
     zero = rot_zero.reshape(1, -1)
     source = jnp.transpose(saved_input, (1, 0, 2))
@@ -494,7 +549,7 @@
     else:
         part = jnp.dot(merge_coef, experts.astype(F32), precision=lax.Precision.HIGHEST).astype(BF16)
         merged = lax.all_gather(part, "yz", axis=1, tiled=True)
-        pieces = [merged.reshape(merged.shape[0], rows, 128)]
+        pieces = [merged.reshape(1, merged.shape[0], rows, 128)]
 
         def places():
             return [0]
@@ -505,19 +560,18 @@
     if direct:
         other, *held = lax.optimization_barrier((other, *held))
         came = swap(other, "gx", 1)
-        parts = pair_sum(own, came, count_yz)
+        away, keep = core_sum(own, came)
+        opposite = swap(away, "gx", 2)
+        held = pack(held)
+        pieces = [held, swap(held, "gx", 1)]
+    grad_own, *ghosts = back(edge, zero, rot_one, rot_two, pulled, pieces, places, rows, atoms, slots, face)
+    across_gx = [neighbour_pairs(ghosts[first], "gx", first) for first in range(2)]
+    if direct:
+        parts = side_sum(keep, opposite, ghosts[2], ghosts[3], count_yz)
         gathered = [parts[0]] + [swap(parts[k], "yz", k) for k in range(1, count_yz)]
-        pieces = held + [swap(piece, "gx", 1) for piece in held]
-    grad_own, *ghosts = back(edge, zero, rot_one, rot_two, pulled, pieces, places, rows, atoms, slots, face)
-    returned = [
-        neighbour_pairs(ghost, axis, first)
-        for ghost, axis, first in zip(ghosts, ("gx", "gx", "yz", "yz"), (0, 1, 0, 1))
-    ]
-    if direct:
-        grad_own, *gathered = lax.optimization_barrier((grad_own, *gathered))
-        summed, *returned = lax.optimization_barrier((total_sum(gathered), *returned))
+        summed, *across_gx = lax.optimization_barrier((total_sum(gathered), *across_gx))
         across = swap(summed, "gx", 2)
-        input_grad = finish(send_index, grad_own, returned)
+        input_grad = finish(send_index, grad_own, [*across_gx, gathered[1], gathered[3]])
         across, input_grad = lax.optimization_barrier((across, input_grad))
         sums = [summed, across, swap(summed, "gx", 1), swap(across, "gx", 1)]
     else:
@@ -527,7 +581,8 @@
         piece = lax.dynamic_slice_in_dim(whole, row * height, height, 1)
         piece = jnp.where(core == 0, piece, piece[::-1])
         sums = [piece[0], piece[1]]
-        input_grad = finish(send_index, grad_own, returned)
+        across_yz = [neighbour_pairs(ghosts[2 + first], "yz", first) for first in range(2)]
+        input_grad = finish(send_index, grad_own, [*across_gx, *across_yz])
     grad_scale = math.sqrt(fanout / (atoms * count_yz * count_gx))
     expert_grad = expert_product(merge_coef, sums, merge_coef.shape[1] // count_gx, grad_scale)
     return (jnp.transpose(input_grad, (1, 0, 2)), expert_grad)

time: 51.4 us -> 53.1 us (1.033)
  waiting for transfers between devices: 13.6 us -> 16.6 us
  starting transfers between devices: 16.9 us -> 15.4 us
    ppermute x14 -> x12, waiting for transfers between devices: 9.96 us -> 16.6 us  [swap(): lax.ppermute(value, axis, [(i, i ^ bit) for i in range(lax.axis_size(axis...]
    ppermute x4 -> x2, waiting for transfers between devices: 3.6 us -> 0.01 us  [neighbour_pairs(): return lax.ppermute(value, axis, moves)]
    ppermute x4 -> x2, starting transfers between devices: 4.12 us -> 1.6 us  [neighbour_pairs(): return lax.ppermute(value, axis, moves)]
    ppermute x14 -> x12, starting transfers between devices: 12.8 us -> 13.8 us  [swap(): lax.ppermute(value, axis, [(i, i ^ bit) for i in range(lax.axis_size(axis...]
  transfers between devices with their start and end apart: 18 -> 14, of which waited for: 6 -> 6; matrix products, arithmetic and copies ran while one was open for 0% -> 0% of each run, Pallas kernels for 28% -> 27%
where the time goes in v4:
time: 53.1 us; the launch traced here: 52.9 us
  Pallas kernels  19.3 us (36%)
  waiting for transfers between devices  16.6 us (31%)
  starting transfers between devices  15.4 us (29%)
  between operations  1.49 us (3%)
    ppermute x12, waiting for transfers between devices, swap(): lax.ppermute(value, axis, [(i, i ^ bit) for i in range(lax.axis_size(axis...  16.6 us
    ppermute x12, starting transfers between devices, swap(): lax.ppermute(value, axis, [(i, i ^ bit) for i in range(lax.axis_size(axis...  13.8 us
    pallas_call x1, Pallas kernels, features(): pl.pallas_call(functools.partial(features_kernel, fanout=fanout), in_spec...  7.32 us
    pallas_call x1, Pallas kernels, back(): pl.pallas_call(functools.partial(back_kernel, pieces=len(pieces), members...  5.46 us
    pallas_call x1, Pallas kernels, merge(): pl.pallas_call(merge_kernel, in_specs=[VMEM, HBM], out_specs=VMEM, out_sh...  3.39 us
    pallas_call x1, Pallas kernels, expert_product(): pl.pallas_call(functools.partial(expert_kernel, scale=scale), in_specs=[V...  1.72 us
    ppermute x2, starting transfers between devices, neighbour_pairs(): return lax.ppermute(value, axis, moves)  1.6 us
    pallas_call x1, Pallas kernels, finish(): pl.pallas_call(finish_kernel, in_specs=[VMEM] * 6, out_specs=VMEM, out_sh...  1.17 us
  transfers between devices with their start and end apart: 14, of which 6 were waited for; matrix products, arithmetic and copies ran while one was open for 0% of the time, Pallas kernels for 27%

profile of v4, /device:TPU:0, one launch (start us, length us, event | category | flops | bytes accessed | tf_op | source)
XLA Modules:
  0.0 52.9 jit_solution(3817844919697728036)
XLA Ops:
  0.7 3.4 %merge.1.refs_0_ = bf16[2,272,128]{2,1,0:T(8,128)(2,1)} custom-call(f32[2,32]{1,0:T(2,128)} %coef_ref.3, bf16[32,69632]{1,0:T(8,128)(2,1)} %experts_ref.1), custom_call_target="tpu_custom_call" | custom-call | flops 53477376 | bytes 2228224 | tf_op jit(solution)/shard_map/merge/pallas_call | solution.py:100
  4.1 3.1 %collective-permute-start = (bf16[2,272,128]{2,1,0:T(8,128)(2,1)}, bf16[2,272,128]{2,1,0:T(8,128)(2,1)S(1)}, u32[]{:S(2)}, u32[]{:S(2)}) collective-permute-start(bf16[2,272,128]{2,1,0:T(8,128)(2,1)} %merge.1.refs_0_), channel_id=1, source_target_pairs={{0,4},{4,0},{8,12},{12,8},{1,5},{5,1},{9,13},{13,9},{2,6},{6,2},{1... | collective-permute-start | bytes 417800 | tf_op jit(solution)/shard_map/ppermute | solution.py:508
  7.2 2.6 %collective-permute-start.1 = (bf16[2,272,128]{2,1,0:T(8,128)(2,1)}, bf16[2,272,128]{2,1,0:T(8,128)(2,1)S(1)}, u32[]{:S(2)}, u32[]{:S(2)}) collective-permute-start(bf16[2,272,128]{2,1,0:T(8,128)(2,1)} %merge.1.refs_0_), channel_id=1, source_target_pairs={{0,8},{4,12},{8,0},{12,4},{1,9},{5,13},{9,1},{13,5},{2,10},{6,14},... | collective-permute-start | bytes 417800 | tf_op jit(solution)/shard_map/ppermute | solution.py:508
  9.8 0.0 collective-permute-start.2
  10.5 0.0 copy-start
  10.5 7.3 %features.1 = (bf16[2176,128]{1,0:T(8,128)(2,1)S(1)}, bf16[2176,128]{1,0:T(8,128)(2,1)S(1)}, bf16[896,1024]{1,0:T(8,128)(2,1)S(1)}, f32[8,1024]{1,0:T(8,128)S(1)}) custom-call(s32[1]{0:T(128)S(6)} %copy.13.live_ref, s32[8,128]{1,0:T(8,128)S(1)} %bitcast.8, s32[1,128]{1,0:T(1,128)S(1)} %bitcast.11, f32[1,1024]{1,0:T(1,128)S(1)} %bitcast.9, ...), custom_call_target="tpu_custom_call" | custom-call | flops 8999999488 | bytes 7000000 | tf_op jit(solution)/shard_map/features/pallas_call | solution.py:208
  17.8 0.0 collective-permute-done.refs_1_
  17.8 3.0 %collective-permute-done.1.refs_2_ = bf16[2,272,128]{2,1,0:T(8,128)(2,1)S(1)} collective-permute-done((bf16[2,272,128]{2,1,0:T(8,128)(2,1)}, bf16[2,272,128]{2,1,0:T(8,128)(2,1)S(1)}, u32[]{:S(2)}, u32[]{:S(2)}) %collective-permute-start.1) | collective-permute-done | bytes 139296 | tf_op jit(solution)/shard_map/ppermute | solution.py:508
  20.9 0.0 collective-permute-done.2.refs_3_
  20.9 0.0 collective-permute-start.3
  20.9 0.6 %collective-permute-start.5 = (bf16[4,2,272,128]{3,2,1,0:T(8,128)(2,1)S(1)}, bf16[4,2,272,128]{3,2,1,0:T(8,128)(2,1)S(1)}, u32[]{:S(2)}, u32[]{:S(2)}) collective-permute-start(bf16[4,2,272,128]{3,2,1,0:T(8,128)(2,1)S(1)} %pack.1.rest_0_), channel_id=1, source_target_pairs={{0,1},{1,0},{2,3},{3,2},{4,5},{5,4},{6,7},{7,6},{8,9},{9,8},{10,11... | collective-permute-start | bytes 1671176 | tf_op jit(solution)/shard_map/ppermute | solution.py:508
  21.5 1.3 %collective-permute-done.3.came_ref = bf16[2176,128]{1,0:T(8,128)(2,1)S(1)} collective-permute-done((bf16[2176,128]{1,0:T(8,128)(2,1)S(1)}, bf16[2176,128]{1,0:T(8,128)(2,1)S(1)}, u32[]{:S(2)}, u32[]{:S(2)}) %collective-permute-start.3) | collective-permute-done | bytes 557088 | tf_op jit(solution)/shard_map/ppermute | solution.py:508
  22.8 0.1 core_sum.1
  23.0 1.6 %collective-permute-start.4 = (bf16[1088,128]{1,0:T(8,128)(2,1)S(1)}, bf16[1088,128]{1,0:T(8,128)(2,1)S(1)}, u32[]{:S(2)}, u32[]{:S(2)}) collective-permute-start(bf16[1088,128]{1,0:T(8,128)(2,1)S(1)} %get-tuple-element.35), channel_id=1, source_target_pairs={{0,2},{1,3},{2,0},{3,1},{4,6},{5,7},{6,4},{7,5},{8,10},{9,11},{10,... | collective-permute-start | bytes 835592 | tf_op jit(solution)/shard_map/ppermute | solution.py:508
  24.5 0.0 collective-permute-done.5.rest_1_
  24.5 5.5 %back.1 = (f32[9,128,128]{2,1,0:T(8,128)S(1)}, bf16[288,128]{1,0:T(8,128)(2,1)S(1)}, bf16[288,128]{1,0:T(8,128)(2,1)S(1)}, bf16[288,128]{1,0:T(8,128)(2,1)S(1)}, bf16[288,128]{1,0:T(8,128)(2,1)S(1)}) custom-call(f32[8,1024]{1,0:T(8,128)S(1)} %get-tuple-element.36.edge_ref, f32[1,1024]{1,0:T(1,128)S(1)} %bitcast.10, f32[3,3,1024]{2,1,0:T(4,128)S(1)} %copy-done.6, ...), custom_call_target="tpu_custom_call" | custom-call | flops 8999999488 | bytes 7000000 | tf_op jit(solution)/shard_map/back/pallas_call | solution.py:325
  30.0 0.0 copy-start.1
  30.0 1.7 %collective-permute-done.4.came_ref = bf16[1088,128]{1,0:T(8,128)(2,1)S(1)} collective-permute-done((bf16[1088,128]{1,0:T(8,128)(2,1)S(1)}, bf16[1088,128]{1,0:T(8,128)(2,1)S(1)}, u32[]{:S(2)}, u32[]{:S(2)}) %collective-permute-start.4) | collective-permute-done | bytes 278560 | tf_op jit(solution)/shard_map/ppermute | solution.py:508
  31.7 0.1 side_sum.1
  31.8 2.2 %collective-permute-start.6 = (bf16[560,128]{1,0:T(8,128)(2,1)S(1)}, bf16[560,128]{1,0:T(8,128)(2,1)S(1)}, u32[]{:S(2)}, u32[]{:S(2)}) collective-permute-start(bf16[560,128]{1,0:T(8,128)(2,1)S(1)} %get-tuple-element.45), channel_id=1, source_target_pairs={{0,4},{4,0},{8,12},{12,8},{1,5},{5,1},{9,13},{13,9},{2,6},{6,2},{1... | collective-permute-start | bytes 430088 | tf_op jit(solution)/shard_map/ppermute | solution.py:508
  34.0 2.5 %collective-permute-start.8 = (bf16[560,128]{1,0:T(8,128)(2,1)S(1)}, bf16[560,128]{1,0:T(8,128)(2,1)S(1)}, u32[]{:S(2)}, u32[]{:S(2)}) collective-permute-start(bf16[560,128]{1,0:T(8,128)(2,1)S(1)} %get-tuple-element.47), channel_id=1, source_target_pairs={{0,12},{4,8},{8,4},{12,0},{1,13},{5,9},{9,5},{13,1},{2,14},{6,10},... | collective-permute-start | bytes 430088 | tf_op jit(solution)/shard_map/ppermute | solution.py:508
  36.5 0.0 collective-permute-start.9
  36.5 1.6 %collective-permute-start.10 = (bf16[288,128]{1,0:T(8,128)(2,1)S(1)}, bf16[288,128]{1,0:T(8,128)(2,1)S(1)}, u32[]{:S(2)}, u32[]{:S(2)}) collective-permute-start(bf16[288,128]{1,0:T(8,128)(2,1)S(1)} %get-tuple-element.49), channel_id=1, source_target_pairs={{1,2},{2,1},{3,0},{0,3},{5,6},{6,5},{7,4},{4,7},{9,10},{10,9},{11,... | collective-permute-start | bytes 221192 | tf_op jit(solution)/shard_map/ppermute | solution.py:517
  38.1 0.0 collective-permute-start.7
  38.1 7.4 %collective-permute-done.7.refs_2_ = bf16[272,128]{1,0:T(8,128)(2,1)S(1)} collective-permute-done((bf16[272,128]{1,0:T(8,128)(2,1)S(1)}, bf16[272,128]{1,0:T(8,128)(2,1)S(1)}, u32[]{:S(2)}, u32[]{:S(2)}) %collective-permute-start.7) | collective-permute-done | bytes 69664 | tf_op jit(solution)/shard_map/ppermute | solution.py:508
  45.5 0.0 collective-permute-done.6.refs_1_.c_ref
  45.5 0.0 collective-permute-done.8.refs_3_.d_ref
  45.5 1.3 %collective-permute-start.11 = (bf16[272,128]{1,0:T(8,128)(2,1)S(1)}, bf16[272,128]{1,0:T(8,128)(2,1)S(1)}, u32[]{:S(2)}, u32[]{:S(2)}) collective-permute-start(bf16[272,128]{1,0:T(8,128)(2,1)S(1)} %total_sum.1.refs_0_), channel_id=1, source_target_pairs={{0,2},{1,3},{2,0},{3,1},{4,6},{5,7},{6,4},{7,5},{8,10},{9,11},{10,... | collective-permute-start | bytes 208904 | tf_op jit(solution)/shard_map/ppermute | solution.py:508
  46.8 1.2 %finish.1 = bf16[9,128,128]{2,1,0:T(8,128)(2,1)} custom-call(s32[4,32]{1,0:T(4,128)S(1)} %copy-done.2, f32[9,128,128]{2,1,0:T(8,128)S(1)} %get-tuple-element.51.own_ref, bf16[288,128]{1,0:T(8,128)(2,1)S(1)} %collective-permute-done.9.a_ref, bf16[288,128]{1,0:T(8,128)(2,1)S(1)} %collective-permute-done.10.b_ref, ...), custom_call_target="tpu_custom_call" | custom-call | flops 100000000 | bytes 2000000 | tf_op jit(solution)/shard_map/finish/pallas_call | solution.py:496
  48.0 1.9 %collective-permute-done.11.refs_1_ = bf16[272,128]{1,0:T(8,128)(2,1)S(1)} collective-permute-done((bf16[272,128]{1,0:T(8,128)(2,1)S(1)}, bf16[272,128]{1,0:T(8,128)(2,1)S(1)}, u32[]{:S(2)}, u32[]{:S(2)}) %collective-permute-start.11) | collective-permute-done | bytes 69664 | tf_op jit(solution)/shard_map/ppermute | solution.py:508
  49.9 1.3 %collective-permute-done.13.refs_3_ = bf16[272,128]{1,0:T(8,128)(2,1)S(1)} collective-permute-done((bf16[272,128]{1,0:T(8,128)(2,1)S(1)}, bf16[272,128]{1,0:T(8,128)(2,1)S(1)}, u32[]{:S(2)}, u32[]{:S(2)}) %collective-permute-start.13) | collective-permute-done | bytes 69664 | tf_op jit(solution)/shard_map/ppermute | solution.py:508
  51.2 1.7 %expert_product.1 = f32[8,69632]{1,0:T(8,128)} custom-call(f32[2,32]{1,0:T(2,128)S(1)} %copy-done.1, bf16[272,128]{1,0:T(8,128)(2,1)S(1)} %total_sum.1.refs_0_, bf16[272,128]{1,0:T(8,128)(2,1)S(1)} %collective-permute-done.11.refs_1_, bf16[272,128]{1,0:T(8,128)(2,1)S(1)} %collective-permute-done.12.refs_2_, bf16[272,128]{1,0:T(8,128)(2,1)S(1)} %collective-permute-done.13.refs_3_), custom_call_target="tpu_custom_call" | custom-call | flops 1000000 | bytes 4000000 | tf_op jit(solution)/shard_map/expert_product/pallas_call | solution.py:465
  (25 shorter events, 0.1 us)
Async XLA Ops:
  0.6 9.8 %copy-start.3 = (bf16[256,9,128]{2,0,1:T(8,128)(2,1)S(1)}, bf16[256,9,128]{2,0,1:T(8,128)(2,1)}, u32[]{:S(2)}) copy-start(bf16[256,9,128]{2,0,1:T(8,128)(2,1)} %param.11) | copy-start | bytes 1769476
  0.6 9.8 %copy-start.4 = (bf16[128,9,128]{2,0,1:T(8,128)(2,1)S(1)}, bf16[128,9,128]{2,0,1:T(8,128)(2,1)}, u32[]{:S(2)}) copy-start(bf16[128,9,128]{2,0,1:T(8,128)(2,1)} %param.12) | copy-start | bytes 884740
  0.7 9.8 %copy-start.7 = (s32[128,8]{0,1:T(8,128)S(1)}, s32[128,8]{0,1:T(8,128)}, u32[]{:S(2)}) copy-start(s32[128,8]{0,1:T(8,128)} %param.13) | copy-start | bytes 12292
  0.7 9.8 %copy-start.9 = (s32[128]{0:T(128)S(1)}, s32[128]{0:T(128)}, u32[]{:S(2)}) copy-start(s32[128]{0:T(128)} %param.18) | copy-start | bytes 1540
  0.7 9.8 %copy-start.8 = (f32[1024]{0:T(1024)S(1)}, f32[1024]{0:T(1024)}, u32[]{:S(2)}) copy-start(f32[1024]{0:T(1024)} %param.14) | copy-start | bytes 12292
  0.7 9.8 %copy-start.6 = (f32[3,3,1024]{2,1,0:T(4,128)S(1)}, f32[3,3,1024]{2,1,0:T(4,128)}, u32[]{:S(2)}) copy-start(f32[3,3,1024]{2,1,0:T(4,128)} %one_ref.3) | copy-start | bytes 110596
  0.7 9.8 %copy-start.5 = (f32[5,5,1024]{2,1,0:T(8,128)S(1)}, f32[5,5,1024]{2,1,0:T(8,128)}, u32[]{:S(2)}) copy-start(f32[5,5,1024]{2,1,0:T(8,128)} %two_ref.3) | copy-start | bytes 307204
  4.1 13.7 %collective-permute-start = (bf16[2,272,128]{2,1,0:T(8,128)(2,1)}, bf16[2,272,128]{2,1,0:T(8,128)(2,1)S(1)}, u32[]{:S(2)}, u32[]{:S(2)}) collective-permute-start(bf16[2,272,128]{2,1,0:T(8,128)(2,1)} %merge.1.refs_0_), channel_id=1, source_target_pairs={{0,4},{4,0},{8,12},{12,8},{1,5},{5,1},{9,13},{13,9},{2,6},{6,2},{1... | collective-permute-start | bytes 417800 | tf_op jit(solution)/shard_map/ppermute | solution.py:508
  7.2 13.7 %collective-permute-start.1 = (bf16[2,272,128]{2,1,0:T(8,128)(2,1)}, bf16[2,272,128]{2,1,0:T(8,128)(2,1)S(1)}, u32[]{:S(2)}, u32[]{:S(2)}) collective-permute-start(bf16[2,272,128]{2,1,0:T(8,128)(2,1)} %merge.1.refs_0_), channel_id=1, source_target_pairs={{0,8},{4,12},{8,0},{12,4},{1,9},{5,13},{9,1},{13,5},{2,10},{6,14},... | collective-permute-start | bytes 417800 | tf_op jit(solution)/shard_map/ppermute | solution.py:508
  9.8 11.1 %collective-permute-start.2 = (bf16[2,272,128]{2,1,0:T(8,128)(2,1)}, bf16[2,272,128]{2,1,0:T(8,128)(2,1)S(1)}, u32[]{:S(2)}, u32[]{:S(2)}) collective-permute-start(bf16[2,272,128]{2,1,0:T(8,128)(2,1)} %merge.1.refs_0_), channel_id=1, source_target_pairs={{0,12},{4,8},{8,4},{12,0},{1,13},{5,9},{9,5},{13,1},{2,14},{6,10},... | collective-permute-start | bytes 417800 | tf_op jit(solution)/shard_map/ppermute | solution.py:508
  10.5 10.4 %copy-start = (bf16[2,272,128]{2,1,0:T(8,128)(2,1)S(1)}, bf16[2,272,128]{2,1,0:T(8,128)(2,1)}, u32[]{:S(2)}) copy-start(bf16[2,272,128]{2,1,0:T(8,128)(2,1)} %merge.1.refs_0_) | copy-start | bytes 417796
  20.9 2.0 %collective-permute-start.3 = (bf16[2176,128]{1,0:T(8,128)(2,1)S(1)}, bf16[2176,128]{1,0:T(8,128)(2,1)S(1)}, u32[]{:S(2)}, u32[]{:S(2)}) collective-permute-start(bf16[2176,128]{1,0:T(8,128)(2,1)S(1)} %get-tuple-element.33), channel_id=1, source_target_pairs={{0,1},{1,0},{2,3},{3,2},{4,5},{5,4},{6,7},{7,6},{8,9},{9,8},{10,11... | collective-permute-start | bytes 1671176 | tf_op jit(solution)/shard_map/ppermute | solution.py:508
  20.9 3.6 %collective-permute-start.5 = (bf16[4,2,272,128]{3,2,1,0:T(8,128)(2,1)S(1)}, bf16[4,2,272,128]{3,2,1,0:T(8,128)(2,1)S(1)}, u32[]{:S(2)}, u32[]{:S(2)}) collective-permute-start(bf16[4,2,272,128]{3,2,1,0:T(8,128)(2,1)S(1)} %pack.1.rest_0_), channel_id=1, source_target_pairs={{0,1},{1,0},{2,3},{3,2},{4,5},{5,4},{6,7},{7,6},{8,9},{9,8},{10,11... | collective-permute-start | bytes 1671176 | tf_op jit(solution)/shard_map/ppermute | solution.py:508
  23.0 8.8 %collective-permute-start.4 = (bf16[1088,128]{1,0:T(8,128)(2,1)S(1)}, bf16[1088,128]{1,0:T(8,128)(2,1)S(1)}, u32[]{:S(2)}, u32[]{:S(2)}) collective-permute-start(bf16[1088,128]{1,0:T(8,128)(2,1)S(1)} %get-tuple-element.35), channel_id=1, source_target_pairs={{0,2},{1,3},{2,0},{3,1},{4,6},{5,7},{6,4},{7,5},{8,10},{9,11},{10,... | collective-permute-start | bytes 835592 | tf_op jit(solution)/shard_map/ppermute | solution.py:508
  24.5 22.3 %copy-start.2 = (s32[4,32]{1,0:T(4,128)S(1)}, s32[4,32]{1,0:T(4,128)}, u32[]{:S(2)}) copy-start(s32[4,32]{1,0:T(4,128)} %send_ref.1) | copy-start | bytes 1540
  30.0 21.2 %copy-start.1 = (f32[2,32]{1,0:T(2,128)S(1)}, f32[2,32]{1,0:T(2,128)}, u32[]{:S(2)}) copy-start(f32[2,32]{1,0:T(2,128)} %coef_ref.3) | copy-start | bytes 772
  31.8 13.7 %collective-permute-start.6 = (bf16[560,128]{1,0:T(8,128)(2,1)S(1)}, bf16[560,128]{1,0:T(8,128)(2,1)S(1)}, u32[]{:S(2)}, u32[]{:S(2)}) collective-permute-start(bf16[560,128]{1,0:T(8,128)(2,1)S(1)} %get-tuple-element.45), channel_id=1, source_target_pairs={{0,4},{4,0},{8,12},{12,8},{1,5},{5,1},{9,13},{13,9},{2,6},{6,2},{1... | collective-permute-start | bytes 430088 | tf_op jit(solution)/shard_map/ppermute | solution.py:508
  34.0 11.5 %collective-permute-start.8 = (bf16[560,128]{1,0:T(8,128)(2,1)S(1)}, bf16[560,128]{1,0:T(8,128)(2,1)S(1)}, u32[]{:S(2)}, u32[]{:S(2)}) collective-permute-start(bf16[560,128]{1,0:T(8,128)(2,1)S(1)} %get-tuple-element.47), channel_id=1, source_target_pairs={{0,12},{4,8},{8,4},{12,0},{1,13},{5,9},{9,5},{13,1},{2,14},{6,10},... | collective-permute-start | bytes 430088 | tf_op jit(solution)/shard_map/ppermute | solution.py:508
  36.5 9.1 %collective-permute-start.9 = (bf16[288,128]{1,0:T(8,128)(2,1)S(1)}, bf16[288,128]{1,0:T(8,128)(2,1)S(1)}, u32[]{:S(2)}, u32[]{:S(2)}) collective-permute-start(bf16[288,128]{1,0:T(8,128)(2,1)S(1)} %get-tuple-element.48), channel_id=1, source_target_pairs={{0,1},{1,0},{2,3},{3,2},{4,5},{5,4},{6,7},{7,6},{8,9},{9,8},{10,11... | collective-permute-start | bytes 221192 | tf_op jit(solution)/shard_map/ppermute | solution.py:517
  36.5 9.1 %collective-permute-start.10 = (bf16[288,128]{1,0:T(8,128)(2,1)S(1)}, bf16[288,128]{1,0:T(8,128)(2,1)S(1)}, u32[]{:S(2)}, u32[]{:S(2)}) collective-permute-start(bf16[288,128]{1,0:T(8,128)(2,1)S(1)} %get-tuple-element.49), channel_id=1, source_target_pairs={{1,2},{2,1},{3,0},{0,3},{5,6},{6,5},{7,4},{4,7},{9,10},{10,9},{11,... | collective-permute-start | bytes 221192 | tf_op jit(solution)/shard_map/ppermute | solution.py:517
  38.1 7.4 %collective-permute-start.7 = (bf16[272,128]{1,0:T(8,128)(2,1)S(1)}, bf16[272,128]{1,0:T(8,128)(2,1)S(1)}, u32[]{:S(2)}, u32[]{:S(2)}) collective-permute-start(bf16[272,128]{1,0:T(8,128)(2,1)S(1)} %get-tuple-element.46), channel_id=1, source_target_pairs={{0,8},{4,12},{8,0},{12,4},{1,9},{5,13},{9,1},{13,5},{2,10},{6,14},... | collective-permute-start | bytes 208904 | tf_op jit(solution)/shard_map/ppermute | solution.py:508
  45.5 4.4 %collective-permute-start.11 = (bf16[272,128]{1,0:T(8,128)(2,1)S(1)}, bf16[272,128]{1,0:T(8,128)(2,1)S(1)}, u32[]{:S(2)}, u32[]{:S(2)}) collective-permute-start(bf16[272,128]{1,0:T(8,128)(2,1)S(1)} %total_sum.1.refs_0_), channel_id=1, source_target_pairs={{0,2},{1,3},{2,0},{3,1},{4,6},{5,7},{6,4},{7,5},{8,10},{9,11},{10,... | collective-permute-start | bytes 208904 | tf_op jit(solution)/shard_map/ppermute | solution.py:508
  46.8 3.1 %collective-permute-start.12 = (bf16[272,128]{1,0:T(8,128)(2,1)S(1)}, bf16[272,128]{1,0:T(8,128)(2,1)S(1)}, u32[]{:S(2)}, u32[]{:S(2)}) collective-permute-start(bf16[272,128]{1,0:T(8,128)(2,1)S(1)} %total_sum.1.refs_0_), channel_id=1, source_target_pairs={{0,1},{1,0},{2,3},{3,2},{4,5},{5,4},{6,7},{7,6},{8,9},{9,8},{10,11... | collective-permute-start | bytes 208904 | tf_op jit(solution)/shard_map/ppermute | solution.py:508
  49.9 1.3 %collective-permute-start.13 = (bf16[272,128]{1,0:T(8,128)(2,1)S(1)}, bf16[272,128]{1,0:T(8,128)(2,1)S(1)}, u32[]{:S(2)}, u32[]{:S(2)}) collective-permute-start(bf16[272,128]{1,0:T(8,128)(2,1)S(1)} %collective-permute-done.11.refs_1_), channel_id=1, source_target_pairs={{0,1},{1,0},{2,3},{3,2},{4,5},{5,4},{6,7},{7,6},{8,9},{9,8},{10,11... | collective-permute-start | bytes 208904 | tf_op jit(solution)/shard_map/ppermute | solution.py:508

commit v5 on v3

--- a/solution.py
+++ b/solution.py
@@ -46,8 +46,8 @@
     return high, middle, low
 
 
-def merge_kernel(coef_ref, experts_ref, out_ref, held, arrived):
-    members, experts = coef_ref.shape
+def merge_kernel(coef_in_ref, experts_ref, out_ref, held, coef_ref, arrived, coef_arrived):
+    members, experts = coef_in_ref.shape
     rows = out_ref.shape[1]
     start = pl.multiple_of(lax.rem(lax.axis_index("gx"), 2) * rows * 128, 128)
     stripes = arrived.shape[0]
@@ -62,6 +62,9 @@
             )
         )
         copies[-1].start()
+    coef_copy = pltpu.make_async_copy(coef_in_ref, coef_ref, coef_arrived)
+    coef_copy.start()
+    coef_copy.wait()
     wide = 8 * experts
     row = lax.broadcasted_iota(jnp.int32, (8, wide), 0)
     col = lax.broadcasted_iota(jnp.int32, (8, wide), 1)
@@ -99,11 +102,16 @@
     rows = columns // 128
     return pl.pallas_call(
         merge_kernel,
-        in_specs=[VMEM, HBM],
+        in_specs=[HBM, HBM],
         out_specs=VMEM,
         out_shape=jax.ShapeDtypeStruct((members, rows, 128), BF16),
-        scratch_shapes=[pltpu.VMEM((count, columns), BF16), pltpu.SemaphoreType.DMA((4,))],
-        compiler_params=limits(60),
+        scratch_shapes=[
+            pltpu.VMEM((count, columns), BF16),
+            pltpu.VMEM((members, count), F32),
+            pltpu.SemaphoreType.DMA((2,)),
+            pltpu.SemaphoreType.DMA,
+        ],
+        compiler_params=limits(52),
         cost_estimate=cost(96 * 16 * columns, 2 * count * columns),
         name="merge",
     )(coef, experts)
@@ -242,11 +250,12 @@
     zw, pw = 3 * channels, 2 * channels
     first = zw * zw // 128
     second = first + pw * pw // 128
-    for piece, place in zip(piece_refs, places()):
-        height = piece.shape[1]
+    placed = [(piece, index) for piece in piece_refs for index in range(piece.shape[0])]
+    for (piece, index), place in zip(placed, places()):
+        height = piece.shape[2]
         at = pl.ds(pl.multiple_of(place, 16), height)
         for k in range(members):
-            flat[k, at, :] = piece[k].astype(F32)
+            flat[k, at, :] = piece[index, k].astype(F32)
     for k in range(members):
         for j in range(zw // 128):
             weight_zero[:, k * zw + j * 128 : k * zw + (j + 1) * 128] = flat[
@@ -311,12 +320,12 @@
         for side in range(2):
             even = lax.rem(lax.axis_index(("gx", "yz")[side]), 2) == 0
             low, high = blocks[2 * side], blocks[2 * side + 1]
-            ghost_refs[2 * side][c] = jnp.where(even, high, low).astype(BF16)
-            ghost_refs[2 * side + 1][c] = jnp.where(even, low, high).astype(BF16)
+            ghost_refs[3 - side][c] = jnp.where(even, high, low).astype(BF16)
+            ghost_refs[1 - side][c] = jnp.where(even, low, high).astype(BF16)
 
 
 def back(edge, zero, one, two, pulled, pieces, places, rows, atoms, slots, face):
-    members = pieces[0].shape[0]
+    members = pieces[0].shape[1]
     edges = pulled.shape[1]
     channels = pulled.shape[0] // 7
     shape = jax.ShapeDtypeStruct
@@ -379,6 +388,23 @@
         cost_estimate=cost(10**6, 10**6),
         name="total_sum",
     )(*parts)
+
+
+def pack_kernel(*refs):
+    for index, ref in enumerate(refs[:-1]):
+        refs[-1][index] = ref[...]
+
+
+def pack(pieces):
+    return pl.pallas_call(
+        pack_kernel,
+        in_specs=[VMEM] * len(pieces),
+        out_specs=VMEM,
+        out_shape=jax.ShapeDtypeStruct((len(pieces), *pieces[0].shape), pieces[0].dtype),
+        compiler_params=limits(6),
+        cost_estimate=cost(10**5, 10**6),
+        name="pack",
+    )(*pieces)
 
 
 def expert_kernel(coef_ref, *refs, scale):
@@ -430,6 +456,7 @@
         below, above = send_ref[2 * side : 2 * side + 1, :], send_ref[2 * side + 1 : 2 * side + 2, :]
         for faces in (jnp.where(even, above, below), jnp.where(even, below, above)):
             picks.append((row == faces).astype(F32).astype(BF16))
+    picks = [picks[3], picks[1], picks[2], picks[0]]
     for c in range(9):
         total = own_ref[c]
         for pick, ref in zip(picks, (a_ref, b_ref, c_ref, d_ref)):
@@ -494,7 +521,7 @@
     else:
         part = jnp.dot(merge_coef, experts.astype(F32), precision=lax.Precision.HIGHEST).astype(BF16)
         merged = lax.all_gather(part, "yz", axis=1, tiled=True)
-        pieces = [merged.reshape(merged.shape[0], rows, 128)]
+        pieces = [merged.reshape(1, merged.shape[0], rows, 128)]
 
         def places():
             return [0]
@@ -506,12 +533,13 @@
         other, *held = lax.optimization_barrier((other, *held))
         came = swap(other, "gx", 1)
         parts = pair_sum(own, came, count_yz)
-        gathered = [parts[0]] + [swap(parts[k], "yz", k) for k in range(1, count_yz)]
-        pieces = held + [swap(piece, "gx", 1) for piece in held]
+        gathered = [parts[0]] + [swap(parts[k], "yz", k) for k in reversed(range(1, count_yz))]
+        held = pack(held)
+        pieces = [held, swap(held, "gx", 1)]
     grad_own, *ghosts = back(edge, zero, rot_one, rot_two, pulled, pieces, places, rows, atoms, slots, face)
     returned = [
         neighbour_pairs(ghost, axis, first)
-        for ghost, axis, first in zip(ghosts, ("gx", "gx", "yz", "yz"), (0, 1, 0, 1))
+        for ghost, axis, first in zip(ghosts, ("yz", "gx", "yz", "gx"), (1, 1, 0, 0))
     ]
     if direct:
         grad_own, *gathered = lax.optimization_barrier((grad_own, *gathered))

time: 51.4 us -> 48.9 us (0.951)
  starting transfers between devices: 16.9 us -> 15.4 us
  Pallas kernels: 19.2 us -> 17.8 us
  local copies, waits for them, and re-layouts: 0.05 us -> 0.7 us
    ppermute x4, starting transfers between devices: 4.12 us -> 2.67 us  [neighbour_pairs(): return lax.ppermute(value, axis, moves)]
    pallas_call x1 -> x2, Pallas kernels: 3.39 us -> 2.06 us  [the longest x1 2.03 us: merge(): pl.pallas_call(merge_kernel, in_specs=[HBM, HBM], out_specs=VMEM, out_sha...]
    ppermute x4, waiting for transfers between devices: 3.6 us -> 2.61 us  [neighbour_pairs(): return lax.ppermute(value, axis, moves)]
    ppermute x14 -> x11, waiting for transfers between devices: 9.96 us -> 10.7 us  [swap(): lax.ppermute(value, axis, [(i, i ^ bit) for i in range(lax.axis_size(axis...]
    unnamed x20 -> x18, local copies, waits for them, and re-layouts: 0.05 us -> 0.7 us
    ppermute x14 -> x11, starting transfers between devices: 12.8 us -> 12.8 us  [swap(): lax.ppermute(value, axis, [(i, i ^ bit) for i in range(lax.axis_size(axis...]
  transfers between devices with their start and end apart: 18 -> 15, of which waited for: 6 -> 8; matrix products, arithmetic and copies ran while one was open for 0% -> 0% of each run, Pallas kernels for 28% -> 29%
where the time goes in v5:
time: 48.9 us; the launch traced here: 48.7 us
  Pallas kernels  17.8 us (36%)
  starting transfers between devices  15.4 us (31%)
  waiting for transfers between devices  13.3 us (27%)
  between operations  1.44 us (3%)
  local copies, waits for them, and re-layouts  0.7 us (1%)
    ppermute x11, starting transfers between devices, swap(): lax.ppermute(value, axis, [(i, i ^ bit) for i in range(lax.axis_size(axis...  12.8 us
    ppermute x11, waiting for transfers between devices, swap(): lax.ppermute(value, axis, [(i, i ^ bit) for i in range(lax.axis_size(axis...  10.7 us
    pallas_call x1, Pallas kernels, features(): pl.pallas_call(functools.partial(features_kernel, fanout=fanout), in_spec...  7.18 us
    pallas_call x1, Pallas kernels, back(): pl.pallas_call(functools.partial(back_kernel, pieces=len(pieces), members...  5.47 us
    ppermute x4, starting transfers between devices, neighbour_pairs(): return lax.ppermute(value, axis, moves)  2.67 us
    ppermute x4, waiting for transfers between devices, neighbour_pairs(): return lax.ppermute(value, axis, moves)  2.61 us
    pallas_call x1, Pallas kernels, merge(): pl.pallas_call(merge_kernel, in_specs=[HBM, HBM], out_specs=VMEM, out_sha...  2.03 us
    pallas_call x1, Pallas kernels, expert_product(): pl.pallas_call(functools.partial(expert_kernel, scale=scale), in_specs=[V...  1.72 us
  transfers between devices with their start and end apart: 15, of which 8 were waited for; matrix products, arithmetic and copies ran while one was open for 0% of the time, Pallas kernels for 29%

profile of v5, /device:TPU:0, one launch (start us, length us, event | category | flops | bytes accessed | tf_op | source)
XLA Modules:
  0.0 48.7 jit_solution(1713625007103002940)
XLA Ops:
  0.6 0.7 %copy-done = f32[2,32]{1,0:T(2,128)S(1)} copy-done((f32[2,32]{1,0:T(2,128)S(1)}, f32[2,32]{1,0:T(2,128)}, u32[]{:S(2)}) %copy-start) | copy-done | bytes 280
  1.4 2.0 %merge.1.refs_0_ = bf16[2,272,128]{2,1,0:T(8,128)(2,1)S(1)} custom-call(f32[2,32]{1,0:T(2,128)S(1)} %copy-done, bf16[32,69632]{1,0:T(8,128)(2,1)} %experts_ref.1), custom_call_target="tpu_custom_call" | custom-call | flops 53477376 | bytes 2228224 | tf_op jit(solution)/shard_map/merge/pallas_call | solution.py:103
  3.4 5.1 %collective-permute-start.2 = (bf16[2,272,128]{2,1,0:T(8,128)(2,1)S(1)}, bf16[2,272,128]{2,1,0:T(8,128)(2,1)S(1)}, u32[]{:S(2)}, u32[]{:S(2)}) collective-permute-start(bf16[2,272,128]{2,1,0:T(8,128)(2,1)S(1)} %merge.1.refs_0_), channel_id=1, source_target_pairs={{0,12},{4,8},{8,4},{12,0},{1,13},{5,9},{9,5},{13,1},{2,14},{6,10},... | collective-permute-start | bytes 417800 | tf_op jit(solution)/shard_map/ppermute | solution.py:480
  8.5 0.0 collective-permute-start.1
  8.5 0.6 %collective-permute-start = (bf16[2,272,128]{2,1,0:T(8,128)(2,1)S(1)}, bf16[2,272,128]{2,1,0:T(8,128)(2,1)S(1)}, u32[]{:S(2)}, u32[]{:S(2)}) collective-permute-start(bf16[2,272,128]{2,1,0:T(8,128)(2,1)S(1)} %merge.1.refs_0_), channel_id=1, source_target_pairs={{0,4},{4,0},{8,12},{12,8},{1,5},{5,1},{9,13},{13,9},{2,6},{6,2},{1... | collective-permute-start | bytes 417800 | tf_op jit(solution)/shard_map/ppermute | solution.py:480
  9.9 7.2 %features.1 = (bf16[2176,128]{1,0:T(8,128)(2,1)S(1)}, bf16[2176,128]{1,0:T(8,128)(2,1)S(1)}, bf16[896,1024]{1,0:T(8,128)(2,1)S(1)}, f32[8,1024]{1,0:T(8,128)S(1)}) custom-call(s32[1]{0:T(128)S(6)} %copy.13.live_ref, s32[8,128]{1,0:T(8,128)S(1)} %bitcast.8, s32[1,128]{1,0:T(1,128)S(1)} %bitcast.11, f32[1,1024]{1,0:T(1,128)S(1)} %bitcast.9, ...), custom_call_target="tpu_custom_call" | custom-call | flops 8999999488 | bytes 7000000 | tf_op jit(solution)/shard_map/features/pallas_call | solution.py:216
  17.1 0.0 collective-permute-done.2.refs_3_
  17.1 3.2 %collective-permute-done.1.refs_2_ = bf16[2,272,128]{2,1,0:T(8,128)(2,1)S(1)} collective-permute-done((bf16[2,272,128]{2,1,0:T(8,128)(2,1)S(1)}, bf16[2,272,128]{2,1,0:T(8,128)(2,1)S(1)}, u32[]{:S(2)}, u32[]{:S(2)}) %collective-permute-start.1) | collective-permute-done | bytes 139296 | tf_op jit(solution)/shard_map/ppermute | solution.py:480
  20.3 0.0 collective-permute-done.refs_1_
  20.3 0.0 collective-permute-start.4
  20.3 0.6 %collective-permute-start.3 = (bf16[4,2,272,128]{3,2,1,0:T(8,128)(2,1)S(1)}, bf16[4,2,272,128]{3,2,1,0:T(8,128)(2,1)S(1)}, u32[]{:S(2)}, u32[]{:S(2)}) collective-permute-start(bf16[4,2,272,128]{3,2,1,0:T(8,128)(2,1)S(1)} %pack.1.rest_0_), channel_id=1, source_target_pairs={{0,1},{1,0},{2,3},{3,2},{4,5},{5,4},{6,7},{7,6},{8,9},{9,8},{10,11... | collective-permute-start | bytes 1671176 | tf_op jit(solution)/shard_map/ppermute | solution.py:480
  20.9 1.3 %collective-permute-done.4.came_ref = bf16[2176,128]{1,0:T(8,128)(2,1)S(1)} collective-permute-done((bf16[2176,128]{1,0:T(8,128)(2,1)S(1)}, bf16[2176,128]{1,0:T(8,128)(2,1)S(1)}, u32[]{:S(2)}, u32[]{:S(2)}) %collective-permute-start.4) | collective-permute-done | bytes 557088 | tf_op jit(solution)/shard_map/ppermute | solution.py:480
  22.2 0.1 pair_sum.1
  22.4 2.6 %collective-permute-start.5 = (bf16[544,128]{1,0:T(8,128)(2,1)S(1)}, bf16[544,128]{1,0:T(8,128)(2,1)S(1)}, u32[]{:S(2)}, u32[]{:S(2)}) collective-permute-start(bf16[544,128]{1,0:T(8,128)(2,1)S(1)} %get-tuple-element.47), channel_id=1, source_target_pairs={{0,12},{4,8},{8,4},{12,0},{1,13},{5,9},{9,5},{13,1},{2,14},{6,10},... | collective-permute-start | bytes 417800 | tf_op jit(solution)/shard_map/ppermute | solution.py:480
  24.9 0.0 collective-permute-start.6
  24.9 1.9 %collective-permute-start.7 = (bf16[544,128]{1,0:T(8,128)(2,1)S(1)}, bf16[544,128]{1,0:T(8,128)(2,1)S(1)}, u32[]{:S(2)}, u32[]{:S(2)}) collective-permute-start(bf16[544,128]{1,0:T(8,128)(2,1)S(1)} %get-tuple-element.49), channel_id=1, source_target_pairs={{0,4},{4,0},{8,12},{12,8},{1,5},{5,1},{9,13},{13,9},{2,6},{6,2},{1... | collective-permute-start | bytes 417800 | tf_op jit(solution)/shard_map/ppermute | solution.py:480
  26.8 0.0 collective-permute-done.3.rest_1_
  26.8 5.5 %back.1 = (f32[9,128,128]{2,1,0:T(8,128)S(1)}, bf16[9,32,128]{2,1,0:T(8,128)(2,1)S(1)}, bf16[9,32,128]{2,1,0:T(8,128)(2,1)S(1)}, bf16[9,32,128]{2,1,0:T(8,128)(2,1)S(1)}, bf16[9,32,128]{2,1,0:T(8,128)(2,1)S(1)}) custom-call(f32[8,1024]{1,0:T(8,128)S(1)} %get-tuple-element.36.edge_ref, f32[1,1024]{1,0:T(1,128)S(1)} %bitcast.10, f32[3,3,1024]{2,1,0:T(4,128)S(1)} %copy-done.5, ...), custom_call_target="tpu_custom_call" | custom-call | flops 8999999488 | bytes 7000000 | tf_op jit(solution)/shard_map/back/pallas_call | solution.py:332
  32.3 2.6 %collective-permute-start.8 = (bf16[9,32,128]{2,1,0:T(8,128)(2,1)S(1)}, bf16[9,32,128]{2,1,0:T(8,128)(2,1)S(1)}, u32[]{:S(2)}, u32[]{:S(2)}) collective-permute-start(bf16[9,32,128]{2,1,0:T(8,128)(2,1)S(1)} %get-tuple-element.54), channel_id=1, source_target_pairs={{4,8},{8,4},{12,0},{0,12},{5,9},{9,5},{13,1},{1,13},{6,10},{10,6},... | collective-permute-start | bytes 221192 | tf_op jit(solution)/shard_map/ppermute | solution.py:489
  34.9 0.1 collective-permute-start.9
  35.0 2.2 %collective-permute-done.6.refs_2_ = bf16[544,128]{1,0:T(8,128)(2,1)S(1)} collective-permute-done((bf16[544,128]{1,0:T(8,128)(2,1)S(1)}, bf16[544,128]{1,0:T(8,128)(2,1)S(1)}, u32[]{:S(2)}, u32[]{:S(2)}) %collective-permute-start.6) | collective-permute-done | bytes 139296 | tf_op jit(solution)/shard_map/ppermute | solution.py:480
  37.1 0.0 collective-permute-done.7.refs_3_
  37.1 0.1 total_sum.1.refs_0_
  37.2 1.4 %collective-permute-done.8.a_ref = bf16[9,32,128]{2,1,0:T(8,128)(2,1)S(1)} collective-permute-done((bf16[9,32,128]{2,1,0:T(8,128)(2,1)S(1)}, bf16[9,32,128]{2,1,0:T(8,128)(2,1)S(1)}, u32[]{:S(2)}, u32[]{:S(2)}) %collective-permute-start.8) | collective-permute-done | bytes 73760 | tf_op jit(solution)/shard_map/ppermute | solution.py:489
  38.6 0.8 %collective-permute-done.9.b_ref = bf16[9,32,128]{2,1,0:T(8,128)(2,1)S(1)} collective-permute-done((bf16[9,32,128]{2,1,0:T(8,128)(2,1)S(1)}, bf16[9,32,128]{2,1,0:T(8,128)(2,1)S(1)}, u32[]{:S(2)}, u32[]{:S(2)}) %collective-permute-start.9) | collective-permute-done | bytes 73760 | tf_op jit(solution)/shard_map/ppermute | solution.py:489
  39.4 0.4 collective-permute-done.10.c_ref
  39.8 2.0 %collective-permute-start.12 = (bf16[544,128]{1,0:T(8,128)(2,1)S(1)}, bf16[544,128]{1,0:T(8,128)(2,1)S(1)}, u32[]{:S(2)}, u32[]{:S(2)}) collective-permute-start(bf16[544,128]{1,0:T(8,128)(2,1)S(1)} %total_sum.1.refs_0_), channel_id=1, source_target_pairs={{0,2},{1,3},{2,0},{3,1},{4,6},{5,7},{6,4},{7,5},{8,10},{9,11},{10,... | collective-permute-start | bytes 417800 | tf_op jit(solution)/shard_map/ppermute | solution.py:480
  41.8 1.2 %finish.1 = bf16[9,128,128]{2,1,0:T(8,128)(2,1)} custom-call(s32[4,32]{1,0:T(4,128)S(1)} %copy-done.1, f32[9,128,128]{2,1,0:T(8,128)S(1)} %get-tuple-element.59.own_ref, bf16[9,32,128]{2,1,0:T(8,128)(2,1)S(1)} %collective-permute-done.8.a_ref, bf16[9,32,128]{2,1,0:T(8,128)(2,1)S(1)} %collective-permute-done.9.b_ref, ...), custom_call_target="tpu_custom_call" | custom-call | flops 100000000 | bytes 2000000 | tf_op jit(solution)/shard_map/finish/pallas_call | solution.py:468
  43.0 2.6 %collective-permute-done.12.refs_1_ = bf16[544,128]{1,0:T(8,128)(2,1)S(1)} collective-permute-done((bf16[544,128]{1,0:T(8,128)(2,1)S(1)}, bf16[544,128]{1,0:T(8,128)(2,1)S(1)}, u32[]{:S(2)}, u32[]{:S(2)}) %collective-permute-start.12) | collective-permute-done | bytes 139296 | tf_op jit(solution)/shard_map/ppermute | solution.py:480
  45.6 0.0 collective-permute-done.13.refs_2_
  45.6 1.4 %collective-permute-done.14.refs_3_ = bf16[544,128]{1,0:T(8,128)(2,1)S(1)} collective-permute-done((bf16[544,128]{1,0:T(8,128)(2,1)S(1)}, bf16[544,128]{1,0:T(8,128)(2,1)S(1)}, u32[]{:S(2)}, u32[]{:S(2)}) %collective-permute-start.14) | collective-permute-done | bytes 139296 | tf_op jit(solution)/shard_map/ppermute | solution.py:480
  47.0 1.7 %expert_product.1 = f32[8,69632]{1,0:T(8,128)} custom-call(f32[2,32]{1,0:T(2,128)S(1)} %copy-done, bf16[544,128]{1,0:T(8,128)(2,1)S(1)} %total_sum.1.refs_0_, bf16[544,128]{1,0:T(8,128)(2,1)S(1)} %collective-permute-done.12.refs_1_, bf16[544,128]{1,0:T(8,128)(2,1)S(1)} %collective-permute-done.13.refs_2_, bf16[544,128]{1,0:T(8,128)(2,1)S(1)} %collective-permute-done.14.refs_3_), custom_call_target="tpu_custom_call" | custom-call | flops 1000000 | bytes 4000000 | tf_op jit(solution)/shard_map/expert_product/pallas_call | solution.py:437
  (24 shorter events, 0.1 us)
Async XLA Ops:
  0.6 0.7 %copy-start = (f32[2,32]{1,0:T(2,128)S(1)}, f32[2,32]{1,0:T(2,128)}, u32[]{:S(2)}) copy-start(f32[2,32]{1,0:T(2,128)} %coef_ref.1) | copy-start | bytes 772
  1.3 8.5 %copy-start.2 = (bf16[256,9,128]{2,0,1:T(8,128)(2,1)S(1)}, bf16[256,9,128]{2,0,1:T(8,128)(2,1)}, u32[]{:S(2)}) copy-start(bf16[256,9,128]{2,0,1:T(8,128)(2,1)} %param.11) | copy-start | bytes 1769476
  1.3 8.5 %copy-start.3 = (bf16[128,9,128]{2,0,1:T(8,128)(2,1)S(1)}, bf16[128,9,128]{2,0,1:T(8,128)(2,1)}, u32[]{:S(2)}) copy-start(bf16[128,9,128]{2,0,1:T(8,128)(2,1)} %param.12) | copy-start | bytes 884740
  1.3 8.5 %copy-start.4 = (f32[5,5,1024]{2,1,0:T(8,128)S(1)}, f32[5,5,1024]{2,1,0:T(8,128)}, u32[]{:S(2)}) copy-start(f32[5,5,1024]{2,1,0:T(8,128)} %two_ref.3) | copy-start | bytes 307204
  1.3 8.5 %copy-start.5 = (f32[3,3,1024]{2,1,0:T(4,128)S(1)}, f32[3,3,1024]{2,1,0:T(4,128)}, u32[]{:S(2)}) copy-start(f32[3,3,1024]{2,1,0:T(4,128)} %one_ref.3) | copy-start | bytes 110596
  1.3 8.5 %copy-start.6 = (s32[128,8]{0,1:T(8,128)S(1)}, s32[128,8]{0,1:T(8,128)}, u32[]{:S(2)}) copy-start(s32[128,8]{0,1:T(8,128)} %param.13) | copy-start | bytes 12292
  1.3 8.5 %copy-start.7 = (f32[1024]{0:T(1024)S(1)}, f32[1024]{0:T(1024)}, u32[]{:S(2)}) copy-start(f32[1024]{0:T(1024)} %param.14) | copy-start | bytes 12292
  1.3 8.5 %copy-start.8 = (s32[128]{0:T(128)S(1)}, s32[128]{0:T(128)}, u32[]{:S(2)}) copy-start(s32[128]{0:T(128)} %param.18) | copy-start | bytes 1540
  3.4 13.7 %collective-permute-start.2 = (bf16[2,272,128]{2,1,0:T(8,128)(2,1)S(1)}, bf16[2,272,128]{2,1,0:T(8,128)(2,1)S(1)}, u32[]{:S(2)}, u32[]{:S(2)}) collective-permute-start(bf16[2,272,128]{2,1,0:T(8,128)(2,1)S(1)} %merge.1.refs_0_), channel_id=1, source_target_pairs={{0,12},{4,8},{8,4},{12,0},{1,13},{5,9},{9,5},{13,1},{2,14},{6,10},... | collective-permute-start | bytes 417800 | tf_op jit(solution)/shard_map/ppermute | solution.py:480
  8.5 11.8 %collective-permute-start.1 = (bf16[2,272,128]{2,1,0:T(8,128)(2,1)S(1)}, bf16[2,272,128]{2,1,0:T(8,128)(2,1)S(1)}, u32[]{:S(2)}, u32[]{:S(2)}) collective-permute-start(bf16[2,272,128]{2,1,0:T(8,128)(2,1)S(1)} %merge.1.refs_0_), channel_id=1, source_target_pairs={{0,8},{4,12},{8,0},{12,4},{1,9},{5,13},{9,1},{13,5},{2,10},{6,14},... | collective-permute-start | bytes 417800 | tf_op jit(solution)/shard_map/ppermute | solution.py:480
  8.5 11.8 %collective-permute-start = (bf16[2,272,128]{2,1,0:T(8,128)(2,1)S(1)}, bf16[2,272,128]{2,1,0:T(8,128)(2,1)S(1)}, u32[]{:S(2)}, u32[]{:S(2)}) collective-permute-start(bf16[2,272,128]{2,1,0:T(8,128)(2,1)S(1)} %merge.1.refs_0_), channel_id=1, source_target_pairs={{0,4},{4,0},{8,12},{12,8},{1,5},{5,1},{9,13},{13,9},{2,6},{6,2},{1... | collective-permute-start | bytes 417800 | tf_op jit(solution)/shard_map/ppermute | solution.py:480
  20.3 2.0 %collective-permute-start.4 = (bf16[2176,128]{1,0:T(8,128)(2,1)S(1)}, bf16[2176,128]{1,0:T(8,128)(2,1)S(1)}, u32[]{:S(2)}, u32[]{:S(2)}) collective-permute-start(bf16[2176,128]{1,0:T(8,128)(2,1)S(1)} %get-tuple-element.45), channel_id=1, source_target_pairs={{0,1},{1,0},{2,3},{3,2},{4,5},{5,4},{6,7},{7,6},{8,9},{9,8},{10,11... | collective-permute-start | bytes 1671176 | tf_op jit(solution)/shard_map/ppermute | solution.py:480
  20.3 6.5 %collective-permute-start.3 = (bf16[4,2,272,128]{3,2,1,0:T(8,128)(2,1)S(1)}, bf16[4,2,272,128]{3,2,1,0:T(8,128)(2,1)S(1)}, u32[]{:S(2)}, u32[]{:S(2)}) collective-permute-start(bf16[4,2,272,128]{3,2,1,0:T(8,128)(2,1)S(1)} %pack.1.rest_0_), channel_id=1, source_target_pairs={{0,1},{1,0},{2,3},{3,2},{4,5},{5,4},{6,7},{7,6},{8,9},{9,8},{10,11... | collective-permute-start | bytes 1671176 | tf_op jit(solution)/shard_map/ppermute | solution.py:480
  22.4 12.6 %collective-permute-start.5 = (bf16[544,128]{1,0:T(8,128)(2,1)S(1)}, bf16[544,128]{1,0:T(8,128)(2,1)S(1)}, u32[]{:S(2)}, u32[]{:S(2)}) collective-permute-start(bf16[544,128]{1,0:T(8,128)(2,1)S(1)} %get-tuple-element.47), channel_id=1, source_target_pairs={{0,12},{4,8},{8,4},{12,0},{1,13},{5,9},{9,5},{13,1},{2,14},{6,10},... | collective-permute-start | bytes 417800 | tf_op jit(solution)/shard_map/ppermute | solution.py:480
  24.9 12.2 %collective-permute-start.6 = (bf16[544,128]{1,0:T(8,128)(2,1)S(1)}, bf16[544,128]{1,0:T(8,128)(2,1)S(1)}, u32[]{:S(2)}, u32[]{:S(2)}) collective-permute-start(bf16[544,128]{1,0:T(8,128)(2,1)S(1)} %get-tuple-element.48), channel_id=1, source_target_pairs={{0,8},{4,12},{8,0},{12,4},{1,9},{5,13},{9,1},{13,5},{2,10},{6,14},... | collective-permute-start | bytes 417800 | tf_op jit(solution)/shard_map/ppermute | solution.py:480
  24.9 12.2 %collective-permute-start.7 = (bf16[544,128]{1,0:T(8,128)(2,1)S(1)}, bf16[544,128]{1,0:T(8,128)(2,1)S(1)}, u32[]{:S(2)}, u32[]{:S(2)}) collective-permute-start(bf16[544,128]{1,0:T(8,128)(2,1)S(1)} %get-tuple-element.49), channel_id=1, source_target_pairs={{0,4},{4,0},{8,12},{12,8},{1,5},{5,1},{9,13},{13,9},{2,6},{6,2},{1... | collective-permute-start | bytes 417800 | tf_op jit(solution)/shard_map/ppermute | solution.py:480
  26.8 15.0 %copy-start.1 = (s32[4,32]{1,0:T(4,128)S(1)}, s32[4,32]{1,0:T(4,128)}, u32[]{:S(2)}) copy-start(s32[4,32]{1,0:T(4,128)} %send_ref.1) | copy-start | bytes 1540
  32.3 6.3 %collective-permute-start.8 = (bf16[9,32,128]{2,1,0:T(8,128)(2,1)S(1)}, bf16[9,32,128]{2,1,0:T(8,128)(2,1)S(1)}, u32[]{:S(2)}, u32[]{:S(2)}) collective-permute-start(bf16[9,32,128]{2,1,0:T(8,128)(2,1)S(1)} %get-tuple-element.54), channel_id=1, source_target_pairs={{4,8},{8,4},{12,0},{0,12},{5,9},{9,5},{13,1},{1,13},{6,10},{10,6},... | collective-permute-start | bytes 221192 | tf_op jit(solution)/shard_map/ppermute | solution.py:489
  34.9 4.5 %collective-permute-start.9 = (bf16[9,32,128]{2,1,0:T(8,128)(2,1)S(1)}, bf16[9,32,128]{2,1,0:T(8,128)(2,1)S(1)}, u32[]{:S(2)}, u32[]{:S(2)}) collective-permute-start(bf16[9,32,128]{2,1,0:T(8,128)(2,1)S(1)} %get-tuple-element.55), channel_id=1, source_target_pairs={{1,2},{2,1},{3,0},{0,3},{5,6},{6,5},{7,4},{4,7},{9,10},{10,9},{11,... | collective-permute-start | bytes 221192 | tf_op jit(solution)/shard_map/ppermute | solution.py:489
  35.0 4.8 %collective-permute-start.10 = (bf16[9,32,128]{2,1,0:T(8,128)(2,1)S(1)}, bf16[9,32,128]{2,1,0:T(8,128)(2,1)S(1)}, u32[]{:S(2)}, u32[]{:S(2)}) collective-permute-start(bf16[9,32,128]{2,1,0:T(8,128)(2,1)S(1)} %get-tuple-element.56), channel_id=1, source_target_pairs={{0,4},{4,0},{8,12},{12,8},{1,5},{5,1},{9,13},{13,9},{2,6},{6,2},{1... | collective-permute-start | bytes 221192 | tf_op jit(solution)/shard_map/ppermute | solution.py:489
  37.1 2.7 %collective-permute-start.11 = (bf16[9,32,128]{2,1,0:T(8,128)(2,1)S(1)}, bf16[9,32,128]{2,1,0:T(8,128)(2,1)S(1)}, u32[]{:S(2)}, u32[]{:S(2)}) collective-permute-start(bf16[9,32,128]{2,1,0:T(8,128)(2,1)S(1)} %get-tuple-element.57), channel_id=1, source_target_pairs={{0,1},{1,0},{2,3},{3,2},{4,5},{5,4},{6,7},{7,6},{8,9},{9,8},{10,11... | collective-permute-start | bytes 221192 | tf_op jit(solution)/shard_map/ppermute | solution.py:489
  39.8 5.8 %collective-permute-start.12 = (bf16[544,128]{1,0:T(8,128)(2,1)S(1)}, bf16[544,128]{1,0:T(8,128)(2,1)S(1)}, u32[]{:S(2)}, u32[]{:S(2)}) collective-permute-start(bf16[544,128]{1,0:T(8,128)(2,1)S(1)} %total_sum.1.refs_0_), channel_id=1, source_target_pairs={{0,2},{1,3},{2,0},{3,1},{4,6},{5,7},{6,4},{7,5},{8,10},{9,11},{10,... | collective-permute-start | bytes 417800 | tf_op jit(solution)/shard_map/ppermute | solution.py:480
  41.8 3.8 %collective-permute-start.13 = (bf16[544,128]{1,0:T(8,128)(2,1)S(1)}, bf16[544,128]{1,0:T(8,128)(2,1)S(1)}, u32[]{:S(2)}, u32[]{:S(2)}) collective-permute-start(bf16[544,128]{1,0:T(8,128)(2,1)S(1)} %total_sum.1.refs_0_), channel_id=1, source_target_pairs={{0,1},{1,0},{2,3},{3,2},{4,5},{5,4},{6,7},{7,6},{8,9},{9,8},{10,11... | collective-permute-start | bytes 417800 | tf_op jit(solution)/shard_map/ppermute | solution.py:480
  45.6 1.4 %collective-permute-start.14 = (bf16[544,128]{1,0:T(8,128)(2,1)S(1)}, bf16[544,128]{1,0:T(8,128)(2,1)S(1)}, u32[]{:S(2)}, u32[]{:S(2)}) collective-permute-start(bf16[544,128]{1,0:T(8,128)(2,1)S(1)} %collective-permute-done.12.refs_1_), channel_id=1, source_target_pairs={{0,1},{1,0},{2,3},{3,2},{4,5},{5,4},{6,7},{7,6},{8,9},{9,8},{10,11... | collective-permute-start | bytes 417800 | tf_op jit(solution)/shard_map/ppermute | solution.py:480

commit v6 on v5

--- a/solution.py
+++ b/solution.py
@@ -119,8 +119,8 @@
 
 def features_kernel(
     live_ref, near_ref, class_ref, zero_ref, one_ref, two_ref, source_ref, target_ref,
-    other_ref, own_ref, pulled_ref, edge_ref,
-    source_t, target_t, moved, spread, rotated, grads,
+    rotated, pulled_ref, edge_ref,
+    source_t, target_t, moved, spread,
     *, fanout,
 ):
     slots, channels = source_ref.shape[1:]
@@ -187,6 +187,10 @@
         return carry
 
     lax.fori_loop(0, edges // CHUNK, chunk_step, 0)
+
+
+def class_grad_kernel(rotated, pulled_ref, edge_ref, other_ref, own_ref, grads):
+    channels = rotated.shape[0] // 7
     zw, pw = 3 * channels, 2 * channels
     first = zw * zw // 128
     second = first + pw * pw // 128
@@ -208,7 +212,7 @@
         out_ref[...] = grads[...].astype(BF16)
 
 
-def features(live, near, classes, zero, one, two, source, target, rows, fanout):
+def features(live, near, classes, zero, one, two, source, target, fanout):
     slots, channels = source.shape[1:]
     atoms = target.shape[1]
     edges = atoms * fanout
@@ -216,10 +220,9 @@
     return pl.pallas_call(
         functools.partial(features_kernel, fanout=fanout),
         in_specs=[SMEM] + [VMEM] * 7,
-        out_specs=[VMEM] * 4,
+        out_specs=[VMEM] * 3,
         out_shape=[
-            shape((rows, 128), BF16),
-            shape((rows, 128), BF16),
+            shape((7 * channels, edges), BF16),
             shape((7 * channels, edges), BF16),
             shape((8, edges), F32),
         ],
@@ -228,13 +231,25 @@
             pltpu.VMEM((9 * channels, atoms), BF16),
             pltpu.VMEM((9 * channels, CHUNK), F32),
             pltpu.VMEM((9 * channels, CHUNK), F32),
-            pltpu.VMEM((7 * channels, edges), BF16),
-            pltpu.VMEM((rows, 128), F32),
         ],
-        compiler_params=limits(24),
-        cost_estimate=cost(9 * 10**9, 7 * 10**6),
+        compiler_params=limits(16),
+        cost_estimate=cost(6 * 10**9, 7 * 10**6),
         name="features",
     )(live, near, classes, zero, one, two, source, target)
+
+
+def class_grads(rotated, pulled, edge, rows):
+    shape = jax.ShapeDtypeStruct((rows, 128), BF16)
+    return pl.pallas_call(
+        class_grad_kernel,
+        in_specs=[VMEM] * 3,
+        out_specs=[VMEM] * 2,
+        out_shape=[shape, shape],
+        scratch_shapes=[pltpu.VMEM((rows, 128), F32)],
+        compiler_params=limits(16),
+        cost_estimate=cost(4 * 10**9, 6 * 10**6),
+        name="class_grads",
+    )(rotated, pulled, edge)
 
 
 def back_kernel(
@@ -350,25 +365,50 @@
     )(edge, zero, one, two, pulled, *pieces)
 
 
-def pair_kernel(own_ref, came_ref, *out_refs):
-    height = out_refs[0].shape[0]
+def core_kernel(own_ref, came_ref, keep_ref, far_ref, send_ref):
+    height = keep_ref.shape[0]
     row = lax.axis_index("yz")
-    for index, out_ref in enumerate(out_refs):
-        at = pl.ds(pl.multiple_of((row ^ index) * height, 16), height)
-        out_ref[...] = (own_ref[at, :].astype(F32) + came_ref[at, :].astype(F32)).astype(BF16)
-
-
-def pair_sum(own, came, count):
-    height = own.shape[0] // count
-    return pl.pallas_call(
-        pair_kernel,
+    for k in range(4):
+        at = pl.ds(pl.multiple_of((row ^ k) * height, 16), height)
+        total = own_ref[at, :].astype(F32) + came_ref[at, :].astype(F32)
+        if k == 0:
+            keep_ref[...] = total
+        elif k == 2:
+            far_ref[...] = total
+        else:
+            send_ref[k // 2] = total.astype(BF16)
+
+
+def core_sum(own, came):
+    height = own.shape[0] // 4
+    shape = jax.ShapeDtypeStruct
+    return pl.pallas_call(
+        core_kernel,
         in_specs=[VMEM, VMEM],
-        out_specs=[VMEM] * count,
-        out_shape=[jax.ShapeDtypeStruct((height, 128), BF16)] * count,
+        out_specs=[VMEM] * 3,
+        out_shape=[shape((height, 128), F32), shape((height, 128), F32), shape((2, height, 128), BF16)],
         compiler_params=limits(6),
         cost_estimate=cost(10**6, 2 * 10**6),
-        name="pair_sum",
+        name="core_sum",
     )(own, came)
+
+
+def near_kernel(keep_ref, far_ref, came_ref, mine_ref, send_ref):
+    mine_ref[...] = keep_ref[...] + came_ref[0].astype(F32)
+    send_ref[...] = (far_ref[...] + came_ref[1].astype(F32)).astype(BF16)
+
+
+def near_sum(keep, far, came):
+    shape = jax.ShapeDtypeStruct
+    return pl.pallas_call(
+        near_kernel,
+        in_specs=[VMEM] * 3,
+        out_specs=[VMEM] * 2,
+        out_shape=[shape(keep.shape, F32), shape(keep.shape, BF16)],
+        compiler_params=limits(6),
+        cost_estimate=cost(10**6, 10**6),
+        name="near_sum",
+    )(keep, far, came)
 
 
 def total_kernel(*refs):
@@ -502,7 +542,7 @@
     core = column % 2
     height = experts.shape[1] // 128
     rows = height * count_yz
-    direct = height % 32 == 0 and count_yz & (count_yz - 1) == 0 and count_gx == 4
+    direct = height % 32 == 0 and count_yz == 4 and count_gx == 4
 
     zero = rot_zero.reshape(1, -1)
     source = jnp.transpose(saved_input, (1, 0, 2))
@@ -511,12 +551,13 @@
     if direct:
         half = height // 2
         mine = merge(merge_coef, experts, 2)
-        held = [mine] + [swap(mine, "yz", k) for k in range(1, count_yz)]
+        far = swap(mine, "yz", 2)
+        near = swap(mine, "yz", 1)
         source, target, mine = lax.optimization_barrier((source, target, mine))
 
         def places():
             here, side = lax.axis_index("yz"), lax.rem(lax.axis_index("gx"), 2)
-            starts = [(here ^ k) * height for k in range(count_yz)]
+            starts = [(here ^ k) * height for k in range(4)]
             return [at + side * half for at in starts] + [at + (1 - side) * half for at in starts]
     else:
         part = jnp.dot(merge_coef, experts.astype(F32), precision=lax.Precision.HIGHEST).astype(BF16)
@@ -526,23 +567,29 @@
         def places():
             return [0]
 
-    other, own, pulled, edge = features(
-        live_blocks, neighbours.T, atom_class.reshape(1, -1), zero, rot_one, rot_two, source, target, rows, fanout
+    rotated, pulled, edge = features(
+        live_blocks, neighbours.T, atom_class.reshape(1, -1), zero, rot_one, rot_two, source, target, fanout
     )
     if direct:
-        other, *held = lax.optimization_barrier((other, *held))
+        rotated, far, near = lax.optimization_barrier((rotated, far, near))
+        passed = swap(far, "yz", 1)
+    other, own = class_grads(rotated, pulled, edge, rows)
+    if direct:
+        other, passed = lax.optimization_barrier((other, passed))
         came = swap(other, "gx", 1)
-        parts = pair_sum(own, came, count_yz)
-        gathered = [parts[0]] + [swap(parts[k], "yz", k) for k in reversed(range(1, count_yz))]
-        held = pack(held)
+        held = pack([mine, near, far, passed])
         pieces = [held, swap(held, "gx", 1)]
+        keep, beyond, away = core_sum(own, came)
+        arrived = swap(away, "yz", 1)
     grad_own, *ghosts = back(edge, zero, rot_one, rot_two, pulled, pieces, places, rows, atoms, slots, face)
     returned = [
         neighbour_pairs(ghost, axis, first)
         for ghost, axis, first in zip(ghosts, ("yz", "gx", "yz", "gx"), (1, 1, 0, 0))
     ]
     if direct:
-        grad_own, *gathered = lax.optimization_barrier((grad_own, *gathered))
+        grad_own, keep, beyond, arrived = lax.optimization_barrier((grad_own, keep, beyond, arrived))
+        partial, away = near_sum(keep, beyond, arrived)
+        gathered = [partial, swap(away, "yz", 2)]
         summed, *returned = lax.optimization_barrier((total_sum(gathered), *returned))
         across = swap(summed, "gx", 2)
         input_grad = finish(send_index, grad_own, returned)

time: 48.9 us -> 51.2 us (1.047)
  waiting for transfers between devices: 13.3 us -> 15.4 us
    ppermute x11 -> x10, waiting for transfers between devices: 10.7 us -> 15.3 us  [swap(): lax.ppermute(value, axis, [(i, i ^ bit) for i in range(lax.axis_size(axis...]
    ppermute x4, waiting for transfers between devices: 2.61 us -> 0.12 us  [neighbour_pairs(): return lax.ppermute(value, axis, moves)]
    pallas_call x1 -> x3, Pallas kernels: 0.13 us -> 2.43 us  [the longest x1 2.26 us: class_grads(): pl.pallas_call(class_grad_kernel, in_specs=[VMEM] * 3, out_specs=[VMEM] *...]
    pallas_call x1, Pallas kernels: 7.18 us -> 4.92 us  [features(): pl.pallas_call(functools.partial(features_kernel, fanout=fanout), in_spec...]
    ppermute x11 -> x10, starting transfers between devices: 12.8 us -> 12.5 us  [swap(): lax.ppermute(value, axis, [(i, i ^ bit) for i in range(lax.axis_size(axis...]
  transfers between devices with their start and end apart: 15 -> 14, of which waited for: 8 -> 7; matrix products, arithmetic and copies ran while one was open for 0% -> 0% of each run, Pallas kernels for 29% -> 27%
where the time goes in v6:
time: 51.2 us; the launch traced here: 51 us
  Pallas kernels  17.8 us (35%)
  starting transfers between devices  15.6 us (30%)
  waiting for transfers between devices  15.4 us (30%)
  between operations  1.47 us (3%)
  local copies, waits for them, and re-layouts  0.71 us (1%)
    ppermute x10, waiting for transfers between devices, swap(): lax.ppermute(value, axis, [(i, i ^ bit) for i in range(lax.axis_size(axis...  15.3 us
    ppermute x10, starting transfers between devices, swap(): lax.ppermute(value, axis, [(i, i ^ bit) for i in range(lax.axis_size(axis...  12.5 us
    pallas_call x1, Pallas kernels, back(): pl.pallas_call(functools.partial(back_kernel, pieces=len(pieces), members...  5.48 us
    pallas_call x1, Pallas kernels, features(): pl.pallas_call(functools.partial(features_kernel, fanout=fanout), in_spec...  4.92 us
    ppermute x4, starting transfers between devices, neighbour_pairs(): return lax.ppermute(value, axis, moves)  3.07 us
    pallas_call x1, Pallas kernels, class_grads(): pl.pallas_call(class_grad_kernel, in_specs=[VMEM] * 3, out_specs=[VMEM] *...  2.26 us
    pallas_call x1, Pallas kernels, merge(): pl.pallas_call(merge_kernel, in_specs=[HBM, HBM], out_specs=VMEM, out_sha...  2.03 us
    pallas_call x1, Pallas kernels, expert_product(): pl.pallas_call(functools.partial(expert_kernel, scale=scale), in_specs=[V...  1.72 us
  transfers between devices with their start and end apart: 14, of which 7 were waited for; matrix products, arithmetic and copies ran while one was open for 0% of the time, Pallas kernels for 27%

profile of v6, /device:TPU:0, one launch (start us, length us, event | category | flops | bytes accessed | tf_op | source)
XLA Modules:
  0.0 51.0 jit_solution(5013096322588764152)
XLA Ops:
  0.6 0.7 %copy-done = f32[2,32]{1,0:T(2,128)S(1)} copy-done((f32[2,32]{1,0:T(2,128)S(1)}, f32[2,32]{1,0:T(2,128)}, u32[]{:S(2)}) %copy-start) | copy-done | bytes 280
  1.4 2.0 %merge.1.refs_0_ = bf16[2,272,128]{2,1,0:T(8,128)(2,1)S(1)} custom-call(f32[2,32]{1,0:T(2,128)S(1)} %copy-done, bf16[32,69632]{1,0:T(8,128)(2,1)} %experts_ref.1), custom_call_target="tpu_custom_call" | custom-call | flops 53477376 | bytes 2228224 | tf_op jit(solution)/shard_map/merge/pallas_call | solution.py:103
  3.4 4.1 %collective-permute-start = (bf16[2,272,128]{2,1,0:T(8,128)(2,1)S(1)}, bf16[2,272,128]{2,1,0:T(8,128)(2,1)S(1)}, u32[]{:S(2)}, u32[]{:S(2)}) collective-permute-start(bf16[2,272,128]{2,1,0:T(8,128)(2,1)S(1)} %merge.1.refs_0_), channel_id=1, source_target_pairs={{0,8},{4,12},{8,0},{12,4},{1,9},{5,13},{9,1},{13,5},{2,10},{6,14},... | collective-permute-start | bytes 417800 | tf_op jit(solution)/shard_map/ppermute | solution.py:520
  7.5 1.6 %collective-permute-start.1 = (bf16[2,272,128]{2,1,0:T(8,128)(2,1)S(1)}, bf16[2,272,128]{2,1,0:T(8,128)(2,1)S(1)}, u32[]{:S(2)}, u32[]{:S(2)}) collective-permute-start(bf16[2,272,128]{2,1,0:T(8,128)(2,1)S(1)} %merge.1.refs_0_), channel_id=1, source_target_pairs={{0,4},{4,0},{8,12},{12,8},{1,5},{5,1},{9,13},{13,9},{2,6},{6,2},{1... | collective-permute-start | bytes 417800 | tf_op jit(solution)/shard_map/ppermute | solution.py:520
  9.8 4.9 %features.1 = (bf16[896,1024]{1,0:T(8,128)(2,1)S(1)}, bf16[896,1024]{1,0:T(8,128)(2,1)S(1)}, f32[8,1024]{1,0:T(8,128)S(1)}) custom-call(s32[1]{0:T(128)S(6)} %copy.13.live_ref, s32[8,128]{1,0:T(8,128)S(1)} %bitcast.8, s32[1,128]{1,0:T(1,128)S(1)} %bitcast.11, f32[1,1024]{1,0:T(1,128)S(1)} %bitcast.9, f32[3,3,1024]{2,1,0:T(4,128)S(1)} %copy-done.5, ...), custom_call_target="tpu_custom_call" | custom-call | flops 6000000000 | bytes 7000000 | tf_op jit(solution)/shard_map/features/pallas_call | solution.py:220
  14.7 0.0 collective-permute-done.1.refs_1_
  14.7 1.2 %collective-permute-start.2 = (bf16[2,272,128]{2,1,0:T(8,128)(2,1)S(1)}, bf16[2,272,128]{2,1,0:T(8,128)(2,1)S(1)}, u32[]{:S(2)}, u32[]{:S(2)}) collective-permute-start(bf16[2,272,128]{2,1,0:T(8,128)(2,1)S(1)} %collective-permute-done.refs_2_), channel_id=1, source_target_pairs={{0,4},{4,0},{8,12},{12,8},{1,5},{5,1},{9,13},{13,9},{2,6},{6,2},{1... | collective-permute-start | bytes 417800 | tf_op jit(solution)/shard_map/ppermute | solution.py:520
  15.9 2.3 %class_grads.1 = (bf16[2176,128]{1,0:T(8,128)(2,1)S(1)}, bf16[2176,128]{1,0:T(8,128)(2,1)S(1)}) custom-call(bf16[896,1024]{1,0:T(8,128)(2,1)S(1)} %get-tuple-element.44.rotated, bf16[896,1024]{1,0:T(8,128)(2,1)S(1)} %get-tuple-element.39.pulled_ref, f32[8,1024]{1,0:T(8,128)S(1)} %get-tuple-element.38.edge_ref), custom_call_target="tpu_custom_call" | custom-call | flops 4000000000 | bytes 6000000 | tf_op jit(solution)/shard_map/class_grads/pallas_call | solution.py:243
  18.2 1.7 %collective-permute-done.2.refs_3_ = bf16[2,272,128]{2,1,0:T(8,128)(2,1)S(1)} collective-permute-done((bf16[2,272,128]{2,1,0:T(8,128)(2,1)S(1)}, bf16[2,272,128]{2,1,0:T(8,128)(2,1)S(1)}, u32[]{:S(2)}, u32[]{:S(2)}) %collective-permute-start.2) | collective-permute-done | bytes 139296 | tf_op jit(solution)/shard_map/ppermute | solution.py:520
  19.9 0.0 collective-permute-start.4
  19.9 0.6 %collective-permute-start.3 = (bf16[4,2,272,128]{3,2,1,0:T(8,128)(2,1)S(1)}, bf16[4,2,272,128]{3,2,1,0:T(8,128)(2,1)S(1)}, u32[]{:S(2)}, u32[]{:S(2)}) collective-permute-start(bf16[4,2,272,128]{3,2,1,0:T(8,128)(2,1)S(1)} %pack.1.rest_0_), channel_id=1, source_target_pairs={{0,1},{1,0},{2,3},{3,2},{4,5},{5,4},{6,7},{7,6},{8,9},{9,8},{10,11... | collective-permute-start | bytes 1671176 | tf_op jit(solution)/shard_map/ppermute | solution.py:520
  20.5 1.3 %collective-permute-done.4.came_ref = bf16[2176,128]{1,0:T(8,128)(2,1)S(1)} collective-permute-done((bf16[2176,128]{1,0:T(8,128)(2,1)S(1)}, bf16[2176,128]{1,0:T(8,128)(2,1)S(1)}, u32[]{:S(2)}, u32[]{:S(2)}) %collective-permute-start.4) | collective-permute-done | bytes 557088 | tf_op jit(solution)/shard_map/ppermute | solution.py:520
  21.8 0.1 core_sum.1
  21.9 0.0 copy-start.1
  21.9 1.2 %collective-permute-start.5 = (bf16[2,544,128]{2,1,0:T(8,128)(2,1)S(1)}, bf16[2,544,128]{2,1,0:T(8,128)(2,1)S(1)}, u32[]{:S(2)}, u32[]{:S(2)}) collective-permute-start(bf16[2,544,128]{2,1,0:T(8,128)(2,1)S(1)} %get-tuple-element.52), channel_id=1, source_target_pairs={{0,4},{4,0},{8,12},{12,8},{1,5},{5,1},{9,13},{13,9},{2,6},{6,2},{1... | collective-permute-start | bytes 835592 | tf_op jit(solution)/shard_map/ppermute | solution.py:520
  23.1 0.0 collective-permute-done.3.rest_1_
  23.1 5.5 %back.1 = (f32[9,128,128]{2,1,0:T(8,128)S(1)}, bf16[9,32,128]{2,1,0:T(8,128)(2,1)S(1)}, bf16[9,32,128]{2,1,0:T(8,128)(2,1)S(1)}, bf16[9,32,128]{2,1,0:T(8,128)(2,1)S(1)}, bf16[9,32,128]{2,1,0:T(8,128)(2,1)S(1)}) custom-call(f32[8,1024]{1,0:T(8,128)S(1)} %get-tuple-element.38.edge_ref, f32[1,1024]{1,0:T(1,128)S(1)} %bitcast.10, f32[3,3,1024]{2,1,0:T(4,128)S(1)} %copy-done.5, ...), custom_call_target="tpu_custom_call" | custom-call | flops 8999999488 | bytes 7000000 | tf_op jit(solution)/shard_map/back/pallas_call | solution.py:347
  28.6 2.1 %collective-permute-done.5.came_ref = bf16[2,544,128]{2,1,0:T(8,128)(2,1)S(1)} collective-permute-done((bf16[2,544,128]{2,1,0:T(8,128)(2,1)S(1)}, bf16[2,544,128]{2,1,0:T(8,128)(2,1)S(1)}, u32[]{:S(2)}, u32[]{:S(2)}) %collective-permute-start.5) | collective-permute-done | bytes 278560 | tf_op jit(solution)/shard_map/ppermute | solution.py:520
  30.8 2.3 %collective-permute-start.6 = (bf16[544,128]{1,0:T(8,128)(2,1)S(1)}, bf16[544,128]{1,0:T(8,128)(2,1)S(1)}, u32[]{:S(2)}, u32[]{:S(2)}) collective-permute-start(bf16[544,128]{1,0:T(8,128)(2,1)S(1)} %get-tuple-element.57), channel_id=1, source_target_pairs={{0,8},{4,12},{8,0},{12,4},{1,9},{5,13},{9,1},{13,5},{2,10},{6,14},... | collective-permute-start | bytes 417800 | tf_op jit(solution)/shard_map/ppermute | solution.py:520
  33.1 1.3 %collective-permute-start.7 = (bf16[9,32,128]{2,1,0:T(8,128)(2,1)S(1)}, bf16[9,32,128]{2,1,0:T(8,128)(2,1)S(1)}, u32[]{:S(2)}, u32[]{:S(2)}) collective-permute-start(bf16[9,32,128]{2,1,0:T(8,128)(2,1)S(1)} %get-tuple-element.58), channel_id=1, source_target_pairs={{4,8},{8,4},{12,0},{0,12},{5,9},{9,5},{13,1},{1,13},{6,10},{10,6},... | collective-permute-start | bytes 221192 | tf_op jit(solution)/shard_map/ppermute | solution.py:529
  34.3 0.1 collective-permute-start.8
  34.5 0.5 collective-permute-start.9
  35.0 1.2 %collective-permute-start.10 = (bf16[9,32,128]{2,1,0:T(8,128)(2,1)S(1)}, bf16[9,32,128]{2,1,0:T(8,128)(2,1)S(1)}, u32[]{:S(2)}, u32[]{:S(2)}) collective-permute-start(bf16[9,32,128]{2,1,0:T(8,128)(2,1)S(1)} %get-tuple-element.61), channel_id=1, source_target_pairs={{0,1},{1,0},{2,3},{3,2},{4,5},{5,4},{6,7},{7,6},{8,9},{9,8},{10,11... | collective-permute-start | bytes 221192 | tf_op jit(solution)/shard_map/ppermute | solution.py:529
  36.2 5.9 %collective-permute-done.6.refs_1_ = bf16[544,128]{1,0:T(8,128)(2,1)S(1)} collective-permute-done((bf16[544,128]{1,0:T(8,128)(2,1)S(1)}, bf16[544,128]{1,0:T(8,128)(2,1)S(1)}, u32[]{:S(2)}, u32[]{:S(2)}) %collective-permute-start.6) | collective-permute-done | bytes 139296 | tf_op jit(solution)/shard_map/ppermute | solution.py:520
  42.1 0.0 collective-permute-done.8.b_ref
  42.1 0.1 collective-permute-done.9.c_ref
  42.2 0.0 collective-permute-done.10.d_ref
  42.2 1.6 %collective-permute-start.11 = (bf16[544,128]{1,0:T(8,128)(2,1)S(1)}, bf16[544,128]{1,0:T(8,128)(2,1)S(1)}, u32[]{:S(2)}, u32[]{:S(2)}) collective-permute-start(bf16[544,128]{1,0:T(8,128)(2,1)S(1)} %total_sum.1.refs_0_), channel_id=1, source_target_pairs={{0,2},{1,3},{2,0},{3,1},{4,6},{5,7},{6,4},{7,5},{8,10},{9,11},{10,... | collective-permute-start | bytes 417800 | tf_op jit(solution)/shard_map/ppermute | solution.py:520
  43.8 1.2 %finish.1 = bf16[9,128,128]{2,1,0:T(8,128)(2,1)} custom-call(s32[4,32]{1,0:T(4,128)S(1)} %copy-done.1, f32[9,128,128]{2,1,0:T(8,128)S(1)} %get-tuple-element.63.own_ref, bf16[9,32,128]{2,1,0:T(8,128)(2,1)S(1)} %collective-permute-done.7.a_ref, bf16[9,32,128]{2,1,0:T(8,128)(2,1)S(1)} %collective-permute-done.8.b_ref, ...), custom_call_target="tpu_custom_call" | custom-call | flops 100000000 | bytes 2000000 | tf_op jit(solution)/shard_map/finish/pallas_call | solution.py:508
  45.0 3.0 %collective-permute-done.11.refs_1_ = bf16[544,128]{1,0:T(8,128)(2,1)S(1)} collective-permute-done((bf16[544,128]{1,0:T(8,128)(2,1)S(1)}, bf16[544,128]{1,0:T(8,128)(2,1)S(1)}, u32[]{:S(2)}, u32[]{:S(2)}) %collective-permute-start.11) | collective-permute-done | bytes 139296 | tf_op jit(solution)/shard_map/ppermute | solution.py:520
  47.9 1.4 %collective-permute-done.13.refs_3_ = bf16[544,128]{1,0:T(8,128)(2,1)S(1)} collective-permute-done((bf16[544,128]{1,0:T(8,128)(2,1)S(1)}, bf16[544,128]{1,0:T(8,128)(2,1)S(1)}, u32[]{:S(2)}, u32[]{:S(2)}) %collective-permute-start.13) | collective-permute-done | bytes 139296 | tf_op jit(solution)/shard_map/ppermute | solution.py:520
  49.3 1.7 %expert_product.1 = f32[8,69632]{1,0:T(8,128)} custom-call(f32[2,32]{1,0:T(2,128)S(1)} %copy-done, bf16[544,128]{1,0:T(8,128)(2,1)S(1)} %total_sum.1.refs_0_, bf16[544,128]{1,0:T(8,128)(2,1)S(1)} %collective-permute-done.11.refs_1_, bf16[544,128]{1,0:T(8,128)(2,1)S(1)} %collective-permute-done.12.refs_2_, bf16[544,128]{1,0:T(8,128)(2,1)S(1)} %collective-permute-done.13.refs_3_), custom_call_target="tpu_custom_call" | custom-call | flops 1000000 | bytes 4000000 | tf_op jit(solution)/shard_map/expert_product/pallas_call | solution.py:477
  (24 shorter events, 0.2 us)
Async XLA Ops:
  0.6 0.7 %copy-start = (f32[2,32]{1,0:T(2,128)S(1)}, f32[2,32]{1,0:T(2,128)}, u32[]{:S(2)}) copy-start(f32[2,32]{1,0:T(2,128)} %coef_ref.1) | copy-start | bytes 772
  1.3 8.4 %copy-start.2 = (bf16[256,9,128]{2,0,1:T(8,128)(2,1)S(1)}, bf16[256,9,128]{2,0,1:T(8,128)(2,1)}, u32[]{:S(2)}) copy-start(bf16[256,9,128]{2,0,1:T(8,128)(2,1)} %param.11) | copy-start | bytes 1769476
  1.3 8.4 %copy-start.3 = (bf16[128,9,128]{2,0,1:T(8,128)(2,1)S(1)}, bf16[128,9,128]{2,0,1:T(8,128)(2,1)}, u32[]{:S(2)}) copy-start(bf16[128,9,128]{2,0,1:T(8,128)(2,1)} %param.12) | copy-start | bytes 884740
  1.3 8.4 %copy-start.4 = (f32[5,5,1024]{2,1,0:T(8,128)S(1)}, f32[5,5,1024]{2,1,0:T(8,128)}, u32[]{:S(2)}) copy-start(f32[5,5,1024]{2,1,0:T(8,128)} %two_ref.3) | copy-start | bytes 307204
  1.3 8.4 %copy-start.5 = (f32[3,3,1024]{2,1,0:T(4,128)S(1)}, f32[3,3,1024]{2,1,0:T(4,128)}, u32[]{:S(2)}) copy-start(f32[3,3,1024]{2,1,0:T(4,128)} %one_ref.3) | copy-start | bytes 110596
  1.3 8.4 %copy-start.6 = (s32[128,8]{0,1:T(8,128)S(1)}, s32[128,8]{0,1:T(8,128)}, u32[]{:S(2)}) copy-start(s32[128,8]{0,1:T(8,128)} %param.13) | copy-start | bytes 12292
  1.3 8.4 %copy-start.7 = (f32[1024]{0:T(1024)S(1)}, f32[1024]{0:T(1024)}, u32[]{:S(2)}) copy-start(f32[1024]{0:T(1024)} %param.14) | copy-start | bytes 12292
  1.3 8.4 %copy-start.8 = (s32[128]{0:T(128)S(1)}, s32[128]{0:T(128)}, u32[]{:S(2)}) copy-start(s32[128]{0:T(128)} %param.18) | copy-start | bytes 1540
  3.4 11.3 %collective-permute-start = (bf16[2,272,128]{2,1,0:T(8,128)(2,1)S(1)}, bf16[2,272,128]{2,1,0:T(8,128)(2,1)S(1)}, u32[]{:S(2)}, u32[]{:S(2)}) collective-permute-start(bf16[2,272,128]{2,1,0:T(8,128)(2,1)S(1)} %merge.1.refs_0_), channel_id=1, source_target_pairs={{0,8},{4,12},{8,0},{12,4},{1,9},{5,13},{9,1},{13,5},{2,10},{6,14},... | collective-permute-start | bytes 417800 | tf_op jit(solution)/shard_map/ppermute | solution.py:520
  7.5 7.2 %collective-permute-start.1 = (bf16[2,272,128]{2,1,0:T(8,128)(2,1)S(1)}, bf16[2,272,128]{2,1,0:T(8,128)(2,1)S(1)}, u32[]{:S(2)}, u32[]{:S(2)}) collective-permute-start(bf16[2,272,128]{2,1,0:T(8,128)(2,1)S(1)} %merge.1.refs_0_), channel_id=1, source_target_pairs={{0,4},{4,0},{8,12},{12,8},{1,5},{5,1},{9,13},{13,9},{2,6},{6,2},{1... | collective-permute-start | bytes 417800 | tf_op jit(solution)/shard_map/ppermute | solution.py:520
  14.7 5.1 %collective-permute-start.2 = (bf16[2,272,128]{2,1,0:T(8,128)(2,1)S(1)}, bf16[2,272,128]{2,1,0:T(8,128)(2,1)S(1)}, u32[]{:S(2)}, u32[]{:S(2)}) collective-permute-start(bf16[2,272,128]{2,1,0:T(8,128)(2,1)S(1)} %collective-permute-done.refs_2_), channel_id=1, source_target_pairs={{0,4},{4,0},{8,12},{12,8},{1,5},{5,1},{9,13},{13,9},{2,6},{6,2},{1... | collective-permute-start | bytes 417800 | tf_op jit(solution)/shard_map/ppermute | solution.py:520
  19.9 2.0 %collective-permute-start.4 = (bf16[2176,128]{1,0:T(8,128)(2,1)S(1)}, bf16[2176,128]{1,0:T(8,128)(2,1)S(1)}, u32[]{:S(2)}, u32[]{:S(2)}) collective-permute-start(bf16[2176,128]{1,0:T(8,128)(2,1)S(1)} %get-tuple-element.49), channel_id=1, source_target_pairs={{0,1},{1,0},{2,3},{3,2},{4,5},{5,4},{6,7},{7,6},{8,9},{9,8},{10,11... | collective-permute-start | bytes 1671176 | tf_op jit(solution)/shard_map/ppermute | solution.py:520
  19.9 3.2 %collective-permute-start.3 = (bf16[4,2,272,128]{3,2,1,0:T(8,128)(2,1)S(1)}, bf16[4,2,272,128]{3,2,1,0:T(8,128)(2,1)S(1)}, u32[]{:S(2)}, u32[]{:S(2)}) collective-permute-start(bf16[4,2,272,128]{3,2,1,0:T(8,128)(2,1)S(1)} %pack.1.rest_0_), channel_id=1, source_target_pairs={{0,1},{1,0},{2,3},{3,2},{4,5},{5,4},{6,7},{7,6},{8,9},{9,8},{10,11... | collective-permute-start | bytes 1671176 | tf_op jit(solution)/shard_map/ppermute | solution.py:520
  21.9 21.9 %copy-start.1 = (s32[4,32]{1,0:T(4,128)S(1)}, s32[4,32]{1,0:T(4,128)}, u32[]{:S(2)}) copy-start(s32[4,32]{1,0:T(4,128)} %send_ref.1) | copy-start | bytes 1540
  21.9 8.8 %collective-permute-start.5 = (bf16[2,544,128]{2,1,0:T(8,128)(2,1)S(1)}, bf16[2,544,128]{2,1,0:T(8,128)(2,1)S(1)}, u32[]{:S(2)}, u32[]{:S(2)}) collective-permute-start(bf16[2,544,128]{2,1,0:T(8,128)(2,1)S(1)} %get-tuple-element.52), channel_id=1, source_target_pairs={{0,4},{4,0},{8,12},{12,8},{1,5},{5,1},{9,13},{13,9},{2,6},{6,2},{1... | collective-permute-start | bytes 835592 | tf_op jit(solution)/shard_map/ppermute | solution.py:520
  30.8 11.3 %collective-permute-start.6 = (bf16[544,128]{1,0:T(8,128)(2,1)S(1)}, bf16[544,128]{1,0:T(8,128)(2,1)S(1)}, u32[]{:S(2)}, u32[]{:S(2)}) collective-permute-start(bf16[544,128]{1,0:T(8,128)(2,1)S(1)} %get-tuple-element.57), channel_id=1, source_target_pairs={{0,8},{4,12},{8,0},{12,4},{1,9},{5,13},{9,1},{13,5},{2,10},{6,14},... | collective-permute-start | bytes 417800 | tf_op jit(solution)/shard_map/ppermute | solution.py:520
  33.1 9.0 %collective-permute-start.7 = (bf16[9,32,128]{2,1,0:T(8,128)(2,1)S(1)}, bf16[9,32,128]{2,1,0:T(8,128)(2,1)S(1)}, u32[]{:S(2)}, u32[]{:S(2)}) collective-permute-start(bf16[9,32,128]{2,1,0:T(8,128)(2,1)S(1)} %get-tuple-element.58), channel_id=1, source_target_pairs={{4,8},{8,4},{12,0},{0,12},{5,9},{9,5},{13,1},{1,13},{6,10},{10,6},... | collective-permute-start | bytes 221192 | tf_op jit(solution)/shard_map/ppermute | solution.py:529
  34.3 7.7 %collective-permute-start.8 = (bf16[9,32,128]{2,1,0:T(8,128)(2,1)S(1)}, bf16[9,32,128]{2,1,0:T(8,128)(2,1)S(1)}, u32[]{:S(2)}, u32[]{:S(2)}) collective-permute-start(bf16[9,32,128]{2,1,0:T(8,128)(2,1)S(1)} %get-tuple-element.59), channel_id=1, source_target_pairs={{1,2},{2,1},{3,0},{0,3},{5,6},{6,5},{7,4},{4,7},{9,10},{10,9},{11,... | collective-permute-start | bytes 221192 | tf_op jit(solution)/shard_map/ppermute | solution.py:529
  34.5 7.7 %collective-permute-start.9 = (bf16[9,32,128]{2,1,0:T(8,128)(2,1)S(1)}, bf16[9,32,128]{2,1,0:T(8,128)(2,1)S(1)}, u32[]{:S(2)}, u32[]{:S(2)}) collective-permute-start(bf16[9,32,128]{2,1,0:T(8,128)(2,1)S(1)} %get-tuple-element.60), channel_id=1, source_target_pairs={{0,4},{4,0},{8,12},{12,8},{1,5},{5,1},{9,13},{13,9},{2,6},{6,2},{1... | collective-permute-start | bytes 221192 | tf_op jit(solution)/shard_map/ppermute | solution.py:529
  35.0 7.2 %collective-permute-start.10 = (bf16[9,32,128]{2,1,0:T(8,128)(2,1)S(1)}, bf16[9,32,128]{2,1,0:T(8,128)(2,1)S(1)}, u32[]{:S(2)}, u32[]{:S(2)}) collective-permute-start(bf16[9,32,128]{2,1,0:T(8,128)(2,1)S(1)} %get-tuple-element.61), channel_id=1, source_target_pairs={{0,1},{1,0},{2,3},{3,2},{4,5},{5,4},{6,7},{7,6},{8,9},{9,8},{10,11... | collective-permute-start | bytes 221192 | tf_op jit(solution)/shard_map/ppermute | solution.py:529
  42.2 5.7 %collective-permute-start.11 = (bf16[544,128]{1,0:T(8,128)(2,1)S(1)}, bf16[544,128]{1,0:T(8,128)(2,1)S(1)}, u32[]{:S(2)}, u32[]{:S(2)}) collective-permute-start(bf16[544,128]{1,0:T(8,128)(2,1)S(1)} %total_sum.1.refs_0_), channel_id=1, source_target_pairs={{0,2},{1,3},{2,0},{3,1},{4,6},{5,7},{6,4},{7,5},{8,10},{9,11},{10,... | collective-permute-start | bytes 417800 | tf_op jit(solution)/shard_map/ppermute | solution.py:520
  43.8 4.1 %collective-permute-start.12 = (bf16[544,128]{1,0:T(8,128)(2,1)S(1)}, bf16[544,128]{1,0:T(8,128)(2,1)S(1)}, u32[]{:S(2)}, u32[]{:S(2)}) collective-permute-start(bf16[544,128]{1,0:T(8,128)(2,1)S(1)} %total_sum.1.refs_0_), channel_id=1, source_target_pairs={{0,1},{1,0},{2,3},{3,2},{4,5},{5,4},{6,7},{7,6},{8,9},{9,8},{10,11... | collective-permute-start | bytes 417800 | tf_op jit(solution)/shard_map/ppermute | solution.py:520
  47.9 1.4 %collective-permute-start.13 = (bf16[544,128]{1,0:T(8,128)(2,1)S(1)}, bf16[544,128]{1,0:T(8,128)(2,1)S(1)}, u32[]{:S(2)}, u32[]{:S(2)}) collective-permute-start(bf16[544,128]{1,0:T(8,128)(2,1)S(1)} %collective-permute-done.11.refs_1_), channel_id=1, source_target_pairs={{0,1},{1,0},{2,3},{3,2},{4,5},{5,4},{6,7},{7,6},{8,9},{9,8},{10,11... | collective-permute-start | bytes 417800 | tf_op jit(solution)/shard_map/ppermute | solution.py:520

commit v7 on v5

--- a/solution.py
+++ b/solution.py
@@ -18,7 +18,6 @@
 SLOT = {component: place for place, component in enumerate(STACK)}
 
 VMEM = pl.BlockSpec(memory_space=pltpu.VMEM)
-SMEM = pl.BlockSpec(memory_space=pltpu.SMEM)
 HBM = pl.BlockSpec(memory_space=pltpu.HBM)
 
 
@@ -118,19 +117,22 @@
 
 
 def features_kernel(
-    live_ref, near_ref, class_ref, zero_ref, one_ref, two_ref, source_ref, target_ref,
+    live_in_ref, near_ref, class_ref, zero_ref, one_ref, two_ref, source_ref, target_ref,
     other_ref, own_ref, pulled_ref, edge_ref,
-    source_t, target_t, moved, spread, rotated, grads,
+    source_t, target_t, moved, spread, rotated, grads, live_ref, live_arrived,
     *, fanout,
 ):
     slots, channels = source_ref.shape[1:]
     atoms = target_ref.shape[1]
     edges = atoms * fanout
+    live_copy = pltpu.make_async_copy(live_in_ref, live_ref, live_arrived)
+    live_copy.start()
     for c in range(9):
         source_t[c * channels : (c + 1) * channels, :] = source_ref[c].T
         target_t[c * channels : (c + 1) * channels, :] = target_ref[c].T
     near = near_ref[...].astype(F32).astype(BF16)
     classes = class_ref[...].astype(F32).astype(BF16)
+    live_copy.wait()
     live_edges = live_ref[0] * LIVE_BLOCK * fanout
     scale = 1.0 / math.sqrt(fanout)
 
@@ -215,7 +217,7 @@
     shape = jax.ShapeDtypeStruct
     return pl.pallas_call(
         functools.partial(features_kernel, fanout=fanout),
-        in_specs=[SMEM] + [VMEM] * 7,
+        in_specs=[HBM] + [VMEM] * 7,
         out_specs=[VMEM] * 4,
         out_shape=[
             shape((rows, 128), BF16),
@@ -230,6 +232,8 @@
             pltpu.VMEM((9 * channels, CHUNK), F32),
             pltpu.VMEM((7 * channels, edges), BF16),
             pltpu.VMEM((rows, 128), F32),
+            pltpu.SMEM((1,), jnp.int32),
+            pltpu.SemaphoreType.DMA,
         ],
         compiler_params=limits(24),
         cost_estimate=cost(9 * 10**9, 7 * 10**6),
@@ -408,7 +412,7 @@
 
 
 def expert_kernel(coef_ref, *refs, scale):
-    sums, out_ref, summed = refs[:-2], refs[-2], refs[-1]
+    sums, out_ref, summed, staged, written = refs[:-4], *refs[-4:]
     owned = out_ref.shape[0]
     place = lax.axis_index("gx")
     row = lax.broadcasted_iota(jnp.int32, (owned, coef_ref.shape[1]), 0)
@@ -426,10 +430,20 @@
         for ref in sums[side * half + 1 : (side + 1) * half]:
             total += ref[...].astype(F32)
         summed[side] = total
-    for row in range(summed.shape[1]):
-        out_ref[:, row * 128 : (row + 1) * 128] = (
-            first * summed[0, row : row + 1, :] + second * summed[1, row : row + 1, :]
-        )
+    rows = summed.shape[1]
+    stripes = written.shape[0]
+    copies = []
+    for stripe in range(stripes):
+        low, high = rows * stripe // stripes, rows * (stripe + 1) // stripes
+        for row in range(low, high):
+            staged[:, row * 128 : (row + 1) * 128] = (
+                first * summed[0, row : row + 1, :] + second * summed[1, row : row + 1, :]
+            )
+        span = pl.ds(low * 128, (high - low) * 128)
+        copies.append(pltpu.make_async_copy(staged.at[:, span], out_ref.at[:, span], written.at[stripe]))
+        copies[-1].start()
+    for copy in copies:
+        copy.wait()
 
 
 def expert_product(coef, sums, owned, scale):
@@ -437,9 +451,13 @@
     return pl.pallas_call(
         functools.partial(expert_kernel, scale=scale),
         in_specs=[VMEM] * (1 + len(sums)),
-        out_specs=VMEM,
+        out_specs=HBM,
         out_shape=jax.ShapeDtypeStruct((owned, rows * 128), F32),
-        scratch_shapes=[pltpu.VMEM((2, rows, 128), F32)],
+        scratch_shapes=[
+            pltpu.VMEM((2, rows, 128), F32),
+            pltpu.VMEM((owned, rows * 128), F32),
+            pltpu.SemaphoreType.DMA((4,)),
+        ],
         compiler_params=limits(8),
         cost_estimate=cost(10**6, 4 * 10**6),
         name="expert_product",
@@ -511,12 +529,13 @@
     if direct:
         half = height // 2
         mine = merge(merge_coef, experts, 2)
-        held = [mine] + [swap(mine, "yz", k) for k in range(1, count_yz)]
+        order = sorted(range(1, count_yz), key=lambda k: (k == 1, k))
+        held = [mine] + [swap(mine, "yz", k) for k in reversed(order)]
         source, target, mine = lax.optimization_barrier((source, target, mine))
 
         def places():
             here, side = lax.axis_index("yz"), lax.rem(lax.axis_index("gx"), 2)
-            starts = [(here ^ k) * height for k in range(count_yz)]
+            starts = [(here ^ k) * height for k in [0, *reversed(order)]]
             return [at + side * half for at in starts] + [at + (1 - side) * half for at in starts]
     else:
         part = jnp.dot(merge_coef, experts.astype(F32), precision=lax.Precision.HIGHEST).astype(BF16)
@@ -533,7 +552,7 @@
         other, *held = lax.optimization_barrier((other, *held))
         came = swap(other, "gx", 1)
         parts = pair_sum(own, came, count_yz)
-        gathered = [parts[0]] + [swap(parts[k], "yz", k) for k in reversed(range(1, count_yz))]
+        gathered = [parts[0]] + [swap(parts[k], "yz", k) for k in order]
         held = pack(held)
         pieces = [held, swap(held, "gx", 1)]
     grad_own, *ghosts = back(edge, zero, rot_one, rot_two, pulled, pieces, places, rows, atoms, slots, face)
@@ -543,7 +562,7 @@
     ]
     if direct:
         grad_own, *gathered = lax.optimization_barrier((grad_own, *gathered))
-        summed, *returned = lax.optimization_barrier((total_sum(gathered), *returned))
+        summed, *returned[:2] = lax.optimization_barrier((total_sum(gathered), *returned[:2]))
         across = swap(summed, "gx", 2)
         input_grad = finish(send_index, grad_own, returned)
         across, input_grad = lax.optimization_barrier((across, input_grad))

time: 48.9 us -> 49.7 us (1.016)
  starting transfers between devices: 15.4 us -> 19.7 us
  waiting for transfers between devices: 13.3 us -> 9.55 us
    ppermute x4, starting transfers between devices: 2.67 us -> 6.93 us  [neighbour_pairs(): return lax.ppermute(value, axis, moves)]
    ppermute x11, waiting for transfers between devices: 10.7 us -> 6.8 us  [swap(): lax.ppermute(value, axis, [(i, i ^ bit) for i in range(lax.axis_size(axis...]
    pallas_call x1, Pallas kernels: 7.18 us -> 7.73 us  [features(): pl.pallas_call(functools.partial(features_kernel, fanout=fanout), in_spec...]
where the time goes in v7:
time: 49.7 us; the launch traced here: 49.6 us
  starting transfers between devices  19.7 us (40%)
  Pallas kernels  18.2 us (37%)
  waiting for transfers between devices  9.55 us (19%)
  between operations  1.44 us (3%)
  local copies, waits for them, and re-layouts  0.7 us (1%)
    ppermute x11, starting transfers between devices, swap(): lax.ppermute(value, axis, [(i, i ^ bit) for i in range(lax.axis_size(axis...  12.8 us
    pallas_call x1, Pallas kernels, features(): pl.pallas_call(functools.partial(features_kernel, fanout=fanout), in_spec...  7.73 us
    ppermute x4, starting transfers between devices, neighbour_pairs(): return lax.ppermute(value, axis, moves)  6.93 us
    ppermute x11, waiting for transfers between devices, swap(): lax.ppermute(value, axis, [(i, i ^ bit) for i in range(lax.axis_size(axis...  6.8 us
    pallas_call x1, Pallas kernels, back(): pl.pallas_call(functools.partial(back_kernel, pieces=len(pieces), members...  5.47 us
    ppermute x4, waiting for transfers between devices, neighbour_pairs(): return lax.ppermute(value, axis, moves)  2.75 us
    pallas_call x1, Pallas kernels, merge(): pl.pallas_call(merge_kernel, in_specs=[HBM, HBM], out_specs=VMEM, out_sha...  2.03 us
    pallas_call x1, Pallas kernels, expert_product(): pl.pallas_call(functools.partial(expert_kernel, scale=scale), in_specs=[V...  1.54 us
  transfers between devices with their start and end apart: 15, of which 8 were waited for; matrix products, arithmetic and copies ran while one was open for 0% of the time, Pallas kernels for 29%

profile of v7, /device:TPU:0, one launch (start us, length us, event | category | flops | bytes accessed | tf_op | source)
XLA Modules:
  0.0 49.6 jit_solution(543660703966964410)
XLA Ops:
  0.6 0.7 %copy-done = f32[2,32]{1,0:T(2,128)S(1)} copy-done((f32[2,32]{1,0:T(2,128)S(1)}, f32[2,32]{1,0:T(2,128)}, u32[]{:S(2)}) %copy-start) | copy-done | bytes 280
  1.4 2.0 %merge.1.refs_0_ = bf16[2,272,128]{2,1,0:T(8,128)(2,1)S(1)} custom-call(f32[2,32]{1,0:T(2,128)S(1)} %copy-done, bf16[32,69632]{1,0:T(8,128)(2,1)} %experts_ref.1), custom_call_target="tpu_custom_call" | custom-call | flops 53477376 | bytes 2228224 | tf_op jit(solution)/shard_map/merge/pallas_call | solution.py:102
  3.4 4.1 %collective-permute-start.2 = (bf16[2,272,128]{2,1,0:T(8,128)(2,1)S(1)}, bf16[2,272,128]{2,1,0:T(8,128)(2,1)S(1)}, u32[]{:S(2)}, u32[]{:S(2)}) collective-permute-start(bf16[2,272,128]{2,1,0:T(8,128)(2,1)S(1)} %merge.1.refs_0_), channel_id=1, source_target_pairs={{0,8},{4,12},{8,0},{12,4},{1,9},{5,13},{9,1},{13,5},{2,10},{6,14},... | collective-permute-start | bytes 417800 | tf_op jit(solution)/shard_map/ppermute | solution.py:498
  7.5 1.3 %collective-permute-start.1 = (bf16[2,272,128]{2,1,0:T(8,128)(2,1)S(1)}, bf16[2,272,128]{2,1,0:T(8,128)(2,1)S(1)}, u32[]{:S(2)}, u32[]{:S(2)}) collective-permute-start(bf16[2,272,128]{2,1,0:T(8,128)(2,1)S(1)} %merge.1.refs_0_), channel_id=1, source_target_pairs={{0,12},{4,8},{8,4},{12,0},{1,13},{5,9},{9,5},{13,1},{2,14},{6,10},... | collective-permute-start | bytes 417800 | tf_op jit(solution)/shard_map/ppermute | solution.py:498
  8.8 0.2 collective-permute-start
  9.8 7.7 %features.1 = (bf16[2176,128]{1,0:T(8,128)(2,1)S(1)}, bf16[2176,128]{1,0:T(8,128)(2,1)S(1)}, bf16[896,1024]{1,0:T(8,128)(2,1)S(1)}, f32[8,1024]{1,0:T(8,128)S(1)}) custom-call(s32[1]{0:T(128)S(6)} %copy.13.live_in_ref, s32[8,128]{1,0:T(8,128)S(1)} %bitcast.8, s32[1,128]{1,0:T(1,128)S(1)} %bitcast.11, f32[1,1024]{1,0:T(1,128)S(1)} %bitcast.9, ...), custom_call_target="tpu_custom_call" | custom-call | flops 8999999488 | bytes 7000000 | tf_op jit(solution)/shard_map/features/pallas_call | solution.py:218
  17.5 0.5 collective-permute-done.2.refs_3_
  18.0 0.5 %collective-permute-done.refs_1_ = bf16[2,272,128]{2,1,0:T(8,128)(2,1)S(1)} collective-permute-done((bf16[2,272,128]{2,1,0:T(8,128)(2,1)S(1)}, bf16[2,272,128]{2,1,0:T(8,128)(2,1)S(1)}, u32[]{:S(2)}, u32[]{:S(2)}) %collective-permute-start) | collective-permute-done | bytes 139296 | tf_op jit(solution)/shard_map/ppermute | solution.py:498
  18.5 0.0 collective-permute-start.4
  18.6 0.6 %collective-permute-start.3 = (bf16[4,2,272,128]{3,2,1,0:T(8,128)(2,1)S(1)}, bf16[4,2,272,128]{3,2,1,0:T(8,128)(2,1)S(1)}, u32[]{:S(2)}, u32[]{:S(2)}) collective-permute-start(bf16[4,2,272,128]{3,2,1,0:T(8,128)(2,1)S(1)} %pack.1.rest_0_), channel_id=1, source_target_pairs={{0,1},{1,0},{2,3},{3,2},{4,5},{5,4},{6,7},{7,6},{8,9},{9,8},{10,11... | collective-permute-start | bytes 1671176 | tf_op jit(solution)/shard_map/ppermute | solution.py:498
  19.1 1.3 %collective-permute-done.4.came_ref = bf16[2176,128]{1,0:T(8,128)(2,1)S(1)} collective-permute-done((bf16[2176,128]{1,0:T(8,128)(2,1)S(1)}, bf16[2176,128]{1,0:T(8,128)(2,1)S(1)}, u32[]{:S(2)}, u32[]{:S(2)}) %collective-permute-start.4) | collective-permute-done | bytes 557088 | tf_op jit(solution)/shard_map/ppermute | solution.py:498
  20.5 0.1 pair_sum.1
  20.6 4.3 %collective-permute-start.5 = (bf16[544,128]{1,0:T(8,128)(2,1)S(1)}, bf16[544,128]{1,0:T(8,128)(2,1)S(1)}, u32[]{:S(2)}, u32[]{:S(2)}) collective-permute-start(bf16[544,128]{1,0:T(8,128)(2,1)S(1)} %get-tuple-element.45), channel_id=1, source_target_pairs={{0,8},{4,12},{8,0},{12,4},{1,9},{5,13},{9,1},{13,5},{2,10},{6,14},... | collective-permute-start | bytes 417800 | tf_op jit(solution)/shard_map/ppermute | solution.py:498
  25.0 0.4 collective-permute-start.6
  25.4 0.2 collective-permute-start.7
  25.6 5.5 %back.1 = (f32[9,128,128]{2,1,0:T(8,128)S(1)}, bf16[9,32,128]{2,1,0:T(8,128)(2,1)S(1)}, bf16[9,32,128]{2,1,0:T(8,128)(2,1)S(1)}, bf16[9,32,128]{2,1,0:T(8,128)(2,1)S(1)}, bf16[9,32,128]{2,1,0:T(8,128)(2,1)S(1)}) custom-call(f32[8,1024]{1,0:T(8,128)S(1)} %get-tuple-element.34.edge_ref, f32[1,1024]{1,0:T(1,128)S(1)} %bitcast.10, f32[3,3,1024]{2,1,0:T(4,128)S(1)} %copy-done.5, ...), custom_call_target="tpu_custom_call" | custom-call | flops 8999999488 | bytes 7000000 | tf_op jit(solution)/shard_map/back/pallas_call | solution.py:336
  31.1 3.3 %collective-permute-start.8 = (bf16[9,32,128]{2,1,0:T(8,128)(2,1)S(1)}, bf16[9,32,128]{2,1,0:T(8,128)(2,1)S(1)}, u32[]{:S(2)}, u32[]{:S(2)}) collective-permute-start(bf16[9,32,128]{2,1,0:T(8,128)(2,1)S(1)} %get-tuple-element.52), channel_id=1, source_target_pairs={{4,8},{8,4},{12,0},{0,12},{5,9},{9,5},{13,1},{1,13},{6,10},{10,6},... | collective-permute-start | bytes 221192 | tf_op jit(solution)/shard_map/ppermute | solution.py:507
  34.3 0.4 collective-permute-start.9
  34.7 0.5 collective-permute-done.5.refs_1_
  35.2 0.0 collective-permute-done.6.refs_2_
  35.2 2.6 %collective-permute-done.7.refs_3_ = bf16[544,128]{1,0:T(8,128)(2,1)S(1)} collective-permute-done((bf16[544,128]{1,0:T(8,128)(2,1)S(1)}, bf16[544,128]{1,0:T(8,128)(2,1)S(1)}, u32[]{:S(2)}, u32[]{:S(2)}) %collective-permute-start.7) | collective-permute-done | bytes 139296 | tf_op jit(solution)/shard_map/ppermute | solution.py:498
  37.8 0.1 total_sum.1.refs_0_
  37.9 0.9 %collective-permute-done.9.b_ref = bf16[9,32,128]{2,1,0:T(8,128)(2,1)S(1)} collective-permute-done((bf16[9,32,128]{2,1,0:T(8,128)(2,1)S(1)}, bf16[9,32,128]{2,1,0:T(8,128)(2,1)S(1)}, u32[]{:S(2)}, u32[]{:S(2)}) %collective-permute-start.9) | collective-permute-done | bytes 73760 | tf_op jit(solution)/shard_map/ppermute | solution.py:507
  38.9 1.0 %collective-permute-start.10 = (bf16[544,128]{1,0:T(8,128)(2,1)S(1)}, bf16[544,128]{1,0:T(8,128)(2,1)S(1)}, u32[]{:S(2)}, u32[]{:S(2)}) collective-permute-start(bf16[544,128]{1,0:T(8,128)(2,1)S(1)} %total_sum.1.refs_0_), channel_id=1, source_target_pairs={{0,2},{1,3},{2,0},{3,1},{4,6},{5,7},{6,4},{7,5},{8,10},{9,11},{10,... | collective-permute-start | bytes 417800 | tf_op jit(solution)/shard_map/ppermute | solution.py:498
  39.9 3.3 %collective-permute-start.11 = (bf16[9,32,128]{2,1,0:T(8,128)(2,1)S(1)}, bf16[9,32,128]{2,1,0:T(8,128)(2,1)S(1)}, u32[]{:S(2)}, u32[]{:S(2)}) collective-permute-start(bf16[9,32,128]{2,1,0:T(8,128)(2,1)S(1)} %get-tuple-element.58), channel_id=1, source_target_pairs={{0,4},{4,0},{8,12},{12,8},{1,5},{5,1},{9,13},{13,9},{2,6},{6,2},{1... | collective-permute-start | bytes 221192 | tf_op jit(solution)/shard_map/ppermute | solution.py:507
  43.1 0.0 collective-permute-start.12
  43.2 0.5 %collective-permute-start.13 = (bf16[544,128]{1,0:T(8,128)(2,1)S(1)}, bf16[544,128]{1,0:T(8,128)(2,1)S(1)}, u32[]{:S(2)}, u32[]{:S(2)}) collective-permute-start(bf16[544,128]{1,0:T(8,128)(2,1)S(1)} %total_sum.1.refs_0_), channel_id=1, source_target_pairs={{0,1},{1,0},{2,3},{3,2},{4,5},{5,4},{6,7},{7,6},{8,9},{9,8},{10,11... | collective-permute-start | bytes 417800 | tf_op jit(solution)/shard_map/ppermute | solution.py:498
  43.7 1.8 %collective-permute-done.11.c_ref = bf16[9,32,128]{2,1,0:T(8,128)(2,1)S(1)} collective-permute-done((bf16[9,32,128]{2,1,0:T(8,128)(2,1)S(1)}, bf16[9,32,128]{2,1,0:T(8,128)(2,1)S(1)}, u32[]{:S(2)}, u32[]{:S(2)}) %collective-permute-start.11) | collective-permute-done | bytes 73760 | tf_op jit(solution)/shard_map/ppermute | solution.py:507
  45.5 0.0 collective-permute-done.12.d_ref
  45.5 1.2 %finish.1 = bf16[9,128,128]{2,1,0:T(8,128)(2,1)} custom-call(s32[4,32]{1,0:T(4,128)S(1)} %copy-done.1, f32[9,128,128]{2,1,0:T(8,128)S(1)} %get-tuple-element.55.own_ref, bf16[9,32,128]{2,1,0:T(8,128)(2,1)S(1)} %collective-permute-done.8.a_ref, bf16[9,32,128]{2,1,0:T(8,128)(2,1)S(1)} %collective-permute-done.9.b_ref, ...), custom_call_target="tpu_custom_call" | custom-call | flops 100000000 | bytes 2000000 | tf_op jit(solution)/shard_map/finish/pallas_call | solution.py:486
  46.7 1.4 %collective-permute-done.14.refs_3_ = bf16[544,128]{1,0:T(8,128)(2,1)S(1)} collective-permute-done((bf16[544,128]{1,0:T(8,128)(2,1)S(1)}, bf16[544,128]{1,0:T(8,128)(2,1)S(1)}, u32[]{:S(2)}, u32[]{:S(2)}) %collective-permute-start.14) | collective-permute-done | bytes 139296 | tf_op jit(solution)/shard_map/ppermute | solution.py:498
  48.0 1.5 %expert_product.1 = f32[8,69632]{1,0:T(8,128)} custom-call(f32[2,32]{1,0:T(2,128)S(1)} %copy-done, bf16[544,128]{1,0:T(8,128)(2,1)S(1)} %total_sum.1.refs_0_, bf16[544,128]{1,0:T(8,128)(2,1)S(1)} %collective-permute-done.10.refs_1_, bf16[544,128]{1,0:T(8,128)(2,1)S(1)} %collective-permute-done.13.refs_2_, bf16[544,128]{1,0:T(8,128)(2,1)S(1)} %collective-permute-done.14.refs_3_), custom_call_target="tpu_custom_call" | custom-call | flops 1000000 | bytes 4000000 | tf_op jit(solution)/shard_map/expert_product/pallas_call | solution.py:451
  (24 shorter events, 0.1 us)
Async XLA Ops:
  0.6 0.7 %copy-start = (f32[2,32]{1,0:T(2,128)S(1)}, f32[2,32]{1,0:T(2,128)}, u32[]{:S(2)}) copy-start(f32[2,32]{1,0:T(2,128)} %coef_ref.1) | copy-start | bytes 772
  1.3 8.4 %copy-start.2 = (bf16[256,9,128]{2,0,1:T(8,128)(2,1)S(1)}, bf16[256,9,128]{2,0,1:T(8,128)(2,1)}, u32[]{:S(2)}) copy-start(bf16[256,9,128]{2,0,1:T(8,128)(2,1)} %param.11) | copy-start | bytes 1769476
  1.3 8.4 %copy-start.3 = (bf16[128,9,128]{2,0,1:T(8,128)(2,1)S(1)}, bf16[128,9,128]{2,0,1:T(8,128)(2,1)}, u32[]{:S(2)}) copy-start(bf16[128,9,128]{2,0,1:T(8,128)(2,1)} %param.12) | copy-start | bytes 884740
  1.3 8.4 %copy-start.4 = (f32[5,5,1024]{2,1,0:T(8,128)S(1)}, f32[5,5,1024]{2,1,0:T(8,128)}, u32[]{:S(2)}) copy-start(f32[5,5,1024]{2,1,0:T(8,128)} %two_ref.3) | copy-start | bytes 307204
  1.3 8.4 %copy-start.5 = (f32[3,3,1024]{2,1,0:T(4,128)S(1)}, f32[3,3,1024]{2,1,0:T(4,128)}, u32[]{:S(2)}) copy-start(f32[3,3,1024]{2,1,0:T(4,128)} %one_ref.3) | copy-start | bytes 110596
  1.3 8.4 %copy-start.6 = (s32[128,8]{0,1:T(8,128)S(1)}, s32[128,8]{0,1:T(8,128)}, u32[]{:S(2)}) copy-start(s32[128,8]{0,1:T(8,128)} %param.13) | copy-start | bytes 12292
  1.3 8.4 %copy-start.7 = (f32[1024]{0:T(1024)S(1)}, f32[1024]{0:T(1024)}, u32[]{:S(2)}) copy-start(f32[1024]{0:T(1024)} %param.14) | copy-start | bytes 12292
  1.3 8.4 %copy-start.8 = (s32[128]{0:T(128)S(1)}, s32[128]{0:T(128)}, u32[]{:S(2)}) copy-start(s32[128]{0:T(128)} %param.18) | copy-start | bytes 1540
  3.4 14.6 %collective-permute-start.2 = (bf16[2,272,128]{2,1,0:T(8,128)(2,1)S(1)}, bf16[2,272,128]{2,1,0:T(8,128)(2,1)S(1)}, u32[]{:S(2)}, u32[]{:S(2)}) collective-permute-start(bf16[2,272,128]{2,1,0:T(8,128)(2,1)S(1)} %merge.1.refs_0_), channel_id=1, source_target_pairs={{0,8},{4,12},{8,0},{12,4},{1,9},{5,13},{9,1},{13,5},{2,10},{6,14},... | collective-permute-start | bytes 417800 | tf_op jit(solution)/shard_map/ppermute | solution.py:498
  7.5 10.5 %collective-permute-start.1 = (bf16[2,272,128]{2,1,0:T(8,128)(2,1)S(1)}, bf16[2,272,128]{2,1,0:T(8,128)(2,1)S(1)}, u32[]{:S(2)}, u32[]{:S(2)}) collective-permute-start(bf16[2,272,128]{2,1,0:T(8,128)(2,1)S(1)} %merge.1.refs_0_), channel_id=1, source_target_pairs={{0,12},{4,8},{8,4},{12,0},{1,13},{5,9},{9,5},{13,1},{2,14},{6,10},... | collective-permute-start | bytes 417800 | tf_op jit(solution)/shard_map/ppermute | solution.py:498
  8.8 9.7 %collective-permute-start = (bf16[2,272,128]{2,1,0:T(8,128)(2,1)S(1)}, bf16[2,272,128]{2,1,0:T(8,128)(2,1)S(1)}, u32[]{:S(2)}, u32[]{:S(2)}) collective-permute-start(bf16[2,272,128]{2,1,0:T(8,128)(2,1)S(1)} %merge.1.refs_0_), channel_id=1, source_target_pairs={{0,4},{4,0},{8,12},{12,8},{1,5},{5,1},{9,13},{13,9},{2,6},{6,2},{1... | collective-permute-start | bytes 417800 | tf_op jit(solution)/shard_map/ppermute | solution.py:498
  18.5 2.0 %collective-permute-start.4 = (bf16[2176,128]{1,0:T(8,128)(2,1)S(1)}, bf16[2176,128]{1,0:T(8,128)(2,1)S(1)}, u32[]{:S(2)}, u32[]{:S(2)}) collective-permute-start(bf16[2176,128]{1,0:T(8,128)(2,1)S(1)} %get-tuple-element.43), channel_id=1, source_target_pairs={{0,1},{1,0},{2,3},{3,2},{4,5},{5,4},{6,7},{7,6},{8,9},{9,8},{10,11... | collective-permute-start | bytes 1671176 | tf_op jit(solution)/shard_map/ppermute | solution.py:498
  18.6 7.0 %collective-permute-start.3 = (bf16[4,2,272,128]{3,2,1,0:T(8,128)(2,1)S(1)}, bf16[4,2,272,128]{3,2,1,0:T(8,128)(2,1)S(1)}, u32[]{:S(2)}, u32[]{:S(2)}) collective-permute-start(bf16[4,2,272,128]{3,2,1,0:T(8,128)(2,1)S(1)} %pack.1.rest_0_), channel_id=1, source_target_pairs={{0,1},{1,0},{2,3},{3,2},{4,5},{5,4},{6,7},{7,6},{8,9},{9,8},{10,11... | collective-permute-start | bytes 1671176 | tf_op jit(solution)/shard_map/ppermute | solution.py:498
  20.6 14.6 %collective-permute-start.5 = (bf16[544,128]{1,0:T(8,128)(2,1)S(1)}, bf16[544,128]{1,0:T(8,128)(2,1)S(1)}, u32[]{:S(2)}, u32[]{:S(2)}) collective-permute-start(bf16[544,128]{1,0:T(8,128)(2,1)S(1)} %get-tuple-element.45), channel_id=1, source_target_pairs={{0,8},{4,12},{8,0},{12,4},{1,9},{5,13},{9,1},{13,5},{2,10},{6,14},... | collective-permute-start | bytes 417800 | tf_op jit(solution)/shard_map/ppermute | solution.py:498
  25.0 10.3 %collective-permute-start.6 = (bf16[544,128]{1,0:T(8,128)(2,1)S(1)}, bf16[544,128]{1,0:T(8,128)(2,1)S(1)}, u32[]{:S(2)}, u32[]{:S(2)}) collective-permute-start(bf16[544,128]{1,0:T(8,128)(2,1)S(1)} %get-tuple-element.46), channel_id=1, source_target_pairs={{0,12},{4,8},{8,4},{12,0},{1,13},{5,9},{9,5},{13,1},{2,14},{6,10},... | collective-permute-start | bytes 417800 | tf_op jit(solution)/shard_map/ppermute | solution.py:498
  25.4 12.4 %collective-permute-start.7 = (bf16[544,128]{1,0:T(8,128)(2,1)S(1)}, bf16[544,128]{1,0:T(8,128)(2,1)S(1)}, u32[]{:S(2)}, u32[]{:S(2)}) collective-permute-start(bf16[544,128]{1,0:T(8,128)(2,1)S(1)} %get-tuple-element.47), channel_id=1, source_target_pairs={{0,4},{4,0},{8,12},{12,8},{1,5},{5,1},{9,13},{13,9},{2,6},{6,2},{1... | collective-permute-start | bytes 417800 | tf_op jit(solution)/shard_map/ppermute | solution.py:498
  25.6 19.9 %copy-start.1 = (s32[4,32]{1,0:T(4,128)S(1)}, s32[4,32]{1,0:T(4,128)}, u32[]{:S(2)}) copy-start(s32[4,32]{1,0:T(4,128)} %send_ref.1) | copy-start | bytes 1540
  31.1 6.8 %collective-permute-start.8 = (bf16[9,32,128]{2,1,0:T(8,128)(2,1)S(1)}, bf16[9,32,128]{2,1,0:T(8,128)(2,1)S(1)}, u32[]{:S(2)}, u32[]{:S(2)}) collective-permute-start(bf16[9,32,128]{2,1,0:T(8,128)(2,1)S(1)} %get-tuple-element.52), channel_id=1, source_target_pairs={{4,8},{8,4},{12,0},{0,12},{5,9},{9,5},{13,1},{1,13},{6,10},{10,6},... | collective-permute-start | bytes 221192 | tf_op jit(solution)/shard_map/ppermute | solution.py:507
  34.3 4.5 %collective-permute-start.9 = (bf16[9,32,128]{2,1,0:T(8,128)(2,1)S(1)}, bf16[9,32,128]{2,1,0:T(8,128)(2,1)S(1)}, u32[]{:S(2)}, u32[]{:S(2)}) collective-permute-start(bf16[9,32,128]{2,1,0:T(8,128)(2,1)S(1)} %get-tuple-element.53), channel_id=1, source_target_pairs={{1,2},{2,1},{3,0},{0,3},{5,6},{6,5},{7,4},{4,7},{9,10},{10,9},{11,... | collective-permute-start | bytes 221192 | tf_op jit(solution)/shard_map/ppermute | solution.py:507
  38.9 7.8 %collective-permute-start.10 = (bf16[544,128]{1,0:T(8,128)(2,1)S(1)}, bf16[544,128]{1,0:T(8,128)(2,1)S(1)}, u32[]{:S(2)}, u32[]{:S(2)}) collective-permute-start(bf16[544,128]{1,0:T(8,128)(2,1)S(1)} %total_sum.1.refs_0_), channel_id=1, source_target_pairs={{0,2},{1,3},{2,0},{3,1},{4,6},{5,7},{6,4},{7,5},{8,10},{9,11},{10,... | collective-permute-start | bytes 417800 | tf_op jit(solution)/shard_map/ppermute | solution.py:498
  39.9 5.6 %collective-permute-start.11 = (bf16[9,32,128]{2,1,0:T(8,128)(2,1)S(1)}, bf16[9,32,128]{2,1,0:T(8,128)(2,1)S(1)}, u32[]{:S(2)}, u32[]{:S(2)}) collective-permute-start(bf16[9,32,128]{2,1,0:T(8,128)(2,1)S(1)} %get-tuple-element.58), channel_id=1, source_target_pairs={{0,4},{4,0},{8,12},{12,8},{1,5},{5,1},{9,13},{13,9},{2,6},{6,2},{1... | collective-permute-start | bytes 221192 | tf_op jit(solution)/shard_map/ppermute | solution.py:507
  43.1 2.3 %collective-permute-start.12 = (bf16[9,32,128]{2,1,0:T(8,128)(2,1)S(1)}, bf16[9,32,128]{2,1,0:T(8,128)(2,1)S(1)}, u32[]{:S(2)}, u32[]{:S(2)}) collective-permute-start(bf16[9,32,128]{2,1,0:T(8,128)(2,1)S(1)} %get-tuple-element.59), channel_id=1, source_target_pairs={{0,1},{1,0},{2,3},{3,2},{4,5},{5,4},{6,7},{7,6},{8,9},{9,8},{10,11... | collective-permute-start | bytes 221192 | tf_op jit(solution)/shard_map/ppermute | solution.py:507
  43.2 3.5 %collective-permute-start.13 = (bf16[544,128]{1,0:T(8,128)(2,1)S(1)}, bf16[544,128]{1,0:T(8,128)(2,1)S(1)}, u32[]{:S(2)}, u32[]{:S(2)}) collective-permute-start(bf16[544,128]{1,0:T(8,128)(2,1)S(1)} %total_sum.1.refs_0_), channel_id=1, source_target_pairs={{0,1},{1,0},{2,3},{3,2},{4,5},{5,4},{6,7},{7,6},{8,9},{9,8},{10,11... | collective-permute-start | bytes 417800 | tf_op jit(solution)/shard_map/ppermute | solution.py:498
  46.7 1.4 %collective-permute-start.14 = (bf16[544,128]{1,0:T(8,128)(2,1)S(1)}, bf16[544,128]{1,0:T(8,128)(2,1)S(1)}, u32[]{:S(2)}, u32[]{:S(2)}) collective-permute-start(bf16[544,128]{1,0:T(8,128)(2,1)S(1)} %collective-permute-done.10.refs_1_), channel_id=1, source_target_pairs={{0,1},{1,0},{2,3},{3,2},{4,5},{5,4},{6,7},{7,6},{8,9},{9,8},{10,11... | collective-permute-start | bytes 417800 | tf_op jit(solution)/shard_map/ppermute | solution.py:498

commit v8 on v7

--- a/solution.py
+++ b/solution.py
@@ -132,8 +132,6 @@
         target_t[c * channels : (c + 1) * channels, :] = target_ref[c].T
     near = near_ref[...].astype(F32).astype(BF16)
     classes = class_ref[...].astype(F32).astype(BF16)
-    live_copy.wait()
-    live_edges = live_ref[0] * LIVE_BLOCK * fanout
     scale = 1.0 / math.sqrt(fanout)
 
     def chunk_step(chunk, carry):
@@ -148,7 +146,7 @@
         near_row = jnp.sum(picked, axis=0, keepdims=True)
         class_row = nn(classes, repeat)
         edge_ref[0:1, here] = near_row
-        edge_ref[1:2, here] = jnp.where(edge8[0:1] < live_edges, class_row, -1.0)
+        edge_ref[1:2, here] = class_row
         slot = lax.broadcasted_iota(jnp.int32, (slots, CHUNK), 0).astype(F32)
         pick = (slot == near_row).astype(F32).astype(BF16)
         moved[...] = nn(source_t[...], pick)
@@ -189,6 +187,9 @@
         return carry
 
     lax.fori_loop(0, edges // CHUNK, chunk_step, 0)
+    live_copy.wait()
+    edge_row = lax.broadcasted_iota(jnp.int32, (1, edges), 1)
+    edge_ref[1:2, :] = jnp.where(edge_row < live_ref[0] * LIVE_BLOCK * fanout, edge_ref[1:2, :], -1.0)
     zw, pw = 3 * channels, 2 * channels
     first = zw * zw // 128
     second = first + pw * pw // 128
@@ -529,13 +530,12 @@
     if direct:
         half = height // 2
         mine = merge(merge_coef, experts, 2)
-        order = sorted(range(1, count_yz), key=lambda k: (k == 1, k))
-        held = [mine] + [swap(mine, "yz", k) for k in reversed(order)]
+        held = [mine] + [swap(mine, "yz", k) for k in range(1, count_yz)]
         source, target, mine = lax.optimization_barrier((source, target, mine))
 
         def places():
             here, side = lax.axis_index("yz"), lax.rem(lax.axis_index("gx"), 2)
-            starts = [(here ^ k) * height for k in [0, *reversed(order)]]
+            starts = [(here ^ k) * height for k in range(count_yz)]
             return [at + side * half for at in starts] + [at + (1 - side) * half for at in starts]
     else:
         part = jnp.dot(merge_coef, experts.astype(F32), precision=lax.Precision.HIGHEST).astype(BF16)
@@ -552,7 +552,7 @@
         other, *held = lax.optimization_barrier((other, *held))
         came = swap(other, "gx", 1)
         parts = pair_sum(own, came, count_yz)
-        gathered = [parts[0]] + [swap(parts[k], "yz", k) for k in order]
+        gathered = [parts[0]] + [swap(parts[k], "yz", k) for k in reversed(range(1, count_yz))]
         held = pack(held)
         pieces = [held, swap(held, "gx", 1)]
     grad_own, *ghosts = back(edge, zero, rot_one, rot_two, pulled, pieces, places, rows, atoms, slots, face)
@@ -562,7 +562,7 @@
     ]
     if direct:
         grad_own, *gathered = lax.optimization_barrier((grad_own, *gathered))
-        summed, *returned[:2] = lax.optimization_barrier((total_sum(gathered), *returned[:2]))
+        summed, *returned = lax.optimization_barrier((total_sum(gathered), *returned))
         across = swap(summed, "gx", 2)
         input_grad = finish(send_index, grad_own, returned)
         across, input_grad = lax.optimization_barrier((across, input_grad))

time: 49.7 us -> 48.7 us (0.980)
  starting transfers between devices: 19.7 us -> 15.4 us
  waiting for transfers between devices: 9.55 us -> 13.2 us
  Pallas kernels: 18.2 us -> 17.7 us
    ppermute x4, starting transfers between devices: 6.93 us -> 2.67 us  [neighbour_pairs(): return lax.ppermute(value, axis, moves)]
    ppermute x11, waiting for transfers between devices: 6.8 us -> 10.6 us  [swap(): lax.ppermute(value, axis, [(i, i ^ bit) for i in range(lax.axis_size(axis...]
where the time goes in v8:
time: 48.7 us; the launch traced here: 48.5 us
  Pallas kernels  17.7 us (36%)
  starting transfers between devices  15.4 us (32%)
  waiting for transfers between devices  13.2 us (27%)
  between operations  1.44 us (3%)
  local copies, waits for them, and re-layouts  0.7 us (1%)
    ppermute x11, starting transfers between devices, swap(): lax.ppermute(value, axis, [(i, i ^ bit) for i in range(lax.axis_size(axis...  12.8 us
    ppermute x11, waiting for transfers between devices, swap(): lax.ppermute(value, axis, [(i, i ^ bit) for i in range(lax.axis_size(axis...  10.6 us
    pallas_call x1, Pallas kernels, features(): pl.pallas_call(functools.partial(features_kernel, fanout=fanout), in_spec...  7.27 us
    pallas_call x1, Pallas kernels, back(): pl.pallas_call(functools.partial(back_kernel, pieces=len(pieces), members...  5.47 us
    ppermute x4, starting transfers between devices, neighbour_pairs(): return lax.ppermute(value, axis, moves)  2.67 us
    ppermute x4, waiting for transfers between devices, neighbour_pairs(): return lax.ppermute(value, axis, moves)  2.61 us
    pallas_call x1, Pallas kernels, merge(): pl.pallas_call(merge_kernel, in_specs=[HBM, HBM], out_specs=VMEM, out_sha...  2.03 us
    pallas_call x1, Pallas kernels, expert_product(): pl.pallas_call(functools.partial(expert_kernel, scale=scale), in_specs=[V...  1.54 us
  transfers between devices with their start and end apart: 15, of which 8 were waited for; matrix products, arithmetic and copies ran while one was open for 0% of the time, Pallas kernels for 29%

profile of v8, /device:TPU:0, one launch (start us, length us, event | category | flops | bytes accessed | tf_op | source)
XLA Modules:
  0.0 48.5 jit_solution(59424977603952360)
XLA Ops:
  0.6 0.7 %copy-done = f32[2,32]{1,0:T(2,128)S(1)} copy-done((f32[2,32]{1,0:T(2,128)S(1)}, f32[2,32]{1,0:T(2,128)}, u32[]{:S(2)}) %copy-start) | copy-done | bytes 280
  1.4 2.0 %merge.1.refs_0_ = bf16[2,272,128]{2,1,0:T(8,128)(2,1)S(1)} custom-call(f32[2,32]{1,0:T(2,128)S(1)} %copy-done, bf16[32,69632]{1,0:T(8,128)(2,1)} %experts_ref.1), custom_call_target="tpu_custom_call" | custom-call | flops 53477376 | bytes 2228224 | tf_op jit(solution)/shard_map/merge/pallas_call | solution.py:102
  3.4 5.1 %collective-permute-start.2 = (bf16[2,272,128]{2,1,0:T(8,128)(2,1)S(1)}, bf16[2,272,128]{2,1,0:T(8,128)(2,1)S(1)}, u32[]{:S(2)}, u32[]{:S(2)}) collective-permute-start(bf16[2,272,128]{2,1,0:T(8,128)(2,1)S(1)} %merge.1.refs_0_), channel_id=1, source_target_pairs={{0,12},{4,8},{8,4},{12,0},{1,13},{5,9},{9,5},{13,1},{2,14},{6,10},... | collective-permute-start | bytes 417800 | tf_op jit(solution)/shard_map/ppermute | solution.py:499
  8.5 0.0 collective-permute-start.1
  8.5 0.6 %collective-permute-start = (bf16[2,272,128]{2,1,0:T(8,128)(2,1)S(1)}, bf16[2,272,128]{2,1,0:T(8,128)(2,1)S(1)}, u32[]{:S(2)}, u32[]{:S(2)}) collective-permute-start(bf16[2,272,128]{2,1,0:T(8,128)(2,1)S(1)} %merge.1.refs_0_), channel_id=1, source_target_pairs={{0,4},{4,0},{8,12},{12,8},{1,5},{5,1},{9,13},{13,9},{2,6},{6,2},{1... | collective-permute-start | bytes 417800 | tf_op jit(solution)/shard_map/ppermute | solution.py:499
  9.9 7.3 %features.1 = (bf16[2176,128]{1,0:T(8,128)(2,1)S(1)}, bf16[2176,128]{1,0:T(8,128)(2,1)S(1)}, bf16[896,1024]{1,0:T(8,128)(2,1)S(1)}, f32[8,1024]{1,0:T(8,128)S(1)}) custom-call(s32[1]{0:T(128)S(6)} %copy.13.live_in_ref, s32[8,128]{1,0:T(8,128)S(1)} %bitcast.8, s32[1,128]{1,0:T(1,128)S(1)} %bitcast.11, f32[1,1024]{1,0:T(1,128)S(1)} %bitcast.9, ...), custom_call_target="tpu_custom_call" | custom-call | flops 8999999488 | bytes 7000000 | tf_op jit(solution)/shard_map/features/pallas_call | solution.py:219
  17.2 3.1 %collective-permute-done.1.refs_2_ = bf16[2,272,128]{2,1,0:T(8,128)(2,1)S(1)} collective-permute-done((bf16[2,272,128]{2,1,0:T(8,128)(2,1)S(1)}, bf16[2,272,128]{2,1,0:T(8,128)(2,1)S(1)}, u32[]{:S(2)}, u32[]{:S(2)}) %collective-permute-start.1) | collective-permute-done | bytes 139296 | tf_op jit(solution)/shard_map/ppermute | solution.py:499
  20.3 0.0 collective-permute-start.4
  20.3 0.6 %collective-permute-start.3 = (bf16[4,2,272,128]{3,2,1,0:T(8,128)(2,1)S(1)}, bf16[4,2,272,128]{3,2,1,0:T(8,128)(2,1)S(1)}, u32[]{:S(2)}, u32[]{:S(2)}) collective-permute-start(bf16[4,2,272,128]{3,2,1,0:T(8,128)(2,1)S(1)} %pack.1.rest_0_), channel_id=1, source_target_pairs={{0,1},{1,0},{2,3},{3,2},{4,5},{5,4},{6,7},{7,6},{8,9},{9,8},{10,11... | collective-permute-start | bytes 1671176 | tf_op jit(solution)/shard_map/ppermute | solution.py:499
  20.9 1.3 %collective-permute-done.4.came_ref = bf16[2176,128]{1,0:T(8,128)(2,1)S(1)} collective-permute-done((bf16[2176,128]{1,0:T(8,128)(2,1)S(1)}, bf16[2176,128]{1,0:T(8,128)(2,1)S(1)}, u32[]{:S(2)}, u32[]{:S(2)}) %collective-permute-start.4) | collective-permute-done | bytes 557088 | tf_op jit(solution)/shard_map/ppermute | solution.py:499
  22.2 0.1 pair_sum.1
  22.4 2.6 %collective-permute-start.5 = (bf16[544,128]{1,0:T(8,128)(2,1)S(1)}, bf16[544,128]{1,0:T(8,128)(2,1)S(1)}, u32[]{:S(2)}, u32[]{:S(2)}) collective-permute-start(bf16[544,128]{1,0:T(8,128)(2,1)S(1)} %get-tuple-element.47), channel_id=1, source_target_pairs={{0,12},{4,8},{8,4},{12,0},{1,13},{5,9},{9,5},{13,1},{2,14},{6,10},... | collective-permute-start | bytes 417800 | tf_op jit(solution)/shard_map/ppermute | solution.py:499
  24.9 0.0 collective-permute-start.6
  24.9 1.9 %collective-permute-start.7 = (bf16[544,128]{1,0:T(8,128)(2,1)S(1)}, bf16[544,128]{1,0:T(8,128)(2,1)S(1)}, u32[]{:S(2)}, u32[]{:S(2)}) collective-permute-start(bf16[544,128]{1,0:T(8,128)(2,1)S(1)} %get-tuple-element.49), channel_id=1, source_target_pairs={{0,4},{4,0},{8,12},{12,8},{1,5},{5,1},{9,13},{13,9},{2,6},{6,2},{1... | collective-permute-start | bytes 417800 | tf_op jit(solution)/shard_map/ppermute | solution.py:499
  26.8 0.0 collective-permute-done.3.rest_1_
  26.8 5.5 %back.1 = (f32[9,128,128]{2,1,0:T(8,128)S(1)}, bf16[9,32,128]{2,1,0:T(8,128)(2,1)S(1)}, bf16[9,32,128]{2,1,0:T(8,128)(2,1)S(1)}, bf16[9,32,128]{2,1,0:T(8,128)(2,1)S(1)}, bf16[9,32,128]{2,1,0:T(8,128)(2,1)S(1)}) custom-call(f32[8,1024]{1,0:T(8,128)S(1)} %get-tuple-element.36.edge_ref, f32[1,1024]{1,0:T(1,128)S(1)} %bitcast.10, f32[3,3,1024]{2,1,0:T(4,128)S(1)} %copy-done.5, ...), custom_call_target="tpu_custom_call" | custom-call | flops 8999999488 | bytes 7000000 | tf_op jit(solution)/shard_map/back/pallas_call | solution.py:337
  32.3 2.6 %collective-permute-start.8 = (bf16[9,32,128]{2,1,0:T(8,128)(2,1)S(1)}, bf16[9,32,128]{2,1,0:T(8,128)(2,1)S(1)}, u32[]{:S(2)}, u32[]{:S(2)}) collective-permute-start(bf16[9,32,128]{2,1,0:T(8,128)(2,1)S(1)} %get-tuple-element.54), channel_id=1, source_target_pairs={{4,8},{8,4},{12,0},{0,12},{5,9},{9,5},{13,1},{1,13},{6,10},{10,6},... | collective-permute-start | bytes 221192 | tf_op jit(solution)/shard_map/ppermute | solution.py:508
  34.9 0.1 collective-permute-start.9
  35.0 0.0 collective-permute-start.10
  35.0 2.2 %collective-permute-done.6.refs_2_ = bf16[544,128]{1,0:T(8,128)(2,1)S(1)} collective-permute-done((bf16[544,128]{1,0:T(8,128)(2,1)S(1)}, bf16[544,128]{1,0:T(8,128)(2,1)S(1)}, u32[]{:S(2)}, u32[]{:S(2)}) %collective-permute-start.6) | collective-permute-done | bytes 139296 | tf_op jit(solution)/shard_map/ppermute | solution.py:499
  37.1 0.0 collective-permute-start.11
  37.1 0.0 collective-permute-done.7.refs_3_
  37.1 0.1 total_sum.1.refs_0_
  37.2 1.4 %collective-permute-done.8.a_ref = bf16[9,32,128]{2,1,0:T(8,128)(2,1)S(1)} collective-permute-done((bf16[9,32,128]{2,1,0:T(8,128)(2,1)S(1)}, bf16[9,32,128]{2,1,0:T(8,128)(2,1)S(1)}, u32[]{:S(2)}, u32[]{:S(2)}) %collective-permute-start.8) | collective-permute-done | bytes 73760 | tf_op jit(solution)/shard_map/ppermute | solution.py:508
  38.6 0.8 %collective-permute-done.9.b_ref = bf16[9,32,128]{2,1,0:T(8,128)(2,1)S(1)} collective-permute-done((bf16[9,32,128]{2,1,0:T(8,128)(2,1)S(1)}, bf16[9,32,128]{2,1,0:T(8,128)(2,1)S(1)}, u32[]{:S(2)}, u32[]{:S(2)}) %collective-permute-start.9) | collective-permute-done | bytes 73760 | tf_op jit(solution)/shard_map/ppermute | solution.py:508
  39.4 0.4 collective-permute-done.10.c_ref
  39.8 0.0 collective-permute-done.11.d_ref
  39.8 2.0 %collective-permute-start.12 = (bf16[544,128]{1,0:T(8,128)(2,1)S(1)}, bf16[544,128]{1,0:T(8,128)(2,1)S(1)}, u32[]{:S(2)}, u32[]{:S(2)}) collective-permute-start(bf16[544,128]{1,0:T(8,128)(2,1)S(1)} %total_sum.1.refs_0_), channel_id=1, source_target_pairs={{0,2},{1,3},{2,0},{3,1},{4,6},{5,7},{6,4},{7,5},{8,10},{9,11},{10,... | collective-permute-start | bytes 417800 | tf_op jit(solution)/shard_map/ppermute | solution.py:499
  41.8 1.2 %finish.1 = bf16[9,128,128]{2,1,0:T(8,128)(2,1)} custom-call(s32[4,32]{1,0:T(4,128)S(1)} %copy-done.1, f32[9,128,128]{2,1,0:T(8,128)S(1)} %get-tuple-element.59.own_ref, bf16[9,32,128]{2,1,0:T(8,128)(2,1)S(1)} %collective-permute-done.8.a_ref, bf16[9,32,128]{2,1,0:T(8,128)(2,1)S(1)} %collective-permute-done.9.b_ref, ...), custom_call_target="tpu_custom_call" | custom-call | flops 100000000 | bytes 2000000 | tf_op jit(solution)/shard_map/finish/pallas_call | solution.py:487
  43.0 2.6 %collective-permute-done.12.refs_1_ = bf16[544,128]{1,0:T(8,128)(2,1)S(1)} collective-permute-done((bf16[544,128]{1,0:T(8,128)(2,1)S(1)}, bf16[544,128]{1,0:T(8,128)(2,1)S(1)}, u32[]{:S(2)}, u32[]{:S(2)}) %collective-permute-start.12) | collective-permute-done | bytes 139296 | tf_op jit(solution)/shard_map/ppermute | solution.py:499
  45.6 1.4 %collective-permute-done.14.refs_3_ = bf16[544,128]{1,0:T(8,128)(2,1)S(1)} collective-permute-done((bf16[544,128]{1,0:T(8,128)(2,1)S(1)}, bf16[544,128]{1,0:T(8,128)(2,1)S(1)}, u32[]{:S(2)}, u32[]{:S(2)}) %collective-permute-start.14) | collective-permute-done | bytes 139296 | tf_op jit(solution)/shard_map/ppermute | solution.py:499
  47.0 1.5 %expert_product.1 = f32[8,69632]{1,0:T(8,128)} custom-call(f32[2,32]{1,0:T(2,128)S(1)} %copy-done, bf16[544,128]{1,0:T(8,128)(2,1)S(1)} %total_sum.1.refs_0_, bf16[544,128]{1,0:T(8,128)(2,1)S(1)} %collective-permute-done.12.refs_1_, bf16[544,128]{1,0:T(8,128)(2,1)S(1)} %collective-permute-done.13.refs_2_, bf16[544,128]{1,0:T(8,128)(2,1)S(1)} %collective-permute-done.14.refs_3_), custom_call_target="tpu_custom_call" | custom-call | flops 1000000 | bytes 4000000 | tf_op jit(solution)/shard_map/expert_product/pallas_call | solution.py:452
  (24 shorter events, 0.1 us)
Async XLA Ops:
  0.6 0.7 %copy-start = (f32[2,32]{1,0:T(2,128)S(1)}, f32[2,32]{1,0:T(2,128)}, u32[]{:S(2)}) copy-start(f32[2,32]{1,0:T(2,128)} %coef_ref.1) | copy-start | bytes 772
  1.3 8.5 %copy-start.2 = (bf16[256,9,128]{2,0,1:T(8,128)(2,1)S(1)}, bf16[256,9,128]{2,0,1:T(8,128)(2,1)}, u32[]{:S(2)}) copy-start(bf16[256,9,128]{2,0,1:T(8,128)(2,1)} %param.11) | copy-start | bytes 1769476
  1.3 8.5 %copy-start.3 = (bf16[128,9,128]{2,0,1:T(8,128)(2,1)S(1)}, bf16[128,9,128]{2,0,1:T(8,128)(2,1)}, u32[]{:S(2)}) copy-start(bf16[128,9,128]{2,0,1:T(8,128)(2,1)} %param.12) | copy-start | bytes 884740
  1.3 8.5 %copy-start.4 = (f32[5,5,1024]{2,1,0:T(8,128)S(1)}, f32[5,5,1024]{2,1,0:T(8,128)}, u32[]{:S(2)}) copy-start(f32[5,5,1024]{2,1,0:T(8,128)} %two_ref.3) | copy-start | bytes 307204
  1.3 8.5 %copy-start.5 = (f32[3,3,1024]{2,1,0:T(4,128)S(1)}, f32[3,3,1024]{2,1,0:T(4,128)}, u32[]{:S(2)}) copy-start(f32[3,3,1024]{2,1,0:T(4,128)} %one_ref.3) | copy-start | bytes 110596
  1.3 8.5 %copy-start.6 = (s32[128,8]{0,1:T(8,128)S(1)}, s32[128,8]{0,1:T(8,128)}, u32[]{:S(2)}) copy-start(s32[128,8]{0,1:T(8,128)} %param.13) | copy-start | bytes 12292
  1.3 8.5 %copy-start.7 = (f32[1024]{0:T(1024)S(1)}, f32[1024]{0:T(1024)}, u32[]{:S(2)}) copy-start(f32[1024]{0:T(1024)} %param.14) | copy-start | bytes 12292
  1.3 8.5 %copy-start.8 = (s32[128]{0:T(128)S(1)}, s32[128]{0:T(128)}, u32[]{:S(2)}) copy-start(s32[128]{0:T(128)} %param.18) | copy-start | bytes 1540
  3.4 13.8 %collective-permute-start.2 = (bf16[2,272,128]{2,1,0:T(8,128)(2,1)S(1)}, bf16[2,272,128]{2,1,0:T(8,128)(2,1)S(1)}, u32[]{:S(2)}, u32[]{:S(2)}) collective-permute-start(bf16[2,272,128]{2,1,0:T(8,128)(2,1)S(1)} %merge.1.refs_0_), channel_id=1, source_target_pairs={{0,12},{4,8},{8,4},{12,0},{1,13},{5,9},{9,5},{13,1},{2,14},{6,10},... | collective-permute-start | bytes 417800 | tf_op jit(solution)/shard_map/ppermute | solution.py:499
  8.5 11.8 %collective-permute-start.1 = (bf16[2,272,128]{2,1,0:T(8,128)(2,1)S(1)}, bf16[2,272,128]{2,1,0:T(8,128)(2,1)S(1)}, u32[]{:S(2)}, u32[]{:S(2)}) collective-permute-start(bf16[2,272,128]{2,1,0:T(8,128)(2,1)S(1)} %merge.1.refs_0_), channel_id=1, source_target_pairs={{0,8},{4,12},{8,0},{12,4},{1,9},{5,13},{9,1},{13,5},{2,10},{6,14},... | collective-permute-start | bytes 417800 | tf_op jit(solution)/shard_map/ppermute | solution.py:499
  8.5 11.8 %collective-permute-start = (bf16[2,272,128]{2,1,0:T(8,128)(2,1)S(1)}, bf16[2,272,128]{2,1,0:T(8,128)(2,1)S(1)}, u32[]{:S(2)}, u32[]{:S(2)}) collective-permute-start(bf16[2,272,128]{2,1,0:T(8,128)(2,1)S(1)} %merge.1.refs_0_), channel_id=1, source_target_pairs={{0,4},{4,0},{8,12},{12,8},{1,5},{5,1},{9,13},{13,9},{2,6},{6,2},{1... | collective-permute-start | bytes 417800 | tf_op jit(solution)/shard_map/ppermute | solution.py:499
  20.3 2.0 %collective-permute-start.4 = (bf16[2176,128]{1,0:T(8,128)(2,1)S(1)}, bf16[2176,128]{1,0:T(8,128)(2,1)S(1)}, u32[]{:S(2)}, u32[]{:S(2)}) collective-permute-start(bf16[2176,128]{1,0:T(8,128)(2,1)S(1)} %get-tuple-element.45), channel_id=1, source_target_pairs={{0,1},{1,0},{2,3},{3,2},{4,5},{5,4},{6,7},{7,6},{8,9},{9,8},{10,11... | collective-permute-start | bytes 1671176 | tf_op jit(solution)/shard_map/ppermute | solution.py:499
  20.3 6.5 %collective-permute-start.3 = (bf16[4,2,272,128]{3,2,1,0:T(8,128)(2,1)S(1)}, bf16[4,2,272,128]{3,2,1,0:T(8,128)(2,1)S(1)}, u32[]{:S(2)}, u32[]{:S(2)}) collective-permute-start(bf16[4,2,272,128]{3,2,1,0:T(8,128)(2,1)S(1)} %pack.1.rest_0_), channel_id=1, source_target_pairs={{0,1},{1,0},{2,3},{3,2},{4,5},{5,4},{6,7},{7,6},{8,9},{9,8},{10,11... | collective-permute-start | bytes 1671176 | tf_op jit(solution)/shard_map/ppermute | solution.py:499
  22.4 12.6 %collective-permute-start.5 = (bf16[544,128]{1,0:T(8,128)(2,1)S(1)}, bf16[544,128]{1,0:T(8,128)(2,1)S(1)}, u32[]{:S(2)}, u32[]{:S(2)}) collective-permute-start(bf16[544,128]{1,0:T(8,128)(2,1)S(1)} %get-tuple-element.47), channel_id=1, source_target_pairs={{0,12},{4,8},{8,4},{12,0},{1,13},{5,9},{9,5},{13,1},{2,14},{6,10},... | collective-permute-start | bytes 417800 | tf_op jit(solution)/shard_map/ppermute | solution.py:499
  24.9 12.2 %collective-permute-start.6 = (bf16[544,128]{1,0:T(8,128)(2,1)S(1)}, bf16[544,128]{1,0:T(8,128)(2,1)S(1)}, u32[]{:S(2)}, u32[]{:S(2)}) collective-permute-start(bf16[544,128]{1,0:T(8,128)(2,1)S(1)} %get-tuple-element.48), channel_id=1, source_target_pairs={{0,8},{4,12},{8,0},{12,4},{1,9},{5,13},{9,1},{13,5},{2,10},{6,14},... | collective-permute-start | bytes 417800 | tf_op jit(solution)/shard_map/ppermute | solution.py:499
  24.9 12.2 %collective-permute-start.7 = (bf16[544,128]{1,0:T(8,128)(2,1)S(1)}, bf16[544,128]{1,0:T(8,128)(2,1)S(1)}, u32[]{:S(2)}, u32[]{:S(2)}) collective-permute-start(bf16[544,128]{1,0:T(8,128)(2,1)S(1)} %get-tuple-element.49), channel_id=1, source_target_pairs={{0,4},{4,0},{8,12},{12,8},{1,5},{5,1},{9,13},{13,9},{2,6},{6,2},{1... | collective-permute-start | bytes 417800 | tf_op jit(solution)/shard_map/ppermute | solution.py:499
  26.8 15.0 %copy-start.1 = (s32[4,32]{1,0:T(4,128)S(1)}, s32[4,32]{1,0:T(4,128)}, u32[]{:S(2)}) copy-start(s32[4,32]{1,0:T(4,128)} %send_ref.1) | copy-start | bytes 1540
  32.3 6.3 %collective-permute-start.8 = (bf16[9,32,128]{2,1,0:T(8,128)(2,1)S(1)}, bf16[9,32,128]{2,1,0:T(8,128)(2,1)S(1)}, u32[]{:S(2)}, u32[]{:S(2)}) collective-permute-start(bf16[9,32,128]{2,1,0:T(8,128)(2,1)S(1)} %get-tuple-element.54), channel_id=1, source_target_pairs={{4,8},{8,4},{12,0},{0,12},{5,9},{9,5},{13,1},{1,13},{6,10},{10,6},... | collective-permute-start | bytes 221192 | tf_op jit(solution)/shard_map/ppermute | solution.py:508
  34.9 4.5 %collective-permute-start.9 = (bf16[9,32,128]{2,1,0:T(8,128)(2,1)S(1)}, bf16[9,32,128]{2,1,0:T(8,128)(2,1)S(1)}, u32[]{:S(2)}, u32[]{:S(2)}) collective-permute-start(bf16[9,32,128]{2,1,0:T(8,128)(2,1)S(1)} %get-tuple-element.55), channel_id=1, source_target_pairs={{1,2},{2,1},{3,0},{0,3},{5,6},{6,5},{7,4},{4,7},{9,10},{10,9},{11,... | collective-permute-start | bytes 221192 | tf_op jit(solution)/shard_map/ppermute | solution.py:508
  35.0 4.8 %collective-permute-start.10 = (bf16[9,32,128]{2,1,0:T(8,128)(2,1)S(1)}, bf16[9,32,128]{2,1,0:T(8,128)(2,1)S(1)}, u32[]{:S(2)}, u32[]{:S(2)}) collective-permute-start(bf16[9,32,128]{2,1,0:T(8,128)(2,1)S(1)} %get-tuple-element.56), channel_id=1, source_target_pairs={{0,4},{4,0},{8,12},{12,8},{1,5},{5,1},{9,13},{13,9},{2,6},{6,2},{1... | collective-permute-start | bytes 221192 | tf_op jit(solution)/shard_map/ppermute | solution.py:508
  37.1 2.7 %collective-permute-start.11 = (bf16[9,32,128]{2,1,0:T(8,128)(2,1)S(1)}, bf16[9,32,128]{2,1,0:T(8,128)(2,1)S(1)}, u32[]{:S(2)}, u32[]{:S(2)}) collective-permute-start(bf16[9,32,128]{2,1,0:T(8,128)(2,1)S(1)} %get-tuple-element.57), channel_id=1, source_target_pairs={{0,1},{1,0},{2,3},{3,2},{4,5},{5,4},{6,7},{7,6},{8,9},{9,8},{10,11... | collective-permute-start | bytes 221192 | tf_op jit(solution)/shard_map/ppermute | solution.py:508
  39.8 5.8 %collective-permute-start.12 = (bf16[544,128]{1,0:T(8,128)(2,1)S(1)}, bf16[544,128]{1,0:T(8,128)(2,1)S(1)}, u32[]{:S(2)}, u32[]{:S(2)}) collective-permute-start(bf16[544,128]{1,0:T(8,128)(2,1)S(1)} %total_sum.1.refs_0_), channel_id=1, source_target_pairs={{0,2},{1,3},{2,0},{3,1},{4,6},{5,7},{6,4},{7,5},{8,10},{9,11},{10,... | collective-permute-start | bytes 417800 | tf_op jit(solution)/shard_map/ppermute | solution.py:499
  41.8 3.8 %collective-permute-start.13 = (bf16[544,128]{1,0:T(8,128)(2,1)S(1)}, bf16[544,128]{1,0:T(8,128)(2,1)S(1)}, u32[]{:S(2)}, u32[]{:S(2)}) collective-permute-start(bf16[544,128]{1,0:T(8,128)(2,1)S(1)} %total_sum.1.refs_0_), channel_id=1, source_target_pairs={{0,1},{1,0},{2,3},{3,2},{4,5},{5,4},{6,7},{7,6},{8,9},{9,8},{10,11... | collective-permute-start | bytes 417800 | tf_op jit(solution)/shard_map/ppermute | solution.py:499
  45.6 1.4 %collective-permute-start.14 = (bf16[544,128]{1,0:T(8,128)(2,1)S(1)}, bf16[544,128]{1,0:T(8,128)(2,1)S(1)}, u32[]{:S(2)}, u32[]{:S(2)}) collective-permute-start(bf16[544,128]{1,0:T(8,128)(2,1)S(1)} %collective-permute-done.12.refs_1_), channel_id=1, source_target_pairs={{0,1},{1,0},{2,3},{3,2},{4,5},{5,4},{6,7},{7,6},{8,9},{9,8},{10,11... | collective-permute-start | bytes 417800 | tf_op jit(solution)/shard_map/ppermute | solution.py:499

commit v9 on v4

--- a/solution.py
+++ b/solution.py
@@ -18,7 +18,6 @@
 SLOT = {component: place for place, component in enumerate(STACK)}
 
 VMEM = pl.BlockSpec(memory_space=pltpu.VMEM)
-SMEM = pl.BlockSpec(memory_space=pltpu.SMEM)
 HBM = pl.BlockSpec(memory_space=pltpu.HBM)
 
 
@@ -46,8 +45,8 @@
     return high, middle, low
 
 
-def merge_kernel(coef_ref, experts_ref, out_ref, held, arrived):
-    members, experts = coef_ref.shape
+def merge_kernel(coef_in_ref, experts_ref, out_ref, held, coef_ref, arrived, coef_arrived):
+    members, experts = coef_in_ref.shape
     rows = out_ref.shape[1]
     start = pl.multiple_of(lax.rem(lax.axis_index("gx"), 2) * rows * 128, 128)
     stripes = arrived.shape[0]
@@ -62,6 +61,9 @@
             )
         )
         copies[-1].start()
+    coef_copy = pltpu.make_async_copy(coef_in_ref, coef_ref, coef_arrived)
+    coef_copy.start()
+    coef_copy.wait()
     wide = 8 * experts
     row = lax.broadcasted_iota(jnp.int32, (8, wide), 0)
     col = lax.broadcasted_iota(jnp.int32, (8, wide), 1)
@@ -99,18 +101,23 @@
     rows = columns // 128
     return pl.pallas_call(
         merge_kernel,
-        in_specs=[VMEM, HBM],
+        in_specs=[HBM, HBM],
         out_specs=VMEM,
         out_shape=jax.ShapeDtypeStruct((members, rows, 128), BF16),
-        scratch_shapes=[pltpu.VMEM((count, columns), BF16), pltpu.SemaphoreType.DMA((4,))],
-        compiler_params=limits(60),
+        scratch_shapes=[
+            pltpu.VMEM((count, columns), BF16),
+            pltpu.VMEM((members, count), F32),
+            pltpu.SemaphoreType.DMA((2,)),
+            pltpu.SemaphoreType.DMA,
+        ],
+        compiler_params=limits(52),
         cost_estimate=cost(96 * 16 * columns, 2 * count * columns),
         name="merge",
     )(coef, experts)
 
 
 def features_kernel(
-    live_ref, near_ref, class_ref, zero_ref, one_ref, two_ref, source_ref, target_ref,
+    near_ref, class_ref, zero_ref, one_ref, two_ref, source_ref, target_ref,
     other_ref, own_ref, pulled_ref, edge_ref,
     source_t, target_t, moved, spread, rotated, grads,
     *, fanout,
@@ -123,7 +130,6 @@
         target_t[c * channels : (c + 1) * channels, :] = target_ref[c].T
     near = near_ref[...].astype(F32).astype(BF16)
     classes = class_ref[...].astype(F32).astype(BF16)
-    live_edges = live_ref[0] * LIVE_BLOCK * fanout
     scale = 1.0 / math.sqrt(fanout)
 
     def chunk_step(chunk, carry):
@@ -138,7 +144,7 @@
         near_row = jnp.sum(picked, axis=0, keepdims=True)
         class_row = nn(classes, repeat)
         edge_ref[0:1, here] = near_row
-        edge_ref[1:2, here] = jnp.where(edge8[0:1] < live_edges, class_row, -1.0)
+        edge_ref[1:2, here] = class_row
         slot = lax.broadcasted_iota(jnp.int32, (slots, CHUNK), 0).astype(F32)
         pick = (slot == near_row).astype(F32).astype(BF16)
         moved[...] = nn(source_t[...], pick)
@@ -200,14 +206,14 @@
         out_ref[...] = grads[...].astype(BF16)
 
 
-def features(live, near, classes, zero, one, two, source, target, rows, fanout):
+def features(near, classes, zero, one, two, source, target, rows, fanout):
     slots, channels = source.shape[1:]
     atoms = target.shape[1]
     edges = atoms * fanout
     shape = jax.ShapeDtypeStruct
     return pl.pallas_call(
         functools.partial(features_kernel, fanout=fanout),
-        in_specs=[SMEM] + [VMEM] * 7,
+        in_specs=[VMEM] * 7,
         out_specs=[VMEM] * 4,
         out_shape=[
             shape((rows, 128), BF16),
@@ -226,7 +232,7 @@
         compiler_params=limits(24),
         cost_estimate=cost(9 * 10**9, 7 * 10**6),
         name="features",
-    )(live, near, classes, zero, one, two, source, target)
+    )(near, classes, zero, one, two, source, target)
 
 
 def back_kernel(
@@ -375,6 +381,8 @@
     for k, out_ref in enumerate(out_refs, 1):
         at = pl.ds(k * half, half)
         out_ref[:half] = (keep_ref[at, :] + came_ref[at, :].astype(F32)).astype(BF16)
+    for out_ref in out_refs[1:-1]:
+        out_ref[half:] = jnp.zeros_like(out_ref[half:])
     out_refs[0][half:] = low_ref[...]
     out_refs[-1][half:] = high_ref[...]
 
@@ -383,7 +391,8 @@
     half = keep.shape[0] // count
     faces = low.shape[0]
     shape = jax.ShapeDtypeStruct
-    sent = [shape((half + (faces if k in (1, count - 1) else 0), 128), BF16) for k in range(1, count)]
+    spare = max(faces + 16 - half, 0)
+    sent = [shape((half + (faces if k in (1, count - 1) else spare), 128), BF16) for k in range(1, count)]
     return pl.pallas_call(
         side_kernel,
         in_specs=[VMEM] * 4,
@@ -433,7 +442,7 @@
 
 
 def expert_kernel(coef_ref, *refs, scale):
-    sums, out_ref, summed = refs[:-2], refs[-2], refs[-1]
+    sums, out_ref, summed, staged, written = refs[:-4], *refs[-4:]
     owned = out_ref.shape[0]
     place = lax.axis_index("gx")
     row = lax.broadcasted_iota(jnp.int32, (owned, coef_ref.shape[1]), 0)
@@ -454,10 +463,20 @@
     else:
         for index, ref in enumerate(sums):
             summed[index] = ref[...].astype(F32)
-    for row in range(summed.shape[1]):
-        out_ref[:, row * 128 : (row + 1) * 128] = (
-            first * summed[0, row : row + 1, :] + second * summed[1, row : row + 1, :]
-        )
+    rows = summed.shape[1]
+    stripes = written.shape[0]
+    copies = []
+    for stripe in range(stripes):
+        low, high = rows * stripe // stripes, rows * (stripe + 1) // stripes
+        for row in range(low, high):
+            staged[:, row * 128 : (row + 1) * 128] = (
+                first * summed[0, row : row + 1, :] + second * summed[1, row : row + 1, :]
+            )
+        span = pl.ds(low * 128, (high - low) * 128)
+        copies.append(pltpu.make_async_copy(staged.at[:, span], out_ref.at[:, span], written.at[stripe]))
+        copies[-1].start()
+    for copy in copies:
+        copy.wait()
 
 
 def expert_product(coef, sums, owned, scale):
@@ -465,9 +484,13 @@
     return pl.pallas_call(
         functools.partial(expert_kernel, scale=scale),
         in_specs=[VMEM] * (1 + len(sums)),
-        out_specs=VMEM,
+        out_specs=HBM,
         out_shape=jax.ShapeDtypeStruct((owned, rows * 128), F32),
-        scratch_shapes=[pltpu.VMEM((2, rows, 128), F32)],
+        scratch_shapes=[
+            pltpu.VMEM((2, rows, 128), F32),
+            pltpu.VMEM((owned, rows * 128), F32),
+            pltpu.SemaphoreType.DMA((4,)),
+        ],
         compiler_params=limits(8),
         cost_estimate=cost(10**6, 4 * 10**6),
         name="expert_product",
@@ -536,15 +559,19 @@
     source = jnp.transpose(saved_input, (1, 0, 2))
     target = jnp.transpose(cotangent, (1, 0, 2))
 
+    alive = jnp.arange(atoms, dtype=jnp.int32) < live_blocks[0] * LIVE_BLOCK
+    classes = jnp.where(alive, atom_class, -1).reshape(1, -1)
+    merge_coef, classes = lax.optimization_barrier((merge_coef, classes))
+
     if direct:
         half = height // 2
         mine = merge(merge_coef, experts, 2)
-        held = [mine] + [swap(mine, "yz", k) for k in range(1, count_yz)]
+        held = [mine] + [swap(mine, "yz", k) for k in (3, 2, 1)]
         source, target, mine = lax.optimization_barrier((source, target, mine))
 
         def places():
             here, side = lax.axis_index("yz"), lax.rem(lax.axis_index("gx"), 2)
-            starts = [(here ^ k) * height for k in range(count_yz)]
+            starts = [(here ^ k) * height for k in (0, 3, 2, 1)]
             return [at + side * half for at in starts] + [at + (1 - side) * half for at in starts]
     else:
         part = jnp.dot(merge_coef, experts.astype(F32), precision=lax.Precision.HIGHEST).astype(BF16)
@@ -555,7 +582,7 @@
             return [0]
 
     other, own, pulled, edge = features(
-        live_blocks, neighbours.T, atom_class.reshape(1, -1), zero, rot_one, rot_two, source, target, rows, fanout
+        neighbours.T, classes, zero, rot_one, rot_two, source, target, rows, fanout
     )
     if direct:
         other, *held = lax.optimization_barrier((other, *held))
@@ -567,11 +594,12 @@
     grad_own, *ghosts = back(edge, zero, rot_one, rot_two, pulled, pieces, places, rows, atoms, slots, face)
     across_gx = [neighbour_pairs(ghosts[first], "gx", first) for first in range(2)]
     if direct:
+        order = (3, 2, 1)
         parts = side_sum(keep, opposite, ghosts[2], ghosts[3], count_yz)
-        gathered = [parts[0]] + [swap(parts[k], "yz", k) for k in range(1, count_yz)]
+        gathered = [parts[0]] + [swap(parts[k], "yz", k) for k in order]
         summed, *across_gx = lax.optimization_barrier((total_sum(gathered), *across_gx))
         across = swap(summed, "gx", 2)
-        input_grad = finish(send_index, grad_own, [*across_gx, gathered[1], gathered[3]])
+        input_grad = finish(send_index, grad_own, [*across_gx, gathered[3], gathered[1]])
         across, input_grad = lax.optimization_barrier((across, input_grad))
         sums = [summed, across, swap(summed, "gx", 1), swap(across, "gx", 1)]
     else:

time: 53.1 us -> 51.6 us (0.972)
  Pallas kernels: 19.3 us -> 17.7 us
  waiting for transfers between devices: 16.6 us -> 15.5 us
  other arithmetic: 0 us -> 0.66 us
  local copies, waits for them, and re-layouts: 0.05 us -> 0.71 us
    pallas_call x1, Pallas kernels: 3.39 us -> 2.03 us  [merge(): pl.pallas_call(merge_kernel, in_specs=[HBM, HBM], out_specs=VMEM, out_sha...]
    ppermute x12, waiting for transfers between devices: 16.6 us -> 15.5 us  [swap(): lax.ppermute(value, axis, [(i, i ^ bit) for i in range(lax.axis_size(axis...]
    unnamed x20 -> x16, local copies, waits for them, and re-layouts: 0.05 us -> 0.71 us
    reshape x0 -> x1, other arithmetic: none -> 0.66 us  [local(): classes = jnp.where(alive, atom_class, -1).reshape(1, -1)]
  transfers between devices with their start and end apart: 14 -> 14, of which waited for: 6 -> 7; matrix products, arithmetic and copies ran while one was open for 0% -> 0% of each run, Pallas kernels for 27% -> 27%
where the time goes in v9:
time: 51.6 us; the launch traced here: 51.4 us
  Pallas kernels  17.7 us (34%)
  starting transfers between devices  15.5 us (30%)
  waiting for transfers between devices  15.5 us (30%)
  between operations  1.39 us (3%)
  local copies, waits for them, and re-layouts  0.71 us (1%)
  other arithmetic  0.66 us (1%)
    ppermute x12, waiting for transfers between devices, swap(): lax.ppermute(value, axis, [(i, i ^ bit) for i in range(lax.axis_size(axis...  15.5 us
    ppermute x12, starting transfers between devices, swap(): lax.ppermute(value, axis, [(i, i ^ bit) for i in range(lax.axis_size(axis...  13.9 us
    pallas_call x1, Pallas kernels, features(): pl.pallas_call(functools.partial(features_kernel, fanout=fanout), in_spec...  7.2 us
    pallas_call x1, Pallas kernels, back(): pl.pallas_call(functools.partial(back_kernel, pieces=len(pieces), members...  5.48 us
    pallas_call x1, Pallas kernels, merge(): pl.pallas_call(merge_kernel, in_specs=[HBM, HBM], out_specs=VMEM, out_sha...  2.03 us
    ppermute x2, starting transfers between devices, neighbour_pairs(): return lax.ppermute(value, axis, moves)  1.6 us
    pallas_call x1, Pallas kernels, expert_product(): pl.pallas_call(functools.partial(expert_kernel, scale=scale), in_specs=[V...  1.54 us
    pallas_call x1, Pallas kernels, finish(): pl.pallas_call(finish_kernel, in_specs=[VMEM] * 6, out_specs=VMEM, out_sh...  1.16 us
  transfers between devices with their start and end apart: 14, of which 7 were waited for; matrix products, arithmetic and copies ran while one was open for 0% of the time, Pallas kernels for 27%

profile of v9, /device:TPU:0, one launch (start us, length us, event | category | flops | bytes accessed | tf_op | source)
XLA Modules:
  0.0 51.4 jit_solution(653614708249798803)
XLA Ops:
  1.3 0.7 %fusion.class_ref = s32[1,128]{1,0:T(1,128)S(1)} fusion(s32[128]{0:T(128)} %param.18, s32[]{:T(128)} %bitcast.1), kind=kLoop, calls=%fused_computation.1 | loop fusion | flops 256 | bytes 1028 | tf_op jit(solution)/shard_map/reshape | solution.py:563
  1.9 0.7 %copy-done = f32[2,32]{1,0:T(2,128)S(1)} copy-done((f32[2,32]{1,0:T(2,128)S(1)}, f32[2,32]{1,0:T(2,128)}, u32[]{:S(2)}) %copy-start) | copy-done | bytes 280
  2.6 0.0 copy-start.6
  2.6 0.0 copy-start.7
  2.7 2.0 %merge.1.refs_0_ = bf16[2,272,128]{2,1,0:T(8,128)(2,1)S(1)} custom-call(f32[2,32]{1,0:T(2,128)S(1)} %copy-done, bf16[32,69632]{1,0:T(8,128)(2,1)} %experts_ref.1), custom_call_target="tpu_custom_call" | custom-call | flops 53477376 | bytes 2228224 | tf_op jit(solution)/shard_map/merge/pallas_call | solution.py:102
  4.7 5.1 %collective-permute-start = (bf16[2,272,128]{2,1,0:T(8,128)(2,1)S(1)}, bf16[2,272,128]{2,1,0:T(8,128)(2,1)S(1)}, u32[]{:S(2)}, u32[]{:S(2)}) collective-permute-start(bf16[2,272,128]{2,1,0:T(8,128)(2,1)S(1)} %merge.1.refs_0_), channel_id=1, source_target_pairs={{0,12},{4,8},{8,4},{12,0},{1,13},{5,9},{9,5},{13,1},{2,14},{6,10},... | collective-permute-start | bytes 417800 | tf_op jit(solution)/shard_map/ppermute | solution.py:531
  9.8 0.0 collective-permute-start.1
  9.8 0.6 %collective-permute-start.2 = (bf16[2,272,128]{2,1,0:T(8,128)(2,1)S(1)}, bf16[2,272,128]{2,1,0:T(8,128)(2,1)S(1)}, u32[]{:S(2)}, u32[]{:S(2)}) collective-permute-start(bf16[2,272,128]{2,1,0:T(8,128)(2,1)S(1)} %merge.1.refs_0_), channel_id=1, source_target_pairs={{0,4},{4,0},{8,12},{12,8},{1,5},{5,1},{9,13},{13,9},{2,6},{6,2},{1... | collective-permute-start | bytes 417800 | tf_op jit(solution)/shard_map/ppermute | solution.py:531
  10.5 7.2 %features.1 = (bf16[2176,128]{1,0:T(8,128)(2,1)S(1)}, bf16[2176,128]{1,0:T(8,128)(2,1)S(1)}, bf16[896,1024]{1,0:T(8,128)(2,1)S(1)}, f32[8,1024]{1,0:T(8,128)S(1)}) custom-call(s32[8,128]{1,0:T(8,128)S(1)} %bitcast.10, s32[1,128]{1,0:T(1,128)S(1)} %fusion.class_ref, f32[1,1024]{1,0:T(1,128)S(1)} %bitcast.11, f32[3,3,1024]{2,1,0:T(4,128)S(1)} %copy-done.5, ...), custom_call_target="tpu_custom_call" | custom-call | flops 8999999488 | bytes 7000000 | tf_op jit(solution)/shard_map/features/pallas_call | solution.py:214
  17.7 0.0 collective-permute-done.refs_1_
  17.7 3.9 %collective-permute-done.1.refs_2_ = bf16[2,272,128]{2,1,0:T(8,128)(2,1)S(1)} collective-permute-done((bf16[2,272,128]{2,1,0:T(8,128)(2,1)S(1)}, bf16[2,272,128]{2,1,0:T(8,128)(2,1)S(1)}, u32[]{:S(2)}, u32[]{:S(2)}) %collective-permute-start.1) | collective-permute-done | bytes 139296 | tf_op jit(solution)/shard_map/ppermute | solution.py:531
  21.6 0.6 %collective-permute-start.5 = (bf16[4,2,272,128]{3,2,1,0:T(8,128)(2,1)S(1)}, bf16[4,2,272,128]{3,2,1,0:T(8,128)(2,1)S(1)}, u32[]{:S(2)}, u32[]{:S(2)}) collective-permute-start(bf16[4,2,272,128]{3,2,1,0:T(8,128)(2,1)S(1)} %pack.1.rest_0_), channel_id=1, source_target_pairs={{0,1},{1,0},{2,3},{3,2},{4,5},{5,4},{6,7},{7,6},{8,9},{9,8},{10,11... | collective-permute-start | bytes 1671176 | tf_op jit(solution)/shard_map/ppermute | solution.py:531
  22.2 1.3 %collective-permute-done.3.came_ref = bf16[2176,128]{1,0:T(8,128)(2,1)S(1)} collective-permute-done((bf16[2176,128]{1,0:T(8,128)(2,1)S(1)}, bf16[2176,128]{1,0:T(8,128)(2,1)S(1)}, u32[]{:S(2)}, u32[]{:S(2)}) %collective-permute-start.3) | collective-permute-done | bytes 557088 | tf_op jit(solution)/shard_map/ppermute | solution.py:531
  23.5 0.1 core_sum.1
  23.7 1.6 %collective-permute-start.4 = (bf16[1088,128]{1,0:T(8,128)(2,1)S(1)}, bf16[1088,128]{1,0:T(8,128)(2,1)S(1)}, u32[]{:S(2)}, u32[]{:S(2)}) collective-permute-start(bf16[1088,128]{1,0:T(8,128)(2,1)S(1)} %get-tuple-element.39), channel_id=1, source_target_pairs={{0,2},{1,3},{2,0},{3,1},{4,6},{5,7},{6,4},{7,5},{8,10},{9,11},{10,... | collective-permute-start | bytes 835592 | tf_op jit(solution)/shard_map/ppermute | solution.py:531
  25.2 0.0 collective-permute-done.5.rest_1_
  25.2 5.5 %back.1 = (f32[9,128,128]{2,1,0:T(8,128)S(1)}, bf16[288,128]{1,0:T(8,128)(2,1)S(1)}, bf16[288,128]{1,0:T(8,128)(2,1)S(1)}, bf16[288,128]{1,0:T(8,128)(2,1)S(1)}, bf16[288,128]{1,0:T(8,128)(2,1)S(1)}) custom-call(f32[8,1024]{1,0:T(8,128)S(1)} %get-tuple-element.40.edge_ref, f32[1,1024]{1,0:T(1,128)S(1)} %bitcast.12, f32[3,3,1024]{2,1,0:T(4,128)S(1)} %copy-done.5, ...), custom_call_target="tpu_custom_call" | custom-call | flops 8999999488 | bytes 7000000 | tf_op jit(solution)/shard_map/back/pallas_call | solution.py:331
  30.7 1.7 %collective-permute-done.4.came_ref = bf16[1088,128]{1,0:T(8,128)(2,1)S(1)} collective-permute-done((bf16[1088,128]{1,0:T(8,128)(2,1)S(1)}, bf16[1088,128]{1,0:T(8,128)(2,1)S(1)}, u32[]{:S(2)}, u32[]{:S(2)}) %collective-permute-start.4) | collective-permute-done | bytes 278560 | tf_op jit(solution)/shard_map/ppermute | solution.py:531
  32.4 0.1 side_sum.1
  32.5 2.6 %collective-permute-start.6 = (bf16[560,128]{1,0:T(8,128)(2,1)S(1)}, bf16[560,128]{1,0:T(8,128)(2,1)S(1)}, u32[]{:S(2)}, u32[]{:S(2)}) collective-permute-start(bf16[560,128]{1,0:T(8,128)(2,1)S(1)} %get-tuple-element.49), channel_id=1, source_target_pairs={{0,12},{4,8},{8,4},{12,0},{1,13},{5,9},{9,5},{13,1},{2,14},{6,10},... | collective-permute-start | bytes 430088 | tf_op jit(solution)/shard_map/ppermute | solution.py:531
  35.0 0.0 collective-permute-start.8
  35.0 1.9 %collective-permute-start.7 = (bf16[304,128]{1,0:T(8,128)(2,1)S(1)}, bf16[304,128]{1,0:T(8,128)(2,1)S(1)}, u32[]{:S(2)}, u32[]{:S(2)}) collective-permute-start(bf16[304,128]{1,0:T(8,128)(2,1)S(1)} %get-tuple-element.50), channel_id=1, source_target_pairs={{0,8},{4,12},{8,0},{12,4},{1,9},{5,13},{9,1},{13,5},{2,10},{6,14},... | collective-permute-start | bytes 233480 | tf_op jit(solution)/shard_map/ppermute | solution.py:531
  36.9 1.6 %collective-permute-start.10 = (bf16[288,128]{1,0:T(8,128)(2,1)S(1)}, bf16[288,128]{1,0:T(8,128)(2,1)S(1)}, u32[]{:S(2)}, u32[]{:S(2)}) collective-permute-start(bf16[288,128]{1,0:T(8,128)(2,1)S(1)} %get-tuple-element.53), channel_id=1, source_target_pairs={{1,2},{2,1},{3,0},{0,3},{5,6},{6,5},{7,4},{4,7},{9,10},{10,9},{11,... | collective-permute-start | bytes 221192 | tf_op jit(solution)/shard_map/ppermute | solution.py:540
  38.5 3.7 %collective-permute-done.7.refs_2_ = bf16[304,128]{1,0:T(8,128)(2,1)S(1)} collective-permute-done((bf16[304,128]{1,0:T(8,128)(2,1)S(1)}, bf16[304,128]{1,0:T(8,128)(2,1)S(1)}, u32[]{:S(2)}, u32[]{:S(2)}) %collective-permute-start.7) | collective-permute-done | bytes 77856 | tf_op jit(solution)/shard_map/ppermute | solution.py:531
  42.3 0.0 collective-permute-done.6.refs_1_.d_ref
  42.3 1.9 %collective-permute-done.8.refs_3_.c_ref = bf16[560,128]{1,0:T(8,128)(2,1)S(1)} collective-permute-done((bf16[560,128]{1,0:T(8,128)(2,1)S(1)}, bf16[560,128]{1,0:T(8,128)(2,1)S(1)}, u32[]{:S(2)}, u32[]{:S(2)}) %collective-permute-start.8) | collective-permute-done | bytes 143392 | tf_op jit(solution)/shard_map/ppermute | solution.py:531
  44.2 0.0 collective-permute-done.10.b_ref
  44.2 1.6 %collective-permute-start.11 = (bf16[272,128]{1,0:T(8,128)(2,1)S(1)}, bf16[272,128]{1,0:T(8,128)(2,1)S(1)}, u32[]{:S(2)}, u32[]{:S(2)}) collective-permute-start(bf16[272,128]{1,0:T(8,128)(2,1)S(1)} %total_sum.1.refs_0_), channel_id=1, source_target_pairs={{0,2},{1,3},{2,0},{3,1},{4,6},{5,7},{6,4},{7,5},{8,10},{9,11},{10,... | collective-permute-start | bytes 208904 | tf_op jit(solution)/shard_map/ppermute | solution.py:531
  45.8 1.2 %finish.1 = bf16[9,128,128]{2,1,0:T(8,128)(2,1)} custom-call(s32[4,32]{1,0:T(4,128)S(1)} %copy-done.1, f32[9,128,128]{2,1,0:T(8,128)S(1)} %get-tuple-element.55.own_ref, bf16[288,128]{1,0:T(8,128)(2,1)S(1)} %collective-permute-done.9.a_ref, bf16[288,128]{1,0:T(8,128)(2,1)S(1)} %collective-permute-done.10.b_ref, ...), custom_call_target="tpu_custom_call" | custom-call | flops 100000000 | bytes 2000000 | tf_op jit(solution)/shard_map/finish/pallas_call | solution.py:519
  47.0 1.7 %collective-permute-done.11.refs_1_ = bf16[272,128]{1,0:T(8,128)(2,1)S(1)} collective-permute-done((bf16[272,128]{1,0:T(8,128)(2,1)S(1)}, bf16[272,128]{1,0:T(8,128)(2,1)S(1)}, u32[]{:S(2)}, u32[]{:S(2)}) %collective-permute-start.11) | collective-permute-done | bytes 69664 | tf_op jit(solution)/shard_map/ppermute | solution.py:531
  48.6 1.3 %collective-permute-done.13.refs_3_ = bf16[272,128]{1,0:T(8,128)(2,1)S(1)} collective-permute-done((bf16[272,128]{1,0:T(8,128)(2,1)S(1)}, bf16[272,128]{1,0:T(8,128)(2,1)S(1)}, u32[]{:S(2)}, u32[]{:S(2)}) %collective-permute-start.13) | collective-permute-done | bytes 69664 | tf_op jit(solution)/shard_map/ppermute | solution.py:531
  49.9 1.5 %expert_product.1 = f32[8,69632]{1,0:T(8,128)} custom-call(f32[2,32]{1,0:T(2,128)S(1)} %copy-done, bf16[272,128]{1,0:T(8,128)(2,1)S(1)} %total_sum.1.refs_0_, bf16[272,128]{1,0:T(8,128)(2,1)S(1)} %collective-permute-done.11.refs_1_, bf16[272,128]{1,0:T(8,128)(2,1)S(1)} %collective-permute-done.12.refs_2_, bf16[272,128]{1,0:T(8,128)(2,1)S(1)} %collective-permute-done.13.refs_3_), custom_call_target="tpu_custom_call" | custom-call | flops 1000000 | bytes 4000000 | tf_op jit(solution)/shard_map/expert_product/pallas_call | solution.py:484
  (22 shorter events, 0.1 us)
Async XLA Ops:
  1.9 0.7 %copy-start = (f32[2,32]{1,0:T(2,128)S(1)}, f32[2,32]{1,0:T(2,128)}, u32[]{:S(2)}) copy-start(f32[2,32]{1,0:T(2,128)} %coef_ref) | copy-start | bytes 772
  2.6 7.8 %copy-start.2 = (bf16[256,9,128]{2,0,1:T(8,128)(2,1)S(1)}, bf16[256,9,128]{2,0,1:T(8,128)(2,1)}, u32[]{:S(2)}) copy-start(bf16[256,9,128]{2,0,1:T(8,128)(2,1)} %param.11) | copy-start | bytes 1769476
  2.6 7.8 %copy-start.3 = (bf16[128,9,128]{2,0,1:T(8,128)(2,1)S(1)}, bf16[128,9,128]{2,0,1:T(8,128)(2,1)}, u32[]{:S(2)}) copy-start(bf16[128,9,128]{2,0,1:T(8,128)(2,1)} %param.12) | copy-start | bytes 884740
  2.6 7.8 %copy-start.4 = (f32[5,5,1024]{2,1,0:T(8,128)S(1)}, f32[5,5,1024]{2,1,0:T(8,128)}, u32[]{:S(2)}) copy-start(f32[5,5,1024]{2,1,0:T(8,128)} %two_ref.3) | copy-start | bytes 307204
  2.6 7.8 %copy-start.5 = (f32[3,3,1024]{2,1,0:T(4,128)S(1)}, f32[3,3,1024]{2,1,0:T(4,128)}, u32[]{:S(2)}) copy-start(f32[3,3,1024]{2,1,0:T(4,128)} %one_ref.3) | copy-start | bytes 110596
  2.6 7.8 %copy-start.6 = (s32[128,8]{0,1:T(8,128)S(1)}, s32[128,8]{0,1:T(8,128)}, u32[]{:S(2)}) copy-start(s32[128,8]{0,1:T(8,128)} %param.13) | copy-start | bytes 12292
  2.6 7.8 %copy-start.7 = (f32[1024]{0:T(1024)S(1)}, f32[1024]{0:T(1024)}, u32[]{:S(2)}) copy-start(f32[1024]{0:T(1024)} %param.14) | copy-start | bytes 12292
  4.7 13.0 %collective-permute-start = (bf16[2,272,128]{2,1,0:T(8,128)(2,1)S(1)}, bf16[2,272,128]{2,1,0:T(8,128)(2,1)S(1)}, u32[]{:S(2)}, u32[]{:S(2)}) collective-permute-start(bf16[2,272,128]{2,1,0:T(8,128)(2,1)S(1)} %merge.1.refs_0_), channel_id=1, source_target_pairs={{0,12},{4,8},{8,4},{12,0},{1,13},{5,9},{9,5},{13,1},{2,14},{6,10},... | collective-permute-start | bytes 417800 | tf_op jit(solution)/shard_map/ppermute | solution.py:531
  9.8 11.8 %collective-permute-start.1 = (bf16[2,272,128]{2,1,0:T(8,128)(2,1)S(1)}, bf16[2,272,128]{2,1,0:T(8,128)(2,1)S(1)}, u32[]{:S(2)}, u32[]{:S(2)}) collective-permute-start(bf16[2,272,128]{2,1,0:T(8,128)(2,1)S(1)} %merge.1.refs_0_), channel_id=1, source_target_pairs={{0,8},{4,12},{8,0},{12,4},{1,9},{5,13},{9,1},{13,5},{2,10},{6,14},... | collective-permute-start | bytes 417800 | tf_op jit(solution)/shard_map/ppermute | solution.py:531
  9.8 11.8 %collective-permute-start.2 = (bf16[2,272,128]{2,1,0:T(8,128)(2,1)S(1)}, bf16[2,272,128]{2,1,0:T(8,128)(2,1)S(1)}, u32[]{:S(2)}, u32[]{:S(2)}) collective-permute-start(bf16[2,272,128]{2,1,0:T(8,128)(2,1)S(1)} %merge.1.refs_0_), channel_id=1, source_target_pairs={{0,4},{4,0},{8,12},{12,8},{1,5},{5,1},{9,13},{13,9},{2,6},{6,2},{1... | collective-permute-start | bytes 417800 | tf_op jit(solution)/shard_map/ppermute | solution.py:531
  21.6 2.0 %collective-permute-start.3 = (bf16[2176,128]{1,0:T(8,128)(2,1)S(1)}, bf16[2176,128]{1,0:T(8,128)(2,1)S(1)}, u32[]{:S(2)}, u32[]{:S(2)}) collective-permute-start(bf16[2176,128]{1,0:T(8,128)(2,1)S(1)} %get-tuple-element.37), channel_id=1, source_target_pairs={{0,1},{1,0},{2,3},{3,2},{4,5},{5,4},{6,7},{7,6},{8,9},{9,8},{10,11... | collective-permute-start | bytes 1671176 | tf_op jit(solution)/shard_map/ppermute | solution.py:531
  21.6 3.6 %collective-permute-start.5 = (bf16[4,2,272,128]{3,2,1,0:T(8,128)(2,1)S(1)}, bf16[4,2,272,128]{3,2,1,0:T(8,128)(2,1)S(1)}, u32[]{:S(2)}, u32[]{:S(2)}) collective-permute-start(bf16[4,2,272,128]{3,2,1,0:T(8,128)(2,1)S(1)} %pack.1.rest_0_), channel_id=1, source_target_pairs={{0,1},{1,0},{2,3},{3,2},{4,5},{5,4},{6,7},{7,6},{8,9},{9,8},{10,11... | collective-permute-start | bytes 1671176 | tf_op jit(solution)/shard_map/ppermute | solution.py:531
  23.7 8.8 %collective-permute-start.4 = (bf16[1088,128]{1,0:T(8,128)(2,1)S(1)}, bf16[1088,128]{1,0:T(8,128)(2,1)S(1)}, u32[]{:S(2)}, u32[]{:S(2)}) collective-permute-start(bf16[1088,128]{1,0:T(8,128)(2,1)S(1)} %get-tuple-element.39), channel_id=1, source_target_pairs={{0,2},{1,3},{2,0},{3,1},{4,6},{5,7},{6,4},{7,5},{8,10},{9,11},{10,... | collective-permute-start | bytes 835592 | tf_op jit(solution)/shard_map/ppermute | solution.py:531
  25.2 20.6 %copy-start.1 = (s32[4,32]{1,0:T(4,128)S(1)}, s32[4,32]{1,0:T(4,128)}, u32[]{:S(2)}) copy-start(s32[4,32]{1,0:T(4,128)} %send_ref.1) | copy-start | bytes 1540
  32.5 9.8 %collective-permute-start.6 = (bf16[560,128]{1,0:T(8,128)(2,1)S(1)}, bf16[560,128]{1,0:T(8,128)(2,1)S(1)}, u32[]{:S(2)}, u32[]{:S(2)}) collective-permute-start(bf16[560,128]{1,0:T(8,128)(2,1)S(1)} %get-tuple-element.49), channel_id=1, source_target_pairs={{0,12},{4,8},{8,4},{12,0},{1,13},{5,9},{9,5},{13,1},{2,14},{6,10},... | collective-permute-start | bytes 430088 | tf_op jit(solution)/shard_map/ppermute | solution.py:531
  35.0 9.1 %collective-permute-start.8 = (bf16[560,128]{1,0:T(8,128)(2,1)S(1)}, bf16[560,128]{1,0:T(8,128)(2,1)S(1)}, u32[]{:S(2)}, u32[]{:S(2)}) collective-permute-start(bf16[560,128]{1,0:T(8,128)(2,1)S(1)} %get-tuple-element.51), channel_id=1, source_target_pairs={{0,4},{4,0},{8,12},{12,8},{1,5},{5,1},{9,13},{13,9},{2,6},{6,2},{1... | collective-permute-start | bytes 430088 | tf_op jit(solution)/shard_map/ppermute | solution.py:531
  35.0 7.2 %collective-permute-start.7 = (bf16[304,128]{1,0:T(8,128)(2,1)S(1)}, bf16[304,128]{1,0:T(8,128)(2,1)S(1)}, u32[]{:S(2)}, u32[]{:S(2)}) collective-permute-start(bf16[304,128]{1,0:T(8,128)(2,1)S(1)} %get-tuple-element.50), channel_id=1, source_target_pairs={{0,8},{4,12},{8,0},{12,4},{1,9},{5,13},{9,1},{13,5},{2,10},{6,14},... | collective-permute-start | bytes 233480 | tf_op jit(solution)/shard_map/ppermute | solution.py:531
  36.9 7.3 %collective-permute-start.9 = (bf16[288,128]{1,0:T(8,128)(2,1)S(1)}, bf16[288,128]{1,0:T(8,128)(2,1)S(1)}, u32[]{:S(2)}, u32[]{:S(2)}) collective-permute-start(bf16[288,128]{1,0:T(8,128)(2,1)S(1)} %get-tuple-element.52), channel_id=1, source_target_pairs={{0,1},{1,0},{2,3},{3,2},{4,5},{5,4},{6,7},{7,6},{8,9},{9,8},{10,11... | collective-permute-start | bytes 221192 | tf_op jit(solution)/shard_map/ppermute | solution.py:540
  36.9 7.3 %collective-permute-start.10 = (bf16[288,128]{1,0:T(8,128)(2,1)S(1)}, bf16[288,128]{1,0:T(8,128)(2,1)S(1)}, u32[]{:S(2)}, u32[]{:S(2)}) collective-permute-start(bf16[288,128]{1,0:T(8,128)(2,1)S(1)} %get-tuple-element.53), channel_id=1, source_target_pairs={{1,2},{2,1},{3,0},{0,3},{5,6},{6,5},{7,4},{4,7},{9,10},{10,9},{11,... | collective-permute-start | bytes 221192 | tf_op jit(solution)/shard_map/ppermute | solution.py:540
  44.2 4.4 %collective-permute-start.11 = (bf16[272,128]{1,0:T(8,128)(2,1)S(1)}, bf16[272,128]{1,0:T(8,128)(2,1)S(1)}, u32[]{:S(2)}, u32[]{:S(2)}) collective-permute-start(bf16[272,128]{1,0:T(8,128)(2,1)S(1)} %total_sum.1.refs_0_), channel_id=1, source_target_pairs={{0,2},{1,3},{2,0},{3,1},{4,6},{5,7},{6,4},{7,5},{8,10},{9,11},{10,... | collective-permute-start | bytes 208904 | tf_op jit(solution)/shard_map/ppermute | solution.py:531
  45.8 2.8 %collective-permute-start.12 = (bf16[272,128]{1,0:T(8,128)(2,1)S(1)}, bf16[272,128]{1,0:T(8,128)(2,1)S(1)}, u32[]{:S(2)}, u32[]{:S(2)}) collective-permute-start(bf16[272,128]{1,0:T(8,128)(2,1)S(1)} %total_sum.1.refs_0_), channel_id=1, source_target_pairs={{0,1},{1,0},{2,3},{3,2},{4,5},{5,4},{6,7},{7,6},{8,9},{9,8},{10,11... | collective-permute-start | bytes 208904 | tf_op jit(solution)/shard_map/ppermute | solution.py:531
  48.6 1.3 %collective-permute-start.13 = (bf16[272,128]{1,0:T(8,128)(2,1)S(1)}, bf16[272,128]{1,0:T(8,128)(2,1)S(1)}, u32[]{:S(2)}, u32[]{:S(2)}) collective-permute-start(bf16[272,128]{1,0:T(8,128)(2,1)S(1)} %collective-permute-done.11.refs_1_), channel_id=1, source_target_pairs={{0,1},{1,0},{2,3},{3,2},{4,5},{5,4},{6,7},{7,6},{8,9},{9,8},{10,11... | collective-permute-start | bytes 208904 | tf_op jit(solution)/shard_map/ppermute | solution.py:531

commit v10 on v8

--- a/solution.py
+++ b/solution.py
@@ -117,16 +117,14 @@
 
 
 def features_kernel(
-    live_in_ref, near_ref, class_ref, zero_ref, one_ref, two_ref, source_ref, target_ref,
-    other_ref, own_ref, pulled_ref, edge_ref,
-    source_t, target_t, moved, spread, rotated, grads, live_ref, live_arrived,
-    *, fanout,
+    near_ref, class_ref, zero_ref, one_ref, two_ref, source_ref, target_ref,
+    *refs, fanout, cuts,
 ):
+    other_refs, own_ref, pulled_ref, edge_ref = refs[:cuts], *refs[cuts : cuts + 3]
+    source_t, target_t, moved, spread, rotated, grads = refs[cuts + 3 :]
     slots, channels = source_ref.shape[1:]
     atoms = target_ref.shape[1]
     edges = atoms * fanout
-    live_copy = pltpu.make_async_copy(live_in_ref, live_ref, live_arrived)
-    live_copy.start()
     for c in range(9):
         source_t[c * channels : (c + 1) * channels, :] = source_ref[c].T
         target_t[c * channels : (c + 1) * channels, :] = target_ref[c].T
@@ -187,14 +185,11 @@
         return carry
 
     lax.fori_loop(0, edges // CHUNK, chunk_step, 0)
-    live_copy.wait()
-    edge_row = lax.broadcasted_iota(jnp.int32, (1, edges), 1)
-    edge_ref[1:2, :] = jnp.where(edge_row < live_ref[0] * LIVE_BLOCK * fanout, edge_ref[1:2, :], -1.0)
     zw, pw = 3 * channels, 2 * channels
     first = zw * zw // 128
     second = first + pw * pw // 128
     own = lax.rem(lax.axis_index("gx"), 2).astype(F32)
-    for out_ref, wanted in ((other_ref, 1.0 - own), (own_ref, own)):
+    for out_refs, wanted in ((other_refs, 1.0 - own), ((own_ref,), own)):
         mask = (edge_ref[1:2, :] == wanted).astype(F32).astype(BF16)
         qz = pulled_ref[0:zw, :] * mask
         qp = pulled_ref[zw : zw + pw, :] * mask
@@ -208,20 +203,25 @@
         for j in range(pw // 128):
             grads[pl.ds(first + j, pw, stride=pw // 128), :] = coupled[:, j * 128 : (j + 1) * 128]
             grads[pl.ds(second + j, pw, stride=pw // 128), :] = crossed[:, j * 128 : (j + 1) * 128]
-        out_ref[...] = grads[...].astype(BF16)
-
-
-def features(live, near, classes, zero, one, two, source, target, rows, fanout):
+        height = out_refs[0].shape[0]
+        for index, out_ref in enumerate(out_refs):
+            per = max(len(out_refs) // 4, 1)
+            at = (lax.axis_index("yz") ^ (index // per)) * per * height + index % per * height
+            at = pl.multiple_of(at, 16) if len(out_refs) > 1 else 0
+            out_ref[...] = grads[pl.ds(at, height), :].astype(BF16)
+
+
+def features(near, classes, zero, one, two, source, target, rows, fanout, cuts):
     slots, channels = source.shape[1:]
     atoms = target.shape[1]
     edges = atoms * fanout
     shape = jax.ShapeDtypeStruct
     return pl.pallas_call(
-        functools.partial(features_kernel, fanout=fanout),
-        in_specs=[HBM] + [VMEM] * 7,
-        out_specs=[VMEM] * 4,
+        functools.partial(features_kernel, fanout=fanout, cuts=cuts),
+        in_specs=[VMEM] * 7,
+        out_specs=[VMEM] * (cuts + 3),
         out_shape=[
-            shape((rows, 128), BF16),
+            *[shape((rows // cuts, 128), BF16)] * cuts,
             shape((rows, 128), BF16),
             shape((7 * channels, edges), BF16),
             shape((8, edges), F32),
@@ -233,13 +233,11 @@
             pltpu.VMEM((9 * channels, CHUNK), F32),
             pltpu.VMEM((7 * channels, edges), BF16),
             pltpu.VMEM((rows, 128), F32),
-            pltpu.SMEM((1,), jnp.int32),
-            pltpu.SemaphoreType.DMA,
         ],
         compiler_params=limits(24),
         cost_estimate=cost(9 * 10**9, 7 * 10**6),
         name="features",
-    )(live, near, classes, zero, one, two, source, target)
+    )(near, classes, zero, one, two, source, target)
 
 
 def back_kernel(
@@ -355,25 +353,28 @@
     )(edge, zero, one, two, pulled, *pieces)
 
 
-def pair_kernel(own_ref, came_ref, *out_refs):
-    height = out_refs[0].shape[0]
+def pair_kernel(own_ref, *refs, cuts):
+    came_refs, out_refs = refs[:cuts], refs[cuts:]
     row = lax.axis_index("yz")
-    for index, out_ref in enumerate(out_refs):
-        at = pl.ds(pl.multiple_of((row ^ index) * height, 16), height)
-        out_ref[...] = (own_ref[at, :].astype(F32) + came_ref[at, :].astype(F32)).astype(BF16)
+    per = cuts // len(out_refs)
+    height = came_refs[0].shape[0]
+    for index, came_ref in enumerate(came_refs):
+        at = pl.multiple_of((row ^ (index // per)) * per * height + index % per * height, 16)
+        total = own_ref[pl.ds(at, height), :].astype(F32) + came_ref[...].astype(F32)
+        out_refs[index // per][pl.ds(index % per * height, height), :] = total.astype(BF16)
 
 
 def pair_sum(own, came, count):
     height = own.shape[0] // count
     return pl.pallas_call(
-        pair_kernel,
-        in_specs=[VMEM, VMEM],
+        functools.partial(pair_kernel, cuts=len(came)),
+        in_specs=[VMEM] * (1 + len(came)),
         out_specs=[VMEM] * count,
         out_shape=[jax.ShapeDtypeStruct((height, 128), BF16)] * count,
         compiler_params=limits(6),
         cost_estimate=cost(10**6, 2 * 10**6),
         name="pair_sum",
-    )(own, came)
+    )(own, *came)
 
 
 def total_kernel(*refs):
@@ -521,11 +522,16 @@
     core = column % 2
     height = experts.shape[1] // 128
     rows = height * count_yz
-    direct = height % 32 == 0 and count_yz & (count_yz - 1) == 0 and count_gx == 4
+    direct = height % 32 == 0 and count_yz == 4 and count_gx == 4
+    cuts = 4 if direct else 1
 
     zero = rot_zero.reshape(1, -1)
     source = jnp.transpose(saved_input, (1, 0, 2))
     target = jnp.transpose(cotangent, (1, 0, 2))
+
+    alive = jnp.arange(atoms, dtype=jnp.int32) < live_blocks[0] * LIVE_BLOCK
+    classes = jnp.where(alive, atom_class, -1).reshape(1, -1)
+    experts, classes = lax.optimization_barrier((experts, classes))
 
     if direct:
         half = height // 2
@@ -545,12 +551,13 @@
         def places():
             return [0]
 
-    other, own, pulled, edge = features(
-        live_blocks, neighbours.T, atom_class.reshape(1, -1), zero, rot_one, rot_two, source, target, rows, fanout
+    *other, own, pulled, edge = features(
+        neighbours.T, classes, zero, rot_one, rot_two, source, target, rows, fanout, cuts
     )
     if direct:
-        other, *held = lax.optimization_barrier((other, *held))
-        came = swap(other, "gx", 1)
+        came = [swap(piece, "gx", 1) for piece in other]
+        received = lax.optimization_barrier((*came, *held))
+        came, held = received[:cuts], received[cuts:]
         parts = pair_sum(own, came, count_yz)
         gathered = [parts[0]] + [swap(parts[k], "yz", k) for k in reversed(range(1, count_yz))]
         held = pack(held)
@@ -568,7 +575,7 @@
         across, input_grad = lax.optimization_barrier((across, input_grad))
         sums = [summed, across, swap(summed, "gx", 1), swap(across, "gx", 1)]
     else:
-        mixed = jnp.stack([own, other]).astype(F32)
+        mixed = jnp.stack([own, other[0]]).astype(F32)
         mixed = jnp.where(core == 0, mixed, mixed[::-1])
         whole = lax.psum(mixed, ("yz", "gx"))
         piece = lax.dynamic_slice_in_dim(whole, row * height, height, 1)

time: 48.7 us -> 49.8 us (1.023)
  other arithmetic: 0 us -> 0.66 us
    reshape x0 -> x1, other arithmetic: none -> 0.66 us  [local(): classes = jnp.where(alive, atom_class, -1).reshape(1, -1)]
    ppermute x11 -> x14, waiting for transfers between devices: 10.6 us -> 10.8 us  [swap(): lax.ppermute(value, axis, [(i, i ^ bit) for i in range(lax.axis_size(axis...]
    ppermute x11 -> x14, starting transfers between devices: 12.8 us -> 12.9 us  [swap(): lax.ppermute(value, axis, [(i, i ^ bit) for i in range(lax.axis_size(axis...]
  transfers between devices with their start and end apart: 15 -> 18, of which waited for: 8 -> 8; matrix products, arithmetic and copies ran while one was open for 0% -> 0% of each run, Pallas kernels for 29% -> 28%
where the time goes in v10:
time: 49.8 us; the launch traced here: 49.6 us
  Pallas kernels  17.7 us (36%)
  starting transfers between devices  15.7 us (32%)
  waiting for transfers between devices  13.5 us (27%)
  between operations  1.4 us (3%)
  local copies, waits for them, and re-layouts  0.71 us (1%)
  other arithmetic  0.66 us (1%)
    ppermute x14, starting transfers between devices, swap(): lax.ppermute(value, axis, [(i, i ^ bit) for i in range(lax.axis_size(axis...  12.9 us
    ppermute x14, waiting for transfers between devices, swap(): lax.ppermute(value, axis, [(i, i ^ bit) for i in range(lax.axis_size(axis...  10.8 us
    pallas_call x1, Pallas kernels, features(): pl.pallas_call(functools.partial(features_kernel, fanout=fanout, cuts=cut...  7.2 us
    pallas_call x1, Pallas kernels, back(): pl.pallas_call(functools.partial(back_kernel, pieces=len(pieces), members...  5.48 us
    ppermute x4, starting transfers between devices, neighbour_pairs(): return lax.ppermute(value, axis, moves)  2.86 us
    ppermute x4, waiting for transfers between devices, neighbour_pairs(): return lax.ppermute(value, axis, moves)  2.62 us
    pallas_call x1, Pallas kernels, merge(): pl.pallas_call(merge_kernel, in_specs=[HBM, HBM], out_specs=VMEM, out_sha...  2.03 us
    pallas_call x1, Pallas kernels, expert_product(): pl.pallas_call(functools.partial(expert_kernel, scale=scale), in_specs=[V...  1.54 us
  transfers between devices with their start and end apart: 18, of which 8 were waited for; matrix products, arithmetic and copies ran while one was open for 0% of the time, Pallas kernels for 28%

profile of v10, /device:TPU:0, one launch (start us, length us, event | category | flops | bytes accessed | tf_op | source)
XLA Modules:
  0.0 49.6 jit_solution(3145278840393571950)
XLA Ops:
  1.3 0.7 %fusion.class_ref = s32[1,128]{1,0:T(1,128)S(1)} fusion(s32[128]{0:T(128)} %param.18, s32[]{:T(128)} %bitcast.1), kind=kLoop, calls=%fused_computation.1 | loop fusion | flops 256 | bytes 1028 | tf_op jit(solution)/shard_map/reshape | solution.py:533
  1.9 0.7 %copy-done = f32[2,32]{1,0:T(2,128)S(1)} copy-done((f32[2,32]{1,0:T(2,128)S(1)}, f32[2,32]{1,0:T(2,128)}, u32[]{:S(2)}) %copy-start) | copy-done | bytes 280
  2.6 0.0 copy-start.6
  2.6 0.0 copy-start.7
  2.7 2.0 %merge.1.refs_0_ = bf16[2,272,128]{2,1,0:T(8,128)(2,1)S(1)} custom-call(f32[2,32]{1,0:T(2,128)S(1)} %copy-done, bf16[32,69632]{1,0:T(8,128)(2,1)} %experts_ref), custom_call_target="tpu_custom_call" | custom-call | flops 53477376 | bytes 2228224 | tf_op jit(solution)/shard_map/merge/pallas_call | solution.py:102
  4.7 5.1 %collective-permute-start.6 = (bf16[2,272,128]{2,1,0:T(8,128)(2,1)S(1)}, bf16[2,272,128]{2,1,0:T(8,128)(2,1)S(1)}, u32[]{:S(2)}, u32[]{:S(2)}) collective-permute-start(bf16[2,272,128]{2,1,0:T(8,128)(2,1)S(1)} %merge.1.refs_0_), channel_id=1, source_target_pairs={{0,12},{4,8},{8,4},{12,0},{1,13},{5,9},{9,5},{13,1},{2,14},{6,10},... | collective-permute-start | bytes 417800 | tf_op jit(solution)/shard_map/ppermute | solution.py:500
  9.8 0.6 %collective-permute-start.4 = (bf16[2,272,128]{2,1,0:T(8,128)(2,1)S(1)}, bf16[2,272,128]{2,1,0:T(8,128)(2,1)S(1)}, u32[]{:S(2)}, u32[]{:S(2)}) collective-permute-start(bf16[2,272,128]{2,1,0:T(8,128)(2,1)S(1)} %merge.1.refs_0_), channel_id=1, source_target_pairs={{0,4},{4,0},{8,12},{12,8},{1,5},{5,1},{9,13},{13,9},{2,6},{6,2},{1... | collective-permute-start | bytes 417800 | tf_op jit(solution)/shard_map/ppermute | solution.py:500
  10.5 7.2 %features.1 = (bf16[544,128]{1,0:T(8,128)(2,1)S(1)}, bf16[544,128]{1,0:T(8,128)(2,1)S(1)}, bf16[544,128]{1,0:T(8,128)(2,1)S(1)}, bf16[544,128]{1,0:T(8,128)(2,1)...) custom-call(s32[8,128]{1,0:T(8,128)S(1)} %bitcast.10, ...), custom_call_target="tpu_custom_call" | custom-call | flops 8999999488 | bytes 7000000 | tf_op jit(solution)/shard_map/features/pallas_call | solution.py:219
  17.7 0.1 collective-permute-start
  17.8 0.5 %collective-permute-start.1 = (bf16[544,128]{1,0:T(8,128)(2,1)S(1)}, bf16[544,128]{1,0:T(8,128)(2,1)S(1)}, u32[]{:S(2)}, u32[]{:S(2)}) collective-permute-start(bf16[544,128]{1,0:T(8,128)(2,1)S(1)} %get-tuple-element.49), channel_id=1, source_target_pairs={{0,1},{1,0},{2,3},{3,2},{4,5},{5,4},{6,7},{7,6},{8,9},{9,8},{10,11... | collective-permute-start | bytes 417800 | tf_op jit(solution)/shard_map/ppermute | solution.py:500
  18.3 0.0 collective-permute-done.6.refs_3_
  18.3 0.1 collective-permute-start.2
  18.3 3.2 %collective-permute-done.5.refs_2_ = bf16[2,272,128]{2,1,0:T(8,128)(2,1)S(1)} collective-permute-done((bf16[2,272,128]{2,1,0:T(8,128)(2,1)S(1)}, bf16[2,272,128]{2,1,0:T(8,128)(2,1)S(1)}, u32[]{:S(2)}, u32[]{:S(2)}) %collective-permute-start.5) | collective-permute-done | bytes 139296 | tf_op jit(solution)/shard_map/ppermute | solution.py:500
  21.6 0.0 collective-permute-start.3
  21.6 1.3 %collective-permute-done.3.refs_3_ = bf16[544,128]{1,0:T(8,128)(2,1)S(1)} collective-permute-done((bf16[544,128]{1,0:T(8,128)(2,1)S(1)}, bf16[544,128]{1,0:T(8,128)(2,1)S(1)}, u32[]{:S(2)}, u32[]{:S(2)}) %collective-permute-start.3) | collective-permute-done | bytes 139296 | tf_op jit(solution)/shard_map/ppermute | solution.py:500
  23.0 0.2 collective-permute-start.7
  23.2 0.2 pair_sum.1
  23.4 2.5 %collective-permute-start.8 = (bf16[544,128]{1,0:T(8,128)(2,1)S(1)}, bf16[544,128]{1,0:T(8,128)(2,1)S(1)}, u32[]{:S(2)}, u32[]{:S(2)}) collective-permute-start(bf16[544,128]{1,0:T(8,128)(2,1)S(1)} %get-tuple-element.63), channel_id=1, source_target_pairs={{0,12},{4,8},{8,4},{12,0},{1,13},{5,9},{9,5},{13,1},{2,14},{6,10},... | collective-permute-start | bytes 417800 | tf_op jit(solution)/shard_map/ppermute | solution.py:500
  25.9 1.9 %collective-permute-start.10 = (bf16[544,128]{1,0:T(8,128)(2,1)S(1)}, bf16[544,128]{1,0:T(8,128)(2,1)S(1)}, u32[]{:S(2)}, u32[]{:S(2)}) collective-permute-start(bf16[544,128]{1,0:T(8,128)(2,1)S(1)} %get-tuple-element.65), channel_id=1, source_target_pairs={{0,4},{4,0},{8,12},{12,8},{1,5},{5,1},{9,13},{13,9},{2,6},{6,2},{1... | collective-permute-start | bytes 417800 | tf_op jit(solution)/shard_map/ppermute | solution.py:500
  27.8 5.5 %back.1 = (f32[9,128,128]{2,1,0:T(8,128)S(1)}, bf16[9,32,128]{2,1,0:T(8,128)(2,1)S(1)}, bf16[9,32,128]{2,1,0:T(8,128)(2,1)S(1)}, bf16[9,32,128]{2,1,0:T(8,128)(2,1)S(1)}, bf16[9,32,128]{2,1,0:T(8,128)(2,1)S(1)}) custom-call(f32[8,1024]{1,0:T(8,128)S(1)} %get-tuple-element.46.edge_ref, f32[1,1024]{1,0:T(1,128)S(1)} %bitcast.12, f32[3,3,1024]{2,1,0:T(4,128)S(1)} %copy-done.5, ...), custom_call_target="tpu_custom_call" | custom-call | flops 8999999488 | bytes 7000000 | tf_op jit(solution)/shard_map/back/pallas_call | solution.py:335
  33.3 2.5 %collective-permute-start.11 = (bf16[9,32,128]{2,1,0:T(8,128)(2,1)S(1)}, bf16[9,32,128]{2,1,0:T(8,128)(2,1)S(1)}, u32[]{:S(2)}, u32[]{:S(2)}) collective-permute-start(bf16[9,32,128]{2,1,0:T(8,128)(2,1)S(1)} %get-tuple-element.70), channel_id=1, source_target_pairs={{4,8},{8,4},{12,0},{0,12},{5,9},{9,5},{13,1},{1,13},{6,10},{10,6},... | collective-permute-start | bytes 221192 | tf_op jit(solution)/shard_map/ppermute | solution.py:509
  35.8 0.3 collective-permute-start.12
  36.2 2.1 %collective-permute-done.9.refs_2_ = bf16[544,128]{1,0:T(8,128)(2,1)S(1)} collective-permute-done((bf16[544,128]{1,0:T(8,128)(2,1)S(1)}, bf16[544,128]{1,0:T(8,128)(2,1)S(1)}, u32[]{:S(2)}, u32[]{:S(2)}) %collective-permute-start.9) | collective-permute-done | bytes 139296 | tf_op jit(solution)/shard_map/ppermute | solution.py:500
  38.3 0.1 total_sum.1.refs_0_
  38.4 1.2 %collective-permute-done.11.a_ref = bf16[9,32,128]{2,1,0:T(8,128)(2,1)S(1)} collective-permute-done((bf16[9,32,128]{2,1,0:T(8,128)(2,1)S(1)}, bf16[9,32,128]{2,1,0:T(8,128)(2,1)S(1)}, u32[]{:S(2)}, u32[]{:S(2)}) %collective-permute-start.11) | collective-permute-done | bytes 73760 | tf_op jit(solution)/shard_map/ppermute | solution.py:509
  39.6 0.7 %collective-permute-done.12.b_ref = bf16[9,32,128]{2,1,0:T(8,128)(2,1)S(1)} collective-permute-done((bf16[9,32,128]{2,1,0:T(8,128)(2,1)S(1)}, bf16[9,32,128]{2,1,0:T(8,128)(2,1)S(1)}, u32[]{:S(2)}, u32[]{:S(2)}) %collective-permute-start.12) | collective-permute-done | bytes 73760 | tf_op jit(solution)/shard_map/ppermute | solution.py:509
  40.4 0.6 %collective-permute-done.13.c_ref = bf16[9,32,128]{2,1,0:T(8,128)(2,1)S(1)} collective-permute-done((bf16[9,32,128]{2,1,0:T(8,128)(2,1)S(1)}, bf16[9,32,128]{2,1,0:T(8,128)(2,1)S(1)}, u32[]{:S(2)}, u32[]{:S(2)}) %collective-permute-start.13) | collective-permute-done | bytes 73760 | tf_op jit(solution)/shard_map/ppermute | solution.py:509
  41.0 1.8 %collective-permute-start.15 = (bf16[544,128]{1,0:T(8,128)(2,1)S(1)}, bf16[544,128]{1,0:T(8,128)(2,1)S(1)}, u32[]{:S(2)}, u32[]{:S(2)}) collective-permute-start(bf16[544,128]{1,0:T(8,128)(2,1)S(1)} %total_sum.1.refs_0_), channel_id=1, source_target_pairs={{0,2},{1,3},{2,0},{3,1},{4,6},{5,7},{6,4},{7,5},{8,10},{9,11},{10,... | collective-permute-start | bytes 417800 | tf_op jit(solution)/shard_map/ppermute | solution.py:500
  42.8 1.2 %finish.1 = bf16[9,128,128]{2,1,0:T(8,128)(2,1)} custom-call(s32[4,32]{1,0:T(4,128)S(1)} %copy-done.1, f32[9,128,128]{2,1,0:T(8,128)S(1)} %get-tuple-element.75.own_ref, bf16[9,32,128]{2,1,0:T(8,128)(2,1)S(1)} %collective-permute-done.11.a_ref, bf16[9,32,128]{2,1,0:T(8,128)(2,1)S(1)} %collective-permute-done.12.b_ref, ...), custom_call_target="tpu_custom_call" | custom-call | flops 100000000 | bytes 2000000 | tf_op jit(solution)/shard_map/finish/pallas_call | solution.py:488
  44.0 2.8 %collective-permute-done.15.refs_1_ = bf16[544,128]{1,0:T(8,128)(2,1)S(1)} collective-permute-done((bf16[544,128]{1,0:T(8,128)(2,1)S(1)}, bf16[544,128]{1,0:T(8,128)(2,1)S(1)}, u32[]{:S(2)}, u32[]{:S(2)}) %collective-permute-start.15) | collective-permute-done | bytes 139296 | tf_op jit(solution)/shard_map/ppermute | solution.py:500
  46.7 1.4 %collective-permute-done.17.refs_3_ = bf16[544,128]{1,0:T(8,128)(2,1)S(1)} collective-permute-done((bf16[544,128]{1,0:T(8,128)(2,1)S(1)}, bf16[544,128]{1,0:T(8,128)(2,1)S(1)}, u32[]{:S(2)}, u32[]{:S(2)}) %collective-permute-start.17) | collective-permute-done | bytes 139296 | tf_op jit(solution)/shard_map/ppermute | solution.py:500
  48.1 1.5 %expert_product.1 = f32[8,69632]{1,0:T(8,128)} custom-call(f32[2,32]{1,0:T(2,128)S(1)} %copy-done, bf16[544,128]{1,0:T(8,128)(2,1)S(1)} %total_sum.1.refs_0_, bf16[544,128]{1,0:T(8,128)(2,1)S(1)} %collective-permute-done.15.refs_1_, bf16[544,128]{1,0:T(8,128)(2,1)S(1)} %collective-permute-done.16.refs_2_, bf16[544,128]{1,0:T(8,128)(2,1)S(1)} %collective-permute-done.17.refs_3_), custom_call_target="tpu_custom_call" | custom-call | flops 1000000 | bytes 4000000 | tf_op jit(solution)/shard_map/expert_product/pallas_call | solution.py:453
  (29 shorter events, 0.1 us)
Async XLA Ops:
  1.9 0.7 %copy-start = (f32[2,32]{1,0:T(2,128)S(1)}, f32[2,32]{1,0:T(2,128)}, u32[]{:S(2)}) copy-start(f32[2,32]{1,0:T(2,128)} %coef_ref.1) | copy-start | bytes 772
  2.6 7.8 %copy-start.2 = (bf16[256,9,128]{2,0,1:T(8,128)(2,1)S(1)}, bf16[256,9,128]{2,0,1:T(8,128)(2,1)}, u32[]{:S(2)}) copy-start(bf16[256,9,128]{2,0,1:T(8,128)(2,1)} %param.11) | copy-start | bytes 1769476
  2.6 7.8 %copy-start.3 = (bf16[128,9,128]{2,0,1:T(8,128)(2,1)S(1)}, bf16[128,9,128]{2,0,1:T(8,128)(2,1)}, u32[]{:S(2)}) copy-start(bf16[128,9,128]{2,0,1:T(8,128)(2,1)} %param.12) | copy-start | bytes 884740
  2.6 7.8 %copy-start.4 = (f32[5,5,1024]{2,1,0:T(8,128)S(1)}, f32[5,5,1024]{2,1,0:T(8,128)}, u32[]{:S(2)}) copy-start(f32[5,5,1024]{2,1,0:T(8,128)} %two_ref.3) | copy-start | bytes 307204
  2.6 7.8 %copy-start.5 = (f32[3,3,1024]{2,1,0:T(4,128)S(1)}, f32[3,3,1024]{2,1,0:T(4,128)}, u32[]{:S(2)}) copy-start(f32[3,3,1024]{2,1,0:T(4,128)} %one_ref.3) | copy-start | bytes 110596
  2.6 7.8 %copy-start.6 = (s32[128,8]{0,1:T(8,128)S(1)}, s32[128,8]{0,1:T(8,128)}, u32[]{:S(2)}) copy-start(s32[128,8]{0,1:T(8,128)} %param.13) | copy-start | bytes 12292
  2.6 7.8 %copy-start.7 = (f32[1024]{0:T(1024)S(1)}, f32[1024]{0:T(1024)}, u32[]{:S(2)}) copy-start(f32[1024]{0:T(1024)} %param.14) | copy-start | bytes 12292
  4.7 13.6 %collective-permute-start.6 = (bf16[2,272,128]{2,1,0:T(8,128)(2,1)S(1)}, bf16[2,272,128]{2,1,0:T(8,128)(2,1)S(1)}, u32[]{:S(2)}, u32[]{:S(2)}) collective-permute-start(bf16[2,272,128]{2,1,0:T(8,128)(2,1)S(1)} %merge.1.refs_0_), channel_id=1, source_target_pairs={{0,12},{4,8},{8,4},{12,0},{1,13},{5,9},{9,5},{13,1},{2,14},{6,10},... | collective-permute-start | bytes 417800 | tf_op jit(solution)/shard_map/ppermute | solution.py:500
  9.8 11.8 %collective-permute-start.5 = (bf16[2,272,128]{2,1,0:T(8,128)(2,1)S(1)}, bf16[2,272,128]{2,1,0:T(8,128)(2,1)S(1)}, u32[]{:S(2)}, u32[]{:S(2)}) collective-permute-start(bf16[2,272,128]{2,1,0:T(8,128)(2,1)S(1)} %merge.1.refs_0_), channel_id=1, source_target_pairs={{0,8},{4,12},{8,0},{12,4},{1,9},{5,13},{9,1},{13,5},{2,10},{6,14},... | collective-permute-start | bytes 417800 | tf_op jit(solution)/shard_map/ppermute | solution.py:500
  9.8 11.8 %collective-permute-start.4 = (bf16[2,272,128]{2,1,0:T(8,128)(2,1)S(1)}, bf16[2,272,128]{2,1,0:T(8,128)(2,1)S(1)}, u32[]{:S(2)}, u32[]{:S(2)}) collective-permute-start(bf16[2,272,128]{2,1,0:T(8,128)(2,1)S(1)} %merge.1.refs_0_), channel_id=1, source_target_pairs={{0,4},{4,0},{8,12},{12,8},{1,5},{5,1},{9,13},{13,9},{2,6},{6,2},{1... | collective-permute-start | bytes 417800 | tf_op jit(solution)/shard_map/ppermute | solution.py:500
  17.7 3.9 %collective-permute-start = (bf16[544,128]{1,0:T(8,128)(2,1)S(1)}, bf16[544,128]{1,0:T(8,128)(2,1)S(1)}, u32[]{:S(2)}, u32[]{:S(2)}) collective-permute-start(bf16[544,128]{1,0:T(8,128)(2,1)S(1)} %get-tuple-element.48), channel_id=1, source_target_pairs={{0,1},{1,0},{2,3},{3,2},{4,5},{5,4},{6,7},{7,6},{8,9},{9,8},{10,11... | collective-permute-start | bytes 417800 | tf_op jit(solution)/shard_map/ppermute | solution.py:500
  17.8 3.8 %collective-permute-start.1 = (bf16[544,128]{1,0:T(8,128)(2,1)S(1)}, bf16[544,128]{1,0:T(8,128)(2,1)S(1)}, u32[]{:S(2)}, u32[]{:S(2)}) collective-permute-start(bf16[544,128]{1,0:T(8,128)(2,1)S(1)} %get-tuple-element.49), channel_id=1, source_target_pairs={{0,1},{1,0},{2,3},{3,2},{4,5},{5,4},{6,7},{7,6},{8,9},{9,8},{10,11... | collective-permute-start | bytes 417800 | tf_op jit(solution)/shard_map/ppermute | solution.py:500
  18.3 3.3 %collective-permute-start.2 = (bf16[544,128]{1,0:T(8,128)(2,1)S(1)}, bf16[544,128]{1,0:T(8,128)(2,1)S(1)}, u32[]{:S(2)}, u32[]{:S(2)}) collective-permute-start(bf16[544,128]{1,0:T(8,128)(2,1)S(1)} %get-tuple-element.50), channel_id=1, source_target_pairs={{0,1},{1,0},{2,3},{3,2},{4,5},{5,4},{6,7},{7,6},{8,9},{9,8},{10,11... | collective-permute-start | bytes 417800 | tf_op jit(solution)/shard_map/ppermute | solution.py:500
  21.6 1.4 %collective-permute-start.3 = (bf16[544,128]{1,0:T(8,128)(2,1)S(1)}, bf16[544,128]{1,0:T(8,128)(2,1)S(1)}, u32[]{:S(2)}, u32[]{:S(2)}) collective-permute-start(bf16[544,128]{1,0:T(8,128)(2,1)S(1)} %get-tuple-element.51), channel_id=1, source_target_pairs={{0,1},{1,0},{2,3},{3,2},{4,5},{5,4},{6,7},{7,6},{8,9},{9,8},{10,11... | collective-permute-start | bytes 417800 | tf_op jit(solution)/shard_map/ppermute | solution.py:500
  23.0 4.8 %collective-permute-start.7 = (bf16[4,2,272,128]{3,2,1,0:T(8,128)(2,1)S(1)}, bf16[4,2,272,128]{3,2,1,0:T(8,128)(2,1)S(1)}, u32[]{:S(2)}, u32[]{:S(2)}) collective-permute-start(bf16[4,2,272,128]{3,2,1,0:T(8,128)(2,1)S(1)} %pack.1.rest_0_), channel_id=1, source_target_pairs={{0,1},{1,0},{2,3},{3,2},{4,5},{5,4},{6,7},{7,6},{8,9},{9,8},{10,11... | collective-permute-start | bytes 1671176 | tf_op jit(solution)/shard_map/ppermute | solution.py:500
  23.4 12.8 %collective-permute-start.8 = (bf16[544,128]{1,0:T(8,128)(2,1)S(1)}, bf16[544,128]{1,0:T(8,128)(2,1)S(1)}, u32[]{:S(2)}, u32[]{:S(2)}) collective-permute-start(bf16[544,128]{1,0:T(8,128)(2,1)S(1)} %get-tuple-element.63), channel_id=1, source_target_pairs={{0,12},{4,8},{8,4},{12,0},{1,13},{5,9},{9,5},{13,1},{2,14},{6,10},... | collective-permute-start | bytes 417800 | tf_op jit(solution)/shard_map/ppermute | solution.py:500
  25.9 12.4 %collective-permute-start.9 = (bf16[544,128]{1,0:T(8,128)(2,1)S(1)}, bf16[544,128]{1,0:T(8,128)(2,1)S(1)}, u32[]{:S(2)}, u32[]{:S(2)}) collective-permute-start(bf16[544,128]{1,0:T(8,128)(2,1)S(1)} %get-tuple-element.64), channel_id=1, source_target_pairs={{0,8},{4,12},{8,0},{12,4},{1,9},{5,13},{9,1},{13,5},{2,10},{6,14},... | collective-permute-start | bytes 417800 | tf_op jit(solution)/shard_map/ppermute | solution.py:500
  25.9 12.4 %collective-permute-start.10 = (bf16[544,128]{1,0:T(8,128)(2,1)S(1)}, bf16[544,128]{1,0:T(8,128)(2,1)S(1)}, u32[]{:S(2)}, u32[]{:S(2)}) collective-permute-start(bf16[544,128]{1,0:T(8,128)(2,1)S(1)} %get-tuple-element.65), channel_id=1, source_target_pairs={{0,4},{4,0},{8,12},{12,8},{1,5},{5,1},{9,13},{13,9},{2,6},{6,2},{1... | collective-permute-start | bytes 417800 | tf_op jit(solution)/shard_map/ppermute | solution.py:500
  27.8 15.0 %copy-start.1 = (s32[4,32]{1,0:T(4,128)S(1)}, s32[4,32]{1,0:T(4,128)}, u32[]{:S(2)}) copy-start(s32[4,32]{1,0:T(4,128)} %send_ref.1) | copy-start | bytes 1540
  33.3 6.3 %collective-permute-start.11 = (bf16[9,32,128]{2,1,0:T(8,128)(2,1)S(1)}, bf16[9,32,128]{2,1,0:T(8,128)(2,1)S(1)}, u32[]{:S(2)}, u32[]{:S(2)}) collective-permute-start(bf16[9,32,128]{2,1,0:T(8,128)(2,1)S(1)} %get-tuple-element.70), channel_id=1, source_target_pairs={{4,8},{8,4},{12,0},{0,12},{5,9},{9,5},{13,1},{1,13},{6,10},{10,6},... | collective-permute-start | bytes 221192 | tf_op jit(solution)/shard_map/ppermute | solution.py:509
  35.8 4.5 %collective-permute-start.12 = (bf16[9,32,128]{2,1,0:T(8,128)(2,1)S(1)}, bf16[9,32,128]{2,1,0:T(8,128)(2,1)S(1)}, u32[]{:S(2)}, u32[]{:S(2)}) collective-permute-start(bf16[9,32,128]{2,1,0:T(8,128)(2,1)S(1)} %get-tuple-element.71), channel_id=1, source_target_pairs={{1,2},{2,1},{3,0},{0,3},{5,6},{6,5},{7,4},{4,7},{9,10},{10,9},{11,... | collective-permute-start | bytes 221192 | tf_op jit(solution)/shard_map/ppermute | solution.py:509
  36.2 4.8 %collective-permute-start.13 = (bf16[9,32,128]{2,1,0:T(8,128)(2,1)S(1)}, bf16[9,32,128]{2,1,0:T(8,128)(2,1)S(1)}, u32[]{:S(2)}, u32[]{:S(2)}) collective-permute-start(bf16[9,32,128]{2,1,0:T(8,128)(2,1)S(1)} %get-tuple-element.72), channel_id=1, source_target_pairs={{0,4},{4,0},{8,12},{12,8},{1,5},{5,1},{9,13},{13,9},{2,6},{6,2},{1... | collective-permute-start | bytes 221192 | tf_op jit(solution)/shard_map/ppermute | solution.py:509
  38.3 2.7 %collective-permute-start.14 = (bf16[9,32,128]{2,1,0:T(8,128)(2,1)S(1)}, bf16[9,32,128]{2,1,0:T(8,128)(2,1)S(1)}, u32[]{:S(2)}, u32[]{:S(2)}) collective-permute-start(bf16[9,32,128]{2,1,0:T(8,128)(2,1)S(1)} %get-tuple-element.73), channel_id=1, source_target_pairs={{0,1},{1,0},{2,3},{3,2},{4,5},{5,4},{6,7},{7,6},{8,9},{9,8},{10,11... | collective-permute-start | bytes 221192 | tf_op jit(solution)/shard_map/ppermute | solution.py:509
  41.0 5.7 %collective-permute-start.15 = (bf16[544,128]{1,0:T(8,128)(2,1)S(1)}, bf16[544,128]{1,0:T(8,128)(2,1)S(1)}, u32[]{:S(2)}, u32[]{:S(2)}) collective-permute-start(bf16[544,128]{1,0:T(8,128)(2,1)S(1)} %total_sum.1.refs_0_), channel_id=1, source_target_pairs={{0,2},{1,3},{2,0},{3,1},{4,6},{5,7},{6,4},{7,5},{8,10},{9,11},{10,... | collective-permute-start | bytes 417800 | tf_op jit(solution)/shard_map/ppermute | solution.py:500
  42.8 4.0 %collective-permute-start.16 = (bf16[544,128]{1,0:T(8,128)(2,1)S(1)}, bf16[544,128]{1,0:T(8,128)(2,1)S(1)}, u32[]{:S(2)}, u32[]{:S(2)}) collective-permute-start(bf16[544,128]{1,0:T(8,128)(2,1)S(1)} %total_sum.1.refs_0_), channel_id=1, source_target_pairs={{0,1},{1,0},{2,3},{3,2},{4,5},{5,4},{6,7},{7,6},{8,9},{9,8},{10,11... | collective-permute-start | bytes 417800 | tf_op jit(solution)/shard_map/ppermute | solution.py:500
  46.7 1.4 %collective-permute-start.17 = (bf16[544,128]{1,0:T(8,128)(2,1)S(1)}, bf16[544,128]{1,0:T(8,128)(2,1)S(1)}, u32[]{:S(2)}, u32[]{:S(2)}) collective-permute-start(bf16[544,128]{1,0:T(8,128)(2,1)S(1)} %collective-permute-done.15.refs_1_), channel_id=1, source_target_pairs={{0,1},{1,0},{2,3},{3,2},{4,5},{5,4},{6,7},{7,6},{8,9},{9,8},{10,11... | collective-permute-start | bytes 417800 | tf_op jit(solution)/shard_map/ppermute | solution.py:500

commit v11 on v8

--- a/solution.py
+++ b/solution.py
@@ -9,8 +9,8 @@
 from jax.sharding import PartitionSpec as P
 
 LIVE_BLOCK = 64
-CHUNK = 256
-SUB = 16
+CHUNK = 512
+SUB = 32
 F32 = jnp.float32
 BF16 = jnp.bfloat16
 

time: 48.7 us -> 48.2 us (0.990)
  Pallas kernels: 17.7 us -> 16.6 us
  waiting for transfers between devices: 13.2 us -> 13.8 us
    ppermute x11, waiting for transfers between devices: 10.6 us -> 11.7 us  [swap(): lax.ppermute(value, axis, [(i, i ^ bit) for i in range(lax.axis_size(axis...]
    pallas_call x1, Pallas kernels: 7.27 us -> 6.6 us  [features(): pl.pallas_call(functools.partial(features_kernel, fanout=fanout), in_spec...]
    ppermute x4, waiting for transfers between devices: 2.61 us -> 2.05 us  [neighbour_pairs(): return lax.ppermute(value, axis, moves)]
  transfers between devices with their start and end apart: 15 -> 15, of which waited for: 8 -> 8; matrix products, arithmetic and copies ran while one was open for 0% -> 0% of each run, Pallas kernels for 29% -> 27%
where the time goes in v11:
time: 48.2 us; the launch traced here: 48 us
  Pallas kernels  16.6 us (34%)
  starting transfers between devices  15.5 us (32%)
  waiting for transfers between devices  13.8 us (29%)
  between operations  1.44 us (3%)
  local copies, waits for them, and re-layouts  0.7 us (1%)
    ppermute x11, starting transfers between devices, swap(): lax.ppermute(value, axis, [(i, i ^ bit) for i in range(lax.axis_size(axis...  12.8 us
    ppermute x11, waiting for transfers between devices, swap(): lax.ppermute(value, axis, [(i, i ^ bit) for i in range(lax.axis_size(axis...  11.7 us
    pallas_call x1, Pallas kernels, features(): pl.pallas_call(functools.partial(features_kernel, fanout=fanout), in_spec...  6.6 us
    pallas_call x1, Pallas kernels, back(): pl.pallas_call(functools.partial(back_kernel, pieces=len(pieces), members...  5.01 us
    ppermute x4, starting transfers between devices, neighbour_pairs(): return lax.ppermute(value, axis, moves)  2.67 us
    ppermute x4, waiting for transfers between devices, neighbour_pairs(): return lax.ppermute(value, axis, moves)  2.05 us
    pallas_call x1, Pallas kernels, merge(): pl.pallas_call(merge_kernel, in_specs=[HBM, HBM], out_specs=VMEM, out_sha...  2.03 us
    pallas_call x1, Pallas kernels, expert_product(): pl.pallas_call(functools.partial(expert_kernel, scale=scale), in_specs=[V...  1.54 us
  transfers between devices with their start and end apart: 15, of which 8 were waited for; matrix products, arithmetic and copies ran while one was open for 0% of the time, Pallas kernels for 27%

profile of v11, /device:TPU:0, one launch (start us, length us, event | category | flops | bytes accessed | tf_op | source)
XLA Modules:
  0.0 48.0 jit_solution(10821589570962971764)
XLA Ops:
  0.6 0.7 %copy-done = f32[2,32]{1,0:T(2,128)S(1)} copy-done((f32[2,32]{1,0:T(2,128)S(1)}, f32[2,32]{1,0:T(2,128)}, u32[]{:S(2)}) %copy-start) | copy-done | bytes 280
  1.4 2.0 %merge.1.refs_0_ = bf16[2,272,128]{2,1,0:T(8,128)(2,1)S(1)} custom-call(f32[2,32]{1,0:T(2,128)S(1)} %copy-done, bf16[32,69632]{1,0:T(8,128)(2,1)} %experts_ref.1), custom_call_target="tpu_custom_call" | custom-call | flops 53477376 | bytes 2228224 | tf_op jit(solution)/shard_map/merge/pallas_call | solution.py:102
  3.4 5.1 %collective-permute-start.2 = (bf16[2,272,128]{2,1,0:T(8,128)(2,1)S(1)}, bf16[2,272,128]{2,1,0:T(8,128)(2,1)S(1)}, u32[]{:S(2)}, u32[]{:S(2)}) collective-permute-start(bf16[2,272,128]{2,1,0:T(8,128)(2,1)S(1)} %merge.1.refs_0_), channel_id=1, source_target_pairs={{0,12},{4,8},{8,4},{12,0},{1,13},{5,9},{9,5},{13,1},{2,14},{6,10},... | collective-permute-start | bytes 417800 | tf_op jit(solution)/shard_map/ppermute | solution.py:499
  8.5 0.0 collective-permute-start.1
  8.5 0.6 %collective-permute-start = (bf16[2,272,128]{2,1,0:T(8,128)(2,1)S(1)}, bf16[2,272,128]{2,1,0:T(8,128)(2,1)S(1)}, u32[]{:S(2)}, u32[]{:S(2)}) collective-permute-start(bf16[2,272,128]{2,1,0:T(8,128)(2,1)S(1)} %merge.1.refs_0_), channel_id=1, source_target_pairs={{0,4},{4,0},{8,12},{12,8},{1,5},{5,1},{9,13},{13,9},{2,6},{6,2},{1... | collective-permute-start | bytes 417800 | tf_op jit(solution)/shard_map/ppermute | solution.py:499
  9.9 6.6 %features.1 = (bf16[2176,128]{1,0:T(8,128)(2,1)S(1)}, bf16[2176,128]{1,0:T(8,128)(2,1)S(1)}, bf16[896,1024]{1,0:T(8,128)(2,1)S(1)}, f32[8,1024]{1,0:T(8,128)S(1)}) custom-call(s32[1]{0:T(128)S(6)} %copy.13.live_in_ref, s32[8,128]{1,0:T(8,128)S(1)} %bitcast.8, s32[1,128]{1,0:T(1,128)S(1)} %bitcast.11, f32[1,1024]{1,0:T(1,128)S(1)} %bitcast.9, ...), custom_call_target="tpu_custom_call" | custom-call | flops 8999999488 | bytes 7000000 | tf_op jit(solution)/shard_map/features/pallas_call | solution.py:219
  16.5 0.0 collective-permute-done.2.refs_3_
  16.5 3.8 %collective-permute-done.1.refs_2_ = bf16[2,272,128]{2,1,0:T(8,128)(2,1)S(1)} collective-permute-done((bf16[2,272,128]{2,1,0:T(8,128)(2,1)S(1)}, bf16[2,272,128]{2,1,0:T(8,128)(2,1)S(1)}, u32[]{:S(2)}, u32[]{:S(2)}) %collective-permute-start.1) | collective-permute-done | bytes 139296 | tf_op jit(solution)/shard_map/ppermute | solution.py:499
  20.3 0.6 %collective-permute-start.3 = (bf16[4,2,272,128]{3,2,1,0:T(8,128)(2,1)S(1)}, bf16[4,2,272,128]{3,2,1,0:T(8,128)(2,1)S(1)}, u32[]{:S(2)}, u32[]{:S(2)}) collective-permute-start(bf16[4,2,272,128]{3,2,1,0:T(8,128)(2,1)S(1)} %pack.1.rest_0_), channel_id=1, source_target_pairs={{0,1},{1,0},{2,3},{3,2},{4,5},{5,4},{6,7},{7,6},{8,9},{9,8},{10,11... | collective-permute-start | bytes 1671176 | tf_op jit(solution)/shard_map/ppermute | solution.py:499
  20.9 1.3 %collective-permute-done.4.came_ref = bf16[2176,128]{1,0:T(8,128)(2,1)S(1)} collective-permute-done((bf16[2176,128]{1,0:T(8,128)(2,1)S(1)}, bf16[2176,128]{1,0:T(8,128)(2,1)S(1)}, u32[]{:S(2)}, u32[]{:S(2)}) %collective-permute-start.4) | collective-permute-done | bytes 557088 | tf_op jit(solution)/shard_map/ppermute | solution.py:499
  22.2 0.1 pair_sum.1
  22.4 2.6 %collective-permute-start.5 = (bf16[544,128]{1,0:T(8,128)(2,1)S(1)}, bf16[544,128]{1,0:T(8,128)(2,1)S(1)}, u32[]{:S(2)}, u32[]{:S(2)}) collective-permute-start(bf16[544,128]{1,0:T(8,128)(2,1)S(1)} %get-tuple-element.47), channel_id=1, source_target_pairs={{0,12},{4,8},{8,4},{12,0},{1,13},{5,9},{9,5},{13,1},{2,14},{6,10},... | collective-permute-start | bytes 417800 | tf_op jit(solution)/shard_map/ppermute | solution.py:499
  24.9 0.0 collective-permute-start.6
  24.9 1.9 %collective-permute-start.7 = (bf16[544,128]{1,0:T(8,128)(2,1)S(1)}, bf16[544,128]{1,0:T(8,128)(2,1)S(1)}, u32[]{:S(2)}, u32[]{:S(2)}) collective-permute-start(bf16[544,128]{1,0:T(8,128)(2,1)S(1)} %get-tuple-element.49), channel_id=1, source_target_pairs={{0,4},{4,0},{8,12},{12,8},{1,5},{5,1},{9,13},{13,9},{2,6},{6,2},{1... | collective-permute-start | bytes 417800 | tf_op jit(solution)/shard_map/ppermute | solution.py:499
  26.8 0.0 collective-permute-done.3.rest_1_
  26.8 5.0 %back.1 = (f32[9,128,128]{2,1,0:T(8,128)S(1)}, bf16[9,32,128]{2,1,0:T(8,128)(2,1)S(1)}, bf16[9,32,128]{2,1,0:T(8,128)(2,1)S(1)}, bf16[9,32,128]{2,1,0:T(8,128)(2,1)S(1)}, bf16[9,32,128]{2,1,0:T(8,128)(2,1)S(1)}) custom-call(f32[8,1024]{1,0:T(8,128)S(1)} %get-tuple-element.36.edge_ref, f32[1,1024]{1,0:T(1,128)S(1)} %bitcast.10, f32[3,3,1024]{2,1,0:T(4,128)S(1)} %copy-done.5, ...), custom_call_target="tpu_custom_call" | custom-call | flops 8999999488 | bytes 7000000 | tf_op jit(solution)/shard_map/back/pallas_call | solution.py:337
  31.9 2.6 %collective-permute-start.8 = (bf16[9,32,128]{2,1,0:T(8,128)(2,1)S(1)}, bf16[9,32,128]{2,1,0:T(8,128)(2,1)S(1)}, u32[]{:S(2)}, u32[]{:S(2)}) collective-permute-start(bf16[9,32,128]{2,1,0:T(8,128)(2,1)S(1)} %get-tuple-element.54), channel_id=1, source_target_pairs={{4,8},{8,4},{12,0},{0,12},{5,9},{9,5},{13,1},{1,13},{6,10},{10,6},... | collective-permute-start | bytes 221192 | tf_op jit(solution)/shard_map/ppermute | solution.py:508
  34.4 0.1 collective-permute-start.9
  34.5 0.0 collective-permute-done.5.refs_1_
  34.5 2.6 %collective-permute-done.6.refs_2_ = bf16[544,128]{1,0:T(8,128)(2,1)S(1)} collective-permute-done((bf16[544,128]{1,0:T(8,128)(2,1)S(1)}, bf16[544,128]{1,0:T(8,128)(2,1)S(1)}, u32[]{:S(2)}, u32[]{:S(2)}) %collective-permute-start.6) | collective-permute-done | bytes 139296 | tf_op jit(solution)/shard_map/ppermute | solution.py:499
  37.1 0.0 collective-permute-start.11
  37.1 0.0 collective-permute-done.7.refs_3_
  37.1 0.1 total_sum.1.refs_0_
  37.2 0.9 %collective-permute-done.8.a_ref = bf16[9,32,128]{2,1,0:T(8,128)(2,1)S(1)} collective-permute-done((bf16[9,32,128]{2,1,0:T(8,128)(2,1)S(1)}, bf16[9,32,128]{2,1,0:T(8,128)(2,1)S(1)}, u32[]{:S(2)}, u32[]{:S(2)}) %collective-permute-start.8) | collective-permute-done | bytes 73760 | tf_op jit(solution)/shard_map/ppermute | solution.py:508
  38.1 0.8 %collective-permute-done.9.b_ref = bf16[9,32,128]{2,1,0:T(8,128)(2,1)S(1)} collective-permute-done((bf16[9,32,128]{2,1,0:T(8,128)(2,1)S(1)}, bf16[9,32,128]{2,1,0:T(8,128)(2,1)S(1)}, u32[]{:S(2)}, u32[]{:S(2)}) %collective-permute-start.9) | collective-permute-done | bytes 73760 | tf_op jit(solution)/shard_map/ppermute | solution.py:508
  38.9 0.3 collective-permute-done.10.c_ref
  39.3 0.0 collective-permute-done.11.d_ref
  39.3 2.1 %collective-permute-start.12 = (bf16[544,128]{1,0:T(8,128)(2,1)S(1)}, bf16[544,128]{1,0:T(8,128)(2,1)S(1)}, u32[]{:S(2)}, u32[]{:S(2)}) collective-permute-start(bf16[544,128]{1,0:T(8,128)(2,1)S(1)} %total_sum.1.refs_0_), channel_id=1, source_target_pairs={{0,2},{1,3},{2,0},{3,1},{4,6},{5,7},{6,4},{7,5},{8,10},{9,11},{10,... | collective-permute-start | bytes 417800 | tf_op jit(solution)/shard_map/ppermute | solution.py:499
  41.3 1.2 %finish.1 = bf16[9,128,128]{2,1,0:T(8,128)(2,1)} custom-call(s32[4,32]{1,0:T(4,128)S(1)} %copy-done.1, f32[9,128,128]{2,1,0:T(8,128)S(1)} %get-tuple-element.59.own_ref, bf16[9,32,128]{2,1,0:T(8,128)(2,1)S(1)} %collective-permute-done.8.a_ref, bf16[9,32,128]{2,1,0:T(8,128)(2,1)S(1)} %collective-permute-done.9.b_ref, ...), custom_call_target="tpu_custom_call" | custom-call | flops 100000000 | bytes 2000000 | tf_op jit(solution)/shard_map/finish/pallas_call | solution.py:487
  42.5 2.6 %collective-permute-done.12.refs_1_ = bf16[544,128]{1,0:T(8,128)(2,1)S(1)} collective-permute-done((bf16[544,128]{1,0:T(8,128)(2,1)S(1)}, bf16[544,128]{1,0:T(8,128)(2,1)S(1)}, u32[]{:S(2)}, u32[]{:S(2)}) %collective-permute-start.12) | collective-permute-done | bytes 139296 | tf_op jit(solution)/shard_map/ppermute | solution.py:499
  45.1 1.4 %collective-permute-done.14.refs_3_ = bf16[544,128]{1,0:T(8,128)(2,1)S(1)} collective-permute-done((bf16[544,128]{1,0:T(8,128)(2,1)S(1)}, bf16[544,128]{1,0:T(8,128)(2,1)S(1)}, u32[]{:S(2)}, u32[]{:S(2)}) %collective-permute-start.14) | collective-permute-done | bytes 139296 | tf_op jit(solution)/shard_map/ppermute | solution.py:499
  46.5 1.5 %expert_product.1 = f32[8,69632]{1,0:T(8,128)} custom-call(f32[2,32]{1,0:T(2,128)S(1)} %copy-done, bf16[544,128]{1,0:T(8,128)(2,1)S(1)} %total_sum.1.refs_0_, bf16[544,128]{1,0:T(8,128)(2,1)S(1)} %collective-permute-done.12.refs_1_, bf16[544,128]{1,0:T(8,128)(2,1)S(1)} %collective-permute-done.13.refs_2_, bf16[544,128]{1,0:T(8,128)(2,1)S(1)} %collective-permute-done.14.refs_3_), custom_call_target="tpu_custom_call" | custom-call | flops 1000000 | bytes 4000000 | tf_op jit(solution)/shard_map/expert_product/pallas_call | solution.py:452
  (24 shorter events, 0.1 us)
Async XLA Ops:
  0.6 0.7 %copy-start = (f32[2,32]{1,0:T(2,128)S(1)}, f32[2,32]{1,0:T(2,128)}, u32[]{:S(2)}) copy-start(f32[2,32]{1,0:T(2,128)} %coef_ref.1) | copy-start | bytes 772
  1.3 8.5 %copy-start.2 = (bf16[256,9,128]{2,0,1:T(8,128)(2,1)S(1)}, bf16[256,9,128]{2,0,1:T(8,128)(2,1)}, u32[]{:S(2)}) copy-start(bf16[256,9,128]{2,0,1:T(8,128)(2,1)} %param.11) | copy-start | bytes 1769476
  1.3 8.5 %copy-start.3 = (bf16[128,9,128]{2,0,1:T(8,128)(2,1)S(1)}, bf16[128,9,128]{2,0,1:T(8,128)(2,1)}, u32[]{:S(2)}) copy-start(bf16[128,9,128]{2,0,1:T(8,128)(2,1)} %param.12) | copy-start | bytes 884740
  1.3 8.5 %copy-start.4 = (f32[5,5,1024]{2,1,0:T(8,128)S(1)}, f32[5,5,1024]{2,1,0:T(8,128)}, u32[]{:S(2)}) copy-start(f32[5,5,1024]{2,1,0:T(8,128)} %two_ref.3) | copy-start | bytes 307204
  1.3 8.5 %copy-start.5 = (f32[3,3,1024]{2,1,0:T(4,128)S(1)}, f32[3,3,1024]{2,1,0:T(4,128)}, u32[]{:S(2)}) copy-start(f32[3,3,1024]{2,1,0:T(4,128)} %one_ref.3) | copy-start | bytes 110596
  1.3 8.5 %copy-start.6 = (s32[128,8]{0,1:T(8,128)S(1)}, s32[128,8]{0,1:T(8,128)}, u32[]{:S(2)}) copy-start(s32[128,8]{0,1:T(8,128)} %param.13) | copy-start | bytes 12292
  1.3 8.5 %copy-start.7 = (f32[1024]{0:T(1024)S(1)}, f32[1024]{0:T(1024)}, u32[]{:S(2)}) copy-start(f32[1024]{0:T(1024)} %param.14) | copy-start | bytes 12292
  1.3 8.5 %copy-start.8 = (s32[128]{0:T(128)S(1)}, s32[128]{0:T(128)}, u32[]{:S(2)}) copy-start(s32[128]{0:T(128)} %param.18) | copy-start | bytes 1540
  3.4 13.1 %collective-permute-start.2 = (bf16[2,272,128]{2,1,0:T(8,128)(2,1)S(1)}, bf16[2,272,128]{2,1,0:T(8,128)(2,1)S(1)}, u32[]{:S(2)}, u32[]{:S(2)}) collective-permute-start(bf16[2,272,128]{2,1,0:T(8,128)(2,1)S(1)} %merge.1.refs_0_), channel_id=1, source_target_pairs={{0,12},{4,8},{8,4},{12,0},{1,13},{5,9},{9,5},{13,1},{2,14},{6,10},... | collective-permute-start | bytes 417800 | tf_op jit(solution)/shard_map/ppermute | solution.py:499
  8.5 11.8 %collective-permute-start.1 = (bf16[2,272,128]{2,1,0:T(8,128)(2,1)S(1)}, bf16[2,272,128]{2,1,0:T(8,128)(2,1)S(1)}, u32[]{:S(2)}, u32[]{:S(2)}) collective-permute-start(bf16[2,272,128]{2,1,0:T(8,128)(2,1)S(1)} %merge.1.refs_0_), channel_id=1, source_target_pairs={{0,8},{4,12},{8,0},{12,4},{1,9},{5,13},{9,1},{13,5},{2,10},{6,14},... | collective-permute-start | bytes 417800 | tf_op jit(solution)/shard_map/ppermute | solution.py:499
  8.5 11.8 %collective-permute-start = (bf16[2,272,128]{2,1,0:T(8,128)(2,1)S(1)}, bf16[2,272,128]{2,1,0:T(8,128)(2,1)S(1)}, u32[]{:S(2)}, u32[]{:S(2)}) collective-permute-start(bf16[2,272,128]{2,1,0:T(8,128)(2,1)S(1)} %merge.1.refs_0_), channel_id=1, source_target_pairs={{0,4},{4,0},{8,12},{12,8},{1,5},{5,1},{9,13},{13,9},{2,6},{6,2},{1... | collective-permute-start | bytes 417800 | tf_op jit(solution)/shard_map/ppermute | solution.py:499
  20.3 2.0 %collective-permute-start.4 = (bf16[2176,128]{1,0:T(8,128)(2,1)S(1)}, bf16[2176,128]{1,0:T(8,128)(2,1)S(1)}, u32[]{:S(2)}, u32[]{:S(2)}) collective-permute-start(bf16[2176,128]{1,0:T(8,128)(2,1)S(1)} %get-tuple-element.45), channel_id=1, source_target_pairs={{0,1},{1,0},{2,3},{3,2},{4,5},{5,4},{6,7},{7,6},{8,9},{9,8},{10,11... | collective-permute-start | bytes 1671176 | tf_op jit(solution)/shard_map/ppermute | solution.py:499
  20.3 6.5 %collective-permute-start.3 = (bf16[4,2,272,128]{3,2,1,0:T(8,128)(2,1)S(1)}, bf16[4,2,272,128]{3,2,1,0:T(8,128)(2,1)S(1)}, u32[]{:S(2)}, u32[]{:S(2)}) collective-permute-start(bf16[4,2,272,128]{3,2,1,0:T(8,128)(2,1)S(1)} %pack.1.rest_0_), channel_id=1, source_target_pairs={{0,1},{1,0},{2,3},{3,2},{4,5},{5,4},{6,7},{7,6},{8,9},{9,8},{10,11... | collective-permute-start | bytes 1671176 | tf_op jit(solution)/shard_map/ppermute | solution.py:499
  22.4 12.2 %collective-permute-start.5 = (bf16[544,128]{1,0:T(8,128)(2,1)S(1)}, bf16[544,128]{1,0:T(8,128)(2,1)S(1)}, u32[]{:S(2)}, u32[]{:S(2)}) collective-permute-start(bf16[544,128]{1,0:T(8,128)(2,1)S(1)} %get-tuple-element.47), channel_id=1, source_target_pairs={{0,12},{4,8},{8,4},{12,0},{1,13},{5,9},{9,5},{13,1},{2,14},{6,10},... | collective-permute-start | bytes 417800 | tf_op jit(solution)/shard_map/ppermute | solution.py:499
  24.9 12.2 %collective-permute-start.6 = (bf16[544,128]{1,0:T(8,128)(2,1)S(1)}, bf16[544,128]{1,0:T(8,128)(2,1)S(1)}, u32[]{:S(2)}, u32[]{:S(2)}) collective-permute-start(bf16[544,128]{1,0:T(8,128)(2,1)S(1)} %get-tuple-element.48), channel_id=1, source_target_pairs={{0,8},{4,12},{8,0},{12,4},{1,9},{5,13},{9,1},{13,5},{2,10},{6,14},... | collective-permute-start | bytes 417800 | tf_op jit(solution)/shard_map/ppermute | solution.py:499
  24.9 12.2 %collective-permute-start.7 = (bf16[544,128]{1,0:T(8,128)(2,1)S(1)}, bf16[544,128]{1,0:T(8,128)(2,1)S(1)}, u32[]{:S(2)}, u32[]{:S(2)}) collective-permute-start(bf16[544,128]{1,0:T(8,128)(2,1)S(1)} %get-tuple-element.49), channel_id=1, source_target_pairs={{0,4},{4,0},{8,12},{12,8},{1,5},{5,1},{9,13},{13,9},{2,6},{6,2},{1... | collective-permute-start | bytes 417800 | tf_op jit(solution)/shard_map/ppermute | solution.py:499
  26.8 14.5 %copy-start.1 = (s32[4,32]{1,0:T(4,128)S(1)}, s32[4,32]{1,0:T(4,128)}, u32[]{:S(2)}) copy-start(s32[4,32]{1,0:T(4,128)} %send_ref.1) | copy-start | bytes 1540
  31.9 6.3 %collective-permute-start.8 = (bf16[9,32,128]{2,1,0:T(8,128)(2,1)S(1)}, bf16[9,32,128]{2,1,0:T(8,128)(2,1)S(1)}, u32[]{:S(2)}, u32[]{:S(2)}) collective-permute-start(bf16[9,32,128]{2,1,0:T(8,128)(2,1)S(1)} %get-tuple-element.54), channel_id=1, source_target_pairs={{4,8},{8,4},{12,0},{0,12},{5,9},{9,5},{13,1},{1,13},{6,10},{10,6},... | collective-permute-start | bytes 221192 | tf_op jit(solution)/shard_map/ppermute | solution.py:508
  34.4 4.5 %collective-permute-start.9 = (bf16[9,32,128]{2,1,0:T(8,128)(2,1)S(1)}, bf16[9,32,128]{2,1,0:T(8,128)(2,1)S(1)}, u32[]{:S(2)}, u32[]{:S(2)}) collective-permute-start(bf16[9,32,128]{2,1,0:T(8,128)(2,1)S(1)} %get-tuple-element.55), channel_id=1, source_target_pairs={{1,2},{2,1},{3,0},{0,3},{5,6},{6,5},{7,4},{4,7},{9,10},{10,9},{11,... | collective-permute-start | bytes 221192 | tf_op jit(solution)/shard_map/ppermute | solution.py:508
  34.5 4.7 %collective-permute-start.10 = (bf16[9,32,128]{2,1,0:T(8,128)(2,1)S(1)}, bf16[9,32,128]{2,1,0:T(8,128)(2,1)S(1)}, u32[]{:S(2)}, u32[]{:S(2)}) collective-permute-start(bf16[9,32,128]{2,1,0:T(8,128)(2,1)S(1)} %get-tuple-element.56), channel_id=1, source_target_pairs={{0,4},{4,0},{8,12},{12,8},{1,5},{5,1},{9,13},{13,9},{2,6},{6,2},{1... | collective-permute-start | bytes 221192 | tf_op jit(solution)/shard_map/ppermute | solution.py:508
  37.1 2.1 %collective-permute-start.11 = (bf16[9,32,128]{2,1,0:T(8,128)(2,1)S(1)}, bf16[9,32,128]{2,1,0:T(8,128)(2,1)S(1)}, u32[]{:S(2)}, u32[]{:S(2)}) collective-permute-start(bf16[9,32,128]{2,1,0:T(8,128)(2,1)S(1)} %get-tuple-element.57), channel_id=1, source_target_pairs={{0,1},{1,0},{2,3},{3,2},{4,5},{5,4},{6,7},{7,6},{8,9},{9,8},{10,11... | collective-permute-start | bytes 221192 | tf_op jit(solution)/shard_map/ppermute | solution.py:508
  39.3 5.8 %collective-permute-start.12 = (bf16[544,128]{1,0:T(8,128)(2,1)S(1)}, bf16[544,128]{1,0:T(8,128)(2,1)S(1)}, u32[]{:S(2)}, u32[]{:S(2)}) collective-permute-start(bf16[544,128]{1,0:T(8,128)(2,1)S(1)} %total_sum.1.refs_0_), channel_id=1, source_target_pairs={{0,2},{1,3},{2,0},{3,1},{4,6},{5,7},{6,4},{7,5},{8,10},{9,11},{10,... | collective-permute-start | bytes 417800 | tf_op jit(solution)/shard_map/ppermute | solution.py:499
  41.3 3.8 %collective-permute-start.13 = (bf16[544,128]{1,0:T(8,128)(2,1)S(1)}, bf16[544,128]{1,0:T(8,128)(2,1)S(1)}, u32[]{:S(2)}, u32[]{:S(2)}) collective-permute-start(bf16[544,128]{1,0:T(8,128)(2,1)S(1)} %total_sum.1.refs_0_), channel_id=1, source_target_pairs={{0,1},{1,0},{2,3},{3,2},{4,5},{5,4},{6,7},{7,6},{8,9},{9,8},{10,11... | collective-permute-start | bytes 417800 | tf_op jit(solution)/shard_map/ppermute | solution.py:499
  45.1 1.4 %collective-permute-start.14 = (bf16[544,128]{1,0:T(8,128)(2,1)S(1)}, bf16[544,128]{1,0:T(8,128)(2,1)S(1)}, u32[]{:S(2)}, u32[]{:S(2)}) collective-permute-start(bf16[544,128]{1,0:T(8,128)(2,1)S(1)} %collective-permute-done.12.refs_1_), channel_id=1, source_target_pairs={{0,1},{1,0},{2,3},{3,2},{4,5},{5,4},{6,7},{7,6},{8,9},{9,8},{10,11... | collective-permute-start | bytes 417800 | tf_op jit(solution)/shard_map/ppermute | solution.py:499

commit v12 on v10

--- a/solution.py
+++ b/solution.py
@@ -9,8 +9,8 @@
 from jax.sharding import PartitionSpec as P
 
 LIVE_BLOCK = 64
-CHUNK = 256
-SUB = 16
+CHUNK = 512
+SUB = 32
 F32 = jnp.float32
 BF16 = jnp.bfloat16
 
@@ -117,14 +117,16 @@
 
 
 def features_kernel(
-    near_ref, class_ref, zero_ref, one_ref, two_ref, source_ref, target_ref,
+    live_in_ref, near_ref, class_ref, zero_ref, one_ref, two_ref, source_ref, target_ref,
     *refs, fanout, cuts,
 ):
     other_refs, own_ref, pulled_ref, edge_ref = refs[:cuts], *refs[cuts : cuts + 3]
-    source_t, target_t, moved, spread, rotated, grads = refs[cuts + 3 :]
+    source_t, target_t, moved, spread, rotated, grads, live_ref, live_arrived = refs[cuts + 3 :]
     slots, channels = source_ref.shape[1:]
     atoms = target_ref.shape[1]
     edges = atoms * fanout
+    live_copy = pltpu.make_async_copy(live_in_ref, live_ref, live_arrived)
+    live_copy.start()
     for c in range(9):
         source_t[c * channels : (c + 1) * channels, :] = source_ref[c].T
         target_t[c * channels : (c + 1) * channels, :] = target_ref[c].T
@@ -185,6 +187,9 @@
         return carry
 
     lax.fori_loop(0, edges // CHUNK, chunk_step, 0)
+    live_copy.wait()
+    edge_row = lax.broadcasted_iota(jnp.int32, (1, edges), 1)
+    edge_ref[1:2, :] = jnp.where(edge_row < live_ref[0] * LIVE_BLOCK * fanout, edge_ref[1:2, :], -1.0)
     zw, pw = 3 * channels, 2 * channels
     first = zw * zw // 128
     second = first + pw * pw // 128
@@ -211,14 +216,14 @@
             out_ref[...] = grads[pl.ds(at, height), :].astype(BF16)
 
 
-def features(near, classes, zero, one, two, source, target, rows, fanout, cuts):
+def features(live, near, classes, zero, one, two, source, target, rows, fanout, cuts):
     slots, channels = source.shape[1:]
     atoms = target.shape[1]
     edges = atoms * fanout
     shape = jax.ShapeDtypeStruct
     return pl.pallas_call(
         functools.partial(features_kernel, fanout=fanout, cuts=cuts),
-        in_specs=[VMEM] * 7,
+        in_specs=[HBM] + [VMEM] * 7,
         out_specs=[VMEM] * (cuts + 3),
         out_shape=[
             *[shape((rows // cuts, 128), BF16)] * cuts,
@@ -233,11 +238,13 @@
             pltpu.VMEM((9 * channels, CHUNK), F32),
             pltpu.VMEM((7 * channels, edges), BF16),
             pltpu.VMEM((rows, 128), F32),
+            pltpu.SMEM((1,), jnp.int32),
+            pltpu.SemaphoreType.DMA,
         ],
         compiler_params=limits(24),
         cost_estimate=cost(9 * 10**9, 7 * 10**6),
         name="features",
-    )(near, classes, zero, one, two, source, target)
+    )(live, near, classes, zero, one, two, source, target)
 
 
 def back_kernel(
@@ -529,19 +536,15 @@
     source = jnp.transpose(saved_input, (1, 0, 2))
     target = jnp.transpose(cotangent, (1, 0, 2))
 
-    alive = jnp.arange(atoms, dtype=jnp.int32) < live_blocks[0] * LIVE_BLOCK
-    classes = jnp.where(alive, atom_class, -1).reshape(1, -1)
-    experts, classes = lax.optimization_barrier((experts, classes))
-
     if direct:
         half = height // 2
         mine = merge(merge_coef, experts, 2)
-        held = [mine] + [swap(mine, "yz", k) for k in range(1, count_yz)]
+        held = [mine] + [swap(mine, "yz", k) for k in (2, 1, 3)]
         source, target, mine = lax.optimization_barrier((source, target, mine))
 
         def places():
             here, side = lax.axis_index("yz"), lax.rem(lax.axis_index("gx"), 2)
-            starts = [(here ^ k) * height for k in range(count_yz)]
+            starts = [(here ^ k) * height for k in (0, 2, 1, 3)]
             return [at + side * half for at in starts] + [at + (1 - side) * half for at in starts]
     else:
         part = jnp.dot(merge_coef, experts.astype(F32), precision=lax.Precision.HIGHEST).astype(BF16)
@@ -552,7 +555,7 @@
             return [0]
 
     *other, own, pulled, edge = features(
-        neighbours.T, classes, zero, rot_one, rot_two, source, target, rows, fanout, cuts
+        live_blocks, neighbours.T, atom_class.reshape(1, -1), zero, rot_one, rot_two, source, target, rows, fanout, cuts
     )
     if direct:
         came = [swap(piece, "gx", 1) for piece in other]

time: 49.8 us -> 46.8 us (0.940)
  waiting for transfers between devices: 13.5 us -> 12 us
  Pallas kernels: 17.7 us -> 16.6 us
  other arithmetic: 0.66 us -> 0 us
    ppermute x4, waiting for transfers between devices: 2.62 us -> 1.45 us  [neighbour_pairs(): return lax.ppermute(value, axis, moves)]
    reshape x1 -> x0, other arithmetic: 0.66 us -> none  [local(): classes = jnp.where(alive, atom_class, -1).reshape(1, -1)]
    pallas_call x1, Pallas kernels: 7.2 us -> 6.59 us  [features(): pl.pallas_call(functools.partial(features_kernel, fanout=fanout, cuts=cut...]
  transfers between devices with their start and end apart: 18 -> 18, of which waited for: 8 -> 6; matrix products, arithmetic and copies ran while one was open for 0% -> 0% of each run, Pallas kernels for 28% -> 28%
where the time goes in v12:
time: 46.8 us; the launch traced here: 46.6 us
  Pallas kernels  16.6 us (35%)
  starting transfers between devices  15.9 us (34%)
  waiting for transfers between devices  12 us (26%)
  between operations  1.47 us (3%)
  local copies, waits for them, and re-layouts  0.7 us (1%)
    ppermute x14, starting transfers between devices, swap(): lax.ppermute(value, axis, [(i, i ^ bit) for i in range(lax.axis_size(axis...  12.9 us
    ppermute x14, waiting for transfers between devices, swap(): lax.ppermute(value, axis, [(i, i ^ bit) for i in range(lax.axis_size(axis...  10.5 us
    pallas_call x1, Pallas kernels, features(): pl.pallas_call(functools.partial(features_kernel, fanout=fanout, cuts=cut...  6.59 us
    pallas_call x1, Pallas kernels, back(): pl.pallas_call(functools.partial(back_kernel, pieces=len(pieces), members...  5 us
    ppermute x4, starting transfers between devices, neighbour_pairs(): return lax.ppermute(value, axis, moves)  2.99 us
    pallas_call x1, Pallas kernels, merge(): pl.pallas_call(merge_kernel, in_specs=[HBM, HBM], out_specs=VMEM, out_sha...  2.03 us
    pallas_call x1, Pallas kernels, expert_product(): pl.pallas_call(functools.partial(expert_kernel, scale=scale), in_specs=[V...  1.54 us
    ppermute x4, waiting for transfers between devices, neighbour_pairs(): return lax.ppermute(value, axis, moves)  1.45 us
  transfers between devices with their start and end apart: 18, of which 6 were waited for; matrix products, arithmetic and copies ran while one was open for 0% of the time, Pallas kernels for 28%

profile of v12, /device:TPU:0, one launch (start us, length us, event | category | flops | bytes accessed | tf_op | source)
XLA Modules:
  0.0 46.6 jit_solution(5340639226627751251)
XLA Ops:
  0.6 0.7 %copy-done = f32[2,32]{1,0:T(2,128)S(1)} copy-done((f32[2,32]{1,0:T(2,128)S(1)}, f32[2,32]{1,0:T(2,128)}, u32[]{:S(2)}) %copy-start) | copy-done | bytes 280
  1.4 2.0 %merge.1.refs_0_ = bf16[2,272,128]{2,1,0:T(8,128)(2,1)S(1)} custom-call(f32[2,32]{1,0:T(2,128)S(1)} %copy-done, bf16[32,69632]{1,0:T(8,128)(2,1)} %experts_ref.1), custom_call_target="tpu_custom_call" | custom-call | flops 53477376 | bytes 2228224 | tf_op jit(solution)/shard_map/merge/pallas_call | solution.py:102
  3.4 5.1 %collective-permute-start.6 = (bf16[2,272,128]{2,1,0:T(8,128)(2,1)S(1)}, bf16[2,272,128]{2,1,0:T(8,128)(2,1)S(1)}, u32[]{:S(2)}, u32[]{:S(2)}) collective-permute-start(bf16[2,272,128]{2,1,0:T(8,128)(2,1)S(1)} %merge.1.refs_0_), channel_id=1, source_target_pairs={{0,12},{4,8},{8,4},{12,0},{1,13},{5,9},{9,5},{13,1},{2,14},{6,10},... | collective-permute-start | bytes 417800 | tf_op jit(solution)/shard_map/ppermute | solution.py:507
  8.5 0.0 collective-permute-start.5
  8.5 0.6 %collective-permute-start.4 = (bf16[2,272,128]{2,1,0:T(8,128)(2,1)S(1)}, bf16[2,272,128]{2,1,0:T(8,128)(2,1)S(1)}, u32[]{:S(2)}, u32[]{:S(2)}) collective-permute-start(bf16[2,272,128]{2,1,0:T(8,128)(2,1)S(1)} %merge.1.refs_0_), channel_id=1, source_target_pairs={{0,8},{4,12},{8,0},{12,4},{1,9},{5,13},{9,1},{13,5},{2,10},{6,14},... | collective-permute-start | bytes 417800 | tf_op jit(solution)/shard_map/ppermute | solution.py:507
  9.9 6.6 %features.1 = (bf16[544,128]{1,0:T(8,128)(2,1)S(1)}, bf16[544,128]{1,0:T(8,128)(2,1)S(1)}, bf16[544,128]{1,0:T(8,128)(2,1)S(1)}, bf16[544,128]{1,0:T(8,128)(2,1)...) custom-call(s32[1]{0:T(128)S(6)} %copy.13.live_in_ref, ...), custom_call_target="tpu_custom_call" | custom-call | flops 8999999488 | bytes 7000000 | tf_op jit(solution)/shard_map/features/pallas_call | solution.py:224
  16.5 0.1 collective-permute-start
  16.5 0.5 %collective-permute-start.1 = (bf16[544,128]{1,0:T(8,128)(2,1)S(1)}, bf16[544,128]{1,0:T(8,128)(2,1)S(1)}, u32[]{:S(2)}, u32[]{:S(2)}) collective-permute-start(bf16[544,128]{1,0:T(8,128)(2,1)S(1)} %get-tuple-element.45), channel_id=1, source_target_pairs={{0,1},{1,0},{2,3},{3,2},{4,5},{5,4},{6,7},{7,6},{8,9},{9,8},{10,11... | collective-permute-start | bytes 417800 | tf_op jit(solution)/shard_map/ppermute | solution.py:507
  17.0 0.0 collective-permute-done.6.refs_3_
  17.0 0.1 collective-permute-start.2
  17.1 0.4 collective-permute-start.3
  17.6 2.7 %collective-permute-done.4.refs_1_ = bf16[2,272,128]{2,1,0:T(8,128)(2,1)S(1)} collective-permute-done((bf16[2,272,128]{2,1,0:T(8,128)(2,1)S(1)}, bf16[2,272,128]{2,1,0:T(8,128)(2,1)S(1)}, u32[]{:S(2)}, u32[]{:S(2)}) %collective-permute-start.4) | collective-permute-done | bytes 139296 | tf_op jit(solution)/shard_map/ppermute | solution.py:507
  20.3 0.0 collective-permute-done.1.refs_1_
  20.3 0.0 collective-permute-done.2.refs_2_
  20.3 0.0 collective-permute-done.3.refs_3_
  20.3 0.1 collective-permute-start.7
  20.4 0.2 pair_sum.1
  20.6 2.5 %collective-permute-start.8 = (bf16[544,128]{1,0:T(8,128)(2,1)S(1)}, bf16[544,128]{1,0:T(8,128)(2,1)S(1)}, u32[]{:S(2)}, u32[]{:S(2)}) collective-permute-start(bf16[544,128]{1,0:T(8,128)(2,1)S(1)} %get-tuple-element.59), channel_id=1, source_target_pairs={{0,12},{4,8},{8,4},{12,0},{1,13},{5,9},{9,5},{13,1},{2,14},{6,10},... | collective-permute-start | bytes 417800 | tf_op jit(solution)/shard_map/ppermute | solution.py:507
  23.1 0.0 collective-permute-start.9
  23.1 1.9 %collective-permute-start.10 = (bf16[544,128]{1,0:T(8,128)(2,1)S(1)}, bf16[544,128]{1,0:T(8,128)(2,1)S(1)}, u32[]{:S(2)}, u32[]{:S(2)}) collective-permute-start(bf16[544,128]{1,0:T(8,128)(2,1)S(1)} %get-tuple-element.61), channel_id=1, source_target_pairs={{0,4},{4,0},{8,12},{12,8},{1,5},{5,1},{9,13},{13,9},{2,6},{6,2},{1... | collective-permute-start | bytes 417800 | tf_op jit(solution)/shard_map/ppermute | solution.py:507
  25.1 5.0 %back.1 = (f32[9,128,128]{2,1,0:T(8,128)S(1)}, bf16[9,32,128]{2,1,0:T(8,128)(2,1)S(1)}, bf16[9,32,128]{2,1,0:T(8,128)(2,1)S(1)}, bf16[9,32,128]{2,1,0:T(8,128)(2,1)S(1)}, bf16[9,32,128]{2,1,0:T(8,128)(2,1)S(1)}) custom-call(f32[8,1024]{1,0:T(8,128)S(1)} %get-tuple-element.42.edge_ref, f32[1,1024]{1,0:T(1,128)S(1)} %bitcast.10, f32[3,3,1024]{2,1,0:T(4,128)S(1)} %copy-done.5, ...), custom_call_target="tpu_custom_call" | custom-call | flops 8999999488 | bytes 7000000 | tf_op jit(solution)/shard_map/back/pallas_call | solution.py:342
  30.1 2.5 %collective-permute-start.11 = (bf16[9,32,128]{2,1,0:T(8,128)(2,1)S(1)}, bf16[9,32,128]{2,1,0:T(8,128)(2,1)S(1)}, u32[]{:S(2)}, u32[]{:S(2)}) collective-permute-start(bf16[9,32,128]{2,1,0:T(8,128)(2,1)S(1)} %get-tuple-element.66), channel_id=1, source_target_pairs={{4,8},{8,4},{12,0},{0,12},{5,9},{9,5},{13,1},{1,13},{6,10},{10,6},... | collective-permute-start | bytes 221192 | tf_op jit(solution)/shard_map/ppermute | solution.py:516
  32.6 0.5 %collective-permute-start.12 = (bf16[9,32,128]{2,1,0:T(8,128)(2,1)S(1)}, bf16[9,32,128]{2,1,0:T(8,128)(2,1)S(1)}, u32[]{:S(2)}, u32[]{:S(2)}) collective-permute-start(bf16[9,32,128]{2,1,0:T(8,128)(2,1)S(1)} %get-tuple-element.67), channel_id=1, source_target_pairs={{1,2},{2,1},{3,0},{0,3},{5,6},{6,5},{7,4},{4,7},{9,10},{10,9},{11,... | collective-permute-start | bytes 221192 | tf_op jit(solution)/shard_map/ppermute | solution.py:516
  33.1 3.4 %collective-permute-done.9.refs_2_ = bf16[544,128]{1,0:T(8,128)(2,1)S(1)} collective-permute-done((bf16[544,128]{1,0:T(8,128)(2,1)S(1)}, bf16[544,128]{1,0:T(8,128)(2,1)S(1)}, u32[]{:S(2)}, u32[]{:S(2)}) %collective-permute-start.9) | collective-permute-done | bytes 139296 | tf_op jit(solution)/shard_map/ppermute | solution.py:507
  36.5 0.1 total_sum.1.refs_0_
  36.6 0.5 %collective-permute-done.12.b_ref = bf16[9,32,128]{2,1,0:T(8,128)(2,1)S(1)} collective-permute-done((bf16[9,32,128]{2,1,0:T(8,128)(2,1)S(1)}, bf16[9,32,128]{2,1,0:T(8,128)(2,1)S(1)}, u32[]{:S(2)}, u32[]{:S(2)}) %collective-permute-start.12) | collective-permute-done | bytes 73760 | tf_op jit(solution)/shard_map/ppermute | solution.py:516
  37.1 0.9 %collective-permute-done.13.c_ref = bf16[9,32,128]{2,1,0:T(8,128)(2,1)S(1)} collective-permute-done((bf16[9,32,128]{2,1,0:T(8,128)(2,1)S(1)}, bf16[9,32,128]{2,1,0:T(8,128)(2,1)S(1)}, u32[]{:S(2)}, u32[]{:S(2)}) %collective-permute-start.13) | collective-permute-done | bytes 73760 | tf_op jit(solution)/shard_map/ppermute | solution.py:516
  38.0 1.5 %collective-permute-start.15 = (bf16[544,128]{1,0:T(8,128)(2,1)S(1)}, bf16[544,128]{1,0:T(8,128)(2,1)S(1)}, u32[]{:S(2)}, u32[]{:S(2)}) collective-permute-start(bf16[544,128]{1,0:T(8,128)(2,1)S(1)} %total_sum.1.refs_0_), channel_id=1, source_target_pairs={{0,2},{1,3},{2,0},{3,1},{4,6},{5,7},{6,4},{7,5},{8,10},{9,11},{10,... | collective-permute-start | bytes 417800 | tf_op jit(solution)/shard_map/ppermute | solution.py:507
  39.5 1.2 %finish.1 = bf16[9,128,128]{2,1,0:T(8,128)(2,1)} custom-call(s32[4,32]{1,0:T(4,128)S(1)} %copy-done.1, f32[9,128,128]{2,1,0:T(8,128)S(1)} %get-tuple-element.71.own_ref, bf16[9,32,128]{2,1,0:T(8,128)(2,1)S(1)} %collective-permute-done.11.a_ref, bf16[9,32,128]{2,1,0:T(8,128)(2,1)S(1)} %collective-permute-done.12.b_ref, ...), custom_call_target="tpu_custom_call" | custom-call | flops 100000000 | bytes 2000000 | tf_op jit(solution)/shard_map/finish/pallas_call | solution.py:495
  40.7 3.0 %collective-permute-done.15.refs_1_ = bf16[544,128]{1,0:T(8,128)(2,1)S(1)} collective-permute-done((bf16[544,128]{1,0:T(8,128)(2,1)S(1)}, bf16[544,128]{1,0:T(8,128)(2,1)S(1)}, u32[]{:S(2)}, u32[]{:S(2)}) %collective-permute-start.15) | collective-permute-done | bytes 139296 | tf_op jit(solution)/shard_map/ppermute | solution.py:507
  43.7 1.4 %collective-permute-done.17.refs_3_ = bf16[544,128]{1,0:T(8,128)(2,1)S(1)} collective-permute-done((bf16[544,128]{1,0:T(8,128)(2,1)S(1)}, bf16[544,128]{1,0:T(8,128)(2,1)S(1)}, u32[]{:S(2)}, u32[]{:S(2)}) %collective-permute-start.17) | collective-permute-done | bytes 139296 | tf_op jit(solution)/shard_map/ppermute | solution.py:507
  45.1 1.5 %expert_product.1 = f32[8,69632]{1,0:T(8,128)} custom-call(f32[2,32]{1,0:T(2,128)S(1)} %copy-done, bf16[544,128]{1,0:T(8,128)(2,1)S(1)} %total_sum.1.refs_0_, bf16[544,128]{1,0:T(8,128)(2,1)S(1)} %collective-permute-done.15.refs_1_, bf16[544,128]{1,0:T(8,128)(2,1)S(1)} %collective-permute-done.16.refs_2_, bf16[544,128]{1,0:T(8,128)(2,1)S(1)} %collective-permute-done.17.refs_3_), custom_call_target="tpu_custom_call" | custom-call | flops 1000000 | bytes 4000000 | tf_op jit(solution)/shard_map/expert_product/pallas_call | solution.py:460
  (30 shorter events, 0.1 us)
Async XLA Ops:
  0.6 0.7 %copy-start = (f32[2,32]{1,0:T(2,128)S(1)}, f32[2,32]{1,0:T(2,128)}, u32[]{:S(2)}) copy-start(f32[2,32]{1,0:T(2,128)} %coef_ref.1) | copy-start | bytes 772
  1.3 8.5 %copy-start.2 = (bf16[256,9,128]{2,0,1:T(8,128)(2,1)S(1)}, bf16[256,9,128]{2,0,1:T(8,128)(2,1)}, u32[]{:S(2)}) copy-start(bf16[256,9,128]{2,0,1:T(8,128)(2,1)} %param.11) | copy-start | bytes 1769476
  1.3 8.5 %copy-start.3 = (bf16[128,9,128]{2,0,1:T(8,128)(2,1)S(1)}, bf16[128,9,128]{2,0,1:T(8,128)(2,1)}, u32[]{:S(2)}) copy-start(bf16[128,9,128]{2,0,1:T(8,128)(2,1)} %param.12) | copy-start | bytes 884740
  1.3 8.5 %copy-start.4 = (f32[5,5,1024]{2,1,0:T(8,128)S(1)}, f32[5,5,1024]{2,1,0:T(8,128)}, u32[]{:S(2)}) copy-start(f32[5,5,1024]{2,1,0:T(8,128)} %two_ref.3) | copy-start | bytes 307204
  1.3 8.5 %copy-start.5 = (f32[3,3,1024]{2,1,0:T(4,128)S(1)}, f32[3,3,1024]{2,1,0:T(4,128)}, u32[]{:S(2)}) copy-start(f32[3,3,1024]{2,1,0:T(4,128)} %one_ref.3) | copy-start | bytes 110596
  1.3 8.5 %copy-start.6 = (s32[128,8]{0,1:T(8,128)S(1)}, s32[128,8]{0,1:T(8,128)}, u32[]{:S(2)}) copy-start(s32[128,8]{0,1:T(8,128)} %param.13) | copy-start | bytes 12292
  1.3 8.5 %copy-start.7 = (f32[1024]{0:T(1024)S(1)}, f32[1024]{0:T(1024)}, u32[]{:S(2)}) copy-start(f32[1024]{0:T(1024)} %param.14) | copy-start | bytes 12292
  1.3 8.5 %copy-start.8 = (s32[128]{0:T(128)S(1)}, s32[128]{0:T(128)}, u32[]{:S(2)}) copy-start(s32[128]{0:T(128)} %param.18) | copy-start | bytes 1540
  3.4 13.7 %collective-permute-start.6 = (bf16[2,272,128]{2,1,0:T(8,128)(2,1)S(1)}, bf16[2,272,128]{2,1,0:T(8,128)(2,1)S(1)}, u32[]{:S(2)}, u32[]{:S(2)}) collective-permute-start(bf16[2,272,128]{2,1,0:T(8,128)(2,1)S(1)} %merge.1.refs_0_), channel_id=1, source_target_pairs={{0,12},{4,8},{8,4},{12,0},{1,13},{5,9},{9,5},{13,1},{2,14},{6,10},... | collective-permute-start | bytes 417800 | tf_op jit(solution)/shard_map/ppermute | solution.py:507
  8.5 8.6 %collective-permute-start.5 = (bf16[2,272,128]{2,1,0:T(8,128)(2,1)S(1)}, bf16[2,272,128]{2,1,0:T(8,128)(2,1)S(1)}, u32[]{:S(2)}, u32[]{:S(2)}) collective-permute-start(bf16[2,272,128]{2,1,0:T(8,128)(2,1)S(1)} %merge.1.refs_0_), channel_id=1, source_target_pairs={{0,4},{4,0},{8,12},{12,8},{1,5},{5,1},{9,13},{13,9},{2,6},{6,2},{1... | collective-permute-start | bytes 417800 | tf_op jit(solution)/shard_map/ppermute | solution.py:507
  8.5 11.8 %collective-permute-start.4 = (bf16[2,272,128]{2,1,0:T(8,128)(2,1)S(1)}, bf16[2,272,128]{2,1,0:T(8,128)(2,1)S(1)}, u32[]{:S(2)}, u32[]{:S(2)}) collective-permute-start(bf16[2,272,128]{2,1,0:T(8,128)(2,1)S(1)} %merge.1.refs_0_), channel_id=1, source_target_pairs={{0,8},{4,12},{8,0},{12,4},{1,9},{5,13},{9,1},{13,5},{2,10},{6,14},... | collective-permute-start | bytes 417800 | tf_op jit(solution)/shard_map/ppermute | solution.py:507
  16.5 3.8 %collective-permute-start = (bf16[544,128]{1,0:T(8,128)(2,1)S(1)}, bf16[544,128]{1,0:T(8,128)(2,1)S(1)}, u32[]{:S(2)}, u32[]{:S(2)}) collective-permute-start(bf16[544,128]{1,0:T(8,128)(2,1)S(1)} %get-tuple-element.44), channel_id=1, source_target_pairs={{0,1},{1,0},{2,3},{3,2},{4,5},{5,4},{6,7},{7,6},{8,9},{9,8},{10,11... | collective-permute-start | bytes 417800 | tf_op jit(solution)/shard_map/ppermute | solution.py:507
  16.5 3.7 %collective-permute-start.1 = (bf16[544,128]{1,0:T(8,128)(2,1)S(1)}, bf16[544,128]{1,0:T(8,128)(2,1)S(1)}, u32[]{:S(2)}, u32[]{:S(2)}) collective-permute-start(bf16[544,128]{1,0:T(8,128)(2,1)S(1)} %get-tuple-element.45), channel_id=1, source_target_pairs={{0,1},{1,0},{2,3},{3,2},{4,5},{5,4},{6,7},{7,6},{8,9},{9,8},{10,11... | collective-permute-start | bytes 417800 | tf_op jit(solution)/shard_map/ppermute | solution.py:507
  17.0 3.2 %collective-permute-start.2 = (bf16[544,128]{1,0:T(8,128)(2,1)S(1)}, bf16[544,128]{1,0:T(8,128)(2,1)S(1)}, u32[]{:S(2)}, u32[]{:S(2)}) collective-permute-start(bf16[544,128]{1,0:T(8,128)(2,1)S(1)} %get-tuple-element.46), channel_id=1, source_target_pairs={{0,1},{1,0},{2,3},{3,2},{4,5},{5,4},{6,7},{7,6},{8,9},{9,8},{10,11... | collective-permute-start | bytes 417800 | tf_op jit(solution)/shard_map/ppermute | solution.py:507
  17.1 3.2 %collective-permute-start.3 = (bf16[544,128]{1,0:T(8,128)(2,1)S(1)}, bf16[544,128]{1,0:T(8,128)(2,1)S(1)}, u32[]{:S(2)}, u32[]{:S(2)}) collective-permute-start(bf16[544,128]{1,0:T(8,128)(2,1)S(1)} %get-tuple-element.47), channel_id=1, source_target_pairs={{0,1},{1,0},{2,3},{3,2},{4,5},{5,4},{6,7},{7,6},{8,9},{9,8},{10,11... | collective-permute-start | bytes 417800 | tf_op jit(solution)/shard_map/ppermute | solution.py:507
  20.3 4.7 %collective-permute-start.7 = (bf16[4,2,272,128]{3,2,1,0:T(8,128)(2,1)S(1)}, bf16[4,2,272,128]{3,2,1,0:T(8,128)(2,1)S(1)}, u32[]{:S(2)}, u32[]{:S(2)}) collective-permute-start(bf16[4,2,272,128]{3,2,1,0:T(8,128)(2,1)S(1)} %pack.1.rest_0_), channel_id=1, source_target_pairs={{0,1},{1,0},{2,3},{3,2},{4,5},{5,4},{6,7},{7,6},{8,9},{9,8},{10,11... | collective-permute-start | bytes 1671176 | tf_op jit(solution)/shard_map/ppermute | solution.py:507
  20.6 12.5 %collective-permute-start.8 = (bf16[544,128]{1,0:T(8,128)(2,1)S(1)}, bf16[544,128]{1,0:T(8,128)(2,1)S(1)}, u32[]{:S(2)}, u32[]{:S(2)}) collective-permute-start(bf16[544,128]{1,0:T(8,128)(2,1)S(1)} %get-tuple-element.59), channel_id=1, source_target_pairs={{0,12},{4,8},{8,4},{12,0},{1,13},{5,9},{9,5},{13,1},{2,14},{6,10},... | collective-permute-start | bytes 417800 | tf_op jit(solution)/shard_map/ppermute | solution.py:507
  23.1 13.4 %collective-permute-start.9 = (bf16[544,128]{1,0:T(8,128)(2,1)S(1)}, bf16[544,128]{1,0:T(8,128)(2,1)S(1)}, u32[]{:S(2)}, u32[]{:S(2)}) collective-permute-start(bf16[544,128]{1,0:T(8,128)(2,1)S(1)} %get-tuple-element.60), channel_id=1, source_target_pairs={{0,8},{4,12},{8,0},{12,4},{1,9},{5,13},{9,1},{13,5},{2,10},{6,14},... | collective-permute-start | bytes 417800 | tf_op jit(solution)/shard_map/ppermute | solution.py:507
  23.1 13.4 %collective-permute-start.10 = (bf16[544,128]{1,0:T(8,128)(2,1)S(1)}, bf16[544,128]{1,0:T(8,128)(2,1)S(1)}, u32[]{:S(2)}, u32[]{:S(2)}) collective-permute-start(bf16[544,128]{1,0:T(8,128)(2,1)S(1)} %get-tuple-element.61), channel_id=1, source_target_pairs={{0,4},{4,0},{8,12},{12,8},{1,5},{5,1},{9,13},{13,9},{2,6},{6,2},{1... | collective-permute-start | bytes 417800 | tf_op jit(solution)/shard_map/ppermute | solution.py:507
  25.1 14.5 %copy-start.1 = (s32[4,32]{1,0:T(4,128)S(1)}, s32[4,32]{1,0:T(4,128)}, u32[]{:S(2)}) copy-start(s32[4,32]{1,0:T(4,128)} %send_ref.1) | copy-start | bytes 1540
  30.1 6.5 %collective-permute-start.11 = (bf16[9,32,128]{2,1,0:T(8,128)(2,1)S(1)}, bf16[9,32,128]{2,1,0:T(8,128)(2,1)S(1)}, u32[]{:S(2)}, u32[]{:S(2)}) collective-permute-start(bf16[9,32,128]{2,1,0:T(8,128)(2,1)S(1)} %get-tuple-element.66), channel_id=1, source_target_pairs={{4,8},{8,4},{12,0},{0,12},{5,9},{9,5},{13,1},{1,13},{6,10},{10,6},... | collective-permute-start | bytes 221192 | tf_op jit(solution)/shard_map/ppermute | solution.py:516
  32.6 4.5 %collective-permute-start.12 = (bf16[9,32,128]{2,1,0:T(8,128)(2,1)S(1)}, bf16[9,32,128]{2,1,0:T(8,128)(2,1)S(1)}, u32[]{:S(2)}, u32[]{:S(2)}) collective-permute-start(bf16[9,32,128]{2,1,0:T(8,128)(2,1)S(1)} %get-tuple-element.67), channel_id=1, source_target_pairs={{1,2},{2,1},{3,0},{0,3},{5,6},{6,5},{7,4},{4,7},{9,10},{10,9},{11,... | collective-permute-start | bytes 221192 | tf_op jit(solution)/shard_map/ppermute | solution.py:516
  33.1 5.0 %collective-permute-start.13 = (bf16[9,32,128]{2,1,0:T(8,128)(2,1)S(1)}, bf16[9,32,128]{2,1,0:T(8,128)(2,1)S(1)}, u32[]{:S(2)}, u32[]{:S(2)}) collective-permute-start(bf16[9,32,128]{2,1,0:T(8,128)(2,1)S(1)} %get-tuple-element.68), channel_id=1, source_target_pairs={{0,4},{4,0},{8,12},{12,8},{1,5},{5,1},{9,13},{13,9},{2,6},{6,2},{1... | collective-permute-start | bytes 221192 | tf_op jit(solution)/shard_map/ppermute | solution.py:516
  36.5 1.5 %collective-permute-start.14 = (bf16[9,32,128]{2,1,0:T(8,128)(2,1)S(1)}, bf16[9,32,128]{2,1,0:T(8,128)(2,1)S(1)}, u32[]{:S(2)}, u32[]{:S(2)}) collective-permute-start(bf16[9,32,128]{2,1,0:T(8,128)(2,1)S(1)} %get-tuple-element.69), channel_id=1, source_target_pairs={{0,1},{1,0},{2,3},{3,2},{4,5},{5,4},{6,7},{7,6},{8,9},{9,8},{10,11... | collective-permute-start | bytes 221192 | tf_op jit(solution)/shard_map/ppermute | solution.py:516
  38.0 5.7 %collective-permute-start.15 = (bf16[544,128]{1,0:T(8,128)(2,1)S(1)}, bf16[544,128]{1,0:T(8,128)(2,1)S(1)}, u32[]{:S(2)}, u32[]{:S(2)}) collective-permute-start(bf16[544,128]{1,0:T(8,128)(2,1)S(1)} %total_sum.1.refs_0_), channel_id=1, source_target_pairs={{0,2},{1,3},{2,0},{3,1},{4,6},{5,7},{6,4},{7,5},{8,10},{9,11},{10,... | collective-permute-start | bytes 417800 | tf_op jit(solution)/shard_map/ppermute | solution.py:507
  39.5 4.2 %collective-permute-start.16 = (bf16[544,128]{1,0:T(8,128)(2,1)S(1)}, bf16[544,128]{1,0:T(8,128)(2,1)S(1)}, u32[]{:S(2)}, u32[]{:S(2)}) collective-permute-start(bf16[544,128]{1,0:T(8,128)(2,1)S(1)} %total_sum.1.refs_0_), channel_id=1, source_target_pairs={{0,1},{1,0},{2,3},{3,2},{4,5},{5,4},{6,7},{7,6},{8,9},{9,8},{10,11... | collective-permute-start | bytes 417800 | tf_op jit(solution)/shard_map/ppermute | solution.py:507
  43.7 1.4 %collective-permute-start.17 = (bf16[544,128]{1,0:T(8,128)(2,1)S(1)}, bf16[544,128]{1,0:T(8,128)(2,1)S(1)}, u32[]{:S(2)}, u32[]{:S(2)}) collective-permute-start(bf16[544,128]{1,0:T(8,128)(2,1)S(1)} %collective-permute-done.15.refs_1_), channel_id=1, source_target_pairs={{0,1},{1,0},{2,3},{3,2},{4,5},{5,4},{6,7},{7,6},{8,9},{9,8},{10,11... | collective-permute-start | bytes 417800 | tf_op jit(solution)/shard_map/ppermute | solution.py:507

commit v13 on v12

--- a/solution.py
+++ b/solution.py
@@ -562,7 +562,7 @@
         received = lax.optimization_barrier((*came, *held))
         came, held = received[:cuts], received[cuts:]
         parts = pair_sum(own, came, count_yz)
-        gathered = [parts[0]] + [swap(parts[k], "yz", k) for k in reversed(range(1, count_yz))]
+        gathered = [parts[0]] + [swap(parts[k], "yz", k) for k in (3, 1, 2)]
         held = pack(held)
         pieces = [held, swap(held, "gx", 1)]
     grad_own, *ghosts = back(edge, zero, rot_one, rot_two, pulled, pieces, places, rows, atoms, slots, face)

time: 46.8 us -> 46.8 us (level)
  transfers between devices with their start and end apart: 18 -> 18, of which waited for: 6 -> 7; matrix products, arithmetic and copies ran while one was open for 0% -> 0% of each run, Pallas kernels for 28% -> 28%
where the time goes in v13:
time: 46.8 us; the launch traced here: 46.6 us
  Pallas kernels  16.6 us (35%)
  starting transfers between devices  15.9 us (34%)
  waiting for transfers between devices  12 us (26%)
  between operations  1.47 us (3%)
  local copies, waits for them, and re-layouts  0.7 us (1%)
    ppermute x14, starting transfers between devices, swap(): lax.ppermute(value, axis, [(i, i ^ bit) for i in range(lax.axis_size(axis...  12.9 us
    ppermute x14, waiting for transfers between devices, swap(): lax.ppermute(value, axis, [(i, i ^ bit) for i in range(lax.axis_size(axis...  10.5 us
    pallas_call x1, Pallas kernels, features(): pl.pallas_call(functools.partial(features_kernel, fanout=fanout, cuts=cut...  6.59 us
    pallas_call x1, Pallas kernels, back(): pl.pallas_call(functools.partial(back_kernel, pieces=len(pieces), members...  5 us
    ppermute x4, starting transfers between devices, neighbour_pairs(): return lax.ppermute(value, axis, moves)  2.99 us
    pallas_call x1, Pallas kernels, merge(): pl.pallas_call(merge_kernel, in_specs=[HBM, HBM], out_specs=VMEM, out_sha...  2.03 us
    pallas_call x1, Pallas kernels, expert_product(): pl.pallas_call(functools.partial(expert_kernel, scale=scale), in_specs=[V...  1.54 us
    ppermute x4, waiting for transfers between devices, neighbour_pairs(): return lax.ppermute(value, axis, moves)  1.46 us
  transfers between devices with their start and end apart: 18, of which 7 were waited for; matrix products, arithmetic and copies ran while one was open for 0% of the time, Pallas kernels for 28%

profile of v13, /device:TPU:0, one launch (start us, length us, event | category | flops | bytes accessed | tf_op | source)
XLA Modules:
  0.0 46.6 jit_solution(5542728534987660898)
XLA Ops:
  0.6 0.7 %copy-done = f32[2,32]{1,0:T(2,128)S(1)} copy-done((f32[2,32]{1,0:T(2,128)S(1)}, f32[2,32]{1,0:T(2,128)}, u32[]{:S(2)}) %copy-start) | copy-done | bytes 280
  1.4 2.0 %merge.1.refs_0_ = bf16[2,272,128]{2,1,0:T(8,128)(2,1)S(1)} custom-call(f32[2,32]{1,0:T(2,128)S(1)} %copy-done, bf16[32,69632]{1,0:T(8,128)(2,1)} %experts_ref.1), custom_call_target="tpu_custom_call" | custom-call | flops 53477376 | bytes 2228224 | tf_op jit(solution)/shard_map/merge/pallas_call | solution.py:102
  3.4 5.1 %collective-permute-start.6 = (bf16[2,272,128]{2,1,0:T(8,128)(2,1)S(1)}, bf16[2,272,128]{2,1,0:T(8,128)(2,1)S(1)}, u32[]{:S(2)}, u32[]{:S(2)}) collective-permute-start(bf16[2,272,128]{2,1,0:T(8,128)(2,1)S(1)} %merge.1.refs_0_), channel_id=1, source_target_pairs={{0,12},{4,8},{8,4},{12,0},{1,13},{5,9},{9,5},{13,1},{2,14},{6,10},... | collective-permute-start | bytes 417800 | tf_op jit(solution)/shard_map/ppermute | solution.py:507
  8.5 0.0 collective-permute-start.5
  8.5 0.6 %collective-permute-start.4 = (bf16[2,272,128]{2,1,0:T(8,128)(2,1)S(1)}, bf16[2,272,128]{2,1,0:T(8,128)(2,1)S(1)}, u32[]{:S(2)}, u32[]{:S(2)}) collective-permute-start(bf16[2,272,128]{2,1,0:T(8,128)(2,1)S(1)} %merge.1.refs_0_), channel_id=1, source_target_pairs={{0,8},{4,12},{8,0},{12,4},{1,9},{5,13},{9,1},{13,5},{2,10},{6,14},... | collective-permute-start | bytes 417800 | tf_op jit(solution)/shard_map/ppermute | solution.py:507
  9.9 6.6 %features.1 = (bf16[544,128]{1,0:T(8,128)(2,1)S(1)}, bf16[544,128]{1,0:T(8,128)(2,1)S(1)}, bf16[544,128]{1,0:T(8,128)(2,1)S(1)}, bf16[544,128]{1,0:T(8,128)(2,1)...) custom-call(s32[1]{0:T(128)S(6)} %copy.13.live_in_ref, ...), custom_call_target="tpu_custom_call" | custom-call | flops 8999999488 | bytes 7000000 | tf_op jit(solution)/shard_map/features/pallas_call | solution.py:224
  16.5 0.1 collective-permute-start
  16.5 0.5 %collective-permute-start.1 = (bf16[544,128]{1,0:T(8,128)(2,1)S(1)}, bf16[544,128]{1,0:T(8,128)(2,1)S(1)}, u32[]{:S(2)}, u32[]{:S(2)}) collective-permute-start(bf16[544,128]{1,0:T(8,128)(2,1)S(1)} %get-tuple-element.45), channel_id=1, source_target_pairs={{0,1},{1,0},{2,3},{3,2},{4,5},{5,4},{6,7},{7,6},{8,9},{9,8},{10,11... | collective-permute-start | bytes 417800 | tf_op jit(solution)/shard_map/ppermute | solution.py:507
  17.0 0.1 collective-permute-start.2
  17.1 0.0 collective-permute-done.5.refs_2_
  17.1 0.4 collective-permute-start.3
  17.6 2.7 %collective-permute-done.4.refs_1_ = bf16[2,272,128]{2,1,0:T(8,128)(2,1)S(1)} collective-permute-done((bf16[2,272,128]{2,1,0:T(8,128)(2,1)S(1)}, bf16[2,272,128]{2,1,0:T(8,128)(2,1)S(1)}, u32[]{:S(2)}, u32[]{:S(2)}) %collective-permute-start.4) | collective-permute-done | bytes 139296 | tf_op jit(solution)/shard_map/ppermute | solution.py:507
  20.3 0.0 collective-permute-done.refs_0_
  20.3 0.1 collective-permute-start.7
  20.4 0.2 pair_sum.1
  20.6 2.5 %collective-permute-start.8 = (bf16[544,128]{1,0:T(8,128)(2,1)S(1)}, bf16[544,128]{1,0:T(8,128)(2,1)S(1)}, u32[]{:S(2)}, u32[]{:S(2)}) collective-permute-start(bf16[544,128]{1,0:T(8,128)(2,1)S(1)} %get-tuple-element.59), channel_id=1, source_target_pairs={{0,12},{4,8},{8,4},{12,0},{1,13},{5,9},{9,5},{13,1},{2,14},{6,10},... | collective-permute-start | bytes 417800 | tf_op jit(solution)/shard_map/ppermute | solution.py:507
  23.1 1.9 %collective-permute-start.10 = (bf16[544,128]{1,0:T(8,128)(2,1)S(1)}, bf16[544,128]{1,0:T(8,128)(2,1)S(1)}, u32[]{:S(2)}, u32[]{:S(2)}) collective-permute-start(bf16[544,128]{1,0:T(8,128)(2,1)S(1)} %get-tuple-element.61), channel_id=1, source_target_pairs={{0,8},{4,12},{8,0},{12,4},{1,9},{5,13},{9,1},{13,5},{2,10},{6,14},... | collective-permute-start | bytes 417800 | tf_op jit(solution)/shard_map/ppermute | solution.py:507
  25.1 5.0 %back.1 = (f32[9,128,128]{2,1,0:T(8,128)S(1)}, bf16[9,32,128]{2,1,0:T(8,128)(2,1)S(1)}, bf16[9,32,128]{2,1,0:T(8,128)(2,1)S(1)}, bf16[9,32,128]{2,1,0:T(8,128)(2,1)S(1)}, bf16[9,32,128]{2,1,0:T(8,128)(2,1)S(1)}) custom-call(f32[8,1024]{1,0:T(8,128)S(1)} %get-tuple-element.42.edge_ref, f32[1,1024]{1,0:T(1,128)S(1)} %bitcast.10, f32[3,3,1024]{2,1,0:T(4,128)S(1)} %copy-done.5, ...), custom_call_target="tpu_custom_call" | custom-call | flops 8999999488 | bytes 7000000 | tf_op jit(solution)/shard_map/back/pallas_call | solution.py:342
  30.1 2.5 %collective-permute-start.11 = (bf16[9,32,128]{2,1,0:T(8,128)(2,1)S(1)}, bf16[9,32,128]{2,1,0:T(8,128)(2,1)S(1)}, u32[]{:S(2)}, u32[]{:S(2)}) collective-permute-start(bf16[9,32,128]{2,1,0:T(8,128)(2,1)S(1)} %get-tuple-element.66), channel_id=1, source_target_pairs={{4,8},{8,4},{12,0},{0,12},{5,9},{9,5},{13,1},{1,13},{6,10},{10,6},... | collective-permute-start | bytes 221192 | tf_op jit(solution)/shard_map/ppermute | solution.py:516
  32.6 0.5 %collective-permute-start.12 = (bf16[9,32,128]{2,1,0:T(8,128)(2,1)S(1)}, bf16[9,32,128]{2,1,0:T(8,128)(2,1)S(1)}, u32[]{:S(2)}, u32[]{:S(2)}) collective-permute-start(bf16[9,32,128]{2,1,0:T(8,128)(2,1)S(1)} %get-tuple-element.67), channel_id=1, source_target_pairs={{1,2},{2,1},{3,0},{0,3},{5,6},{6,5},{7,4},{4,7},{9,10},{10,9},{11,... | collective-permute-start | bytes 221192 | tf_op jit(solution)/shard_map/ppermute | solution.py:516
  33.1 1.6 %collective-permute-done.9.refs_2_ = bf16[544,128]{1,0:T(8,128)(2,1)S(1)} collective-permute-done((bf16[544,128]{1,0:T(8,128)(2,1)S(1)}, bf16[544,128]{1,0:T(8,128)(2,1)S(1)}, u32[]{:S(2)}, u32[]{:S(2)}) %collective-permute-start.9) | collective-permute-done | bytes 139296 | tf_op jit(solution)/shard_map/ppermute | solution.py:507
  34.7 0.0 collective-permute-start.14
  34.7 1.8 %collective-permute-done.10.refs_3_ = bf16[544,128]{1,0:T(8,128)(2,1)S(1)} collective-permute-done((bf16[544,128]{1,0:T(8,128)(2,1)S(1)}, bf16[544,128]{1,0:T(8,128)(2,1)S(1)}, u32[]{:S(2)}, u32[]{:S(2)}) %collective-permute-start.10) | collective-permute-done | bytes 139296 | tf_op jit(solution)/shard_map/ppermute | solution.py:507
  36.5 0.1 total_sum.1.refs_0_
  36.6 0.5 %collective-permute-done.12.b_ref = bf16[9,32,128]{2,1,0:T(8,128)(2,1)S(1)} collective-permute-done((bf16[9,32,128]{2,1,0:T(8,128)(2,1)S(1)}, bf16[9,32,128]{2,1,0:T(8,128)(2,1)S(1)}, u32[]{:S(2)}, u32[]{:S(2)}) %collective-permute-start.12) | collective-permute-done | bytes 73760 | tf_op jit(solution)/shard_map/ppermute | solution.py:516
  37.1 0.9 %collective-permute-done.13.c_ref = bf16[9,32,128]{2,1,0:T(8,128)(2,1)S(1)} collective-permute-done((bf16[9,32,128]{2,1,0:T(8,128)(2,1)S(1)}, bf16[9,32,128]{2,1,0:T(8,128)(2,1)S(1)}, u32[]{:S(2)}, u32[]{:S(2)}) %collective-permute-start.13) | collective-permute-done | bytes 73760 | tf_op jit(solution)/shard_map/ppermute | solution.py:516
  38.0 0.0 collective-permute-done.14.d_ref
  38.0 1.5 %collective-permute-start.15 = (bf16[544,128]{1,0:T(8,128)(2,1)S(1)}, bf16[544,128]{1,0:T(8,128)(2,1)S(1)}, u32[]{:S(2)}, u32[]{:S(2)}) collective-permute-start(bf16[544,128]{1,0:T(8,128)(2,1)S(1)} %total_sum.1.refs_0_), channel_id=1, source_target_pairs={{0,2},{1,3},{2,0},{3,1},{4,6},{5,7},{6,4},{7,5},{8,10},{9,11},{10,... | collective-permute-start | bytes 417800 | tf_op jit(solution)/shard_map/ppermute | solution.py:507
  39.5 1.2 %finish.1 = bf16[9,128,128]{2,1,0:T(8,128)(2,1)} custom-call(s32[4,32]{1,0:T(4,128)S(1)} %copy-done.1, f32[9,128,128]{2,1,0:T(8,128)S(1)} %get-tuple-element.71.own_ref, bf16[9,32,128]{2,1,0:T(8,128)(2,1)S(1)} %collective-permute-done.11.a_ref, bf16[9,32,128]{2,1,0:T(8,128)(2,1)S(1)} %collective-permute-done.12.b_ref, ...), custom_call_target="tpu_custom_call" | custom-call | flops 100000000 | bytes 2000000 | tf_op jit(solution)/shard_map/finish/pallas_call | solution.py:495
  40.7 3.0 %collective-permute-done.15.refs_1_ = bf16[544,128]{1,0:T(8,128)(2,1)S(1)} collective-permute-done((bf16[544,128]{1,0:T(8,128)(2,1)S(1)}, bf16[544,128]{1,0:T(8,128)(2,1)S(1)}, u32[]{:S(2)}, u32[]{:S(2)}) %collective-permute-start.15) | collective-permute-done | bytes 139296 | tf_op jit(solution)/shard_map/ppermute | solution.py:507
  43.7 1.4 %collective-permute-done.17.refs_3_ = bf16[544,128]{1,0:T(8,128)(2,1)S(1)} collective-permute-done((bf16[544,128]{1,0:T(8,128)(2,1)S(1)}, bf16[544,128]{1,0:T(8,128)(2,1)S(1)}, u32[]{:S(2)}, u32[]{:S(2)}) %collective-permute-start.17) | collective-permute-done | bytes 139296 | tf_op jit(solution)/shard_map/ppermute | solution.py:507
  45.1 1.5 %expert_product.1 = f32[8,69632]{1,0:T(8,128)} custom-call(f32[2,32]{1,0:T(2,128)S(1)} %copy-done, bf16[544,128]{1,0:T(8,128)(2,1)S(1)} %total_sum.1.refs_0_, bf16[544,128]{1,0:T(8,128)(2,1)S(1)} %collective-permute-done.15.refs_1_, bf16[544,128]{1,0:T(8,128)(2,1)S(1)} %collective-permute-done.16.refs_2_, bf16[544,128]{1,0:T(8,128)(2,1)S(1)} %collective-permute-done.17.refs_3_), custom_call_target="tpu_custom_call" | custom-call | flops 1000000 | bytes 4000000 | tf_op jit(solution)/shard_map/expert_product/pallas_call | solution.py:460
  (30 shorter events, 0.1 us)
Async XLA Ops:
  0.6 0.7 %copy-start = (f32[2,32]{1,0:T(2,128)S(1)}, f32[2,32]{1,0:T(2,128)}, u32[]{:S(2)}) copy-start(f32[2,32]{1,0:T(2,128)} %coef_ref.1) | copy-start | bytes 772
  1.3 8.5 %copy-start.2 = (bf16[256,9,128]{2,0,1:T(8,128)(2,1)S(1)}, bf16[256,9,128]{2,0,1:T(8,128)(2,1)}, u32[]{:S(2)}) copy-start(bf16[256,9,128]{2,0,1:T(8,128)(2,1)} %param.11) | copy-start | bytes 1769476
  1.3 8.5 %copy-start.3 = (bf16[128,9,128]{2,0,1:T(8,128)(2,1)S(1)}, bf16[128,9,128]{2,0,1:T(8,128)(2,1)}, u32[]{:S(2)}) copy-start(bf16[128,9,128]{2,0,1:T(8,128)(2,1)} %param.12) | copy-start | bytes 884740
  1.3 8.5 %copy-start.4 = (f32[5,5,1024]{2,1,0:T(8,128)S(1)}, f32[5,5,1024]{2,1,0:T(8,128)}, u32[]{:S(2)}) copy-start(f32[5,5,1024]{2,1,0:T(8,128)} %two_ref.3) | copy-start | bytes 307204
  1.3 8.5 %copy-start.5 = (f32[3,3,1024]{2,1,0:T(4,128)S(1)}, f32[3,3,1024]{2,1,0:T(4,128)}, u32[]{:S(2)}) copy-start(f32[3,3,1024]{2,1,0:T(4,128)} %one_ref.3) | copy-start | bytes 110596
  1.3 8.5 %copy-start.6 = (s32[128,8]{0,1:T(8,128)S(1)}, s32[128,8]{0,1:T(8,128)}, u32[]{:S(2)}) copy-start(s32[128,8]{0,1:T(8,128)} %param.13) | copy-start | bytes 12292
  1.3 8.5 %copy-start.7 = (f32[1024]{0:T(1024)S(1)}, f32[1024]{0:T(1024)}, u32[]{:S(2)}) copy-start(f32[1024]{0:T(1024)} %param.14) | copy-start | bytes 12292
  1.3 8.5 %copy-start.8 = (s32[128]{0:T(128)S(1)}, s32[128]{0:T(128)}, u32[]{:S(2)}) copy-start(s32[128]{0:T(128)} %param.18) | copy-start | bytes 1540
  3.4 13.7 %collective-permute-start.6 = (bf16[2,272,128]{2,1,0:T(8,128)(2,1)S(1)}, bf16[2,272,128]{2,1,0:T(8,128)(2,1)S(1)}, u32[]{:S(2)}, u32[]{:S(2)}) collective-permute-start(bf16[2,272,128]{2,1,0:T(8,128)(2,1)S(1)} %merge.1.refs_0_), channel_id=1, source_target_pairs={{0,12},{4,8},{8,4},{12,0},{1,13},{5,9},{9,5},{13,1},{2,14},{6,10},... | collective-permute-start | bytes 417800 | tf_op jit(solution)/shard_map/ppermute | solution.py:507
  8.5 8.6 %collective-permute-start.5 = (bf16[2,272,128]{2,1,0:T(8,128)(2,1)S(1)}, bf16[2,272,128]{2,1,0:T(8,128)(2,1)S(1)}, u32[]{:S(2)}, u32[]{:S(2)}) collective-permute-start(bf16[2,272,128]{2,1,0:T(8,128)(2,1)S(1)} %merge.1.refs_0_), channel_id=1, source_target_pairs={{0,4},{4,0},{8,12},{12,8},{1,5},{5,1},{9,13},{13,9},{2,6},{6,2},{1... | collective-permute-start | bytes 417800 | tf_op jit(solution)/shard_map/ppermute | solution.py:507
  8.5 11.8 %collective-permute-start.4 = (bf16[2,272,128]{2,1,0:T(8,128)(2,1)S(1)}, bf16[2,272,128]{2,1,0:T(8,128)(2,1)S(1)}, u32[]{:S(2)}, u32[]{:S(2)}) collective-permute-start(bf16[2,272,128]{2,1,0:T(8,128)(2,1)S(1)} %merge.1.refs_0_), channel_id=1, source_target_pairs={{0,8},{4,12},{8,0},{12,4},{1,9},{5,13},{9,1},{13,5},{2,10},{6,14},... | collective-permute-start | bytes 417800 | tf_op jit(solution)/shard_map/ppermute | solution.py:507
  16.5 3.8 %collective-permute-start = (bf16[544,128]{1,0:T(8,128)(2,1)S(1)}, bf16[544,128]{1,0:T(8,128)(2,1)S(1)}, u32[]{:S(2)}, u32[]{:S(2)}) collective-permute-start(bf16[544,128]{1,0:T(8,128)(2,1)S(1)} %get-tuple-element.44), channel_id=1, source_target_pairs={{0,1},{1,0},{2,3},{3,2},{4,5},{5,4},{6,7},{7,6},{8,9},{9,8},{10,11... | collective-permute-start | bytes 417800 | tf_op jit(solution)/shard_map/ppermute | solution.py:507
  16.5 3.7 %collective-permute-start.1 = (bf16[544,128]{1,0:T(8,128)(2,1)S(1)}, bf16[544,128]{1,0:T(8,128)(2,1)S(1)}, u32[]{:S(2)}, u32[]{:S(2)}) collective-permute-start(bf16[544,128]{1,0:T(8,128)(2,1)S(1)} %get-tuple-element.45), channel_id=1, source_target_pairs={{0,1},{1,0},{2,3},{3,2},{4,5},{5,4},{6,7},{7,6},{8,9},{9,8},{10,11... | collective-permute-start | bytes 417800 | tf_op jit(solution)/shard_map/ppermute | solution.py:507
  17.0 3.2 %collective-permute-start.2 = (bf16[544,128]{1,0:T(8,128)(2,1)S(1)}, bf16[544,128]{1,0:T(8,128)(2,1)S(1)}, u32[]{:S(2)}, u32[]{:S(2)}) collective-permute-start(bf16[544,128]{1,0:T(8,128)(2,1)S(1)} %get-tuple-element.46), channel_id=1, source_target_pairs={{0,1},{1,0},{2,3},{3,2},{4,5},{5,4},{6,7},{7,6},{8,9},{9,8},{10,11... | collective-permute-start | bytes 417800 | tf_op jit(solution)/shard_map/ppermute | solution.py:507
  17.1 3.2 %collective-permute-start.3 = (bf16[544,128]{1,0:T(8,128)(2,1)S(1)}, bf16[544,128]{1,0:T(8,128)(2,1)S(1)}, u32[]{:S(2)}, u32[]{:S(2)}) collective-permute-start(bf16[544,128]{1,0:T(8,128)(2,1)S(1)} %get-tuple-element.47), channel_id=1, source_target_pairs={{0,1},{1,0},{2,3},{3,2},{4,5},{5,4},{6,7},{7,6},{8,9},{9,8},{10,11... | collective-permute-start | bytes 417800 | tf_op jit(solution)/shard_map/ppermute | solution.py:507
  20.3 4.7 %collective-permute-start.7 = (bf16[4,2,272,128]{3,2,1,0:T(8,128)(2,1)S(1)}, bf16[4,2,272,128]{3,2,1,0:T(8,128)(2,1)S(1)}, u32[]{:S(2)}, u32[]{:S(2)}) collective-permute-start(bf16[4,2,272,128]{3,2,1,0:T(8,128)(2,1)S(1)} %pack.1.rest_0_), channel_id=1, source_target_pairs={{0,1},{1,0},{2,3},{3,2},{4,5},{5,4},{6,7},{7,6},{8,9},{9,8},{10,11... | collective-permute-start | bytes 1671176 | tf_op jit(solution)/shard_map/ppermute | solution.py:507
  20.6 12.5 %collective-permute-start.8 = (bf16[544,128]{1,0:T(8,128)(2,1)S(1)}, bf16[544,128]{1,0:T(8,128)(2,1)S(1)}, u32[]{:S(2)}, u32[]{:S(2)}) collective-permute-start(bf16[544,128]{1,0:T(8,128)(2,1)S(1)} %get-tuple-element.59), channel_id=1, source_target_pairs={{0,12},{4,8},{8,4},{12,0},{1,13},{5,9},{9,5},{13,1},{2,14},{6,10},... | collective-permute-start | bytes 417800 | tf_op jit(solution)/shard_map/ppermute | solution.py:507
  23.1 11.6 %collective-permute-start.9 = (bf16[544,128]{1,0:T(8,128)(2,1)S(1)}, bf16[544,128]{1,0:T(8,128)(2,1)S(1)}, u32[]{:S(2)}, u32[]{:S(2)}) collective-permute-start(bf16[544,128]{1,0:T(8,128)(2,1)S(1)} %get-tuple-element.60), channel_id=1, source_target_pairs={{0,4},{4,0},{8,12},{12,8},{1,5},{5,1},{9,13},{13,9},{2,6},{6,2},{1... | collective-permute-start | bytes 417800 | tf_op jit(solution)/shard_map/ppermute | solution.py:507
  23.1 13.4 %collective-permute-start.10 = (bf16[544,128]{1,0:T(8,128)(2,1)S(1)}, bf16[544,128]{1,0:T(8,128)(2,1)S(1)}, u32[]{:S(2)}, u32[]{:S(2)}) collective-permute-start(bf16[544,128]{1,0:T(8,128)(2,1)S(1)} %get-tuple-element.61), channel_id=1, source_target_pairs={{0,8},{4,12},{8,0},{12,4},{1,9},{5,13},{9,1},{13,5},{2,10},{6,14},... | collective-permute-start | bytes 417800 | tf_op jit(solution)/shard_map/ppermute | solution.py:507
  25.1 14.5 %copy-start.1 = (s32[4,32]{1,0:T(4,128)S(1)}, s32[4,32]{1,0:T(4,128)}, u32[]{:S(2)}) copy-start(s32[4,32]{1,0:T(4,128)} %send_ref.1) | copy-start | bytes 1540
  30.1 6.5 %collective-permute-start.11 = (bf16[9,32,128]{2,1,0:T(8,128)(2,1)S(1)}, bf16[9,32,128]{2,1,0:T(8,128)(2,1)S(1)}, u32[]{:S(2)}, u32[]{:S(2)}) collective-permute-start(bf16[9,32,128]{2,1,0:T(8,128)(2,1)S(1)} %get-tuple-element.66), channel_id=1, source_target_pairs={{4,8},{8,4},{12,0},{0,12},{5,9},{9,5},{13,1},{1,13},{6,10},{10,6},... | collective-permute-start | bytes 221192 | tf_op jit(solution)/shard_map/ppermute | solution.py:516
  32.6 4.5 %collective-permute-start.12 = (bf16[9,32,128]{2,1,0:T(8,128)(2,1)S(1)}, bf16[9,32,128]{2,1,0:T(8,128)(2,1)S(1)}, u32[]{:S(2)}, u32[]{:S(2)}) collective-permute-start(bf16[9,32,128]{2,1,0:T(8,128)(2,1)S(1)} %get-tuple-element.67), channel_id=1, source_target_pairs={{1,2},{2,1},{3,0},{0,3},{5,6},{6,5},{7,4},{4,7},{9,10},{10,9},{11,... | collective-permute-start | bytes 221192 | tf_op jit(solution)/shard_map/ppermute | solution.py:516
  33.1 5.0 %collective-permute-start.13 = (bf16[9,32,128]{2,1,0:T(8,128)(2,1)S(1)}, bf16[9,32,128]{2,1,0:T(8,128)(2,1)S(1)}, u32[]{:S(2)}, u32[]{:S(2)}) collective-permute-start(bf16[9,32,128]{2,1,0:T(8,128)(2,1)S(1)} %get-tuple-element.68), channel_id=1, source_target_pairs={{0,4},{4,0},{8,12},{12,8},{1,5},{5,1},{9,13},{13,9},{2,6},{6,2},{1... | collective-permute-start | bytes 221192 | tf_op jit(solution)/shard_map/ppermute | solution.py:516
  34.7 3.4 %collective-permute-start.14 = (bf16[9,32,128]{2,1,0:T(8,128)(2,1)S(1)}, bf16[9,32,128]{2,1,0:T(8,128)(2,1)S(1)}, u32[]{:S(2)}, u32[]{:S(2)}) collective-permute-start(bf16[9,32,128]{2,1,0:T(8,128)(2,1)S(1)} %get-tuple-element.69), channel_id=1, source_target_pairs={{0,1},{1,0},{2,3},{3,2},{4,5},{5,4},{6,7},{7,6},{8,9},{9,8},{10,11... | collective-permute-start | bytes 221192 | tf_op jit(solution)/shard_map/ppermute | solution.py:516
  38.0 5.7 %collective-permute-start.15 = (bf16[544,128]{1,0:T(8,128)(2,1)S(1)}, bf16[544,128]{1,0:T(8,128)(2,1)S(1)}, u32[]{:S(2)}, u32[]{:S(2)}) collective-permute-start(bf16[544,128]{1,0:T(8,128)(2,1)S(1)} %total_sum.1.refs_0_), channel_id=1, source_target_pairs={{0,2},{1,3},{2,0},{3,1},{4,6},{5,7},{6,4},{7,5},{8,10},{9,11},{10,... | collective-permute-start | bytes 417800 | tf_op jit(solution)/shard_map/ppermute | solution.py:507
  39.5 4.2 %collective-permute-start.16 = (bf16[544,128]{1,0:T(8,128)(2,1)S(1)}, bf16[544,128]{1,0:T(8,128)(2,1)S(1)}, u32[]{:S(2)}, u32[]{:S(2)}) collective-permute-start(bf16[544,128]{1,0:T(8,128)(2,1)S(1)} %total_sum.1.refs_0_), channel_id=1, source_target_pairs={{0,1},{1,0},{2,3},{3,2},{4,5},{5,4},{6,7},{7,6},{8,9},{9,8},{10,11... | collective-permute-start | bytes 417800 | tf_op jit(solution)/shard_map/ppermute | solution.py:507
  43.7 1.4 %collective-permute-start.17 = (bf16[544,128]{1,0:T(8,128)(2,1)S(1)}, bf16[544,128]{1,0:T(8,128)(2,1)S(1)}, u32[]{:S(2)}, u32[]{:S(2)}) collective-permute-start(bf16[544,128]{1,0:T(8,128)(2,1)S(1)} %collective-permute-done.15.refs_1_), channel_id=1, source_target_pairs={{0,1},{1,0},{2,3},{3,2},{4,5},{5,4},{6,7},{7,6},{8,9},{9,8},{10,11... | collective-permute-start | bytes 417800 | tf_op jit(solution)/shard_map/ppermute | solution.py:507

commit v14 on v13

--- a/solution.py
+++ b/solution.py
@@ -330,8 +330,8 @@
         for side in range(2):
             even = lax.rem(lax.axis_index(("gx", "yz")[side]), 2) == 0
             low, high = blocks[2 * side], blocks[2 * side + 1]
-            ghost_refs[3 - side][c] = jnp.where(even, high, low).astype(BF16)
-            ghost_refs[1 - side][c] = jnp.where(even, low, high).astype(BF16)
+            ghost_refs[3 - 2 * side][c] = jnp.where(even, high, low).astype(BF16)
+            ghost_refs[2 - 2 * side][c] = jnp.where(even, low, high).astype(BF16)
 
 
 def back(edge, zero, one, two, pulled, pieces, places, rows, atoms, slots, face):
@@ -483,7 +483,7 @@
         below, above = send_ref[2 * side : 2 * side + 1, :], send_ref[2 * side + 1 : 2 * side + 2, :]
         for faces in (jnp.where(even, above, below), jnp.where(even, below, above)):
             picks.append((row == faces).astype(F32).astype(BF16))
-    picks = [picks[3], picks[1], picks[2], picks[0]]
+    picks = [picks[3], picks[2], picks[1], picks[0]]
     for c in range(9):
         total = own_ref[c]
         for pick, ref in zip(picks, (a_ref, b_ref, c_ref, d_ref)):
@@ -568,7 +568,7 @@
     grad_own, *ghosts = back(edge, zero, rot_one, rot_two, pulled, pieces, places, rows, atoms, slots, face)
     returned = [
         neighbour_pairs(ghost, axis, first)
-        for ghost, axis, first in zip(ghosts, ("yz", "gx", "yz", "gx"), (1, 1, 0, 0))
+        for ghost, axis, first in zip(ghosts, ("yz", "yz", "gx", "gx"), (1, 0, 1, 0))
     ]
     if direct:
         grad_own, *gathered = lax.optimization_barrier((grad_own, *gathered))

time: 46.8 us -> 46 us (0.983)
  waiting for transfers between devices: 12 us -> 11.2 us
    ppermute x14, waiting for transfers between devices: 10.5 us -> 9.35 us  [swap(): lax.ppermute(value, axis, [(i, i ^ bit) for i in range(lax.axis_size(axis...]
where the time goes in v14:
time: 46 us; the launch traced here: 45.8 us
  Pallas kernels  16.6 us (36%)
  starting transfers between devices  15.9 us (35%)
  waiting for transfers between devices  11.2 us (24%)
  between operations  1.46 us (3%)
  local copies, waits for them, and re-layouts  0.7 us (2%)
    ppermute x14, starting transfers between devices, swap(): lax.ppermute(value, axis, [(i, i ^ bit) for i in range(lax.axis_size(axis...  12.9 us
    ppermute x14, waiting for transfers between devices, swap(): lax.ppermute(value, axis, [(i, i ^ bit) for i in range(lax.axis_size(axis...  9.35 us
    pallas_call x1, Pallas kernels, features(): pl.pallas_call(functools.partial(features_kernel, fanout=fanout, cuts=cut...  6.59 us
    pallas_call x1, Pallas kernels, back(): pl.pallas_call(functools.partial(back_kernel, pieces=len(pieces), members...  5 us
    ppermute x4, starting transfers between devices, neighbour_pairs(): return lax.ppermute(value, axis, moves)  3 us
    pallas_call x1, Pallas kernels, merge(): pl.pallas_call(merge_kernel, in_specs=[HBM, HBM], out_specs=VMEM, out_sha...  2.03 us
    ppermute x4, waiting for transfers between devices, neighbour_pairs(): return lax.ppermute(value, axis, moves)  1.85 us
    pallas_call x1, Pallas kernels, expert_product(): pl.pallas_call(functools.partial(expert_kernel, scale=scale), in_specs=[V...  1.54 us
  transfers between devices with their start and end apart: 18, of which 7 were waited for; matrix products, arithmetic and copies ran while one was open for 0% of the time, Pallas kernels for 28%

profile of v14, /device:TPU:0, one launch (start us, length us, event | category | flops | bytes accessed | tf_op | source)
XLA Modules:
  0.0 45.8 jit_solution(16329149115774731981)
XLA Ops:
  0.6 0.7 %copy-done = f32[2,32]{1,0:T(2,128)S(1)} copy-done((f32[2,32]{1,0:T(2,128)S(1)}, f32[2,32]{1,0:T(2,128)}, u32[]{:S(2)}) %copy-start) | copy-done | bytes 280
  1.4 2.0 %merge.1.refs_0_ = bf16[2,272,128]{2,1,0:T(8,128)(2,1)S(1)} custom-call(f32[2,32]{1,0:T(2,128)S(1)} %copy-done, bf16[32,69632]{1,0:T(8,128)(2,1)} %experts_ref.1), custom_call_target="tpu_custom_call" | custom-call | flops 53477376 | bytes 2228224 | tf_op jit(solution)/shard_map/merge/pallas_call | solution.py:102
  3.4 5.1 %collective-permute-start.6 = (bf16[2,272,128]{2,1,0:T(8,128)(2,1)S(1)}, bf16[2,272,128]{2,1,0:T(8,128)(2,1)S(1)}, u32[]{:S(2)}, u32[]{:S(2)}) collective-permute-start(bf16[2,272,128]{2,1,0:T(8,128)(2,1)S(1)} %merge.1.refs_0_), channel_id=1, source_target_pairs={{0,12},{4,8},{8,4},{12,0},{1,13},{5,9},{9,5},{13,1},{2,14},{6,10},... | collective-permute-start | bytes 417800 | tf_op jit(solution)/shard_map/ppermute | solution.py:507
  8.5 0.6 %collective-permute-start.4 = (bf16[2,272,128]{2,1,0:T(8,128)(2,1)S(1)}, bf16[2,272,128]{2,1,0:T(8,128)(2,1)S(1)}, u32[]{:S(2)}, u32[]{:S(2)}) collective-permute-start(bf16[2,272,128]{2,1,0:T(8,128)(2,1)S(1)} %merge.1.refs_0_), channel_id=1, source_target_pairs={{0,8},{4,12},{8,0},{12,4},{1,9},{5,13},{9,1},{13,5},{2,10},{6,14},... | collective-permute-start | bytes 417800 | tf_op jit(solution)/shard_map/ppermute | solution.py:507
  9.9 6.6 %features.1 = (bf16[544,128]{1,0:T(8,128)(2,1)S(1)}, bf16[544,128]{1,0:T(8,128)(2,1)S(1)}, bf16[544,128]{1,0:T(8,128)(2,1)S(1)}, bf16[544,128]{1,0:T(8,128)(2,1)...) custom-call(s32[1]{0:T(128)S(6)} %copy.13.live_in_ref, ...), custom_call_target="tpu_custom_call" | custom-call | flops 8999999488 | bytes 7000000 | tf_op jit(solution)/shard_map/features/pallas_call | solution.py:224
  16.5 0.1 collective-permute-start
  16.5 0.5 %collective-permute-start.1 = (bf16[544,128]{1,0:T(8,128)(2,1)S(1)}, bf16[544,128]{1,0:T(8,128)(2,1)S(1)}, u32[]{:S(2)}, u32[]{:S(2)}) collective-permute-start(bf16[544,128]{1,0:T(8,128)(2,1)S(1)} %get-tuple-element.45), channel_id=1, source_target_pairs={{0,1},{1,0},{2,3},{3,2},{4,5},{5,4},{6,7},{7,6},{8,9},{9,8},{10,11... | collective-permute-start | bytes 417800 | tf_op jit(solution)/shard_map/ppermute | solution.py:507
  17.0 0.1 collective-permute-start.2
  17.1 0.0 collective-permute-done.5.refs_2_
  17.1 0.4 collective-permute-start.3
  17.6 2.7 %collective-permute-done.4.refs_1_ = bf16[2,272,128]{2,1,0:T(8,128)(2,1)S(1)} collective-permute-done((bf16[2,272,128]{2,1,0:T(8,128)(2,1)S(1)}, bf16[2,272,128]{2,1,0:T(8,128)(2,1)S(1)}, u32[]{:S(2)}, u32[]{:S(2)}) %collective-permute-start.4) | collective-permute-done | bytes 139296 | tf_op jit(solution)/shard_map/ppermute | solution.py:507
  20.3 0.0 collective-permute-done.refs_0_
  20.3 0.1 collective-permute-start.7
  20.4 0.2 pair_sum.1
  20.6 2.5 %collective-permute-start.8 = (bf16[544,128]{1,0:T(8,128)(2,1)S(1)}, bf16[544,128]{1,0:T(8,128)(2,1)S(1)}, u32[]{:S(2)}, u32[]{:S(2)}) collective-permute-start(bf16[544,128]{1,0:T(8,128)(2,1)S(1)} %get-tuple-element.59), channel_id=1, source_target_pairs={{0,12},{4,8},{8,4},{12,0},{1,13},{5,9},{9,5},{13,1},{2,14},{6,10},... | collective-permute-start | bytes 417800 | tf_op jit(solution)/shard_map/ppermute | solution.py:507
  23.1 1.9 %collective-permute-start.10 = (bf16[544,128]{1,0:T(8,128)(2,1)S(1)}, bf16[544,128]{1,0:T(8,128)(2,1)S(1)}, u32[]{:S(2)}, u32[]{:S(2)}) collective-permute-start(bf16[544,128]{1,0:T(8,128)(2,1)S(1)} %get-tuple-element.61), channel_id=1, source_target_pairs={{0,8},{4,12},{8,0},{12,4},{1,9},{5,13},{9,1},{13,5},{2,10},{6,14},... | collective-permute-start | bytes 417800 | tf_op jit(solution)/shard_map/ppermute | solution.py:507
  25.1 5.0 %back.1 = (f32[9,128,128]{2,1,0:T(8,128)S(1)}, bf16[9,32,128]{2,1,0:T(8,128)(2,1)S(1)}, bf16[9,32,128]{2,1,0:T(8,128)(2,1)S(1)}, bf16[9,32,128]{2,1,0:T(8,128)(2,1)S(1)}, bf16[9,32,128]{2,1,0:T(8,128)(2,1)S(1)}) custom-call(f32[8,1024]{1,0:T(8,128)S(1)} %get-tuple-element.42.edge_ref, f32[1,1024]{1,0:T(1,128)S(1)} %bitcast.10, f32[3,3,1024]{2,1,0:T(4,128)S(1)} %copy-done.5, ...), custom_call_target="tpu_custom_call" | custom-call | flops 8999999488 | bytes 7000000 | tf_op jit(solution)/shard_map/back/pallas_call | solution.py:342
  30.1 2.5 %collective-permute-start.11 = (bf16[9,32,128]{2,1,0:T(8,128)(2,1)S(1)}, bf16[9,32,128]{2,1,0:T(8,128)(2,1)S(1)}, u32[]{:S(2)}, u32[]{:S(2)}) collective-permute-start(bf16[9,32,128]{2,1,0:T(8,128)(2,1)S(1)} %get-tuple-element.66), channel_id=1, source_target_pairs={{4,8},{8,4},{12,0},{0,12},{5,9},{9,5},{13,1},{1,13},{6,10},{10,6},... | collective-permute-start | bytes 221192 | tf_op jit(solution)/shard_map/ppermute | solution.py:516
  32.6 0.0 collective-permute-start.12
  32.6 0.0 collective-permute-done.8.refs_1_
  32.6 0.5 %collective-permute-start.13 = (bf16[9,32,128]{2,1,0:T(8,128)(2,1)S(1)}, bf16[9,32,128]{2,1,0:T(8,128)(2,1)S(1)}, u32[]{:S(2)}, u32[]{:S(2)}) collective-permute-start(bf16[9,32,128]{2,1,0:T(8,128)(2,1)S(1)} %get-tuple-element.68), channel_id=1, source_target_pairs={{1,2},{2,1},{3,0},{0,3},{5,6},{6,5},{7,4},{4,7},{9,10},{10,9},{11,... | collective-permute-start | bytes 221192 | tf_op jit(solution)/shard_map/ppermute | solution.py:516
  33.1 1.6 %collective-permute-done.9.refs_2_ = bf16[544,128]{1,0:T(8,128)(2,1)S(1)} collective-permute-done((bf16[544,128]{1,0:T(8,128)(2,1)S(1)}, bf16[544,128]{1,0:T(8,128)(2,1)S(1)}, u32[]{:S(2)}, u32[]{:S(2)}) %collective-permute-start.9) | collective-permute-done | bytes 139296 | tf_op jit(solution)/shard_map/ppermute | solution.py:507
  34.7 0.0 collective-permute-start.14
  34.7 1.2 %collective-permute-done.10.refs_3_ = bf16[544,128]{1,0:T(8,128)(2,1)S(1)} collective-permute-done((bf16[544,128]{1,0:T(8,128)(2,1)S(1)}, bf16[544,128]{1,0:T(8,128)(2,1)S(1)}, u32[]{:S(2)}, u32[]{:S(2)}) %collective-permute-start.10) | collective-permute-done | bytes 139296 | tf_op jit(solution)/shard_map/ppermute | solution.py:507
  35.8 0.1 total_sum.1.refs_0_
  35.9 1.1 %collective-permute-done.11.a_ref = bf16[9,32,128]{2,1,0:T(8,128)(2,1)S(1)} collective-permute-done((bf16[9,32,128]{2,1,0:T(8,128)(2,1)S(1)}, bf16[9,32,128]{2,1,0:T(8,128)(2,1)S(1)}, u32[]{:S(2)}, u32[]{:S(2)}) %collective-permute-start.11) | collective-permute-done | bytes 73760 | tf_op jit(solution)/shard_map/ppermute | solution.py:516
  37.0 0.8 %collective-permute-done.12.b_ref = bf16[9,32,128]{2,1,0:T(8,128)(2,1)S(1)} collective-permute-done((bf16[9,32,128]{2,1,0:T(8,128)(2,1)S(1)}, bf16[9,32,128]{2,1,0:T(8,128)(2,1)S(1)}, u32[]{:S(2)}, u32[]{:S(2)}) %collective-permute-start.12) | collective-permute-done | bytes 73760 | tf_op jit(solution)/shard_map/ppermute | solution.py:516
  37.8 1.5 %collective-permute-start.15 = (bf16[544,128]{1,0:T(8,128)(2,1)S(1)}, bf16[544,128]{1,0:T(8,128)(2,1)S(1)}, u32[]{:S(2)}, u32[]{:S(2)}) collective-permute-start(bf16[544,128]{1,0:T(8,128)(2,1)S(1)} %total_sum.1.refs_0_), channel_id=1, source_target_pairs={{0,2},{1,3},{2,0},{3,1},{4,6},{5,7},{6,4},{7,5},{8,10},{9,11},{10,... | collective-permute-start | bytes 417800 | tf_op jit(solution)/shard_map/ppermute | solution.py:507
  39.3 1.2 %finish.1 = bf16[9,128,128]{2,1,0:T(8,128)(2,1)} custom-call(s32[4,32]{1,0:T(4,128)S(1)} %copy-done.1, f32[9,128,128]{2,1,0:T(8,128)S(1)} %get-tuple-element.71.own_ref, bf16[9,32,128]{2,1,0:T(8,128)(2,1)S(1)} %collective-permute-done.11.a_ref, bf16[9,32,128]{2,1,0:T(8,128)(2,1)S(1)} %collective-permute-done.12.b_ref, ...), custom_call_target="tpu_custom_call" | custom-call | flops 100000000 | bytes 2000000 | tf_op jit(solution)/shard_map/finish/pallas_call | solution.py:495
  40.4 2.5 %collective-permute-done.15.refs_1_ = bf16[544,128]{1,0:T(8,128)(2,1)S(1)} collective-permute-done((bf16[544,128]{1,0:T(8,128)(2,1)S(1)}, bf16[544,128]{1,0:T(8,128)(2,1)S(1)}, u32[]{:S(2)}, u32[]{:S(2)}) %collective-permute-start.15) | collective-permute-done | bytes 139296 | tf_op jit(solution)/shard_map/ppermute | solution.py:507
  42.9 1.4 %collective-permute-done.17.refs_3_ = bf16[544,128]{1,0:T(8,128)(2,1)S(1)} collective-permute-done((bf16[544,128]{1,0:T(8,128)(2,1)S(1)}, bf16[544,128]{1,0:T(8,128)(2,1)S(1)}, u32[]{:S(2)}, u32[]{:S(2)}) %collective-permute-start.17) | collective-permute-done | bytes 139296 | tf_op jit(solution)/shard_map/ppermute | solution.py:507
  44.3 1.5 %expert_product.1 = f32[8,69632]{1,0:T(8,128)} custom-call(f32[2,32]{1,0:T(2,128)S(1)} %copy-done, bf16[544,128]{1,0:T(8,128)(2,1)S(1)} %total_sum.1.refs_0_, bf16[544,128]{1,0:T(8,128)(2,1)S(1)} %collective-permute-done.15.refs_1_, bf16[544,128]{1,0:T(8,128)(2,1)S(1)} %collective-permute-done.16.refs_2_, bf16[544,128]{1,0:T(8,128)(2,1)S(1)} %collective-permute-done.17.refs_3_), custom_call_target="tpu_custom_call" | custom-call | flops 1000000 | bytes 4000000 | tf_op jit(solution)/shard_map/expert_product/pallas_call | solution.py:460
  (30 shorter events, 0.1 us)
Async XLA Ops:
  0.6 0.7 %copy-start = (f32[2,32]{1,0:T(2,128)S(1)}, f32[2,32]{1,0:T(2,128)}, u32[]{:S(2)}) copy-start(f32[2,32]{1,0:T(2,128)} %coef_ref.1) | copy-start | bytes 772
  1.3 8.5 %copy-start.2 = (bf16[256,9,128]{2,0,1:T(8,128)(2,1)S(1)}, bf16[256,9,128]{2,0,1:T(8,128)(2,1)}, u32[]{:S(2)}) copy-start(bf16[256,9,128]{2,0,1:T(8,128)(2,1)} %param.11) | copy-start | bytes 1769476
  1.3 8.5 %copy-start.3 = (bf16[128,9,128]{2,0,1:T(8,128)(2,1)S(1)}, bf16[128,9,128]{2,0,1:T(8,128)(2,1)}, u32[]{:S(2)}) copy-start(bf16[128,9,128]{2,0,1:T(8,128)(2,1)} %param.12) | copy-start | bytes 884740
  1.3 8.5 %copy-start.4 = (f32[5,5,1024]{2,1,0:T(8,128)S(1)}, f32[5,5,1024]{2,1,0:T(8,128)}, u32[]{:S(2)}) copy-start(f32[5,5,1024]{2,1,0:T(8,128)} %two_ref.3) | copy-start | bytes 307204
  1.3 8.5 %copy-start.5 = (f32[3,3,1024]{2,1,0:T(4,128)S(1)}, f32[3,3,1024]{2,1,0:T(4,128)}, u32[]{:S(2)}) copy-start(f32[3,3,1024]{2,1,0:T(4,128)} %one_ref.3) | copy-start | bytes 110596
  1.3 8.5 %copy-start.6 = (s32[128,8]{0,1:T(8,128)S(1)}, s32[128,8]{0,1:T(8,128)}, u32[]{:S(2)}) copy-start(s32[128,8]{0,1:T(8,128)} %param.13) | copy-start | bytes 12292
  1.3 8.5 %copy-start.7 = (f32[1024]{0:T(1024)S(1)}, f32[1024]{0:T(1024)}, u32[]{:S(2)}) copy-start(f32[1024]{0:T(1024)} %param.14) | copy-start | bytes 12292
  1.3 8.5 %copy-start.8 = (s32[128]{0:T(128)S(1)}, s32[128]{0:T(128)}, u32[]{:S(2)}) copy-start(s32[128]{0:T(128)} %param.18) | copy-start | bytes 1540
  3.4 13.7 %collective-permute-start.6 = (bf16[2,272,128]{2,1,0:T(8,128)(2,1)S(1)}, bf16[2,272,128]{2,1,0:T(8,128)(2,1)S(1)}, u32[]{:S(2)}, u32[]{:S(2)}) collective-permute-start(bf16[2,272,128]{2,1,0:T(8,128)(2,1)S(1)} %merge.1.refs_0_), channel_id=1, source_target_pairs={{0,12},{4,8},{8,4},{12,0},{1,13},{5,9},{9,5},{13,1},{2,14},{6,10},... | collective-permute-start | bytes 417800 | tf_op jit(solution)/shard_map/ppermute | solution.py:507
  8.5 8.6 %collective-permute-start.5 = (bf16[2,272,128]{2,1,0:T(8,128)(2,1)S(1)}, bf16[2,272,128]{2,1,0:T(8,128)(2,1)S(1)}, u32[]{:S(2)}, u32[]{:S(2)}) collective-permute-start(bf16[2,272,128]{2,1,0:T(8,128)(2,1)S(1)} %merge.1.refs_0_), channel_id=1, source_target_pairs={{0,4},{4,0},{8,12},{12,8},{1,5},{5,1},{9,13},{13,9},{2,6},{6,2},{1... | collective-permute-start | bytes 417800 | tf_op jit(solution)/shard_map/ppermute | solution.py:507
  8.5 11.8 %collective-permute-start.4 = (bf16[2,272,128]{2,1,0:T(8,128)(2,1)S(1)}, bf16[2,272,128]{2,1,0:T(8,128)(2,1)S(1)}, u32[]{:S(2)}, u32[]{:S(2)}) collective-permute-start(bf16[2,272,128]{2,1,0:T(8,128)(2,1)S(1)} %merge.1.refs_0_), channel_id=1, source_target_pairs={{0,8},{4,12},{8,0},{12,4},{1,9},{5,13},{9,1},{13,5},{2,10},{6,14},... | collective-permute-start | bytes 417800 | tf_op jit(solution)/shard_map/ppermute | solution.py:507
  16.5 3.8 %collective-permute-start = (bf16[544,128]{1,0:T(8,128)(2,1)S(1)}, bf16[544,128]{1,0:T(8,128)(2,1)S(1)}, u32[]{:S(2)}, u32[]{:S(2)}) collective-permute-start(bf16[544,128]{1,0:T(8,128)(2,1)S(1)} %get-tuple-element.44), channel_id=1, source_target_pairs={{0,1},{1,0},{2,3},{3,2},{4,5},{5,4},{6,7},{7,6},{8,9},{9,8},{10,11... | collective-permute-start | bytes 417800 | tf_op jit(solution)/shard_map/ppermute | solution.py:507
  16.5 3.7 %collective-permute-start.1 = (bf16[544,128]{1,0:T(8,128)(2,1)S(1)}, bf16[544,128]{1,0:T(8,128)(2,1)S(1)}, u32[]{:S(2)}, u32[]{:S(2)}) collective-permute-start(bf16[544,128]{1,0:T(8,128)(2,1)S(1)} %get-tuple-element.45), channel_id=1, source_target_pairs={{0,1},{1,0},{2,3},{3,2},{4,5},{5,4},{6,7},{7,6},{8,9},{9,8},{10,11... | collective-permute-start | bytes 417800 | tf_op jit(solution)/shard_map/ppermute | solution.py:507
  17.0 3.2 %collective-permute-start.2 = (bf16[544,128]{1,0:T(8,128)(2,1)S(1)}, bf16[544,128]{1,0:T(8,128)(2,1)S(1)}, u32[]{:S(2)}, u32[]{:S(2)}) collective-permute-start(bf16[544,128]{1,0:T(8,128)(2,1)S(1)} %get-tuple-element.46), channel_id=1, source_target_pairs={{0,1},{1,0},{2,3},{3,2},{4,5},{5,4},{6,7},{7,6},{8,9},{9,8},{10,11... | collective-permute-start | bytes 417800 | tf_op jit(solution)/shard_map/ppermute | solution.py:507
  17.1 3.2 %collective-permute-start.3 = (bf16[544,128]{1,0:T(8,128)(2,1)S(1)}, bf16[544,128]{1,0:T(8,128)(2,1)S(1)}, u32[]{:S(2)}, u32[]{:S(2)}) collective-permute-start(bf16[544,128]{1,0:T(8,128)(2,1)S(1)} %get-tuple-element.47), channel_id=1, source_target_pairs={{0,1},{1,0},{2,3},{3,2},{4,5},{5,4},{6,7},{7,6},{8,9},{9,8},{10,11... | collective-permute-start | bytes 417800 | tf_op jit(solution)/shard_map/ppermute | solution.py:507
  20.3 4.7 %collective-permute-start.7 = (bf16[4,2,272,128]{3,2,1,0:T(8,128)(2,1)S(1)}, bf16[4,2,272,128]{3,2,1,0:T(8,128)(2,1)S(1)}, u32[]{:S(2)}, u32[]{:S(2)}) collective-permute-start(bf16[4,2,272,128]{3,2,1,0:T(8,128)(2,1)S(1)} %pack.1.rest_0_), channel_id=1, source_target_pairs={{0,1},{1,0},{2,3},{3,2},{4,5},{5,4},{6,7},{7,6},{8,9},{9,8},{10,11... | collective-permute-start | bytes 1671176 | tf_op jit(solution)/shard_map/ppermute | solution.py:507
  20.6 12.0 %collective-permute-start.8 = (bf16[544,128]{1,0:T(8,128)(2,1)S(1)}, bf16[544,128]{1,0:T(8,128)(2,1)S(1)}, u32[]{:S(2)}, u32[]{:S(2)}) collective-permute-start(bf16[544,128]{1,0:T(8,128)(2,1)S(1)} %get-tuple-element.59), channel_id=1, source_target_pairs={{0,12},{4,8},{8,4},{12,0},{1,13},{5,9},{9,5},{13,1},{2,14},{6,10},... | collective-permute-start | bytes 417800 | tf_op jit(solution)/shard_map/ppermute | solution.py:507
  23.1 11.6 %collective-permute-start.9 = (bf16[544,128]{1,0:T(8,128)(2,1)S(1)}, bf16[544,128]{1,0:T(8,128)(2,1)S(1)}, u32[]{:S(2)}, u32[]{:S(2)}) collective-permute-start(bf16[544,128]{1,0:T(8,128)(2,1)S(1)} %get-tuple-element.60), channel_id=1, source_target_pairs={{0,4},{4,0},{8,12},{12,8},{1,5},{5,1},{9,13},{13,9},{2,6},{6,2},{1... | collective-permute-start | bytes 417800 | tf_op jit(solution)/shard_map/ppermute | solution.py:507
  23.1 12.7 %collective-permute-start.10 = (bf16[544,128]{1,0:T(8,128)(2,1)S(1)}, bf16[544,128]{1,0:T(8,128)(2,1)S(1)}, u32[]{:S(2)}, u32[]{:S(2)}) collective-permute-start(bf16[544,128]{1,0:T(8,128)(2,1)S(1)} %get-tuple-element.61), channel_id=1, source_target_pairs={{0,8},{4,12},{8,0},{12,4},{1,9},{5,13},{9,1},{13,5},{2,10},{6,14},... | collective-permute-start | bytes 417800 | tf_op jit(solution)/shard_map/ppermute | solution.py:507
  25.1 14.2 %copy-start.1 = (s32[4,32]{1,0:T(4,128)S(1)}, s32[4,32]{1,0:T(4,128)}, u32[]{:S(2)}) copy-start(s32[4,32]{1,0:T(4,128)} %send_ref.1) | copy-start | bytes 1540
  30.1 6.9 %collective-permute-start.11 = (bf16[9,32,128]{2,1,0:T(8,128)(2,1)S(1)}, bf16[9,32,128]{2,1,0:T(8,128)(2,1)S(1)}, u32[]{:S(2)}, u32[]{:S(2)}) collective-permute-start(bf16[9,32,128]{2,1,0:T(8,128)(2,1)S(1)} %get-tuple-element.66), channel_id=1, source_target_pairs={{4,8},{8,4},{12,0},{0,12},{5,9},{9,5},{13,1},{1,13},{6,10},{10,6},... | collective-permute-start | bytes 221192 | tf_op jit(solution)/shard_map/ppermute | solution.py:516
  32.6 5.2 %collective-permute-start.12 = (bf16[9,32,128]{2,1,0:T(8,128)(2,1)S(1)}, bf16[9,32,128]{2,1,0:T(8,128)(2,1)S(1)}, u32[]{:S(2)}, u32[]{:S(2)}) collective-permute-start(bf16[9,32,128]{2,1,0:T(8,128)(2,1)S(1)} %get-tuple-element.67), channel_id=1, source_target_pairs={{0,4},{4,0},{8,12},{12,8},{1,5},{5,1},{9,13},{13,9},{2,6},{6,2},{1... | collective-permute-start | bytes 221192 | tf_op jit(solution)/shard_map/ppermute | solution.py:516
  32.6 5.2 %collective-permute-start.13 = (bf16[9,32,128]{2,1,0:T(8,128)(2,1)S(1)}, bf16[9,32,128]{2,1,0:T(8,128)(2,1)S(1)}, u32[]{:S(2)}, u32[]{:S(2)}) collective-permute-start(bf16[9,32,128]{2,1,0:T(8,128)(2,1)S(1)} %get-tuple-element.68), channel_id=1, source_target_pairs={{1,2},{2,1},{3,0},{0,3},{5,6},{6,5},{7,4},{4,7},{9,10},{10,9},{11,... | collective-permute-start | bytes 221192 | tf_op jit(solution)/shard_map/ppermute | solution.py:516
  34.7 3.1 %collective-permute-start.14 = (bf16[9,32,128]{2,1,0:T(8,128)(2,1)S(1)}, bf16[9,32,128]{2,1,0:T(8,128)(2,1)S(1)}, u32[]{:S(2)}, u32[]{:S(2)}) collective-permute-start(bf16[9,32,128]{2,1,0:T(8,128)(2,1)S(1)} %get-tuple-element.69), channel_id=1, source_target_pairs={{0,1},{1,0},{2,3},{3,2},{4,5},{5,4},{6,7},{7,6},{8,9},{9,8},{10,11... | collective-permute-start | bytes 221192 | tf_op jit(solution)/shard_map/ppermute | solution.py:516
  37.8 5.2 %collective-permute-start.15 = (bf16[544,128]{1,0:T(8,128)(2,1)S(1)}, bf16[544,128]{1,0:T(8,128)(2,1)S(1)}, u32[]{:S(2)}, u32[]{:S(2)}) collective-permute-start(bf16[544,128]{1,0:T(8,128)(2,1)S(1)} %total_sum.1.refs_0_), channel_id=1, source_target_pairs={{0,2},{1,3},{2,0},{3,1},{4,6},{5,7},{6,4},{7,5},{8,10},{9,11},{10,... | collective-permute-start | bytes 417800 | tf_op jit(solution)/shard_map/ppermute | solution.py:507
  39.3 3.7 %collective-permute-start.16 = (bf16[544,128]{1,0:T(8,128)(2,1)S(1)}, bf16[544,128]{1,0:T(8,128)(2,1)S(1)}, u32[]{:S(2)}, u32[]{:S(2)}) collective-permute-start(bf16[544,128]{1,0:T(8,128)(2,1)S(1)} %total_sum.1.refs_0_), channel_id=1, source_target_pairs={{0,1},{1,0},{2,3},{3,2},{4,5},{5,4},{6,7},{7,6},{8,9},{9,8},{10,11... | collective-permute-start | bytes 417800 | tf_op jit(solution)/shard_map/ppermute | solution.py:507
  42.9 1.4 %collective-permute-start.17 = (bf16[544,128]{1,0:T(8,128)(2,1)S(1)}, bf16[544,128]{1,0:T(8,128)(2,1)S(1)}, u32[]{:S(2)}, u32[]{:S(2)}) collective-permute-start(bf16[544,128]{1,0:T(8,128)(2,1)S(1)} %collective-permute-done.15.refs_1_), channel_id=1, source_target_pairs={{0,1},{1,0},{2,3},{3,2},{4,5},{5,4},{6,7},{7,6},{8,9},{9,8},{10,11... | collective-permute-start | bytes 417800 | tf_op jit(solution)/shard_map/ppermute | solution.py:507

commit v15 on v14

--- a/solution.py
+++ b/solution.py
@@ -9,7 +9,7 @@
 from jax.sharding import PartitionSpec as P
 
 LIVE_BLOCK = 64
-CHUNK = 512
+CHUNK = 1024
 SUB = 32
 F32 = jnp.float32
 BF16 = jnp.bfloat16

time: 46 us -> 46.1 us (level)
  waiting for transfers between devices: 11.2 us -> 12 us
  Pallas kernels: 16.6 us -> 15.9 us
    ppermute x14, waiting for transfers between devices: 9.35 us -> 10.1 us  [swap(): lax.ppermute(value, axis, [(i, i ^ bit) for i in range(lax.axis_size(axis...]
    pallas_call x1, Pallas kernels: 6.59 us -> 5.96 us  [features(): pl.pallas_call(functools.partial(features_kernel, fanout=fanout, cuts=cut...]
  transfers between devices with their start and end apart: 18 -> 18, of which waited for: 7 -> 7; matrix products, arithmetic and copies ran while one was open for 0% -> 0% of each run, Pallas kernels for 28% -> 27%
where the time goes in v15:
time: 46.1 us; the launch traced here: 45.9 us
  Pallas kernels  15.9 us (34%)
  starting transfers between devices  15.9 us (34%)
  waiting for transfers between devices  12 us (26%)
  between operations  1.46 us (3%)
  local copies, waits for them, and re-layouts  0.7 us (2%)
    ppermute x14, starting transfers between devices, swap(): lax.ppermute(value, axis, [(i, i ^ bit) for i in range(lax.axis_size(axis...  12.9 us
    ppermute x14, waiting for transfers between devices, swap(): lax.ppermute(value, axis, [(i, i ^ bit) for i in range(lax.axis_size(axis...  10.1 us
    pallas_call x1, Pallas kernels, features(): pl.pallas_call(functools.partial(features_kernel, fanout=fanout, cuts=cut...  5.96 us
    pallas_call x1, Pallas kernels, back(): pl.pallas_call(functools.partial(back_kernel, pieces=len(pieces), members...  4.95 us
    ppermute x4, starting transfers between devices, neighbour_pairs(): return lax.ppermute(value, axis, moves)  3 us
    pallas_call x1, Pallas kernels, merge(): pl.pallas_call(merge_kernel, in_specs=[HBM, HBM], out_specs=VMEM, out_sha...  2.03 us
    ppermute x4, waiting for transfers between devices, neighbour_pairs(): return lax.ppermute(value, axis, moves)  1.89 us
    pallas_call x1, Pallas kernels, expert_product(): pl.pallas_call(functools.partial(expert_kernel, scale=scale), in_specs=[V...  1.54 us
  transfers between devices with their start and end apart: 18, of which 7 were waited for; matrix products, arithmetic and copies ran while one was open for 0% of the time, Pallas kernels for 27%

profile of v15, /device:TPU:0, one launch (start us, length us, event | category | flops | bytes accessed | tf_op | source)
XLA Modules:
  0.0 45.9 jit_solution(17714195932628193199)
XLA Ops:
  0.6 0.7 %copy-done = f32[2,32]{1,0:T(2,128)S(1)} copy-done((f32[2,32]{1,0:T(2,128)S(1)}, f32[2,32]{1,0:T(2,128)}, u32[]{:S(2)}) %copy-start) | copy-done | bytes 280
  1.4 2.0 %merge.1.refs_0_ = bf16[2,272,128]{2,1,0:T(8,128)(2,1)S(1)} custom-call(f32[2,32]{1,0:T(2,128)S(1)} %copy-done, bf16[32,69632]{1,0:T(8,128)(2,1)} %experts_ref.1), custom_call_target="tpu_custom_call" | custom-call | flops 53477376 | bytes 2228224 | tf_op jit(solution)/shard_map/merge/pallas_call | solution.py:102
  3.4 5.1 %collective-permute-start.6 = (bf16[2,272,128]{2,1,0:T(8,128)(2,1)S(1)}, bf16[2,272,128]{2,1,0:T(8,128)(2,1)S(1)}, u32[]{:S(2)}, u32[]{:S(2)}) collective-permute-start(bf16[2,272,128]{2,1,0:T(8,128)(2,1)S(1)} %merge.1.refs_0_), channel_id=1, source_target_pairs={{0,12},{4,8},{8,4},{12,0},{1,13},{5,9},{9,5},{13,1},{2,14},{6,10},... | collective-permute-start | bytes 417800 | tf_op jit(solution)/shard_map/ppermute | solution.py:507
  8.5 0.0 collective-permute-start.5
  8.5 0.6 %collective-permute-start.4 = (bf16[2,272,128]{2,1,0:T(8,128)(2,1)S(1)}, bf16[2,272,128]{2,1,0:T(8,128)(2,1)S(1)}, u32[]{:S(2)}, u32[]{:S(2)}) collective-permute-start(bf16[2,272,128]{2,1,0:T(8,128)(2,1)S(1)} %merge.1.refs_0_), channel_id=1, source_target_pairs={{0,8},{4,12},{8,0},{12,4},{1,9},{5,13},{9,1},{13,5},{2,10},{6,14},... | collective-permute-start | bytes 417800 | tf_op jit(solution)/shard_map/ppermute | solution.py:507
  9.9 6.0 %features.1 = (bf16[544,128]{1,0:T(8,128)(2,1)S(1)}, bf16[544,128]{1,0:T(8,128)(2,1)S(1)}, bf16[544,128]{1,0:T(8,128)(2,1)S(1)}, bf16[544,128]{1,0:T(8,128)(2,1)...) custom-call(s32[1]{0:T(128)S(6)} %copy.13.live_in_ref, ...), custom_call_target="tpu_custom_call" | custom-call | flops 8999999488 | bytes 7000000 | tf_op jit(solution)/shard_map/features/pallas_call | solution.py:224
  15.8 0.1 collective-permute-start
  15.9 0.5 %collective-permute-start.1 = (bf16[544,128]{1,0:T(8,128)(2,1)S(1)}, bf16[544,128]{1,0:T(8,128)(2,1)S(1)}, u32[]{:S(2)}, u32[]{:S(2)}) collective-permute-start(bf16[544,128]{1,0:T(8,128)(2,1)S(1)} %get-tuple-element.45), channel_id=1, source_target_pairs={{0,1},{1,0},{2,3},{3,2},{4,5},{5,4},{6,7},{7,6},{8,9},{9,8},{10,11... | collective-permute-start | bytes 417800 | tf_op jit(solution)/shard_map/ppermute | solution.py:507
  16.4 0.0 collective-permute-done.6.refs_3_
  16.4 0.1 collective-permute-start.2
  16.5 0.4 collective-permute-start.3
  16.9 3.4 %collective-permute-done.4.refs_1_ = bf16[2,272,128]{2,1,0:T(8,128)(2,1)S(1)} collective-permute-done((bf16[2,272,128]{2,1,0:T(8,128)(2,1)S(1)}, bf16[2,272,128]{2,1,0:T(8,128)(2,1)S(1)}, u32[]{:S(2)}, u32[]{:S(2)}) %collective-permute-start.4) | collective-permute-done | bytes 139296 | tf_op jit(solution)/shard_map/ppermute | solution.py:507
  20.3 0.0 collective-permute-done.refs_0_
  20.3 0.0 collective-permute-done.1.refs_1_
  20.3 0.0 collective-permute-done.2.refs_2_
  20.3 0.1 collective-permute-start.7
  20.4 0.2 pair_sum.1
  20.6 2.5 %collective-permute-start.8 = (bf16[544,128]{1,0:T(8,128)(2,1)S(1)}, bf16[544,128]{1,0:T(8,128)(2,1)S(1)}, u32[]{:S(2)}, u32[]{:S(2)}) collective-permute-start(bf16[544,128]{1,0:T(8,128)(2,1)S(1)} %get-tuple-element.59), channel_id=1, source_target_pairs={{0,12},{4,8},{8,4},{12,0},{1,13},{5,9},{9,5},{13,1},{2,14},{6,10},... | collective-permute-start | bytes 417800 | tf_op jit(solution)/shard_map/ppermute | solution.py:507
  23.1 1.9 %collective-permute-start.10 = (bf16[544,128]{1,0:T(8,128)(2,1)S(1)}, bf16[544,128]{1,0:T(8,128)(2,1)S(1)}, u32[]{:S(2)}, u32[]{:S(2)}) collective-permute-start(bf16[544,128]{1,0:T(8,128)(2,1)S(1)} %get-tuple-element.61), channel_id=1, source_target_pairs={{0,8},{4,12},{8,0},{12,4},{1,9},{5,13},{9,1},{13,5},{2,10},{6,14},... | collective-permute-start | bytes 417800 | tf_op jit(solution)/shard_map/ppermute | solution.py:507
  25.1 4.9 %back.1 = (f32[9,128,128]{2,1,0:T(8,128)S(1)}, bf16[9,32,128]{2,1,0:T(8,128)(2,1)S(1)}, bf16[9,32,128]{2,1,0:T(8,128)(2,1)S(1)}, bf16[9,32,128]{2,1,0:T(8,128)(2,1)S(1)}, bf16[9,32,128]{2,1,0:T(8,128)(2,1)S(1)}) custom-call(f32[8,1024]{1,0:T(8,128)S(1)} %get-tuple-element.42.edge_ref, f32[1,1024]{1,0:T(1,128)S(1)} %bitcast.10, f32[3,3,1024]{2,1,0:T(4,128)S(1)} %copy-done.5, ...), custom_call_target="tpu_custom_call" | custom-call | flops 8999999488 | bytes 7000000 | tf_op jit(solution)/shard_map/back/pallas_call | solution.py:342
  30.0 2.5 %collective-permute-start.11 = (bf16[9,32,128]{2,1,0:T(8,128)(2,1)S(1)}, bf16[9,32,128]{2,1,0:T(8,128)(2,1)S(1)}, u32[]{:S(2)}, u32[]{:S(2)}) collective-permute-start(bf16[9,32,128]{2,1,0:T(8,128)(2,1)S(1)} %get-tuple-element.66), channel_id=1, source_target_pairs={{4,8},{8,4},{12,0},{0,12},{5,9},{9,5},{13,1},{1,13},{6,10},{10,6},... | collective-permute-start | bytes 221192 | tf_op jit(solution)/shard_map/ppermute | solution.py:516
  32.5 0.5 %collective-permute-start.13 = (bf16[9,32,128]{2,1,0:T(8,128)(2,1)S(1)}, bf16[9,32,128]{2,1,0:T(8,128)(2,1)S(1)}, u32[]{:S(2)}, u32[]{:S(2)}) collective-permute-start(bf16[9,32,128]{2,1,0:T(8,128)(2,1)S(1)} %get-tuple-element.68), channel_id=1, source_target_pairs={{1,2},{2,1},{3,0},{0,3},{5,6},{6,5},{7,4},{4,7},{9,10},{10,9},{11,... | collective-permute-start | bytes 221192 | tf_op jit(solution)/shard_map/ppermute | solution.py:516
  33.0 1.9 %collective-permute-done.9.refs_2_ = bf16[544,128]{1,0:T(8,128)(2,1)S(1)} collective-permute-done((bf16[544,128]{1,0:T(8,128)(2,1)S(1)}, bf16[544,128]{1,0:T(8,128)(2,1)S(1)}, u32[]{:S(2)}, u32[]{:S(2)}) %collective-permute-start.9) | collective-permute-done | bytes 139296 | tf_op jit(solution)/shard_map/ppermute | solution.py:507
  34.9 0.9 %collective-permute-done.10.refs_3_ = bf16[544,128]{1,0:T(8,128)(2,1)S(1)} collective-permute-done((bf16[544,128]{1,0:T(8,128)(2,1)S(1)}, bf16[544,128]{1,0:T(8,128)(2,1)S(1)}, u32[]{:S(2)}, u32[]{:S(2)}) %collective-permute-start.10) | collective-permute-done | bytes 139296 | tf_op jit(solution)/shard_map/ppermute | solution.py:507
  35.8 0.1 total_sum.1.refs_0_
  35.9 1.1 %collective-permute-done.11.a_ref = bf16[9,32,128]{2,1,0:T(8,128)(2,1)S(1)} collective-permute-done((bf16[9,32,128]{2,1,0:T(8,128)(2,1)S(1)}, bf16[9,32,128]{2,1,0:T(8,128)(2,1)S(1)}, u32[]{:S(2)}, u32[]{:S(2)}) %collective-permute-start.11) | collective-permute-done | bytes 73760 | tf_op jit(solution)/shard_map/ppermute | solution.py:516
  37.0 0.8 %collective-permute-done.12.b_ref = bf16[9,32,128]{2,1,0:T(8,128)(2,1)S(1)} collective-permute-done((bf16[9,32,128]{2,1,0:T(8,128)(2,1)S(1)}, bf16[9,32,128]{2,1,0:T(8,128)(2,1)S(1)}, u32[]{:S(2)}, u32[]{:S(2)}) %collective-permute-start.12) | collective-permute-done | bytes 73760 | tf_op jit(solution)/shard_map/ppermute | solution.py:516
  37.8 1.5 %collective-permute-start.15 = (bf16[544,128]{1,0:T(8,128)(2,1)S(1)}, bf16[544,128]{1,0:T(8,128)(2,1)S(1)}, u32[]{:S(2)}, u32[]{:S(2)}) collective-permute-start(bf16[544,128]{1,0:T(8,128)(2,1)S(1)} %total_sum.1.refs_0_), channel_id=1, source_target_pairs={{0,2},{1,3},{2,0},{3,1},{4,6},{5,7},{6,4},{7,5},{8,10},{9,11},{10,... | collective-permute-start | bytes 417800 | tf_op jit(solution)/shard_map/ppermute | solution.py:507
  39.3 1.2 %finish.1 = bf16[9,128,128]{2,1,0:T(8,128)(2,1)} custom-call(s32[4,32]{1,0:T(4,128)S(1)} %copy-done.1, f32[9,128,128]{2,1,0:T(8,128)S(1)} %get-tuple-element.71.own_ref, bf16[9,32,128]{2,1,0:T(8,128)(2,1)S(1)} %collective-permute-done.11.a_ref, bf16[9,32,128]{2,1,0:T(8,128)(2,1)S(1)} %collective-permute-done.12.b_ref, ...), custom_call_target="tpu_custom_call" | custom-call | flops 100000000 | bytes 2000000 | tf_op jit(solution)/shard_map/finish/pallas_call | solution.py:495
  40.4 2.5 %collective-permute-done.15.refs_1_ = bf16[544,128]{1,0:T(8,128)(2,1)S(1)} collective-permute-done((bf16[544,128]{1,0:T(8,128)(2,1)S(1)}, bf16[544,128]{1,0:T(8,128)(2,1)S(1)}, u32[]{:S(2)}, u32[]{:S(2)}) %collective-permute-start.15) | collective-permute-done | bytes 139296 | tf_op jit(solution)/shard_map/ppermute | solution.py:507
  43.0 1.4 %collective-permute-done.17.refs_3_ = bf16[544,128]{1,0:T(8,128)(2,1)S(1)} collective-permute-done((bf16[544,128]{1,0:T(8,128)(2,1)S(1)}, bf16[544,128]{1,0:T(8,128)(2,1)S(1)}, u32[]{:S(2)}, u32[]{:S(2)}) %collective-permute-start.17) | collective-permute-done | bytes 139296 | tf_op jit(solution)/shard_map/ppermute | solution.py:507
  44.3 1.5 %expert_product.1 = f32[8,69632]{1,0:T(8,128)} custom-call(f32[2,32]{1,0:T(2,128)S(1)} %copy-done, bf16[544,128]{1,0:T(8,128)(2,1)S(1)} %total_sum.1.refs_0_, bf16[544,128]{1,0:T(8,128)(2,1)S(1)} %collective-permute-done.15.refs_1_, bf16[544,128]{1,0:T(8,128)(2,1)S(1)} %collective-permute-done.16.refs_2_, bf16[544,128]{1,0:T(8,128)(2,1)S(1)} %collective-permute-done.17.refs_3_), custom_call_target="tpu_custom_call" | custom-call | flops 1000000 | bytes 4000000 | tf_op jit(solution)/shard_map/expert_product/pallas_call | solution.py:460
  (30 shorter events, 0.1 us)
Async XLA Ops:
  0.6 0.7 %copy-start = (f32[2,32]{1,0:T(2,128)S(1)}, f32[2,32]{1,0:T(2,128)}, u32[]{:S(2)}) copy-start(f32[2,32]{1,0:T(2,128)} %coef_ref.1) | copy-start | bytes 772
  1.3 8.5 %copy-start.2 = (bf16[256,9,128]{2,0,1:T(8,128)(2,1)S(1)}, bf16[256,9,128]{2,0,1:T(8,128)(2,1)}, u32[]{:S(2)}) copy-start(bf16[256,9,128]{2,0,1:T(8,128)(2,1)} %param.11) | copy-start | bytes 1769476
  1.3 8.5 %copy-start.3 = (bf16[128,9,128]{2,0,1:T(8,128)(2,1)S(1)}, bf16[128,9,128]{2,0,1:T(8,128)(2,1)}, u32[]{:S(2)}) copy-start(bf16[128,9,128]{2,0,1:T(8,128)(2,1)} %param.12) | copy-start | bytes 884740
  1.3 8.5 %copy-start.4 = (f32[5,5,1024]{2,1,0:T(8,128)S(1)}, f32[5,5,1024]{2,1,0:T(8,128)}, u32[]{:S(2)}) copy-start(f32[5,5,1024]{2,1,0:T(8,128)} %two_ref.3) | copy-start | bytes 307204
  1.3 8.5 %copy-start.5 = (f32[3,3,1024]{2,1,0:T(4,128)S(1)}, f32[3,3,1024]{2,1,0:T(4,128)}, u32[]{:S(2)}) copy-start(f32[3,3,1024]{2,1,0:T(4,128)} %one_ref.3) | copy-start | bytes 110596
  1.3 8.5 %copy-start.6 = (s32[128,8]{0,1:T(8,128)S(1)}, s32[128,8]{0,1:T(8,128)}, u32[]{:S(2)}) copy-start(s32[128,8]{0,1:T(8,128)} %param.13) | copy-start | bytes 12292
  1.3 8.5 %copy-start.7 = (f32[1024]{0:T(1024)S(1)}, f32[1024]{0:T(1024)}, u32[]{:S(2)}) copy-start(f32[1024]{0:T(1024)} %param.14) | copy-start | bytes 12292
  1.3 8.5 %copy-start.8 = (s32[128]{0:T(128)S(1)}, s32[128]{0:T(128)}, u32[]{:S(2)}) copy-start(s32[128]{0:T(128)} %param.18) | copy-start | bytes 1540
  3.4 13.0 %collective-permute-start.6 = (bf16[2,272,128]{2,1,0:T(8,128)(2,1)S(1)}, bf16[2,272,128]{2,1,0:T(8,128)(2,1)S(1)}, u32[]{:S(2)}, u32[]{:S(2)}) collective-permute-start(bf16[2,272,128]{2,1,0:T(8,128)(2,1)S(1)} %merge.1.refs_0_), channel_id=1, source_target_pairs={{0,12},{4,8},{8,4},{12,0},{1,13},{5,9},{9,5},{13,1},{2,14},{6,10},... | collective-permute-start | bytes 417800 | tf_op jit(solution)/shard_map/ppermute | solution.py:507
  8.5 8.0 %collective-permute-start.5 = (bf16[2,272,128]{2,1,0:T(8,128)(2,1)S(1)}, bf16[2,272,128]{2,1,0:T(8,128)(2,1)S(1)}, u32[]{:S(2)}, u32[]{:S(2)}) collective-permute-start(bf16[2,272,128]{2,1,0:T(8,128)(2,1)S(1)} %merge.1.refs_0_), channel_id=1, source_target_pairs={{0,4},{4,0},{8,12},{12,8},{1,5},{5,1},{9,13},{13,9},{2,6},{6,2},{1... | collective-permute-start | bytes 417800 | tf_op jit(solution)/shard_map/ppermute | solution.py:507
  8.5 11.8 %collective-permute-start.4 = (bf16[2,272,128]{2,1,0:T(8,128)(2,1)S(1)}, bf16[2,272,128]{2,1,0:T(8,128)(2,1)S(1)}, u32[]{:S(2)}, u32[]{:S(2)}) collective-permute-start(bf16[2,272,128]{2,1,0:T(8,128)(2,1)S(1)} %merge.1.refs_0_), channel_id=1, source_target_pairs={{0,8},{4,12},{8,0},{12,4},{1,9},{5,13},{9,1},{13,5},{2,10},{6,14},... | collective-permute-start | bytes 417800 | tf_op jit(solution)/shard_map/ppermute | solution.py:507
  15.8 4.4 %collective-permute-start = (bf16[544,128]{1,0:T(8,128)(2,1)S(1)}, bf16[544,128]{1,0:T(8,128)(2,1)S(1)}, u32[]{:S(2)}, u32[]{:S(2)}) collective-permute-start(bf16[544,128]{1,0:T(8,128)(2,1)S(1)} %get-tuple-element.44), channel_id=1, source_target_pairs={{0,1},{1,0},{2,3},{3,2},{4,5},{5,4},{6,7},{7,6},{8,9},{9,8},{10,11... | collective-permute-start | bytes 417800 | tf_op jit(solution)/shard_map/ppermute | solution.py:507
  15.9 4.4 %collective-permute-start.1 = (bf16[544,128]{1,0:T(8,128)(2,1)S(1)}, bf16[544,128]{1,0:T(8,128)(2,1)S(1)}, u32[]{:S(2)}, u32[]{:S(2)}) collective-permute-start(bf16[544,128]{1,0:T(8,128)(2,1)S(1)} %get-tuple-element.45), channel_id=1, source_target_pairs={{0,1},{1,0},{2,3},{3,2},{4,5},{5,4},{6,7},{7,6},{8,9},{9,8},{10,11... | collective-permute-start | bytes 417800 | tf_op jit(solution)/shard_map/ppermute | solution.py:507
  16.4 3.9 %collective-permute-start.2 = (bf16[544,128]{1,0:T(8,128)(2,1)S(1)}, bf16[544,128]{1,0:T(8,128)(2,1)S(1)}, u32[]{:S(2)}, u32[]{:S(2)}) collective-permute-start(bf16[544,128]{1,0:T(8,128)(2,1)S(1)} %get-tuple-element.46), channel_id=1, source_target_pairs={{0,1},{1,0},{2,3},{3,2},{4,5},{5,4},{6,7},{7,6},{8,9},{9,8},{10,11... | collective-permute-start | bytes 417800 | tf_op jit(solution)/shard_map/ppermute | solution.py:507
  16.5 3.8 %collective-permute-start.3 = (bf16[544,128]{1,0:T(8,128)(2,1)S(1)}, bf16[544,128]{1,0:T(8,128)(2,1)S(1)}, u32[]{:S(2)}, u32[]{:S(2)}) collective-permute-start(bf16[544,128]{1,0:T(8,128)(2,1)S(1)} %get-tuple-element.47), channel_id=1, source_target_pairs={{0,1},{1,0},{2,3},{3,2},{4,5},{5,4},{6,7},{7,6},{8,9},{9,8},{10,11... | collective-permute-start | bytes 417800 | tf_op jit(solution)/shard_map/ppermute | solution.py:507
  20.3 4.7 %collective-permute-start.7 = (bf16[4,2,272,128]{3,2,1,0:T(8,128)(2,1)S(1)}, bf16[4,2,272,128]{3,2,1,0:T(8,128)(2,1)S(1)}, u32[]{:S(2)}, u32[]{:S(2)}) collective-permute-start(bf16[4,2,272,128]{3,2,1,0:T(8,128)(2,1)S(1)} %pack.1.rest_0_), channel_id=1, source_target_pairs={{0,1},{1,0},{2,3},{3,2},{4,5},{5,4},{6,7},{7,6},{8,9},{9,8},{10,11... | collective-permute-start | bytes 1671176 | tf_op jit(solution)/shard_map/ppermute | solution.py:507
  20.6 11.9 %collective-permute-start.8 = (bf16[544,128]{1,0:T(8,128)(2,1)S(1)}, bf16[544,128]{1,0:T(8,128)(2,1)S(1)}, u32[]{:S(2)}, u32[]{:S(2)}) collective-permute-start(bf16[544,128]{1,0:T(8,128)(2,1)S(1)} %get-tuple-element.59), channel_id=1, source_target_pairs={{0,12},{4,8},{8,4},{12,0},{1,13},{5,9},{9,5},{13,1},{2,14},{6,10},... | collective-permute-start | bytes 417800 | tf_op jit(solution)/shard_map/ppermute | solution.py:507
  23.1 11.7 %collective-permute-start.9 = (bf16[544,128]{1,0:T(8,128)(2,1)S(1)}, bf16[544,128]{1,0:T(8,128)(2,1)S(1)}, u32[]{:S(2)}, u32[]{:S(2)}) collective-permute-start(bf16[544,128]{1,0:T(8,128)(2,1)S(1)} %get-tuple-element.60), channel_id=1, source_target_pairs={{0,4},{4,0},{8,12},{12,8},{1,5},{5,1},{9,13},{13,9},{2,6},{6,2},{1... | collective-permute-start | bytes 417800 | tf_op jit(solution)/shard_map/ppermute | solution.py:507
  23.1 12.7 %collective-permute-start.10 = (bf16[544,128]{1,0:T(8,128)(2,1)S(1)}, bf16[544,128]{1,0:T(8,128)(2,1)S(1)}, u32[]{:S(2)}, u32[]{:S(2)}) collective-permute-start(bf16[544,128]{1,0:T(8,128)(2,1)S(1)} %get-tuple-element.61), channel_id=1, source_target_pairs={{0,8},{4,12},{8,0},{12,4},{1,9},{5,13},{9,1},{13,5},{2,10},{6,14},... | collective-permute-start | bytes 417800 | tf_op jit(solution)/shard_map/ppermute | solution.py:507
  25.1 14.2 %copy-start.1 = (s32[4,32]{1,0:T(4,128)S(1)}, s32[4,32]{1,0:T(4,128)}, u32[]{:S(2)}) copy-start(s32[4,32]{1,0:T(4,128)} %send_ref.1) | copy-start | bytes 1540
  30.0 7.0 %collective-permute-start.11 = (bf16[9,32,128]{2,1,0:T(8,128)(2,1)S(1)}, bf16[9,32,128]{2,1,0:T(8,128)(2,1)S(1)}, u32[]{:S(2)}, u32[]{:S(2)}) collective-permute-start(bf16[9,32,128]{2,1,0:T(8,128)(2,1)S(1)} %get-tuple-element.66), channel_id=1, source_target_pairs={{4,8},{8,4},{12,0},{0,12},{5,9},{9,5},{13,1},{1,13},{6,10},{10,6},... | collective-permute-start | bytes 221192 | tf_op jit(solution)/shard_map/ppermute | solution.py:516
  32.5 5.2 %collective-permute-start.12 = (bf16[9,32,128]{2,1,0:T(8,128)(2,1)S(1)}, bf16[9,32,128]{2,1,0:T(8,128)(2,1)S(1)}, u32[]{:S(2)}, u32[]{:S(2)}) collective-permute-start(bf16[9,32,128]{2,1,0:T(8,128)(2,1)S(1)} %get-tuple-element.67), channel_id=1, source_target_pairs={{0,4},{4,0},{8,12},{12,8},{1,5},{5,1},{9,13},{13,9},{2,6},{6,2},{1... | collective-permute-start | bytes 221192 | tf_op jit(solution)/shard_map/ppermute | solution.py:516
  32.5 5.2 %collective-permute-start.13 = (bf16[9,32,128]{2,1,0:T(8,128)(2,1)S(1)}, bf16[9,32,128]{2,1,0:T(8,128)(2,1)S(1)}, u32[]{:S(2)}, u32[]{:S(2)}) collective-permute-start(bf16[9,32,128]{2,1,0:T(8,128)(2,1)S(1)} %get-tuple-element.68), channel_id=1, source_target_pairs={{1,2},{2,1},{3,0},{0,3},{5,6},{6,5},{7,4},{4,7},{9,10},{10,9},{11,... | collective-permute-start | bytes 221192 | tf_op jit(solution)/shard_map/ppermute | solution.py:516
  34.9 2.9 %collective-permute-start.14 = (bf16[9,32,128]{2,1,0:T(8,128)(2,1)S(1)}, bf16[9,32,128]{2,1,0:T(8,128)(2,1)S(1)}, u32[]{:S(2)}, u32[]{:S(2)}) collective-permute-start(bf16[9,32,128]{2,1,0:T(8,128)(2,1)S(1)} %get-tuple-element.69), channel_id=1, source_target_pairs={{0,1},{1,0},{2,3},{3,2},{4,5},{5,4},{6,7},{7,6},{8,9},{9,8},{10,11... | collective-permute-start | bytes 221192 | tf_op jit(solution)/shard_map/ppermute | solution.py:516
  37.8 5.2 %collective-permute-start.15 = (bf16[544,128]{1,0:T(8,128)(2,1)S(1)}, bf16[544,128]{1,0:T(8,128)(2,1)S(1)}, u32[]{:S(2)}, u32[]{:S(2)}) collective-permute-start(bf16[544,128]{1,0:T(8,128)(2,1)S(1)} %total_sum.1.refs_0_), channel_id=1, source_target_pairs={{0,2},{1,3},{2,0},{3,1},{4,6},{5,7},{6,4},{7,5},{8,10},{9,11},{10,... | collective-permute-start | bytes 417800 | tf_op jit(solution)/shard_map/ppermute | solution.py:507
  39.3 3.7 %collective-permute-start.16 = (bf16[544,128]{1,0:T(8,128)(2,1)S(1)}, bf16[544,128]{1,0:T(8,128)(2,1)S(1)}, u32[]{:S(2)}, u32[]{:S(2)}) collective-permute-start(bf16[544,128]{1,0:T(8,128)(2,1)S(1)} %total_sum.1.refs_0_), channel_id=1, source_target_pairs={{0,1},{1,0},{2,3},{3,2},{4,5},{5,4},{6,7},{7,6},{8,9},{9,8},{10,11... | collective-permute-start | bytes 417800 | tf_op jit(solution)/shard_map/ppermute | solution.py:507
  43.0 1.4 %collective-permute-start.17 = (bf16[544,128]{1,0:T(8,128)(2,1)S(1)}, bf16[544,128]{1,0:T(8,128)(2,1)S(1)}, u32[]{:S(2)}, u32[]{:S(2)}) collective-permute-start(bf16[544,128]{1,0:T(8,128)(2,1)S(1)} %collective-permute-done.15.refs_1_), channel_id=1, source_target_pairs={{0,1},{1,0},{2,3},{3,2},{4,5},{5,4},{6,7},{7,6},{8,9},{9,8},{10,11... | collective-permute-start | bytes 417800 | tf_op jit(solution)/shard_map/ppermute | solution.py:507
